TPU v7x, 32 devices: a whole 2x2x4 slice. The times are simulated.
32 devices in a mesh: section: 2 (over core), dp: 4 (over z), tensor: 4 (over y, x).
Axes of the slice: x: 2, y: 2, z: 4, core: 2. Of those that a mesh axis runs over, the one named last changes fastest.
Arguments:
- tokens: bfloat16 [2, 8192, 768], P(None, ('dp', 'tensor')), may hold values from -6 to 6
- cotangent: bfloat16 [2, 8192, 768], P(None, ('dp', 'tensor')), may hold values from -6 to 6
- segments: int32 [2, 4, 2048], P(None, 'dp'), may hold values from 0 to 2, never falling along the last dimension, each value on 1 to 1536 neighbouring positions
- heads_in: float32 [2, 3, 768, 768], P('section', None, 'dp', 'tensor'), may hold values from -0.21875 to 0.21875
- heads_out: float32 [2, 768, 768], P('section', 'tensor', 'dp'), may hold values from -1.75 to 1.75
- gate_up: float32 [2, 2, 768, 3072], P('section', None, 'dp', 'tensor'), may hold values from -0.21875 to 0.21875
- project_down: float32 [2, 3072, 768], P('section', 'tensor', 'dp'), may hold values from -0.109375 to 0.109375
- norm_gain: float32 [2, 2, 768], P('section'), may hold values from 0.5 to 1.5
- norm_bias: float32 [2, 2, 768], P('section'), may hold values from -3 to 3
- heads_in_first: float32 [2, 3, 768, 768], P('section', None, 'dp', 'tensor'), may hold values from -26.714922 to 26.714922
- heads_in_second: float32 [2, 3, 768, 768], P('section', None, 'dp', 'tensor'), may hold values from 0.8192 to 13.1072
- heads_out_first: float32 [2, 768, 768], P('section', 'tensor', 'dp'), may hold values from -8.448 to 8.448
- heads_out_second: float32 [2, 768, 768], P('section', 'tensor', 'dp'), may hold values from 0.08192 to 1.31072
- gate_up_first: float32 [2, 2, 768, 3072], P('section', None, 'dp', 'tensor'), may hold values from -42.24 to 42.24
- gate_up_second: float32 [2, 2, 768, 3072], P('section', None, 'dp', 'tensor'), may hold values from 2.048 to 32.768
- project_down_first: float32 [2, 3072, 768], P('section', 'tensor', 'dp'), may hold values from -46.271603 to 46.271603
- project_down_second: float32 [2, 3072, 768], P('section', 'tensor', 'dp'), may hold values from 2.4576 to 39.3216
- norm_first: float32 [2, 2, 2, 768], P('section'), may hold values from -84.48 to 84.48
- norm_second: float32 [2, 2, 2, 768], P('section'), may hold values from 8.192 to 131.072
Outputs:
- layer_out: bfloat16 [2, 2, 8192, 768], P('section', None, ('dp', 'tensor'))
- input_grads: float32 [2, 2, 8192, 768], P('section', None, ('dp', 'tensor'))
- heads_in_new: float32 [2, 3, 768, 768], P('section', None, 'dp', 'tensor')
- heads_in_first_new: float32 [2, 3, 768, 768], P('section', None, 'dp', 'tensor')
- heads_in_second_new: float32 [2, 3, 768, 768], P('section', None, 'dp', 'tensor')
- heads_out_new: float32 [2, 768, 768], P('section', 'tensor', 'dp')
- heads_out_first_new: float32 [2, 768, 768], P('section', 'tensor', 'dp')
- heads_out_second_new: float32 [2, 768, 768], P('section', 'tensor', 'dp')
- gate_up_new: float32 [2, 2, 768, 3072], P('section', None, 'dp', 'tensor')
- gate_up_first_new: float32 [2, 2, 768, 3072], P('section', None, 'dp', 'tensor')
- gate_up_second_new: float32 [2, 2, 768, 3072], P('section', None, 'dp', 'tensor')
- project_down_new: float32 [2, 3072, 768], P('section', 'tensor', 'dp')
- project_down_first_new: float32 [2, 3072, 768], P('section', 'tensor', 'dp')
- project_down_second_new: float32 [2, 3072, 768], P('section', 'tensor', 'dp')
- norm_params_new: float32 [2, 2, 2, 768], P('section')
- norm_first_new: float32 [2, 2, 2, 768], P('section')
- norm_second_new: float32 [2, 2, 2, 768], P('section')
- trust_norms: float32 [2, 4, 2], P('section')
Inputs may be any that keep to these rules, and one draw needn't show every extreme that they name: `segments`: along each sequence of 2048 rows the numbers never fall; each of the 3 documents has 1 to 1536 rows, and some document has exactly 1536.
All inputs are finite; a program needn't handle non-finite values.
Results may differ from a plain program's by a relative error of at most 0.03.
Values may be sent and summed in bfloat16 or wider, within the bound.
No kernel may reach another device: no remote copies, remote signals or barrier semaphores. Data moves between devices by JAX's collectives and lax.ppermute only.
A program may use at most 320 MiB of HBM per device.

v0:
```python
import jax
import jax.numpy as jnp
from jax import lax
from jax.sharding import PartitionSpec as P

HEAD = 64
WINDOW = 1024
BLOCK = 512
STEP = 10


BETA_ONE = 0.9
BETA_TWO = 0.999
ADAM_EPS = 1e-06
DECAY_RATE = 0.01
LEARN_RATE = 0.2
NORM_EPS = 1e-05
ROPE_BASE = 1000.0


def passed_along(shard, axis, by):
    size = lax.axis_size(axis)
    pairs = [(i, i + by) for i in range(size) if 0 <= i + by < size]
    return lax.ppermute(shard, axis, pairs)


def rope_tables(length):
    half_size = HEAD // 2
    freq_vals = ROPE_BASE ** (-jnp.arange(half_size, dtype=jnp.float32) * 2.0 / HEAD)
    angles = jnp.arange(length, dtype=jnp.float32)[:, None] * freq_vals[None, :]
    cos_tab = jnp.concatenate([jnp.cos(angles), jnp.cos(angles)], axis=1)
    sine_tab = jnp.concatenate([jnp.sin(angles), jnp.sin(angles)], axis=1)
    return (cos_tab, sine_tab)


def rotate_fwd(values, cos_tab, sine_tab):
    half_size = HEAD // 2
    turned = jnp.concatenate([-values[..., half_size:], values[..., :half_size]], axis=-1)
    return values * cos_tab[:, None, :] + turned * sine_tab[:, None, :]


def rotate_back(grad_vals, cos_tab, sine_tab):
    half_size = HEAD // 2
    sined = grad_vals * sine_tab[:, None, :]
    turned = jnp.concatenate([sined[..., half_size:], -sined[..., :half_size]], axis=-1)
    return grad_vals * cos_tab[:, None, :] + turned


def norm_fwd(values, gain_row, bias_row):
    mean_val = jnp.mean(values, axis=-1, keepdims=True)
    centred = values - mean_val
    variance = jnp.mean(centred * centred, axis=-1, keepdims=True)
    inv_std = lax.rsqrt(variance + NORM_EPS)
    normed = centred * inv_std
    return (normed * gain_row + bias_row, normed, inv_std)


def norm_back(grad_out, normed, inv_std, gain_row):
    grad_gain = jnp.sum(grad_out * normed, axis=0)
    grad_bias = jnp.sum(grad_out, axis=0)
    grad_normed = grad_out * gain_row
    grad_vals = inv_std * (
        grad_normed
        - jnp.mean(grad_normed, axis=-1, keepdims=True)
        - normed * jnp.mean(grad_normed * normed, axis=-1, keepdims=True)
    )
    return (grad_vals, grad_gain, grad_bias)


def block_scores(query_rows, key_rot, query_seg, seq_seg, row_start):
    length = key_rot.shape[0]
    positions = jnp.arange(length, dtype=jnp.int32)
    query_pos = row_start + jnp.arange(BLOCK, dtype=jnp.int32)
    scores = jnp.einsum(
        "qhd,khd->hqk", query_rows, key_rot, preferred_element_type=jnp.float32
    ) * HEAD ** (-0.5)
    allowed = (query_seg[:, None] == seq_seg[None, :]) & (
        jnp.abs(query_pos[:, None] - positions[None, :]) < WINDOW
    )
    return jnp.where(allowed[None], scores, -1e30)


def attend_forward(query_rot, key_rot, value_low, seq_seg):
    length = query_rot.shape[0]
    blocks = length // BLOCK

    def one_block(block_index):
        row_start = block_index * BLOCK
        query_rows = lax.dynamic_slice_in_dim(query_rot, row_start, BLOCK, 0)
        query_seg = lax.dynamic_slice_in_dim(seq_seg, row_start, BLOCK, 0)
        scores = block_scores(query_rows, key_rot, query_seg, seq_seg, row_start)
        top_score = jnp.max(scores, axis=-1, keepdims=True)
        exp_scores = jnp.exp(scores - top_score)
        total_sum = jnp.sum(exp_scores, axis=-1, keepdims=True)
        probs_low = (exp_scores / total_sum).astype(jnp.bfloat16)
        head_rows = jnp.einsum(
            "hqk,khd->qhd", probs_low, value_low, preferred_element_type=jnp.float32
        )
        return (head_rows.astype(jnp.bfloat16), (top_score + jnp.log(total_sum))[..., 0])

    head_rows, log_sums = lax.map(one_block, jnp.arange(blocks, dtype=jnp.int32))
    return (head_rows.reshape(length, -1), log_sums)


def attend_backward(query_rot, key_rot, value_low, grad_heads, log_sums, seq_seg):
    length = query_rot.shape[0]
    blocks = length // BLOCK
    score_scale = HEAD ** (-0.5)

    def one_block(running, block_index):
        grad_key, grad_value = running
        row_start = block_index * BLOCK
        query_rows = lax.dynamic_slice_in_dim(query_rot, row_start, BLOCK, 0)
        query_seg = lax.dynamic_slice_in_dim(seq_seg, row_start, BLOCK, 0)
        grad_rows = lax.dynamic_slice_in_dim(grad_heads, row_start, BLOCK, 0)
        scores = block_scores(query_rows, key_rot, query_seg, seq_seg, row_start)
        probs_f = jnp.exp(scores - log_sums[block_index][:, :, None])
        grad_probs = jnp.einsum(
            "qhd,khd->hqk", grad_rows, value_low, preferred_element_type=jnp.float32
        )
        delta_sum = jnp.sum(probs_f * grad_probs, axis=-1, keepdims=True)
        grad_scores = (probs_f * (grad_probs - delta_sum)).astype(jnp.bfloat16)
        grad_query = (
            jnp.einsum("hqk,khd->qhd", grad_scores, key_rot, preferred_element_type=jnp.float32)
            * score_scale
        )
        grad_key = (
            grad_key
            + jnp.einsum(
                "hqk,qhd->khd", grad_scores, query_rows, preferred_element_type=jnp.float32
            )
            * score_scale
        )
        grad_value = grad_value + jnp.einsum(
            "hqk,qhd->khd",
            probs_f.astype(jnp.bfloat16),
            grad_rows,
            preferred_element_type=jnp.float32,
        )
        return ((grad_key, grad_value), grad_query)

    zero_state = jnp.zeros(query_rot.shape, jnp.float32)
    (grad_key, grad_value), grad_query = lax.scan(
        one_block, (zero_state, zero_state), jnp.arange(blocks, dtype=jnp.int32)
    )
    return (grad_query.reshape(query_rot.shape), grad_key, grad_value)


def forward_layer(section_feed, weights, gain_rows, biases, seq_seg):
    in_matrix, out_matrix, gate_matrix, down_matrix = weights
    rows_full = lax.all_gather(section_feed, "tensor", axis=0, tiled=True)
    length = rows_full.shape[0]
    cos_tab, sine_tab = rope_tables(length)
    projected = jnp.einsum("ld,cde->lce", rows_full, in_matrix, preferred_element_type=jnp.float32)
    head_count = projected.shape[2] // HEAD
    query_rot = rotate_fwd(
        projected[:, 0].reshape(length, head_count, HEAD), cos_tab, sine_tab
    ).astype(jnp.bfloat16)
    key_rot = rotate_fwd(
        projected[:, 1].reshape(length, head_count, HEAD), cos_tab, sine_tab
    ).astype(jnp.bfloat16)
    value_low = projected[:, 2].reshape(length, head_count, HEAD).astype(jnp.bfloat16)
    heads_flat, log_sums = attend_forward(query_rot, key_rot, value_low, seq_seg)
    attn_out = lax.psum_scatter(
        jnp.dot(heads_flat, out_matrix, preferred_element_type=jnp.float32),
        "tensor",
        scatter_dimension=0,
        tiled=True,
    )
    mixed_one = section_feed.astype(jnp.float32) + attn_out
    hidden, normed_one, inv_one = norm_fwd(mixed_one, gain_rows[0], biases[0])
    hidden_full = lax.all_gather(hidden.astype(jnp.bfloat16), "tensor", axis=0, tiled=True)
    gate_vals = jnp.einsum(
        "ld,cdf->lcf", hidden_full, gate_matrix, preferred_element_type=jnp.float32
    )
    inner_act = (jax.nn.silu(gate_vals[:, 0]) * gate_vals[:, 1]).astype(jnp.bfloat16)
    ffn_out = lax.psum_scatter(
        jnp.dot(inner_act, down_matrix, preferred_element_type=jnp.float32).astype(jnp.bfloat16),
        "tensor",
        scatter_dimension=0,
        tiled=True,
    ).astype(jnp.float32)
    mixed_two = hidden + ffn_out
    output, normed_two, inv_two = norm_fwd(mixed_two, gain_rows[1], biases[1])
    kept_state = (
        rows_full,
        query_rot,
        key_rot,
        value_low,
        heads_flat,
        log_sums,
        normed_one,
        inv_one,
        hidden_full,
        gate_vals,
        inner_act,
        normed_two,
        inv_two,
        seq_seg,
    )
    return (output, kept_state)


def backward_layer(grad_out, kept_state, weights, gain_rows):
    in_matrix, out_matrix, gate_matrix, down_matrix = weights
    (
        rows_full,
        query_rot,
        key_rot,
        value_low,
        heads_flat,
        log_sums,
        normed_one,
        inv_one,
        hidden_full,
        gate_vals,
        inner_act,
        normed_two,
        inv_two,
        seq_seg,
    ) = kept_state
    length = rows_full.shape[0]
    cos_tab, sine_tab = rope_tables(length)
    grad_mixed_two, gain_two, bias_two = norm_back(grad_out, normed_two, inv_two, gain_rows[1])
    ffn_full = lax.all_gather(grad_mixed_two.astype(jnp.bfloat16), "tensor", axis=0, tiled=True)
    grad_inner = jnp.einsum("ld,fd->lf", ffn_full, down_matrix, preferred_element_type=jnp.float32)
    grad_down = jnp.einsum("lf,ld->fd", inner_act, ffn_full, preferred_element_type=jnp.float32)
    gate_part = gate_vals[:, 0]
    up_part = gate_vals[:, 1]
    sig_gate = jax.nn.sigmoid(gate_part)
    grad_gate = grad_inner * up_part * (sig_gate * (1.0 + gate_part * (1.0 - sig_gate)))
    grad_up = grad_inner * (gate_part * sig_gate)
    grad_gate_up = jnp.stack([grad_gate, grad_up], axis=1).astype(jnp.bfloat16)
    grad_gate_w = jnp.einsum(
        "ld,lcf->cdf", hidden_full, grad_gate_up, preferred_element_type=jnp.float32
    )
    row_piece = grad_gate_up
    hidden_sum = lax.psum_scatter(
        jnp.einsum(
            "lcf,cdf->ld", row_piece, gate_matrix, preferred_element_type=jnp.float32
        ).astype(jnp.bfloat16),
        "tensor",
        scatter_dimension=0,
        tiled=True,
    ).astype(jnp.float32)
    grad_hidden = grad_mixed_two + hidden_sum
    grad_mixed_one, gain_one, bias_one = norm_back(grad_hidden, normed_one, inv_one, gain_rows[0])
    attn_full = lax.all_gather(grad_mixed_one.astype(jnp.bfloat16), "tensor", axis=0, tiled=True)
    grad_heads = jnp.einsum(
        "ld,ed->le", attn_full, out_matrix, preferred_element_type=jnp.float32
    ).astype(jnp.bfloat16)
    grad_out_w = jnp.einsum("le,ld->ed", heads_flat, attn_full, preferred_element_type=jnp.float32)
    grad_query, grad_key, grad_value = attend_backward(
        query_rot, key_rot, value_low, grad_heads.reshape(query_rot.shape), log_sums, seq_seg
    )
    grad_proj = jnp.stack(
        [
            rotate_back(grad_query, cos_tab, sine_tab).reshape(length, -1),
            rotate_back(grad_key, cos_tab, sine_tab).reshape(length, -1),
            grad_value.reshape(length, -1),
        ],
        axis=1,
    ).astype(jnp.bfloat16)
    grad_in_w = jnp.einsum("ld,lce->cde", rows_full, grad_proj, preferred_element_type=jnp.float32)
    row_piece = grad_proj
    rows_sum = lax.psum_scatter(
        jnp.einsum("lce,cde->ld", row_piece, in_matrix, preferred_element_type=jnp.float32).astype(
            jnp.bfloat16
        ),
        "tensor",
        scatter_dimension=0,
        tiled=True,
    ).astype(jnp.float32)
    grad_feed = grad_mixed_one + rows_sum
    norm_grads = jnp.stack([jnp.stack([gain_one, gain_two]), jnp.stack([bias_one, bias_two])])
    return (grad_feed, (grad_in_w, grad_out_w, grad_gate_w, grad_down), norm_grads)


def pick_slot(chosen, fresh, older):
    return jax.tree.map(lambda new_val, old_val: jnp.where(chosen, new_val, old_val), fresh, older)


def reduce_grads(four_grads):
    return (
        lax.psum_scatter(
            four_grads[0].astype(jnp.bfloat16), "dp", scatter_dimension=1, tiled=True
        ).astype(jnp.float32),
        lax.psum_scatter(
            four_grads[1].astype(jnp.bfloat16), "dp", scatter_dimension=1, tiled=True
        ).astype(jnp.float32),
        lax.psum_scatter(
            four_grads[2].astype(jnp.bfloat16), "dp", scatter_dimension=1, tiled=True
        ).astype(jnp.float32),
        lax.psum_scatter(
            four_grads[3].astype(jnp.bfloat16), "dp", scatter_dimension=1, tiled=True
        ).astype(jnp.float32),
    )


def lamb_parts(weight, gradient, first_old, second):
    first_new = BETA_ONE * first_old + (1.0 - BETA_ONE) * gradient
    second_new = BETA_TWO * second + (1.0 - BETA_TWO) * gradient * gradient
    update = (
        first_new
        / (1.0 - BETA_ONE**STEP)
        / (jnp.sqrt(second_new / (1.0 - BETA_TWO**STEP)) + ADAM_EPS)
        + DECAY_RATE * weight
    )
    return (first_new, second_new, update)


def body(
    tokens,
    cotangent,
    segments,
    heads_in,
    heads_out,
    gate_up,
    project_down,
    norm_gain,
    norm_bias,
    heads_in_first,
    heads_in_second,
    heads_out_first,
    heads_out_second,
    gate_up_first,
    gate_up_second,
    project_down_first,
    project_down_second,
    norm_first,
    norm_second,
):
    section_index = lax.axis_index("section")
    micro_count = tokens.shape[0]
    masters = (heads_in[0], heads_out[0], gate_up[0], project_down[0])
    gathered = (
        lax.all_gather(masters[0].astype(jnp.bfloat16), "dp", axis=1, tiled=True),
        lax.all_gather(masters[1].astype(jnp.bfloat16), "dp", axis=1, tiled=True),
        lax.all_gather(masters[2].astype(jnp.bfloat16), "dp", axis=1, tiled=True),
        lax.all_gather(masters[3].astype(jnp.bfloat16), "dp", axis=1, tiled=True),
    )
    gain_rows = norm_gain[0]
    biases = norm_bias[0]
    incoming = jnp.zeros(tokens.shape[1:], jnp.bfloat16)
    kept_slots = []
    output_slots = []
    for tick_num in range(micro_count + 1):
        micro_index = tick_num - section_index
        slot_index = jnp.clip(micro_index, 0, micro_count - 1)
        section_feed = jnp.where(
            section_index == 0, tokens[min(tick_num, micro_count - 1)], incoming
        )
        seq_seg = lax.dynamic_index_in_dim(segments, slot_index, 0, keepdims=False)[0]
        result, kept_state = forward_layer(section_feed, gathered, gain_rows, biases, seq_seg)
        if tick_num == 0:
            kept_slots = [kept_state for slot_num in range(micro_count)]
            output_slots = [result for slot_num in range(micro_count)]
        else:
            for slot_num in range(micro_count):
                chosen = micro_index == slot_num
                kept_slots[slot_num] = pick_slot(chosen, kept_state, kept_slots[slot_num])
                output_slots[slot_num] = jnp.where(chosen, result, output_slots[slot_num])
        if tick_num < micro_count:
            incoming = passed_along(result.astype(jnp.bfloat16), "section", 1)
    stacked_kept = jax.tree.map(lambda *items: jnp.stack(items), *kept_slots)
    grad_incoming = jnp.zeros(tokens.shape[1:], jnp.bfloat16)
    grad_slots = []
    for tick_num in range(micro_count + 1):
        micro_index = tick_num - (1 - section_index)
        is_valid = (micro_index >= 0) & (micro_index < micro_count)
        slot_index = jnp.clip(micro_index, 0, micro_count - 1)
        grad_feed = jnp.where(
            section_index == 1,
            cotangent[min(tick_num, micro_count - 1)].astype(jnp.float32),
            grad_incoming.astype(jnp.float32),
        )
        kept_state = jax.tree.map(
            lambda item: lax.dynamic_index_in_dim(item, slot_index, 0, keepdims=False), stacked_kept
        )
        grad_inputs, matrix_grads, norm_grads = backward_layer(
            grad_feed, kept_state, gathered, gain_rows
        )
        masked = jax.tree.map(lambda item: jnp.where(is_valid, item, 0.0), matrix_grads)
        norm_masked = jnp.where(is_valid, norm_grads, 0.0)
        grad_total = masked if tick_num == 0 else jax.tree.map(jnp.add, grad_total, masked)
        norm_acc = norm_masked if tick_num == 0 else norm_acc + norm_masked
        sent = grad_inputs.astype(jnp.bfloat16)
        record = jnp.where(section_index == 1, sent.astype(jnp.float32), grad_inputs)
        if tick_num == 0:
            grad_slots = [record for slot_num in range(micro_count)]
        else:
            for slot_num in range(micro_count):
                grad_slots[slot_num] = jnp.where(
                    micro_index == slot_num, record, grad_slots[slot_num]
                )
        if tick_num < micro_count:
            grad_incoming = passed_along(sent, "section", -1)
    grad_shards = reduce_grads(grad_total)
    firsts = (heads_in_first[0], heads_out_first[0], gate_up_first[0], project_down_first[0])
    seconds = (heads_in_second[0], heads_out_second[0], gate_up_second[0], project_down_second[0])
    parts = [
        lamb_parts(masters[pos_num], grad_shards[pos_num], firsts[pos_num], seconds[pos_num])
        for pos_num in range(4)
    ]
    update_squares = jnp.stack([jnp.sum(item[2] * item[2]) for item in parts])
    squares = jnp.concatenate(
        [jnp.stack([jnp.sum(matrix * matrix) for matrix in masters]), update_squares]
    )
    norm_total, square_total = lax.psum((norm_acc, squares), ("dp", "tensor"))
    weight_norms = jnp.sqrt(square_total[:4])
    update_norms = jnp.sqrt(square_total[-4:])
    new_mats = [
        masters[pos_num]
        - LEARN_RATE * (weight_norms[pos_num] / update_norms[pos_num]) * parts[pos_num][2]
        for pos_num in range(4)
    ]
    norm_now = jnp.stack([gain_rows, biases])
    norm_first_new, norm_second_new, norm_update = lamb_parts(
        norm_now, norm_total, norm_first[0], norm_second[0]
    )
    norm_wn = jnp.sqrt(jnp.sum(norm_now * norm_now, axis=-1, keepdims=True))
    norm_un = jnp.sqrt(jnp.sum(norm_update * norm_update, axis=-1, keepdims=True))
    norm_params_new = norm_now - LEARN_RATE * (norm_wn / norm_un) * norm_update
    trust_norms = jnp.stack([weight_norms, update_norms], axis=1)
    layer_out = jnp.stack(output_slots).astype(jnp.bfloat16)
    input_grads = jnp.stack(grad_slots)
    return (
        layer_out[None],
        input_grads[None],
        new_mats[0][None],
        parts[0][0][None],
        parts[0][1][None],
        new_mats[1][None],
        parts[1][0][None],
        parts[1][1][None],
        new_mats[2][None],
        parts[2][0][None],
        parts[2][1][None],
        new_mats[3][None],
        parts[3][0][None],
        parts[3][1][None],
        norm_params_new[None],
        norm_first_new[None],
        norm_second_new[None],
        trust_norms[None],
    )


def solution(mesh):
    placed = (
        P(None, ("dp", "tensor"), None),
        P(None, ("dp", "tensor"), None),
        P(None, "dp", None),
        P("section", None, "dp", "tensor"),
        P("section", "tensor", "dp"),
        P("section", None, "dp", "tensor"),
        P("section", "tensor", "dp"),
        P("section", None, None),
        P("section", None, None),
        P("section", None, "dp", "tensor"),
        P("section", None, "dp", "tensor"),
        P("section", "tensor", "dp"),
        P("section", "tensor", "dp"),
        P("section", None, "dp", "tensor"),
        P("section", None, "dp", "tensor"),
        P("section", "tensor", "dp"),
        P("section", "tensor", "dp"),
        P("section", None, None, None),
        P("section", None, None, None),
    )
    return jax.shard_map(
        body,
        mesh=mesh,
        in_specs=placed,
        out_specs=(
            P("section", None, ("dp", "tensor"), None),
            P("section", None, ("dp", "tensor"), None),
            P("section", None, "dp", "tensor"),
            P("section", None, "dp", "tensor"),
            P("section", None, "dp", "tensor"),
            P("section", "tensor", "dp"),
            P("section", "tensor", "dp"),
            P("section", "tensor", "dp"),
            P("section", None, "dp", "tensor"),
            P("section", None, "dp", "tensor"),
            P("section", None, "dp", "tensor"),
            P("section", "tensor", "dp"),
            P("section", "tensor", "dp"),
            P("section", "tensor", "dp"),
            P("section", None, None, None),
            P("section", None, None, None),
            P("section", None, None, None),
            P("section", None, None),
        ),
        check_vma=False,
    )
```

profile of v0, /device:TPU:0, one launch (start us, length us, event | category | flops | bytes accessed | tf_op | source)
XLA Modules:
  0.0 2418.6 jit_solution(2307928194513978309)
XLA Ops:
  10.9 31.4 %all_gather.49 = bf16[3,768,192]{2,0,1:T(4,128)(2,1)S(1)} all-gather(bf16[3,192,192]{2,0,1:T(4,128)(2,1)S(1)} %bitcast.1014), channel_id=1, replica_groups=mesh['section'=2,'dp'=4,'tensor'=4] {'dp'}, dimensions={1}, use_global_device_ids=true | all-gather | bytes 1105920 | tf_op jit(solution)/shard_map/all_gather | solution.py:337
  43.3 14.5 all_gather.50
  70.1 90.5 %while.81 = (s32[]{:T(128)}, bf16[4,512,3,64]{1,3,2,0:T(8,128)(2,1)S(1)}, f32[4,3,512]{2,1,0:T(4,128)S(1)}, s32[4]{0:T(128)S(1)}, s32[2048]{0:T(1024)S(1)}, /*in...) while((s32[]{:T(128)}, ...), condition=%wide.region_3.4_spmd, body=%wide.region_0.3_spmd.sunk | while | flops 848395264 | bytes 47132908 | solution.py:101
  79.5 6.8 fusion.578
  102.0 6.8 fusion.578
  124.5 6.8 fusion.578
  147.0 6.8 fusion.578
  167.6 69.7 %reduce-scatter.21.cloned.1.call-done = f32[512,768]{1,0:T(8,128)} async-done(((f32[2048,768]{1,0:T(8,128)}), f32[512,768]{1,0:T(8,128)}) %reduce-scatter.21.cloned.1.call-update) | async-done | bytes 1572880 | tf_op jit(solution)/shard_map/reduce_scatter | solution.py:164
  243.2 42.0 %all-gather.16.cloned.1.call-done = bf16[2048,768]{1,0:T(8,128)(2,1)} async-done(((bf16[512,768]{1,0:T(8,128)(2,1)}), bf16[2048,768]{1,0:T(8,128)(2,1)}) %all-gather.16.cloned.1.call-update) | async-done | bytes 3145744 | tf_op jit(solution)/shard_map/all_gather | solution.py:172
  285.2 10.1 fusion.196
  295.3 22.1 all-gather.20.cloned.1.call-done
  317.4 10.0 convolution_convert_fusion.2
  327.5 43.1 %reduce-scatter.23.cloned.1.call-done = bf16[512,768]{1,0:T(8,128)(2,1)} async-done(((bf16[2048,768]{1,0:T(8,128)(2,1)}), bf16[512,768]{1,0:T(8,128)(2,1)}) %reduce-scatter.23.cloned.1.call-update) | async-done | bytes 786448 | tf_op jit(solution)/shard_map/reduce_scatter | solution.py:177
  378.3 43.8 %all-gather.22.cloned.1.call-done = bf16[2048,768]{1,0:T(8,128)(2,1)} async-done(((bf16[512,768]{1,0:T(8,128)(2,1)}), bf16[2048,768]{1,0:T(8,128)(2,1)}) %all-gather.22.cloned.1.call-update) | async-done | bytes 3145744 | tf_op jit(solution)/shard_map/all_gather | solution.py:151
  432.3 89.9 %while.82 = (s32[]{:T(128)}, bf16[4,512,3,64]{1,3,2,0:T(8,128)(2,1)S(1)}, f32[4,3,512]{2,1,0:T(4,128)S(1)}, s32[4]{0:T(128)S(1)}, s32[2048]{0:T(1024)S(1)}, /*in...) while((s32[]{:T(128)}, ...), condition=%wide.region_13.14_spmd, body=%wide.region_10.13_spmd.sunk | while | flops 848395264 | bytes 43987156 | solution.py:101
  441.5 6.8 fusion.584
  463.9 6.8 fusion.584
  486.3 6.8 fusion.584
  527.3 70.3 %reduce-scatter.25.cloned.1.call-done = f32[512,768]{1,0:T(8,128)} async-done(((f32[2048,768]{1,0:T(8,128)}), f32[512,768]{1,0:T(8,128)}) %reduce-scatter.25.cloned.1.call-update) | async-done | bytes 1572880 | tf_op jit(solution)/shard_map/reduce_scatter | solution.py:164
  601.3 43.4 %all-gather.24.cloned.1.call-done = bf16[2048,768]{1,0:T(8,128)(2,1)} async-done(((bf16[512,768]{1,0:T(8,128)(2,1)}), bf16[2048,768]{1,0:T(8,128)(2,1)}) %all-gather.24.cloned.1.call-update) | async-done | bytes 3145744 | tf_op jit(solution)/shard_map/all_gather | solution.py:172
  644.8 7.7 fusion.194
  662.1 43.9 %reduce-scatter.27.cloned.1.call-done = bf16[512,768]{1,0:T(8,128)(2,1)} async-done(((bf16[2048,768]{1,0:T(8,128)(2,1)}), bf16[512,768]{1,0:T(8,128)(2,1)}) %reduce-scatter.27.cloned.1.call-update) | async-done | bytes 786448 | tf_op jit(solution)/shard_map/reduce_scatter | solution.py:177
  714.0 43.9 %all-gather.26.cloned.1.call-done = bf16[2048,768]{1,0:T(8,128)(2,1)} async-done(((bf16[512,768]{1,0:T(8,128)(2,1)}), bf16[2048,768]{1,0:T(8,128)(2,1)}) %all-gather.26.cloned.1.call-update) | async-done | bytes 3145744 | tf_op jit(solution)/shard_map/all_gather | solution.py:151
  769.6 91.5 %while.83 = (s32[]{:T(128)}, bf16[4,512,3,64]{1,3,2,0:T(8,128)(2,1)S(1)}, f32[4,3,512]{2,1,0:T(4,128)}, s32[4]{0:T(128)S(1)}, s32[2048]{0:T(1024)S(1)}, /*index=...) while((s32[]{:T(128)}, ...), condition=%wide.region_23.24_spmd, body=%wide.region_20.23_spmd.sunk | while | flops 848395264 | bytes 43983060 | solution.py:101
  778.5 6.8 fusion.590
  801.3 6.8 fusion.590
  824.2 6.8 fusion.590
  866.6 69.7 %reduce-scatter.29.cloned.1.call-done = f32[512,768]{1,0:T(8,128)} async-done(((f32[2048,768]{1,0:T(8,128)}), f32[512,768]{1,0:T(8,128)}) %reduce-scatter.29.cloned.1.call-update) | async-done | bytes 1572880 | tf_op jit(solution)/shard_map/reduce_scatter | solution.py:164
  940.9 44.1 %all-gather.28.cloned.1.call-done = bf16[2048,768]{1,0:T(8,128)(2,1)} async-done(((bf16[512,768]{1,0:T(8,128)(2,1)}), bf16[2048,768]{1,0:T(8,128)(2,1)}) %all-gather.28.cloned.1.call-update) | async-done | bytes 3145744 | tf_op jit(solution)/shard_map/all_gather | solution.py:172
  985.0 7.7 fusion.192
  1002.1 44.0 %reduce-scatter.31.cloned.1.call-done = bf16[512,768]{1,0:T(8,128)(2,1)} async-done(((bf16[2048,768]{1,0:T(8,128)(2,1)}), bf16[512,768]{1,0:T(8,128)(2,1)}) %reduce-scatter.31.cloned.1.call-update) | async-done | bytes 786448 | tf_op jit(solution)/shard_map/reduce_scatter | solution.py:177
  1059.2 22.2 select_bitcast_fusion
  1081.4 26.4 %fusion.115 = (f32[2048,2,768]{2,0,1:T(8,128)}, f32[2048,2,768]{2,0,1:T(8,128)}, f32[2048,2,768]{2,0,1:T(8,128)}) fusion(s32[]{:T(128)S(6)} %min.22, f32[1,2048,2,768]{3,1,2,0:T(8,128)} %get-tuple-element.736, f32[1,2048,2,768]{3,1,2,0:T(8,128)} %get-tuple-element.735, s32[]{:T(128)S(6)} %min.24, s32[]{:T(128)S(6)} %min.23), kind=kLoop, calls=%fused_computation.148 | loop fusion | flops 9437184 | bytes 62914572 | tf_op jit(solution)/shard_map/jit(dynamic_index_in_dim)/squeeze | solution.py:378
  1107.8 9.3 fusion.210
  1127.7 42.7 %reduce-scatter.33.cloned.1.call-done = bf16[512,768]{1,0:T(8,128)(2,1)} async-done(((bf16[2048,768]{1,0:T(8,128)(2,1)}), bf16[512,768]{1,0:T(8,128)(2,1)}) %reduce-scatter.33.cloned.1.call-update) | async-done | bytes 786448 | tf_op jit(solution)/shard_map/reduce_scatter | solution.py:238
  1194.7 24.8 %all-gather.32.cloned.1.call-done = bf16[2048,768]{1,0:T(8,128)(2,1)} async-done(((bf16[512,768]{1,0:T(8,128)(2,1)}), bf16[2048,768]{1,0:T(8,128)(2,1)}) %all-gather.32.cloned.1.call-update) | async-done | bytes 3145744 | tf_op jit(solution)/shard_map/all_gather | solution.py:248
  1224.9 179.6 %while.84 = (s32[]{:T(128)}, f32[2048,3,64]{0,2,1:T(8,128)}, f32[2048,3,64]{0,2,1:T(8,128)}, f32[4,512,3,64]{1,0,3,2:T(4,128)}, s32[4]{0:T(128)S(1)}, /*index=5*...) while((s32[]{:T(128)}, f32[2048,3,64]{0,2,1:T(8,128)}, ...), condition=%wide.region_37.38_spmd.clone, body=%wide.region_35.37_spmd.clone.sunk | while | flops 2067758080 | bytes 145682832 | solution.py:143
  1260.5 8.7 dynamic_update_slice.54
  1305.5 8.7 dynamic_update_slice.54
  1350.6 8.7 dynamic_update_slice.54
  1395.6 8.7 dynamic_update_slice.54
  1421.8 44.0 %reduce-scatter.35.cloned.1.call-done = bf16[512,768]{1,0:T(8,128)(2,1)} async-done(((bf16[2048,768]{1,0:T(8,128)(2,1)}), bf16[512,768]{1,0:T(8,128)(2,1)}) %reduce-scatter.35.cloned.1.call-update) | async-done | bytes 786448 | tf_op jit(solution)/shard_map/reduce_scatter | solution.py:266
  1476.4 43.9 %all-gather.34.cloned.1.call-done = bf16[2048,768]{1,0:T(8,128)(2,1)} async-done(((bf16[512,768]{1,0:T(8,128)(2,1)}), bf16[2048,768]{1,0:T(8,128)(2,1)}) %all-gather.34.cloned.1.call-update) | async-done | bytes 3145744 | tf_op jit(solution)/shard_map/all_gather | solution.py:225
  1520.3 9.3 fusion.211
  1538.7 44.0 %reduce-scatter.37.cloned.1.call-done = bf16[512,768]{1,0:T(8,128)(2,1)} async-done(((bf16[2048,768]{1,0:T(8,128)(2,1)}), bf16[512,768]{1,0:T(8,128)(2,1)}) %reduce-scatter.37.cloned.1.call-update) | async-done | bytes 786448 | tf_op jit(solution)/shard_map/reduce_scatter | solution.py:238
  1587.9 43.8 %all-gather.36.cloned.1.call-done = bf16[2048,768]{1,0:T(8,128)(2,1)} async-done(((bf16[512,768]{1,0:T(8,128)(2,1)}), bf16[2048,768]{1,0:T(8,128)(2,1)}) %all-gather.36.cloned.1.call-update) | async-done | bytes 3145744 | tf_op jit(solution)/shard_map/all_gather | solution.py:248
  1636.2 178.3 %while.85 = (s32[]{:T(128)}, f32[2048,3,64]{0,2,1:T(8,128)}, f32[2048,3,64]{0,2,1:T(8,128)}, f32[4,512,3,64]{1,0,3,2:T(4,128)}, s32[4]{0:T(128)S(1)}, /*index=5*...) while((s32[]{:T(128)}, f32[2048,3,64]{0,2,1:T(8,128)}, ...), condition=%wide.region_46.47_spmd.clone, body=%wide.region_44.46_spmd.clone.sunk | while | flops 2067758080 | bytes 148830640 | solution.py:143
  1670.9 8.6 dynamic_update_slice.55
  1715.9 8.6 dynamic_update_slice.55
  1760.8 8.6 dynamic_update_slice.55
  1805.7 8.6 dynamic_update_slice.55
  1831.0 43.9 %reduce-scatter.39.cloned.1.call-done = bf16[512,768]{1,0:T(8,128)(2,1)} async-done(((bf16[2048,768]{1,0:T(8,128)(2,1)}), bf16[512,768]{1,0:T(8,128)(2,1)}) %reduce-scatter.39.cloned.1.call-update) | async-done | bytes 786448 | tf_op jit(solution)/shard_map/reduce_scatter | solution.py:266
  1885.6 44.0 %all-gather.38.cloned.1.call-done = bf16[2048,768]{1,0:T(8,128)(2,1)} async-done(((bf16[512,768]{1,0:T(8,128)(2,1)}), bf16[2048,768]{1,0:T(8,128)(2,1)}) %all-gather.38.cloned.1.call-update) | async-done | bytes 3145744 | tf_op jit(solution)/shard_map/all_gather | solution.py:225
  1929.6 9.3 fusion.212
  1960.5 16.8 select_select_fusion
  2011.2 8.5 fusion.155
  2034.6 8.8 fusion.153
  2043.4 10.7 fusion.213
  2059.6 178.9 %while.86 = (s32[]{:T(128)}, f32[2048,3,64]{0,2,1:T(8,128)}, f32[2048,3,64]{0,2,1:T(8,128)}, f32[4,512,3,64]{1,0,3,2:T(4,128)}, s32[4]{0:T(128)S(1)}, /*index=5*...) while((s32[]{:T(128)}, f32[2048,3,64]{0,2,1:T(8,128)}, ...), condition=%wide.region_55.56_spmd.clone, body=%wide.region_53.55_spmd.clone.sunk | while | flops 2067758080 | bytes 148830640 | solution.py:143
  2094.5 8.6 dynamic_update_slice.56
  2139.7 8.6 dynamic_update_slice.56
  2184.7 8.6 dynamic_update_slice.56
  2229.7 8.6 dynamic_update_slice.56
  2314.1 74.8 %all-reduce = (f32[8]{0:T(128)S(1)}, f32[2,2,768]{2,1,0:T(2,128)S(1)}) all-reduce(f32[8]{0:T(128)S(1)} %concatenate.206, f32[2,2,768]{2,1,0:T(2,128)} %fusion.364), channel_id=1, replica_groups=mesh['section'=2,'dp'=4,'tensor'=4] {'dp','tensor'}, use_global_device_ids=true, to_apply=%region_69.70 | all-reduce | flops 3080 | bytes 24640 | tf_op jit(solution)/shard_map/psum | solution.py:409
  (1168 shorter events, 991.5 us)
Async XLA Ops:
  8.0 51.6 %all-gather.42.cloned.1.call-start = ((), (), s32[]{:S(2)}) async-start(), calls=%async_computation.43 | async-start | bytes 3932160 | tf_op jit(solution)/shard_map/all_gather | solution.py:151
  10.3 227.0 %reduce-scatter.21.cloned.1.call-start = ((), (), s32[]{:S(2)}) async-start(), calls=%async_computation.16 | async-start | bytes 7864320 | tf_op jit(solution)/shard_map/reduce_scatter | solution.py:164
  57.7 103.8 %copy-start.65 = (bf16[192,768]{0,1:T(8,128)(2,1)}, bf16[192,768]{0,1:T(8,128)(2,1)S(1)}, u32[]{:S(2)}) copy-start(bf16[192,768]{0,1:T(8,128)(2,1)S(1)} %all_gather.50) | copy-start | bytes 884740
  165.3 71.9 %copy-start.94 = (bf16[2,512,768]{2,1,0:T(8,128)(2,1)S(1)}, bf16[2,512,768]{2,1,0:T(8,128)(2,1)}, u32[]{:S(2)}) copy-start(bf16[2,512,768]{2,1,0:T(8,128)(2,1)} %param.31) | copy-start | bytes 4718596
  165.3 77.9 %all-gather.18.cloned.1.call-start = ((), (), s32[]{:S(2)}) async-start(), calls=%async_computation.18 | async-start | bytes 2949120 | tf_op jit(solution)/shard_map/all_gather | solution.py:339
  167.4 117.8 %all-gather.16.cloned.1.call-start = ((), (), s32[]{:S(2)}) async-start(), calls=%async_computation.17 | async-start | bytes 3932160 | tf_op jit(solution)/shard_map/all_gather | solution.py:172
  167.5 203.1 %copy-start.166 = (f32[768]{0:T(1024)}, f32[768]{0:T(1024)S(1)}, u32[]{:S(2)}) copy-start(f32[768]{0:T(1024)S(1)} %get-tuple-element.540) | copy-start | bytes 9220
  167.5 205.9 %copy-start.178 = (f32[768]{0:T(1024)}, f32[768]{0:T(1024)S(1)}, u32[]{:S(2)}) copy-start(f32[768]{0:T(1024)S(1)} %get-tuple-element.539) | copy-start | bytes 9220
  167.6 203.0 %copy-start.183 = (f32[768]{0:T(1024)}, f32[768]{0:T(1024)S(1)}, u32[]{:S(2)}) copy-start(f32[768]{0:T(1024)S(1)} %get-tuple-element.542) | copy-start | bytes 9220
  167.6 205.8 %copy-start.192 = (f32[768]{0:T(1024)}, f32[768]{0:T(1024)S(1)}, u32[]{:S(2)}) copy-start(f32[768]{0:T(1024)S(1)} %get-tuple-element.541) | copy-start | bytes 9220
  238.9 131.7 %copy-start.31 = (f32[512,768]{1,0:T(8,128)}, f32[512,768]{1,0:T(8,128)S(1)}, u32[]{:S(2)}) copy-start(f32[512,768]{1,0:T(8,128)S(1)} %get-tuple-element.722) | copy-start | bytes 4718596
  238.9 131.6 %copy-start.195 = (f32[512]{0:T(512)}, f32[512]{0:T(512)S(1)}, u32[]{:S(2)}) copy-start(f32[512]{0:T(512)S(1)} %broadcast_multiply_fusion.25) | copy-start | bytes 6148
  240.0 130.6 %copy-start.198 = (f32[512]{0:T(512)}, f32[512]{0:T(512)S(1)}, u32[]{:S(2)}) copy-start(f32[512]{0:T(512)S(1)} %add_rsqrt_fusion.5) | copy-start | bytes 6148
  241.2 76.2 %all-gather.20.cloned.1.call-start = ((), (), s32[]{:S(2)}) async-start(), calls=%async_computation.19 | async-start | bytes 1474560 | tf_op jit(solution)/shard_map/all_gather | solution.py:340
  243.1 127.5 %reduce-scatter.23.cloned.1.call-start = ((), (), s32[]{:S(2)}) async-start(), calls=%async_computation.20 | async-start | bytes 3932160 | tf_op jit(solution)/shard_map/reduce_scatter | solution.py:177
  327.4 94.7 %all-gather.22.cloned.1.call-start = ((), (), s32[]{:S(2)}) async-start(), calls=%async_computation.21 | async-start | bytes 3932160 | tf_op jit(solution)/shard_map/all_gather | solution.py:151
  373.8 3.5 collective-permute-start
  378.3 219.3 %reduce-scatter.25.cloned.1.call-start = ((), (), s32[]{:S(2)}) async-start(), calls=%async_computation.22 | async-start | bytes 7864320 | tf_op jit(solution)/shard_map/reduce_scatter | solution.py:164
  527.2 70.4 %copy-start.85 = (bf16[512,768]{1,0:T(8,128)(2,1)S(1)}, bf16[512,768]{1,0:T(8,128)(2,1)}, u32[]{:S(2)}) copy-start(bf16[512,768]{1,0:T(8,128)(2,1)} %bitcast_select_fusion.3) | copy-start | bytes 2359300
  527.3 72.4 %copy-start.167 = (f32[768]{0:T(1024)S(1)}, f32[768]{0:T(1024)}, u32[]{:S(2)}) copy-start(f32[768]{0:T(1024)} %copy-done.166) | copy-start | bytes 9220
  527.3 72.4 %copy-start.184 = (f32[768]{0:T(1024)S(1)}, f32[768]{0:T(1024)}, u32[]{:S(2)}) copy-start(f32[768]{0:T(1024)} %copy-done.183) | copy-start | bytes 9220
  527.3 117.5 %all-gather.24.cloned.1.call-start = ((), (), s32[]{:S(2)}) async-start(), calls=%async_computation.23 | async-start | bytes 3932160 | tf_op jit(solution)/shard_map/all_gather | solution.py:172
  599.3 106.7 %copy-start.33 = (f32[512,768]{1,0:T(8,128)}, f32[512,768]{1,0:T(8,128)S(1)}, u32[]{:S(2)}) copy-start(f32[512,768]{1,0:T(8,128)S(1)} %get-tuple-element.718) | copy-start | bytes 4718596
  599.3 106.7 %copy-start.196 = (f32[512]{0:T(512)}, f32[512]{0:T(512)S(1)}, u32[]{:S(2)}) copy-start(f32[512]{0:T(512)S(1)} %broadcast_multiply_fusion.23) | copy-start | bytes 6148
  599.6 52.9 %copy-start.223 = (f32[512]{0:T(512)}, f32[512]{0:T(512)S(1)}, u32[]{:S(2)}) copy-start(f32[512]{0:T(512)S(1)} %multiply_reduce_fusion.17) | copy-start | bytes 6148
  599.6 106.3 %copy-start.201 = (f32[512]{0:T(512)}, f32[512]{0:T(512)S(1)}, u32[]{:S(2)}) copy-start(f32[512]{0:T(512)S(1)} %add_rsqrt_fusion.3) | copy-start | bytes 6148
  600.9 56.2 %copy-start.249 = (bf16[768,768]{0,1:T(8,128)(2,1)S(1)}, bf16[768,768]{0,1:T(8,128)(2,1)}, u32[]{:S(2)}) copy-start(bf16[768,768]{0,1:T(8,128)(2,1)} %all-gather.20.cloned.1.call-done) | copy-start | bytes 3538948
  600.9 105.1 %reduce-scatter.27.cloned.1.call-start = ((), (), s32[]{:S(2)}) async-start(), calls=%async_computation.24 | async-start | bytes 3932160 | tf_op jit(solution)/shard_map/reduce_scatter | solution.py:177
  662.0 95.8 %all-gather.26.cloned.1.call-start = ((), (), s32[]{:S(2)}) async-start(), calls=%async_computation.25 | async-start | bytes 3932160 | tf_op jit(solution)/shard_map/all_gather | solution.py:151
  708.8 49.1 %copy-start.143 = (bf16[3,768,192]{1,2,0:T(8,128)(2,1)S(1)}, bf16[3,768,192]{1,2,0:T(8,128)(2,1)}, u32[]{:S(2)}) copy-start(bf16[3,768,192]{1,2,0:T(8,128)(2,1)} %copy-done.141) | copy-start | bytes 2654212
  709.1 3.5 collective-permute-start.1
  713.7 222.6 %reduce-scatter.29.cloned.1.call-start = ((), (), s32[]{:S(2)}) async-start(), calls=%async_computation.26 | async-start | bytes 7864320 | tf_op jit(solution)/shard_map/reduce_scatter | solution.py:164
  866.1 70.2 %copy-start.84 = (bf16[512,768]{1,0:T(8,128)(2,1)S(1)}, bf16[512,768]{1,0:T(8,128)(2,1)}, u32[]{:S(2)}) copy-start(bf16[512,768]{1,0:T(8,128)(2,1)} %bitcast_select_fusion.2) | copy-start | bytes 2359300
  866.1 72.1 %copy-start.220 = (f32[512]{0:T(512)S(1)}, f32[512]{0:T(512)}, u32[]{:S(2)}) copy-start(f32[512]{0:T(512)} %copy-done.219) | copy-start | bytes 6148
  866.2 72.1 %copy-start.224 = (f32[512]{0:T(512)S(1)}, f32[512]{0:T(512)}, u32[]{:S(2)}) copy-start(f32[512]{0:T(512)} %copy-done.223) | copy-start | bytes 6148
  866.2 73.5 %copy-start.168 = (f32[768]{0:T(1024)S(1)}, f32[768]{0:T(1024)}, u32[]{:S(2)}) copy-start(f32[768]{0:T(1024)} %copy-done.166) | copy-start | bytes 9220
  866.2 73.4 %copy-start.185 = (f32[768]{0:T(1024)S(1)}, f32[768]{0:T(1024)}, u32[]{:S(2)}) copy-start(f32[768]{0:T(1024)} %copy-done.183) | copy-start | bytes 9220
  866.2 118.8 %all-gather.28.cloned.1.call-start = ((), (), s32[]{:S(2)}) async-start(), calls=%async_computation.27 | async-start | bytes 3932160 | tf_op jit(solution)/shard_map/all_gather | solution.py:172
  940.8 56.3 %copy-start.250 = (bf16[768,768]{0,1:T(8,128)(2,1)S(1)}, bf16[768,768]{0,1:T(8,128)(2,1)}, u32[]{:S(2)}) copy-start(bf16[768,768]{0,1:T(8,128)(2,1)} %all-gather.20.cloned.1.call-done) | copy-start | bytes 3538948
  940.8 105.2 %reduce-scatter.31.cloned.1.call-start = ((), (), s32[]{:S(2)}) async-start(), calls=%async_computation.28 | async-start | bytes 3932160 | tf_op jit(solution)/shard_map/reduce_scatter | solution.py:177
  1002.0 105.8 %all-gather.30.cloned.1.call-start = ((), (), s32[]{:S(2)}) async-start(), calls=%async_computation.29 | async-start | bytes 3932160 | tf_op jit(solution)/shard_map/all_gather | solution.py:225
  1059.0 111.5 %reduce-scatter.33.cloned.1.call-start = ((), (), s32[]{:S(2)}) async-start(), calls=%async_computation.30 | async-start | bytes 3932160 | tf_op jit(solution)/shard_map/reduce_scatter | solution.py:238
  1126.2 93.3 %all-gather.32.cloned.1.call-start = ((), (), s32[]{:S(2)}) async-start(), calls=%async_computation.31 | async-start | bytes 3932160 | tf_op jit(solution)/shard_map/all_gather | solution.py:248
  1175.6 290.2 %reduce-scatter.35.cloned.1.call-start = ((), (), s32[]{:S(2)}) async-start(), calls=%async_computation.32 | async-start | bytes 3932160 | tf_op jit(solution)/shard_map/reduce_scatter | solution.py:266
  1421.7 50.2 %copy-start.181 = (f32[768]{0:T(1024)S(1)}, f32[768]{0:T(1024)}, u32[]{:S(2)}) copy-start(f32[768]{0:T(1024)} %copy-done.178) | copy-start | bytes 9220
  1421.7 50.2 %copy-start.50 = (f32[1,512,768]{2,1,0:T(8,128)S(1)}, f32[1,512,768]{2,1,0:T(8,128)}, u32[]{:S(2)}) copy-start(f32[1,512,768]{2,1,0:T(8,128)} %copy-done.49) | copy-start | bytes 4718596
  1421.7 50.2 %copy-start.53 = (f32[1,512,768]{2,1,0:T(8,128)S(1)}, f32[1,512,768]{2,1,0:T(8,128)}, u32[]{:S(2)}) copy-start(f32[1,512,768]{2,1,0:T(8,128)} %copy-done.52) | copy-start | bytes 4718596
  1421.7 98.6 %all-gather.34.cloned.1.call-start = ((), (), s32[]{:S(2)}) async-start(), calls=%async_computation.33 | async-start | bytes 3932160 | tf_op jit(solution)/shard_map/all_gather | solution.py:225
  1467.6 4.3 collective-permute-start.2
  1476.4 106.3 %reduce-scatter.37.cloned.1.call-start = ((), (), s32[]{:S(2)}) async-start(), calls=%async_computation.34 | async-start | bytes 3932160 | tf_op jit(solution)/shard_map/reduce_scatter | solution.py:238
  1538.6 93.0 %all-gather.36.cloned.1.call-start = ((), (), s32[]{:S(2)}) async-start(), calls=%async_computation.35 | async-start | bytes 3932160 | tf_op jit(solution)/shard_map/all_gather | solution.py:248
  1587.8 287.1 %reduce-scatter.39.cloned.1.call-start = ((), (), s32[]{:S(2)}) async-start(), calls=%async_computation.36 | async-start | bytes 3932160 | tf_op jit(solution)/shard_map/reduce_scatter | solution.py:266
  1830.9 50.1 %copy-start.182 = (f32[768]{0:T(1024)S(1)}, f32[768]{0:T(1024)}, u32[]{:S(2)}) copy-start(f32[768]{0:T(1024)} %copy-done.178) | copy-start | bytes 9220
  1831.0 50.0 %copy-start.51 = (f32[1,512,768]{2,1,0:T(8,128)S(1)}, f32[1,512,768]{2,1,0:T(8,128)}, u32[]{:S(2)}) copy-start(f32[1,512,768]{2,1,0:T(8,128)} %copy-done.49) | copy-start | bytes 4718596
  1831.0 50.0 %copy-start.54 = (f32[1,512,768]{2,1,0:T(8,128)S(1)}, f32[1,512,768]{2,1,0:T(8,128)}, u32[]{:S(2)}) copy-start(f32[1,512,768]{2,1,0:T(8,128)} %copy-done.52) | copy-start | bytes 4718596
  1831.0 98.6 %all-gather.38.cloned.1.call-start = ((), (), s32[]{:S(2)}) async-start(), calls=%async_computation.37 | async-start | bytes 3932160 | tf_op jit(solution)/shard_map/all_gather | solution.py:225
  1876.7 4.3 collective-permute-start.3
  1885.5 106.7 %reduce-scatter.41.cloned.1.call-start = ((), (), s32[]{:S(2)}) async-start(), calls=%async_computation.38 | async-start | bytes 3932160 | tf_op jit(solution)/shard_map/reduce_scatter | solution.py:238
  1948.1 106.1 %all-gather.40.cloned.1.call-start = ((), (), s32[]{:S(2)}) async-start(), calls=%async_computation.39 | async-start | bytes 3932160 | tf_op jit(solution)/shard_map/all_gather | solution.py:248
  1997.2 288.6 %reduce-scatter.47.cloned.1.call-start = ((), (), s32[]{:S(2)}) async-start(), calls=%async_computation.42 | async-start | bytes 1474560 | tf_op jit(solution)/shard_map/reduce_scatter | solution.py:294
  2034.5 254.9 %reduce-scatter.45.cloned.1.call-start = ((), (), s32[]{:S(2)}) async-start(), calls=%async_computation.41 | async-start | bytes 2949120 | tf_op jit(solution)/shard_map/reduce_scatter | solution.py:291
  2054.1 240.7 %reduce-scatter.51.cloned.1.call-start = ((), (), s32[]{:S(2)}) async-start(), calls=%async_computation.45 | async-start | bytes 491520
  2254.5 47.7 %reduce-scatter.49.cloned.1.call-start = ((), (), s32[]{:S(2)}) async-start(), calls=%async_computation.44 | async-start | bytes 1228800
  2267.6 139.0 %reduce-scatter.43.cloned.1.call-start = ((), (), s32[]{:S(2)}) async-start(), calls=%async_computation.40 | async-start | bytes 3932160 | tf_op jit(solution)/shard_map/reduce_scatter | solution.py:266
  (278 other events, 2140.4 us)
Sparse Core Ops, SparseCore 0:
  11.3 46.6 all-gather.41
  165.4 71.7 reduce-scatter.20
  527.4 70.2 reduce-scatter.24
  713.8 44.0 all-gather.25
  941.0 43.9 all-gather.27
  1002.1 43.9 reduce-scatter.30
  1126.3 44.0 reduce-scatter.32
  1421.8 43.9 reduce-scatter.34
  1538.7 43.9 reduce-scatter.36
  1885.6 43.9 all-gather.37
  1948.2 43.9 reduce-scatter.40
Sparse Core Ops, SparseCore 1:
  167.9 51.5 all-gather.17
  241.3 43.8 all-gather.15
  287.2 30.2 all-gather.19
  327.5 43.0 reduce-scatter.22
  378.4 43.8 all-gather.21
  601.0 43.8 all-gather.23
  662.1 43.8 reduce-scatter.26
  866.2 70.0 reduce-scatter.28
  1059.0 43.8 all-gather.29
  1175.7 43.8 all-gather.31
  1476.5 43.8 all-gather.33
  1587.8 43.8 all-gather.35
  1831.0 43.8 reduce-scatter.38
  1997.3 43.7 all-gather.39
  2044.0 29.2 reduce-scatter.46
  2075.6 46.3 reduce-scatter.44
  2254.6 21.0 reduce-scatter.50
  2278.1 24.1 reduce-scatter.48
  2305.7 43.2 reduce-scatter.42
where the time goes:
time: 2430 us; the launch traced here: 2420 us
  waiting for transfers between devices  932 us (38%)
  matrix products  635 us (26%)
  other arithmetic  415 us (17%)
  local copies, waits for them, and re-layouts  240 us (10%)
  blocking collectives  121 us (5%)
  loops' own time  42.8 us (2%)
  between operations  24.3 us (1%)
    reduce_scatter x3, waiting for transfers between devices, forward_layer(): lax.psum_scatter(jnp.dot(heads_flat, out_matrix, preferred_element_type=j...  210 us
    reduce_scatter x3, waiting for transfers between devices, forward_layer(): lax.psum_scatter(jnp.dot(inner_act, down_matrix, preferred_element_type=j...  131 us
    all_gather x3, waiting for transfers between devices, forward_layer(): lax.all_gather(hidden.astype(jnp.bfloat16), 'tensor', axis=0, tiled=True)  129 us
    dynamic_update_slice x24, local copies, waits for them, and re-layouts, attend_backward(): lax.scan(one_block, (zero_state, zero_state), jnp.arange(blocks, dtype=jn...  108 us
    dot_general x24, matrix products, block_scores(): jnp.einsum('qhd,khd->hqk', query_rows, key_rot, preferred_element_type=jn...  107 us
    reduce_scatter x3, waiting for transfers between devices, backward_layer(): lax.psum_scatter(jnp.einsum('lcf,cdf->ld', row_piece, gate_matrix, prefer...  93.1 us
    all_gather x3, waiting for transfers between devices, backward_layer(): lax.all_gather(grad_mixed_two.astype(jnp.bfloat16), 'tensor', axis=0, til...  87.9 us
    reduce_scatter x3, waiting for transfers between devices, backward_layer(): lax.psum_scatter(jnp.einsum('lce,cde->ld', row_piece, in_matrix, preferre...  87.9 us
  transfers between devices with their start and end apart: 34, of which 26 were waited for; matrix products, arithmetic and copies ran while one was open for 17% of the time, Pallas kernels for 0%

commit v1 on v0

v1 whole, which is shorter than its diff:
```python
import functools
import jax
import jax.numpy as jnp
from jax import lax
from jax.experimental import pallas as pl
from jax.experimental.pallas import tpu as pltpu
from jax.sharding import PartitionSpec as P

HEAD = 64
QB = 512
KT = 512


def attn_fwd_kernel(place, spans, near, far, lo, hi, out, lse_out, q_t, k_n, v_t, o_t, *, heads, keys):
    step = pl.program_id(0)
    width = heads * HEAD
    rows = near.shape[1] // 2

    @pl.when(step == 0)
    def _():
        for slab in range(4):
            src = near if slab < 2 else far
            at = (slab % 2) * rows
            start = pl.multiple_of(place[slab] * rows, rows)
            q_t[:, pl.ds(start, rows)] = src[0:width, at : at + rows]
            v_t[:, pl.ds(start, rows)] = src[2 * width : 3 * width, at : at + rows]
            for h in range(heads):
                k_n[h, pl.ds(start, rows), :] = src[width + h * HEAD : width + (h + 1) * HEAD, at : at + rows].T

    q_start = pl.multiple_of(step * QB, QB)
    low, high = lo[:, pl.ds(q_start, QB)], hi[:, pl.ds(q_start, QB)]
    queries = [q_t[h * HEAD : (h + 1) * HEAD, pl.ds(q_start, QB)] for h in range(heads)]

    def tile(t, carry):
        k_start = pl.multiple_of(t * KT, KT)
        pos = k_start + lax.broadcasted_iota(jnp.int32, (KT, QB), 0)
        allowed = (pos >= low) & (pos <= high)
        out_carry = []
        for h in range(heads):
            top, total, acc = carry[h]
            s = jnp.dot(k_n[h, pl.ds(k_start, KT), :], queries[h], preferred_element_type=jnp.float32)
            s = jnp.where(allowed, s, -1e30)
            new_top = jnp.maximum(top, jnp.max(s, axis=0, keepdims=True))
            p = jnp.exp(s - new_top)
            alpha = jnp.exp(top - new_top)
            total = total * alpha + jnp.sum(p, axis=0, keepdims=True)
            acc = acc * alpha + jnp.dot(
                v_t[h * HEAD : (h + 1) * HEAD, pl.ds(k_start, KT)], p.astype(jnp.bfloat16),
                preferred_element_type=jnp.float32)
            out_carry.append((new_top, total, acc))
        return tuple(out_carry)

    init = tuple((jnp.full((1, QB), -1e30, jnp.float32), jnp.zeros((1, QB), jnp.float32),
                  jnp.zeros((HEAD, QB), jnp.float32)) for _ in range(heads))
    done = lax.fori_loop(spans[0, step], spans[1, step], tile, init)
    for h in range(heads):
        top, total, acc = done[h]
        o_t[h * HEAD : (h + 1) * HEAD, pl.ds(q_start, QB)] = (acc / total).astype(jnp.bfloat16)
        lse_out[h : h + 1, pl.ds(q_start, QB)] = top + jnp.log(total)

    @pl.when(step == pl.num_programs(0) - 1)
    def _():
        for slab in range(4):
            start = pl.multiple_of(place[slab] * rows, rows)
            out[slab] = o_t[:, pl.ds(start, rows)]


def attn_fwd(place, spans, near, far, lo, hi, heads):
    length = 2 * near.shape[1]
    rows = near.shape[1] // 2
    width = heads * HEAD
    smem = pl.BlockSpec(memory_space=pltpu.SMEM)
    whole = lambda s: pl.BlockSpec(s, lambda i: (0,) * len(s))
    return pl.pallas_call(
        functools.partial(attn_fwd_kernel, heads=heads, keys=length),
        grid=(length // QB,),
        in_specs=[smem, smem, whole(near.shape), whole(far.shape), whole(lo.shape), whole(hi.shape)],
        out_specs=(whole((4, width, rows)), whole((heads, length))),
        out_shape=(jax.ShapeDtypeStruct((4, width, rows), jnp.bfloat16),
                   jax.ShapeDtypeStruct((heads, length), jnp.float32)),
        scratch_shapes=[
            pltpu.VMEM((width, length), jnp.bfloat16),
            pltpu.VMEM((heads, length, HEAD), jnp.bfloat16),
            pltpu.VMEM((width, length), jnp.bfloat16),
            pltpu.VMEM((width, length), jnp.bfloat16),
        ],
        compiler_params=pltpu.CompilerParams(vmem_limit_bytes=48 << 20),
        cost_estimate=pl.CostEstimate(flops=4 * length * length * width, bytes_accessed=4 * length * width * 2, transcendentals=heads * length * length),
        name="attn_fwd",
    )(place, spans, near, far, lo, hi)


def attn_bwd_kernel(place, spans, near, far, dout, out_t, lse, lo, hi, cos, sin, dproj,
                    q_t, q_n, k_t, k_n, v_n, do_t, do_n, delta, dq_t, dk, dv, *, heads):
    step = pl.program_id(0)
    width = heads * HEAD
    rows = near.shape[1] // 2
    length = 2 * near.shape[1]

    @pl.when(step == 0)
    def _():
        for slab in range(4):
            src = near if slab < 2 else far
            at = (slab % 2) * rows
            start = pl.multiple_of(place[slab] * rows, rows)
            q_t[:, pl.ds(start, rows)] = src[0:width, at : at + rows]
            k_t[:, pl.ds(start, rows)] = src[width : 2 * width, at : at + rows]
            do_t[:, pl.ds(start, rows)] = dout[slab]
            prod = dout[slab].astype(jnp.float32) * out_t[slab].astype(jnp.float32)
            for h in range(heads):
                piece = slice(h * HEAD, (h + 1) * HEAD)
                delta[h : h + 1, pl.ds(start, rows)] = jnp.sum(prod[piece], axis=0, keepdims=True)
                q_n[h, pl.ds(start, rows), :] = src[h * HEAD : (h + 1) * HEAD, at : at + rows].T
                k_n[h, pl.ds(start, rows), :] = src[width + h * HEAD : width + (h + 1) * HEAD, at : at + rows].T
                v_n[h, pl.ds(start, rows), :] = src[2 * width + h * HEAD : 2 * width + (h + 1) * HEAD, at : at + rows].T
                do_n[h, pl.ds(start, rows), :] = dout[slab, piece, :].T
        dk[...] = jnp.zeros_like(dk)
        dv[...] = jnp.zeros_like(dv)

    q_start = pl.multiple_of(step * QB, QB)
    low, high = lo[:, pl.ds(q_start, QB)], hi[:, pl.ds(q_start, QB)]

    def tile(t, carry):
        k_start = pl.multiple_of(t * KT, KT)
        pos = k_start + lax.broadcasted_iota(jnp.int32, (KT, QB), 0)
        allowed = (pos >= low) & (pos <= high)
        new = []
        for h in range(heads):
            piece = slice(h * HEAD, (h + 1) * HEAD)
            qs, ks = pl.ds(q_start, QB), pl.ds(k_start, KT)
            s = jnp.dot(k_n[h, ks, :], q_t[piece, qs], preferred_element_type=jnp.float32)
            p = jnp.where(allowed, jnp.exp(s - lse[h : h + 1, qs]), 0.0)
            dp = jnp.dot(v_n[h, ks, :], do_t[piece, qs], preferred_element_type=jnp.float32)
            ds = (p * (dp - delta[h : h + 1, qs])).astype(jnp.bfloat16)
            dv[h, ks, :] += jnp.dot(p.astype(jnp.bfloat16), do_n[h, qs, :], preferred_element_type=jnp.float32)
            dk[h, ks, :] += jnp.dot(ds, q_n[h, qs, :], preferred_element_type=jnp.float32)
            new.append(carry[h] + jnp.dot(k_t[piece, ks], ds, preferred_element_type=jnp.float32))
        return tuple(new)

    init = tuple(jnp.zeros((HEAD, QB), jnp.float32) for _ in range(heads))
    done = lax.fori_loop(spans[0, step], spans[1, step], tile, init)
    for h in range(heads):
        dq_t[h * HEAD : (h + 1) * HEAD, pl.ds(q_start, QB)] = done[h]

    @pl.when(step == pl.num_programs(0) - 1)
    def _():
        half = HEAD // 2
        for slab in range(4):
            start = pl.multiple_of(place[slab] * rows, rows)
            c, s = cos[:, pl.ds(start, rows)], sin[:, pl.ds(start, rows)]
            for h in range(heads):
                gq = dq_t[h * HEAD : (h + 1) * HEAD, pl.ds(start, rows)] * HEAD**-0.5
                gk = dk[h, pl.ds(start, rows), :].T
                gv = dv[h, pl.ds(start, rows), :].T
                for kind, g in ((0, gq), (1, gk)):
                    g1, g2 = g[:half], g[half:]
                    at = kind * width + h * HEAD
                    dproj[slab, at : at + half, :] = (g1 * c + g2 * s).astype(jnp.bfloat16)
                    dproj[slab, at + half : at + HEAD, :] = (g2 * c - g1 * s).astype(jnp.bfloat16)
                at = 2 * width + h * HEAD
                dproj[slab, at : at + HEAD, :] = gv.astype(jnp.bfloat16)


def attn_bwd(place, spans, near, far, dout, out_t, lse, lo, hi, cos, sin, heads):
    length = 2 * near.shape[1]
    rows = near.shape[1] // 2
    width = heads * HEAD
    smem = pl.BlockSpec(memory_space=pltpu.SMEM)
    whole = lambda a: pl.BlockSpec(a.shape, lambda i: (0,) * len(a.shape))
    ops = (near, far, dout, out_t, lse, lo, hi, cos, sin)
    return pl.pallas_call(
        functools.partial(attn_bwd_kernel, heads=heads),
        grid=(length // QB,),
        in_specs=[smem, smem] + [whole(a) for a in ops],
        out_specs=pl.BlockSpec((4, 3 * width, rows), lambda i: (0, 0, 0)),
        out_shape=jax.ShapeDtypeStruct((4, 3 * width, rows), jnp.bfloat16),
        scratch_shapes=[
            pltpu.VMEM((width, length), jnp.bfloat16),
            pltpu.VMEM((heads, length, HEAD), jnp.bfloat16),
            pltpu.VMEM((width, length), jnp.bfloat16),
            pltpu.VMEM((heads, length, HEAD), jnp.bfloat16),
            pltpu.VMEM((heads, length, HEAD), jnp.bfloat16),
            pltpu.VMEM((width, length), jnp.bfloat16),
            pltpu.VMEM((heads, length, HEAD), jnp.bfloat16),
            pltpu.VMEM((heads, length), jnp.float32),
            pltpu.VMEM((width, length), jnp.float32),
            pltpu.VMEM((heads, length, HEAD), jnp.float32),
            pltpu.VMEM((heads, length, HEAD), jnp.float32),
        ],
        compiler_params=pltpu.CompilerParams(vmem_limit_bytes=56 << 20),
        cost_estimate=pl.CostEstimate(flops=10 * length * length * width, bytes_accessed=12 * length * width * 2, transcendentals=heads * length * length),
        name="attn_bwd",
    )(place, spans, *ops)


def spans_of(seg, window, length):
    pos = jnp.arange(length, dtype=jnp.int32)
    start = jnp.sum((seg[None, :] < jnp.arange(3, dtype=seg.dtype)[:, None]).astype(jnp.int32), axis=1)
    end = jnp.sum((seg[None, :] <= jnp.arange(3, dtype=seg.dtype)[:, None]).astype(jnp.int32), axis=1) - 1
    pick = lambda t: jnp.where(seg == 0, t[0], jnp.where(seg == 1, t[1], t[2]))
    lo = jnp.maximum(pick(start), pos - (window - 1))
    hi = jnp.minimum(pick(end), pos + (window - 1))
    spans = jnp.stack([lo[::QB] // KT, hi[QB - 1 :: QB] // KT + 1])
    return lo[None], hi[None], spans


WINDOW = 1024
STEP = 10

BETA_ONE = 0.9
BETA_TWO = 0.999
ADAM_EPS = 1e-06
DECAY_RATE = 0.01
LEARN_RATE = 0.2
NORM_EPS = 1e-05
ROPE_BASE = 1000.0

bf16 = jnp.bfloat16
f32 = jnp.float32

BOTH = ("section", "tensor")
CELLS = [(c, y, x) for c in range(2) for y in range(2) for x in range(2)]


def number(c, y, x):
    return c * 4 + y * 2 + x


def moves(target):
    return [(number(*cell), number(*target(*cell))) for cell in CELLS]


SWAP = moves(lambda c, y, x: (y, c, x))
SWAP_BACK = moves(lambda c, y, x: (1 - y, c, x))
SWAP_OUT = moves(lambda c, y, x: (y, 1 - c, x))
CORNER = moves(lambda c, y, x: (1 - c, y, 1 - x))


def over_section(v):
    return lax.ppermute(v, "section", [(0, 1), (1, 0)])


def over_x(v):
    return lax.ppermute(v, "tensor", [(0, 1), (1, 0), (2, 3), (3, 2)])


def over_y(v):
    return lax.ppermute(v, "tensor", [(0, 2), (1, 3), (2, 0), (3, 1)])


def over_diag(v):
    return lax.ppermute(v, "tensor", [(0, 3), (1, 2), (2, 1), (3, 0)])


def over_both(v, pairs):
    return lax.ppermute(v, BOTH, pairs)


def over_z(v, k):
    return lax.ppermute(v, "dp", [(i, i ^ k) for i in range(4)])


def gather_dp(piece, axis):
    if lax.axis_size("dp") != 4:
        return lax.all_gather(piece, "dp", axis=axis, tiled=True)
    z = lax.axis_index("dp")
    deep = piece.shape[axis]
    whole = jnp.zeros(piece.shape[:axis] + (4 * deep,) + piece.shape[axis + 1 :], piece.dtype)
    for k in range(4):
        got = piece if k == 0 else over_z(piece, k)
        whole = lax.dynamic_update_slice_in_dim(whole, got, (z ^ k) * deep, axis)
    return whole


def scatter_dp(whole, axis):
    if lax.axis_size("dp") != 4:
        return lax.psum_scatter(whole, "dp", scatter_dimension=axis, tiled=True).astype(f32)
    z = lax.axis_index("dp")
    deep = whole.shape[axis] // 4
    parts = [lax.dynamic_slice_in_dim(whole, (z ^ k) * deep, deep, axis) for k in range(4)]
    got = [parts[0]] + [over_z(parts[k], k) for k in range(1, 4)]
    got = [g.astype(f32) for g in got]
    return (got[0] + got[1]) + (got[2] + got[3])


def chips_total(v):
    v = (v + over_x(v)) + (over_y(v) + over_diag(v))
    if lax.axis_size("dp") != 4:
        return lax.psum(v, "dp")
    return (v + over_z(v, 1)) + (over_z(v, 2) + over_z(v, 3))


def rope_tables(length):
    half_size = HEAD // 2
    freq_vals = ROPE_BASE ** (-jnp.arange(half_size, dtype=f32) * 2.0 / HEAD)
    angles = freq_vals[:, None] * jnp.arange(length, dtype=f32)[None, :]
    return jnp.cos(angles), jnp.sin(angles)


def norm_fwd(values, gain_row, bias_row):
    mean_val = jnp.mean(values, axis=-1, keepdims=True)
    centred = values - mean_val
    variance = jnp.mean(centred * centred, axis=-1, keepdims=True)
    inv_std = lax.rsqrt(variance + NORM_EPS)
    normed = centred * inv_std
    return (normed * gain_row + bias_row, normed, inv_std)


def norm_back(grad_out, normed, inv_std, gain_row):
    grad_gain = jnp.sum(grad_out * normed, axis=0)
    grad_bias = jnp.sum(grad_out, axis=0)
    grad_normed = grad_out * gain_row
    grad_vals = inv_std * (
        grad_normed
        - jnp.mean(grad_normed, axis=-1, keepdims=True)
        - normed * jnp.mean(grad_normed * normed, axis=-1, keepdims=True)
    )
    return (grad_vals, grad_gain, grad_bias)


def dot(spec, a, b):
    return jnp.einsum(spec, a, b, preferred_element_type=f32)


def project_in(rows, matrix, cos, sin):
    width = matrix.shape[1] // 4
    heads = width // HEAD
    got = dot("de,ld->el", matrix[:, : 3 * width], rows)
    length = got.shape[1]
    parts = got.reshape(3, heads, 2, HEAD // 2, length)
    first, second = parts[:2, :, 0], parts[:2, :, 1]
    turned = jnp.stack([first * cos - second * sin, second * cos + first * sin], axis=2).astype(bf16)
    scale = jnp.array([HEAD**-0.5, 1.0], bf16).reshape(2, 1, 1, 1, 1)
    return jnp.concatenate([(turned * scale).reshape(2 * width, length), got[2 * width :].astype(bf16)], axis=0)


def layer_forward(own, weights, gains, biases, env):
    matrix, out_matrix, ffn = weights
    place, spans, low, high, tables = env
    heads = matrix.shape[1] // 4 // HEAD
    across = over_x(own)
    near = jnp.concatenate([own, over_section(own)], axis=0)
    far = jnp.concatenate([across, over_section(across)], axis=0)
    near_qkv = project_in(near, matrix, *tables[0])
    far_qkv = project_in(far, matrix, *tables[1])
    mine, log_sums = attn_fwd(place, spans, near_qkv, far_qkv, low, high, heads)
    all_heads = jnp.concatenate(
        [mine[0], over_section(mine[1]), over_x(mine[2]), over_both(mine[3], CORNER)], axis=0
    )
    mixed = own.astype(f32) + dot("el,ed->ld", all_heads, out_matrix)
    hidden, normed_one, inv_one = norm_fwd(mixed, gains[0], biases[0])
    hidden_low = hidden.astype(bf16)
    hidden_rows = [hidden_low, over_x(hidden_low)]
    partial, acts = [], []
    for rows in hidden_rows:
        total, kept = 0.0, []
        for gate_up_down in ffn:
            gate = dot("ld,df->lf", rows, gate_up_down[0])
            up = dot("ld,df->lf", rows, gate_up_down[1])
            inner = (jax.nn.silu(gate) * up).astype(bf16)
            total = total + dot("lf,df->ld", inner, gate_up_down[2])
            kept.append((gate.astype(bf16), up.astype(bf16), inner))
        partial.append(total)
        acts.append(kept)
    ffn_out = partial[0] + over_x(partial[1].astype(bf16)).astype(f32)
    output, normed_two, inv_two = norm_fwd(hidden + ffn_out, gains[1], biases[1])
    kept = (near, far, near_qkv, far_qkv, mine, log_sums, all_heads, normed_one, inv_one, hidden_rows, acts, normed_two, inv_two)
    return output, kept


def layer_backward(grad_out, kept, weights, gains, env):
    matrix, out_matrix, ffn = weights
    place, spans, low, high, tables = env
    (near, far, near_qkv, far_qkv, mine, log_sums, all_heads, normed_one, inv_one, hidden_rows, acts, normed_two, inv_two) = kept
    width = matrix.shape[1] // 4
    heads = width // HEAD
    grad_mixed, gain_two, bias_two = norm_back(grad_out, normed_two, inv_two, gains[1])
    grad_low = grad_mixed.astype(bf16)
    grad_rows = [grad_low, over_x(grad_low)]
    partial, grads = [], []
    for rows, row_acts in zip(grad_rows, acts):
        total, made = 0.0, []
        for gate_up_down, (gate, up, inner) in zip(ffn, row_acts):
            grad_inner = dot("ld,df->lf", rows, gate_up_down[2])
            gate, up = gate.astype(f32), up.astype(f32)
            sig = jax.nn.sigmoid(gate)
            grad_gate = (grad_inner * up * (sig * (1.0 + gate * (1.0 - sig)))).astype(bf16)
            grad_up = (grad_inner * (gate * sig)).astype(bf16)
            total = total + dot("lf,df->ld", grad_gate, gate_up_down[0]) + dot("lf,df->ld", grad_up, gate_up_down[1])
            made.append((grad_gate, grad_up))
        partial.append(total)
        grads.append(made)
    hidden_sum = partial[0] + over_x(partial[1].astype(bf16)).astype(f32)
    hidden_both = jnp.concatenate(hidden_rows, axis=0)
    grad_both = jnp.concatenate(grad_rows, axis=0)
    ffn_grads = []
    for b in range(2):
        grad_gate, grad_up, inner = (
            jnp.concatenate([grads[r][b][0] for r in range(2)], axis=0),
            jnp.concatenate([grads[r][b][1] for r in range(2)], axis=0),
            jnp.concatenate([acts[r][b][2] for r in range(2)], axis=0),
        )
        ffn_grads.append(
            jnp.stack(
                [
                    dot("ld,lf->df", hidden_both, grad_gate).astype(bf16),
                    dot("ld,lf->df", hidden_both, grad_up).astype(bf16),
                    dot("ld,lf->df", grad_both, inner).astype(bf16),
                ]
            )
        )
    ffn_grad = (ffn_grads[0].astype(f32) + over_section(ffn_grads[1]).astype(f32)).astype(bf16)
    grad_hidden = grad_mixed + hidden_sum
    grad_mixed_one, gain_one, bias_one = norm_back(grad_hidden, normed_one, inv_one, gains[0])
    attn_low = grad_mixed_one.astype(bf16)
    grad_heads = dot("ed,ld->el", out_matrix, attn_low).astype(bf16).reshape(4, width, -1)
    out_grad = dot("el,ld->ed", all_heads, attn_low).astype(bf16).reshape(4, width, -1)
    out_pair = out_grad[::2].astype(f32) + over_section(out_grad[1::2]).astype(f32)
    out_own = out_pair[0] + over_x(out_pair[1].astype(bf16)).astype(f32)
    grad_mine = jnp.stack(
        [grad_heads[0], over_section(grad_heads[1]), over_x(grad_heads[2]), over_both(grad_heads[3], CORNER)]
    )
    cos, sin = env[4][2]
    grad_proj = attn_bwd(place, spans, near_qkv, far_qkv, grad_mine, mine, log_sums, low, high, cos, sin, heads)
    rows_part = [dot("el,de->ld", grad_proj[p], matrix[:, : 3 * width]).astype(bf16) for p in (1, 3, 2, 0)]
    pair = over_section(jnp.stack(rows_part[:2])).astype(f32)
    near_sum = rows_part[3].astype(f32) + pair[0]
    far_sum = (rows_part[2].astype(f32) + pair[1]).astype(bf16)
    rows_sum = near_sum + over_x(far_sum).astype(f32)
    half = near.shape[0] // 2
    slabs = (near[:half], near[half:], far[:half], far[half:])
    in_grad = sum(dot("el,ld->ed", grad_proj[p], slabs[p]) for p in range(4))
    matrix_grad = jnp.concatenate([in_grad, out_own], axis=0).T.astype(bf16)
    norm_grads = jnp.stack([jnp.stack([gain_one, gain_two]), jnp.stack([bias_one, bias_two])])
    return grad_mixed_one + rows_sum, matrix_grad, ffn_grad, norm_grads


def lamb_parts(weight, gradient, first_old, second):
    first_new = BETA_ONE * first_old + (1.0 - BETA_ONE) * gradient
    second_new = BETA_TWO * second + (1.0 - BETA_TWO) * gradient * gradient
    update = (
        first_new
        / (1.0 - BETA_ONE**STEP)
        / (jnp.sqrt(second_new / (1.0 - BETA_TWO**STEP)) + ADAM_EPS)
        + DECAY_RATE * weight
    )
    return (first_new, second_new, update)


def body(
    tokens,
    cotangent,
    segments,
    heads_in,
    heads_out,
    gate_up,
    project_down,
    norm_gain,
    norm_bias,
    heads_in_first,
    heads_in_second,
    heads_out_first,
    heads_out_second,
    gate_up_first,
    gate_up_second,
    project_down_first,
    project_down_second,
    norm_first,
    norm_second,
):
    section = lax.axis_index("section")
    spot = lax.axis_index("tensor")
    y, x = spot // 2, spot % 2
    rows = tokens.shape[1]
    length = segments.shape[-1]
    masters = (heads_in[0], heads_out[0], gate_up[0], project_down[0])
    deep, width = masters[0].shape[1:]

    own = over_both(lax.dynamic_index_in_dim(tokens, section, 0, keepdims=False), SWAP)
    grad_top = over_both(lax.dynamic_index_in_dim(cotangent, section, 0, keepdims=False), SWAP)

    attn_piece = jnp.concatenate(
        [masters[0].transpose(1, 0, 2).reshape(deep, 3 * width), masters[1].T], axis=1
    ).astype(bf16)
    ffn_piece = jnp.concatenate([masters[2], masters[3].T[None]], axis=0).astype(bf16)

    def to_blocks(piece):
        same, other = over_both(piece, SWAP), over_both(piece, SWAP_OUT)
        return jnp.where(y == 0, same, other), jnp.where(y == 0, other, same)

    attn_pieces, ffn_pieces = to_blocks(attn_piece), to_blocks(ffn_piece)
    weights = []
    for layer in range(2):
        matrix = gather_dp(attn_pieces[layer], 0)
        ffn_own = lax.all_gather(ffn_pieces[layer], "dp", axis=1, tiled=True)
        out_own = matrix[:, 3 * width :].T
        pair = jnp.stack([out_own, over_x(out_own)])
        pair_other = over_section(pair)
        out_matrix = jnp.concatenate([pair[0], pair_other[0], pair[1], pair_other[1]], axis=0)
        weights.append((matrix, out_matrix, (ffn_own, over_section(ffn_own))))

    both_params = jnp.stack([norm_gain[0], norm_bias[0]])
    other_params = over_section(both_params)
    params = [
        jnp.where(section == 0, both_params, other_params),
        jnp.where(section == 0, other_params, both_params),
    ]

    block = 2 * section + x
    place = jnp.stack([block, block ^ 2, block ^ 1, block ^ 3]).astype(jnp.int32)
    seq_seg = lax.dynamic_index_in_dim(segments, y, 0, keepdims=False)[0]
    low, high, spans = spans_of(seq_seg, WINDOW, length)
    cos, sin = rope_tables(length)

    def pick(table, slabs):
        return jnp.concatenate(
            [lax.dynamic_slice_in_dim(table, place[s] * rows, rows, 1) for s in slabs], axis=1
        )

    tables = (
        (pick(cos, (0, 1)), pick(sin, (0, 1))),
        (pick(cos, (2, 3)), pick(sin, (2, 3))),
        (cos, sin),
    )
    env = (place, spans, low, high, tables)

    out_zero, kept_zero = layer_forward(own, weights[0], params[0][0], params[0][1], env)
    low_zero = out_zero.astype(bf16)
    out_one, kept_one = layer_forward(low_zero, weights[1], params[1][0], params[1][1], env)
    low_one = out_one.astype(bf16)
    grad_one, matrix_one, ffn_one, norm_one = layer_backward(
        grad_top.astype(f32), kept_one, weights[1], params[1][0], env
    )
    sent = grad_one.astype(bf16)
    grad_zero, matrix_zero, ffn_zero, norm_zero = layer_backward(
        sent.astype(f32), kept_zero, weights[0], params[0][0], env
    )

    def home(zero, one):
        same = over_both(jnp.where(y == 0, zero, one), SWAP)
        other = over_both(jnp.where(y == 0, one, zero), SWAP_BACK)
        return same, other

    def by_micro(zero, one):
        same, other = home(zero, one)
        return jnp.stack([jnp.where(section == 0, same, other), jnp.where(section == 0, other, same)])

    layer_out = by_micro(low_zero, low_one)
    input_grads = by_micro(grad_zero.astype(bf16), sent).astype(f32)

    ffn_shards = [
        lax.psum_scatter(g, "dp", scatter_dimension=1, tiled=True) for g in (ffn_zero, ffn_one)
    ]
    ffn_home = home(*ffn_shards)
    ffn_grad = ffn_home[0].astype(f32) + ffn_home[1].astype(f32)
    attn_shards = [scatter_dp(g, 0).astype(bf16) for g in (matrix_zero, matrix_one)]
    attn_home = home(*attn_shards)
    attn_grad = attn_home[0].astype(f32) + attn_home[1].astype(f32)
    grad_shards = (
        attn_grad[:, : 3 * width].reshape(deep, 3, width).transpose(1, 0, 2),
        attn_grad[:, 3 * width :].T,
        ffn_grad[:2],
        ffn_grad[2].T,
    )
    norm_mine = jnp.where(section == 0, norm_zero, norm_one) + over_section(
        jnp.where(section == 0, norm_one, norm_zero)
    )
    norm_total = chips_total(norm_mine)

    firsts = (heads_in_first[0], heads_out_first[0], gate_up_first[0], project_down_first[0])
    seconds = (heads_in_second[0], heads_out_second[0], gate_up_second[0], project_down_second[0])
    parts = [lamb_parts(masters[i], grad_shards[i], firsts[i], seconds[i]) for i in range(4)]
    squares = jnp.stack(
        [jnp.sum(matrix * matrix) for matrix in masters] + [jnp.sum(item[2] * item[2]) for item in parts]
    )
    square_total = chips_total(jnp.broadcast_to(squares[:, None], (8, 128)))[:, 0]
    weight_norms = jnp.sqrt(square_total[:4])
    update_norms = jnp.sqrt(square_total[-4:])
    new_mats = [
        masters[i] - LEARN_RATE * (weight_norms[i] / update_norms[i]) * parts[i][2] for i in range(4)
    ]
    norm_now = both_params
    norm_first_new, norm_second_new, norm_update = lamb_parts(
        norm_now, norm_total, norm_first[0], norm_second[0]
    )
    norm_wn = jnp.sqrt(jnp.sum(norm_now * norm_now, axis=-1, keepdims=True))
    norm_un = jnp.sqrt(jnp.sum(norm_update * norm_update, axis=-1, keepdims=True))
    norm_params_new = norm_now - LEARN_RATE * (norm_wn / norm_un) * norm_update
    trust_norms = jnp.stack([weight_norms, update_norms], axis=1)
    outs = [layer_out, input_grads]
    for i in range(4):
        outs += [new_mats[i], parts[i][0], parts[i][1]]
    outs += [norm_params_new, norm_first_new, norm_second_new, trust_norms]
    return tuple(item[None] for item in outs)


def solution(mesh):
    rows = P(None, ("dp", "tensor"), None)
    out_rows = P("section", None, ("dp", "tensor"), None)
    columns = P("section", None, "dp", "tensor")
    turned = P("section", "tensor", "dp")
    vectors = P("section", None, None)
    pairs = P("section", None, None, None)
    return jax.shard_map(
        body,
        mesh=mesh,
        in_specs=(rows, rows, P(None, "dp", None), columns, turned, columns, turned, vectors, vectors)
        + (columns, columns, turned, turned, columns, columns, turned, turned, pairs, pairs),
        out_specs=(out_rows, out_rows)
        + (columns,) * 3
        + (turned,) * 3
        + (columns,) * 3
        + (turned,) * 3
        + (pairs,) * 3
        + (vectors,),
        check_vma=False,
    )
```

time: 2430 us -> 818 us (0.34)
  waiting for transfers between devices: 932 us -> 240 us
  matrix products: 635 us -> 123 us
  other arithmetic: 415 us -> 82.4 us
  local copies, waits for them, and re-layouts: 240 us -> 63.3 us
  Pallas kernels: 0 us -> 140 us
  starting transfers between devices: 9.3 us -> 138 us
  blocking collectives: 121 us -> 0 us
  loops' own time: 42.8 us -> 0 us
    reduce_scatter x14 -> x2, waiting for transfers between devices: 522 us -> 0.01 us  [body(): lax.psum_scatter(g, 'dp', scatter_dimension=1, tiled=True)]
    dot_general x117 -> x86, matrix products: 623 us -> 123 us  [dot(): return jnp.einsum(spec, a, b, preferred_element_type=f32)]
    all_gather x14 -> x2, waiting for transfers between devices: 396 us -> 0.04 us  [body(): ffn_own = lax.all_gather(ffn_pieces[layer], 'dp', axis=1, tiled=True)]
    ppermute x4 -> x82, waiting for transfers between devices: 9.45 us -> 240 us  [the longest x22 131 us: over_x(): return lax.ppermute(v, 'tensor', [(0, 1), (1, 0), (2, 3), (3, 2)])]
    pallas_call x0 -> x4, Pallas kernels: none -> 140 us  [the longest x2 84.4 us: attn_bwd(): pl.pallas_call(functools.partial(attn_bwd_kernel, heads=heads), grid=(len...]
    ppermute x4 -> x82, starting transfers between devices: 6.23 us -> 138 us  [the longest x18 70.4 us: over_z(): return lax.ppermute(v, 'dp', [(i, i ^ k) for i in range(4)])]
    reduce_sum x22 -> x5, other arithmetic: 104 us -> 10 us  [the longest x4 9.83 us: body(): jnp.sum(item[2] * item[2])]
    convert_element_type x31 -> x10, other arithmetic: 98.2 us -> 12.9 us  [the longest x2 6.29 us: layer_backward(): (ffn_grads[0].astype(f32) + over_section(ffn_grads[1]).astype(f32)).astyp...]
  transfers between devices with their start and end apart: 34 -> 86, of which waited for: 26 -> 30; matrix products, arithmetic and copies ran while one was open for 17% -> 31% of each run, Pallas kernels for 0% -> 17%
where the time goes in v1:
time: 818 us; the launch traced here: 808 us
  waiting for transfers between devices  240 us (29%)
  Pallas kernels  140 us (17%)
  starting transfers between devices  138 us (17%)
  matrix products  123 us (15%)
  other arithmetic  82.4 us (10%)
  local copies, waits for them, and re-layouts  63.3 us (8%)
  between operations  22 us (3%)
    ppermute x22, waiting for transfers between devices, over_x(): return lax.ppermute(v, 'tensor', [(0, 1), (1, 0), (2, 3), (3, 2)])  131 us
    dot_general x86, matrix products, dot(): return jnp.einsum(spec, a, b, preferred_element_type=f32)  123 us
    pallas_call x2, Pallas kernels, attn_bwd(): pl.pallas_call(functools.partial(attn_bwd_kernel, heads=heads), grid=(len...  84.4 us
    ppermute x18, waiting for transfers between devices, over_z(): return lax.ppermute(v, 'dp', [(i, i ^ k) for i in range(4)])  70.6 us
    ppermute x18, starting transfers between devices, over_z(): return lax.ppermute(v, 'dp', [(i, i ^ k) for i in range(4)])  70.4 us
    pallas_call x2, Pallas kernels, attn_fwd(): pl.pallas_call(functools.partial(attn_fwd_kernel, heads=heads, keys=lengt...  55.2 us
    dynamic_update_slice x8, local copies, waits for them, and re-layouts, gather_dp(): whole = lax.dynamic_update_slice_in_dim(whole, got, (z ^ k) * deep, axis)  36.7 us
    ppermute x18, waiting for transfers between devices, over_both(): return lax.ppermute(v, BOTH, pairs)  34.9 us
  transfers between devices with their start and end apart: 86, of which 30 were waited for; matrix products, arithmetic and copies ran while one was open for 31% of the time, Pallas kernels for 17%

profile of v1, /device:TPU:0, one launch (start us, length us, event | category | flops | bytes accessed | tf_op | source)
XLA Modules:
  0.0 807.6 jit_solution(2939145342619139781)
XLA Ops:
  10.4 3.4 collective-permute-start.16
  13.8 19.4 %collective-permute-done.16 = bf16[3,192,768]{2,1,0:T(8,128)(2,1)} collective-permute-done((bf16[3,192,768]{2,1,0:T(8,128)(2,1)S(1)}, bf16[3,192,768]{2,1,0:T(8,128)(2,1)}, u32[]{:S(2)}, u32[]{:S(2)}) %collective-permute-start.16) | collective-permute-done | bytes 884768 | tf_op jit(solution)/shard_map/ppermute | solution.py:256
  33.2 2.8 broadcast_select_fusion.2
  38.4 3.1 collective-permute-start.2
  50.0 3.9 fusion.365
  57.5 2.6 collective-permute-start.4
  62.2 3.9 dynamic_update_slice.24
  66.1 27.2 %collective-permute-done.3 = bf16[192,768]{0,1:T(8,128)(2,1)} collective-permute-done((bf16[192,768]{0,1:T(8,128)(2,1)S(1)}, bf16[192,768]{0,1:T(8,128)(2,1)}, u32[]{:S(2)}, u32[]{:S(2)}) %collective-permute-start.3) | collective-permute-done | bytes 294944 | tf_op jit(solution)/shard_map/ppermute | solution.py:260
  93.4 5.8 dynamic_update_slice.25
  99.2 4.7 dynamic_update_slice.26
  103.9 8.0 collective-permute-done.5
  111.9 3.4 dynamic_update_slice.27
  117.1 23.0 %collective-permute-start.20 = (bf16[192,768]{0,1:T(8,128)(2,1)}, bf16[192,768]{0,1:T(8,128)(2,1)}, u32[]{:S(2)}, u32[]{:S(2)}) collective-permute-start(bf16[192,768]{0,1:T(8,128)(2,1)} %get-tuple-element.140), channel_id=1, source_target_pairs={{0,4},{4,0},{8,12},{12,8},{1,5},{5,1},{9,13},{13,9},{2,6},{6,2},{1... | collective-permute-start | bytes 884744 | tf_op jit(solution)/shard_map/ppermute | solution.py:260
  148.0 27.7 %attn_fwd.2 = (bf16[4,192,512]{2,1,0:T(8,128)(2,1)S(1)}, f32[3,2048]{1,0:T(4,128)S(1)}) custom-call(s32[4]{0:T(128)S(1)} %pad_add_fusion.1.place, s32[2,4]{1,0:T(2,128)S(1)} %pad_add_fusion.spans, bf16[576,1024]{1,0:T(8,128)(2,1)S(1)} %pad_maximum_fusion.8.near, bf16[576,1024]{1,0:T(8,128)(2,1)S(1)} %pad_maximum_fusion.9.far, ...), custom_call_target="tpu_custom_call" | custom-call | flops 3221225472 | bytes 3145728 | tf_op jit(solution)/shard_map/attn_fwd/pallas_call | solution.py:74
  179.2 4.5 collective-permute-done.10
  183.7 8.4 %collective-permute-start.21 = (bf16[192,768]{0,1:T(8,128)(2,1)}, bf16[192,768]{0,1:T(8,128)(2,1)}, u32[]{:S(2)}, u32[]{:S(2)}) collective-permute-start(bf16[192,768]{0,1:T(8,128)(2,1)} %get-tuple-element.140), channel_id=1, source_target_pairs={{0,8},{4,12},{8,0},{12,4},{1,9},{5,13},{9,1},{13,5},{2,10},{6,14},... | collective-permute-start | bytes 884744 | tf_op jit(solution)/shard_map/ppermute | solution.py:260
  199.8 12.9 %collective-permute-done.18 = bf16[512,768]{1,0:T(8,128)(2,1)S(1)} collective-permute-done((bf16[512,768]{1,0:T(8,128)(2,1)S(1)}, bf16[512,768]{1,0:T(8,128)(2,1)S(1)}, u32[]{:S(2)}, u32[]{:S(2)}) %collective-permute-start.18) | collective-permute-done | bytes 786464 | tf_op jit(solution)/shard_map/ppermute | solution.py:244
  224.9 11.6 %collective-permute-done.19 = bf16[512,768]{1,0:T(8,128)(2,1)S(1)} collective-permute-done((bf16[512,768]{1,0:T(8,128)(2,1)S(1)}, bf16[512,768]{1,0:T(8,128)(2,1)S(1)}, u32[]{:S(2)}, u32[]{:S(2)}) %collective-permute-start.19) | collective-permute-done | bytes 786464 | tf_op jit(solution)/shard_map/ppermute | solution.py:244
  241.1 4.6 dynamic_update_slice.28
  245.8 5.1 dynamic_update_slice.29
  250.9 4.6 dynamic_update_slice.30
  255.5 4.6 dynamic_update_slice.31
  267.0 3.5 collective-permute-done.29
  279.3 27.4 %attn_fwd.3 = (bf16[4,192,512]{2,1,0:T(8,128)(2,1)S(1)}, f32[3,2048]{1,0:T(4,128)S(1)}) custom-call(s32[4]{0:T(128)S(1)} %pad_add_fusion.1.place, s32[2,4]{1,0:T(2,128)S(1)} %pad_add_fusion.spans, bf16[576,1024]{1,0:T(8,128)(2,1)S(1)} %pad_maximum_fusion.11.near, bf16[576,1024]{1,0:T(8,128)(2,1)S(1)} %pad_maximum_fusion.12.far, ...), custom_call_target="tpu_custom_call" | custom-call | flops 3221225472 | bytes 3145728 | tf_op jit(solution)/shard_map/attn_fwd/pallas_call | solution.py:74
  309.9 4.8 collective-permute-done.27
  314.8 3.3 collective-permute-done.28
  323.5 15.9 %collective-permute-done.32 = bf16[512,768]{1,0:T(8,128)(2,1)S(1)} collective-permute-done((bf16[512,768]{1,0:T(8,128)(2,1)S(1)}, bf16[512,768]{1,0:T(8,128)(2,1)S(1)}, u32[]{:S(2)}, u32[]{:S(2)}) %collective-permute-start.32) | collective-permute-done | bytes 786464 | tf_op jit(solution)/shard_map/ppermute | solution.py:244
  346.5 16.9 %collective-permute-done.33 = bf16[512,768]{1,0:T(8,128)(2,1)S(1)} collective-permute-done((bf16[512,768]{1,0:T(8,128)(2,1)S(1)}, bf16[512,768]{1,0:T(8,128)(2,1)S(1)}, u32[]{:S(2)}, u32[]{:S(2)}) %collective-permute-start.33) | collective-permute-done | bytes 786464 | tf_op jit(solution)/shard_map/ppermute | solution.py:244
  374.1 10.2 %collective-permute-done.37 = bf16[512,768]{1,0:T(8,128)(2,1)S(1)} collective-permute-done((bf16[512,768]{1,0:T(8,128)(2,1)S(1)}, bf16[512,768]{1,0:T(8,128)(2,1)S(1)}, u32[]{:S(2)}, u32[]{:S(2)}) %collective-permute-start.37) | collective-permute-done | bytes 786464 | tf_op jit(solution)/shard_map/ppermute | solution.py:244
  400.9 2.5 fusion.219
  405.9 10.7 %collective-permute-done.38 = bf16[512,768]{1,0:T(8,128)(2,1)S(1)} collective-permute-done((bf16[512,768]{1,0:T(8,128)(2,1)S(1)}, bf16[512,768]{1,0:T(8,128)(2,1)S(1)}, u32[]{:S(2)}, u32[]{:S(2)}) %collective-permute-start.38) | collective-permute-done | bytes 786464 | tf_op jit(solution)/shard_map/ppermute | solution.py:244
  423.9 3.8 collective-permute-done.40
  427.7 3.3 collective-permute-done.41
  432.1 42.2 %attn_bwd.2 = bf16[4,576,512]{2,1,0:T(8,128)(2,1)} custom-call(s32[4]{0:T(128)} %copy-done.11, s32[2,4]{1,0:T(2,128)} %copy-done.10, bf16[576,1024]{1,0:T(8,128)(2,1)} %copy-done.5, bf16[576,1024]{1,0:T(8,128)(2,1)} %copy-done.4, bf16[4,192,512]{2,1,0:T(8,128)(2,1)} %pad_maximum_fusion.25.dout, bf16[4,192,512]{2,1,0:T(8,128)(2,1)} %copy-done.7, ...), custom_call_target="tpu_custom_call" | custom-call | flops 8053063680 | bytes 9437184 | tf_op jit(solution)/shard_map/attn_bwd/pallas_call | solution.py:171
  489.6 4.1 collective-permute-done.59
  496.0 8.4 %collective-permute-start.61 = (bf16[192,768]{0,1:T(8,128)(2,1)}, bf16[192,768]{0,1:T(8,128)(2,1)}, u32[]{:S(2)}, u32[]{:S(2)}) collective-permute-start(bf16[192,768]{0,1:T(8,128)(2,1)} %get-tuple-element.117), channel_id=1, source_target_pairs={{0,8},{4,12},{8,0},{12,4},{1,9},{5,13},{9,1},{13,5},{2,10},{6,14},... | collective-permute-start | bytes 884744 | tf_op jit(solution)/shard_map/ppermute | solution.py:260
  504.4 5.5 collective-permute-done.43
  513.3 3.4 fusion.58
  526.1 3.8 add_convert_fusion
  532.0 3.3 fusion.213
  553.9 3.0 fusion.204
  557.0 10.9 %collective-permute-done.45 = bf16[512,768]{1,0:T(8,128)(2,1)S(1)} collective-permute-done((bf16[512,768]{1,0:T(8,128)(2,1)S(1)}, bf16[512,768]{1,0:T(8,128)(2,1)S(1)}, u32[]{:S(2)}, u32[]{:S(2)}) %collective-permute-start.45) | collective-permute-done | bytes 786464 | tf_op jit(solution)/shard_map/ppermute | solution.py:244
  573.9 3.2 collective-permute-start.78
  582.7 7.1 collective-permute-start.79
  592.4 4.6 collective-permute-done.80
  600.3 3.7 collective-permute-done.47
  606.8 42.2 %attn_bwd.3 = bf16[4,576,512]{2,1,0:T(8,128)(2,1)} custom-call(s32[4]{0:T(128)} %copy-done.11, s32[2,4]{1,0:T(2,128)} %copy-done.10, bf16[576,1024]{1,0:T(8,128)(2,1)} %copy-done.3, bf16[576,1024]{1,0:T(8,128)(2,1)} %copy-done.2, bf16[4,192,512]{2,1,0:T(8,128)(2,1)} %pad_maximum_fusion.26.dout, bf16[4,192,512]{2,1,0:T(8,128)(2,1)} %copy-done.6, ...), custom_call_target="tpu_custom_call" | custom-call | flops 8053063680 | bytes 9437184 | tf_op jit(solution)/shard_map/attn_bwd/pallas_call | solution.py:171
  663.2 5.7 collective-permute-done.54
  670.4 4.3 collective-permute-start.57
  675.4 10.1 %collective-permute-done.55 = bf16[192,768]{0,1:T(8,128)(2,1)S(1)} collective-permute-done((bf16[192,768]{0,1:T(8,128)(2,1)S(1)}, bf16[192,768]{0,1:T(8,128)(2,1)S(1)}, u32[]{:S(2)}, u32[]{:S(2)}) %collective-permute-start.55) | collective-permute-done | bytes 294944 | tf_op jit(solution)/shard_map/ppermute | solution.py:260
  685.4 16.6 %collective-permute-done.56 = bf16[192,768]{0,1:T(8,128)(2,1)S(1)} collective-permute-done((bf16[192,768]{0,1:T(8,128)(2,1)S(1)}, bf16[192,768]{0,1:T(8,128)(2,1)S(1)}, u32[]{:S(2)}, u32[]{:S(2)}) %collective-permute-start.56) | collective-permute-done | bytes 294944 | tf_op jit(solution)/shard_map/ppermute | solution.py:260
  707.2 4.7 collective-permute-done.64
  716.9 3.4 fusion.87
  726.6 5.1 collective-permute-start.68
  734.1 3.8 collective-permute-done.50
  737.9 2.5 broadcast_select_fusion.5
  740.5 3.0 collective-permute-start.52
  743.5 7.7 collective-permute-start.51
  756.5 3.1 multiply_reduce_fusion.10
  759.6 5.0 stack.326
  765.2 2.9 collective-permute-start.71
  769.7 3.6 collective-permute-done.70
  773.3 8.5 %collective-permute-start.72 = (f32[8,128]{0,1:T(8,128)S(1)}, f32[8,128]{0,1:T(8,128)S(1)}, u32[]{:S(2)}, u32[]{:S(2)}) collective-permute-start(f32[8,128]{0,1:T(8,128)S(1)} %add_add_fusion.5), channel_id=1, source_target_pairs={{0,4},{4,0},{8,12},{12,8},{1,5},{5,1},{9,13},{13,9},{2,6},{6,2},{1... | collective-permute-start | bytes 12296 | tf_op jit(solution)/shard_map/ppermute | solution.py:260
  786.1 4.1 collective-permute-done.73
  (674 shorter events, 248.4 us)
Async XLA Ops:
  7.2 140.5 %all-gather.3.cloned.1.call-start = ((), (), s32[]{:S(2)}) async-start(), calls=%async_computation.2 | async-start | bytes 4423680 | tf_op jit(solution)/shard_map/all_gather | solution.py:495
  10.4 22.8 %collective-permute-start.16 = (bf16[3,192,768]{2,1,0:T(8,128)(2,1)S(1)}, bf16[3,192,768]{2,1,0:T(8,128)(2,1)}, u32[]{:S(2)}, u32[]{:S(2)}) collective-permute-start(bf16[3,192,768]{2,1,0:T(8,128)(2,1)S(1)} %pad_maximum_fusion.18), channel_id=1, source_target_pairs={{0,2},{1,3},{2,18},{3,19},{16,0},{17,1},{18,16},{19,17},{4,6},{5,7... | collective-permute-start | bytes 2654216 | tf_op jit(solution)/shard_map/ppermute | solution.py:256
  36.0 235.5 %all-gather.5.cloned.1.call-start = ((), (), s32[]{:S(2)}) async-start(), calls=%async_computation.3 | async-start | bytes 4423680 | tf_op jit(solution)/shard_map/all_gather | solution.py:495
  37.0 17.0 %collective-permute-start.1 = (bf16[192,768]{0,1:T(8,128)(2,1)S(1)}, bf16[192,768]{0,1:T(8,128)(2,1)}, u32[]{:S(2)}, u32[]{:S(2)}) collective-permute-start(bf16[192,768]{0,1:T(8,128)(2,1)S(1)} %pad_maximum_fusion.29), channel_id=1, source_target_pairs={{0,0},{1,1},{2,16},{3,17},{16,2},{17,3},{18,18},{19,19},{4,4},{5,5... | collective-permute-start | bytes 884744 | tf_op jit(solution)/shard_map/ppermute | solution.py:256
  38.4 15.6 %collective-permute-start.2 = (bf16[192,768]{0,1:T(8,128)(2,1)S(1)}, bf16[192,768]{0,1:T(8,128)(2,1)}, u32[]{:S(2)}, u32[]{:S(2)}) collective-permute-start(bf16[192,768]{0,1:T(8,128)(2,1)S(1)} %pad_maximum_fusion.29), channel_id=1, source_target_pairs={{0,2},{1,3},{2,18},{3,19},{16,0},{17,1},{18,16},{19,17},{4,6},{5,7... | collective-permute-start | bytes 884744 | tf_op jit(solution)/shard_map/ppermute | solution.py:256
  41.6 18.8 %collective-permute-start = (bf16[512,768]{1,0:T(8,128)(2,1)S(1)}, bf16[512,768]{1,0:T(8,128)(2,1)}, u32[]{:S(2)}, u32[]{:S(2)}) collective-permute-start(bf16[512,768]{1,0:T(8,128)(2,1)S(1)} %dynamic-slice_bitcast_fusion.1), channel_id=1, source_target_pairs={{0,0},{1,1},{2,16},{3,17},{16,2},{17,3},{18,18},{19,19},{4,4},{5,5... | collective-permute-start | bytes 2359304 | tf_op jit(solution)/shard_map/ppermute | solution.py:256
  55.9 37.3 %collective-permute-start.3 = (bf16[192,768]{0,1:T(8,128)(2,1)S(1)}, bf16[192,768]{0,1:T(8,128)(2,1)}, u32[]{:S(2)}, u32[]{:S(2)}) collective-permute-start(bf16[192,768]{0,1:T(8,128)(2,1)S(1)} %get-tuple-element.141), channel_id=1, source_target_pairs={{0,4},{4,0},{8,12},{12,8},{1,5},{5,1},{9,13},{13,9},{2,6},{6,2},{1... | collective-permute-start | bytes 884744 | tf_op jit(solution)/shard_map/ppermute | solution.py:260
  57.5 41.6 %collective-permute-start.4 = (bf16[192,768]{0,1:T(8,128)(2,1)S(1)}, bf16[192,768]{0,1:T(8,128)(2,1)}, u32[]{:S(2)}, u32[]{:S(2)}) collective-permute-start(bf16[192,768]{0,1:T(8,128)(2,1)S(1)} %get-tuple-element.141), channel_id=1, source_target_pairs={{0,8},{4,12},{8,0},{12,4},{1,9},{5,13},{9,1},{13,5},{2,10},{6,14},... | collective-permute-start | bytes 884744 | tf_op jit(solution)/shard_map/ppermute | solution.py:260
  60.1 51.8 %collective-permute-start.5 = (bf16[192,768]{0,1:T(8,128)(2,1)S(1)}, bf16[192,768]{0,1:T(8,128)(2,1)S(1)}, u32[]{:S(2)}, u32[]{:S(2)}) collective-permute-start(bf16[192,768]{0,1:T(8,128)(2,1)S(1)} %get-tuple-element.141), channel_id=1, source_target_pairs={{0,12},{4,8},{8,4},{12,0},{1,13},{5,9},{9,5},{13,1},{2,14},{6,10},... | collective-permute-start | bytes 884744 | tf_op jit(solution)/shard_map/ppermute | solution.py:260
  60.4 79.7 %collective-permute-start.7 = (bf16[512,768]{1,0:T(8,128)(2,1)}, bf16[512,768]{1,0:T(8,128)(2,1)S(1)}, u32[]{:S(2)}, u32[]{:S(2)}) collective-permute-start(bf16[512,768]{1,0:T(8,128)(2,1)} %collective-permute-done), channel_id=1, source_target_pairs={{0,1},{1,0},{2,3},{3,2},{4,5},{5,4},{6,7},{7,6},{8,9},{9,8},{10,11... | collective-permute-start | bytes 2359304 | tf_op jit(solution)/shard_map/ppermute | solution.py:244
  61.9 79.7 %collective-permute-start.6 = (bf16[512,768]{1,0:T(8,128)(2,1)}, bf16[512,768]{1,0:T(8,128)(2,1)}, u32[]{:S(2)}, u32[]{:S(2)}) collective-permute-start(bf16[512,768]{1,0:T(8,128)(2,1)} %collective-permute-done), channel_id=1, source_target_pairs={{0,16},{16,0},{1,17},{17,1},{2,18},{18,2},{3,19},{19,3},{4,20},{20... | collective-permute-start | bytes 2359304 | tf_op jit(solution)/shard_map/ppermute | solution.py:240
  93.3 23.7 %collective-permute-start.14 = (f32[2,2,768]{2,1,0:T(2,128)S(1)}, f32[2,2,768]{2,1,0:T(2,128)S(1)}, u32[]{:S(2)}, u32[]{:S(2)}) collective-permute-start(f32[2,2,768]{2,1,0:T(2,128)S(1)} %constant_dynamic-update-slice_fusion), channel_id=1, source_target_pairs={{0,16},{16,0},{1,17},{17,1},{2,18},{18,2},{3,19},{19,3},{4,20},{20... | collective-permute-start | bytes 36872 | tf_op jit(solution)/shard_map/ppermute | solution.py:240
  115.5 24.6 %collective-permute-start.12 = (bf16[192,768]{1,0:T(8,128)(2,1)S(1)}, bf16[192,768]{1,0:T(8,128)(2,1)S(1)}, u32[]{:S(2)}, u32[]{:S(2)}) collective-permute-start(bf16[192,768]{1,0:T(8,128)(2,1)S(1)} %get-tuple-element.125), channel_id=1, source_target_pairs={{0,1},{1,0},{2,3},{3,2},{4,5},{5,4},{6,7},{7,6},{8,9},{9,8},{10,11... | collective-permute-start | bytes 884744 | tf_op jit(solution)/shard_map/ppermute | solution.py:244
  117.1 128.7 %collective-permute-start.20 = (bf16[192,768]{0,1:T(8,128)(2,1)}, bf16[192,768]{0,1:T(8,128)(2,1)}, u32[]{:S(2)}, u32[]{:S(2)}) collective-permute-start(bf16[192,768]{0,1:T(8,128)(2,1)} %get-tuple-element.140), channel_id=1, source_target_pairs={{0,4},{4,0},{8,12},{12,8},{1,5},{5,1},{9,13},{13,9},{2,6},{6,2},{1... | collective-permute-start | bytes 884744 | tf_op jit(solution)/shard_map/ppermute | solution.py:260
  141.2 36.3 %collective-permute-start.13 = (bf16[2,192,768]{2,1,0:T(8,128)(2,1)}, bf16[2,192,768]{2,1,0:T(8,128)(2,1)}, u32[]{:S(2)}, u32[]{:S(2)}) collective-permute-start(bf16[2,192,768]{2,1,0:T(8,128)(2,1)} %pad_maximum_fusion.27), channel_id=1, source_target_pairs={{0,16},{16,0},{1,17},{17,1},{2,18},{18,2},{3,19},{19,3},{4,20},{20... | collective-permute-start | bytes 1769480 | tf_op jit(solution)/shard_map/ppermute | solution.py:240
  141.5 582.4 %reduce-scatter.5.cloned.1.call-start = ((), (), s32[]{:S(2)}) async-start(), calls=%async_computation.5 | async-start | bytes 4423680 | tf_op jit(solution)/shard_map/reduce_scatter | solution.py:552
  147.7 67.5 %collective-permute-start.17 = (bf16[3,768,768]{2,1,0:T(8,128)(2,1)}, bf16[3,768,768]{2,1,0:T(8,128)(2,1)S(1)}, u32[]{:S(2)}, u32[]{:S(2)}) collective-permute-start(bf16[3,768,768]{2,1,0:T(8,128)(2,1)} %all-gather.3.cloned.1.call-done), channel_id=1, source_target_pairs={{0,16},{16,0},{1,17},{17,1},{2,18},{18,2},{3,19},{19,3},{4,20},{20... | collective-permute-start | bytes 10616840 | tf_op jit(solution)/shard_map/ppermute | solution.py:240
  176.5 15.6 %collective-permute-start.11 = (bf16[192,512]{1,0:T(8,128)(2,1)S(1)}, bf16[192,512]{1,0:T(8,128)(2,1)S(1)}, u32[]{:S(2)}, u32[]{:S(2)}) collective-permute-start(bf16[192,512]{1,0:T(8,128)(2,1)S(1)} %get-tuple-element.143), channel_id=1, source_target_pairs={{0,17},{1,16},{2,19},{3,18},{16,1},{17,0},{18,3},{19,2},{4,21},{5,... | collective-permute-start | bytes 589832 | tf_op jit(solution)/shard_map/ppermute | solution.py:256
  177.6 14.6 %collective-permute-start.9 = (bf16[192,512]{1,0:T(8,128)(2,1)S(1)}, bf16[192,512]{1,0:T(8,128)(2,1)S(1)}, u32[]{:S(2)}, u32[]{:S(2)}) collective-permute-start(bf16[192,512]{1,0:T(8,128)(2,1)S(1)} %get-tuple-element.145), channel_id=1, source_target_pairs={{0,16},{16,0},{1,17},{17,1},{2,18},{18,2},{3,19},{19,3},{4,20},{20... | collective-permute-start | bytes 589832 | tf_op jit(solution)/shard_map/ppermute | solution.py:240
  183.7 67.2 %collective-permute-start.21 = (bf16[192,768]{0,1:T(8,128)(2,1)}, bf16[192,768]{0,1:T(8,128)(2,1)}, u32[]{:S(2)}, u32[]{:S(2)}) collective-permute-start(bf16[192,768]{0,1:T(8,128)(2,1)} %get-tuple-element.140), channel_id=1, source_target_pairs={{0,8},{4,12},{8,0},{12,4},{1,9},{5,13},{9,1},{13,5},{2,10},{6,14},... | collective-permute-start | bytes 884744 | tf_op jit(solution)/shard_map/ppermute | solution.py:260
  192.1 63.3 %collective-permute-start.22 = (bf16[192,768]{0,1:T(8,128)(2,1)}, bf16[192,768]{0,1:T(8,128)(2,1)}, u32[]{:S(2)}, u32[]{:S(2)}) collective-permute-start(bf16[192,768]{0,1:T(8,128)(2,1)} %get-tuple-element.140), channel_id=1, source_target_pairs={{0,12},{4,8},{8,4},{12,0},{1,13},{5,9},{9,5},{13,1},{2,14},{6,10},... | collective-permute-start | bytes 884744 | tf_op jit(solution)/shard_map/ppermute | solution.py:260
  195.1 17.6 %collective-permute-start.18 = (bf16[512,768]{1,0:T(8,128)(2,1)S(1)}, bf16[512,768]{1,0:T(8,128)(2,1)S(1)}, u32[]{:S(2)}, u32[]{:S(2)}) collective-permute-start(bf16[512,768]{1,0:T(8,128)(2,1)S(1)} %fusion.234), channel_id=1, source_target_pairs={{0,1},{1,0},{2,3},{3,2},{4,5},{5,4},{6,7},{7,6},{8,9},{9,8},{10,11... | collective-permute-start | bytes 2359304 | tf_op jit(solution)/shard_map/ppermute | solution.py:244
  219.7 16.8 %collective-permute-start.19 = (bf16[512,768]{1,0:T(8,128)(2,1)S(1)}, bf16[512,768]{1,0:T(8,128)(2,1)S(1)}, u32[]{:S(2)}, u32[]{:S(2)}) collective-permute-start(bf16[512,768]{1,0:T(8,128)(2,1)S(1)} %add_convert_fusion.9), channel_id=1, source_target_pairs={{0,1},{1,0},{2,3},{3,2},{4,5},{5,4},{6,7},{7,6},{8,9},{9,8},{10,11... | collective-permute-start | bytes 2359304 | tf_op jit(solution)/shard_map/ppermute | solution.py:244
  238.2 27.1 %collective-permute-start.24 = (bf16[512,768]{1,0:T(8,128)(2,1)S(1)}, bf16[512,768]{1,0:T(8,128)(2,1)}, u32[]{:S(2)}, u32[]{:S(2)}) collective-permute-start(bf16[512,768]{1,0:T(8,128)(2,1)S(1)} %add_convert_fusion.8), channel_id=1, source_target_pairs={{0,1},{1,0},{2,3},{3,2},{4,5},{5,4},{6,7},{7,6},{8,9},{9,8},{10,11... | collective-permute-start | bytes 2359304 | tf_op jit(solution)/shard_map/ppermute | solution.py:244
  240.0 31.9 %collective-permute-start.23 = (bf16[512,768]{1,0:T(8,128)(2,1)S(1)}, bf16[512,768]{1,0:T(8,128)(2,1)}, u32[]{:S(2)}, u32[]{:S(2)}) collective-permute-start(bf16[512,768]{1,0:T(8,128)(2,1)S(1)} %add_convert_fusion.8), channel_id=1, source_target_pairs={{0,16},{16,0},{1,17},{17,1},{2,18},{18,2},{3,19},{19,3},{4,20},{20... | collective-permute-start | bytes 2359304 | tf_op jit(solution)/shard_map/ppermute | solution.py:240
  261.0 9.5 %collective-permute-start.29 = (bf16[192,768]{1,0:T(8,128)(2,1)S(1)}, bf16[192,768]{1,0:T(8,128)(2,1)S(1)}, u32[]{:S(2)}, u32[]{:S(2)}) collective-permute-start(bf16[192,768]{1,0:T(8,128)(2,1)S(1)} %get-tuple-element.123), channel_id=1, source_target_pairs={{0,1},{1,0},{2,3},{3,2},{4,5},{5,4},{6,7},{7,6},{8,9},{9,8},{10,11... | collective-permute-start | bytes 884744 | tf_op jit(solution)/shard_map/ppermute | solution.py:244
  263.5 101.5 %collective-permute-start.36 = (bf16[512,768]{1,0:T(8,128)(2,1)}, bf16[512,768]{1,0:T(8,128)(2,1)S(1)}, u32[]{:S(2)}, u32[]{:S(2)}) collective-permute-start(bf16[512,768]{1,0:T(8,128)(2,1)} %dynamic-slice_bitcast_fusion), channel_id=1, source_target_pairs={{0,0},{1,1},{2,16},{3,17},{16,2},{17,3},{18,18},{19,19},{4,4},{5,5... | collective-permute-start | bytes 2359304 | tf_op jit(solution)/shard_map/ppermute | solution.py:256
  265.3 9.6 %collective-permute-start.25 = (bf16[512,768]{1,0:T(8,128)(2,1)}, bf16[512,768]{1,0:T(8,128)(2,1)}, u32[]{:S(2)}, u32[]{:S(2)}) collective-permute-start(bf16[512,768]{1,0:T(8,128)(2,1)} %collective-permute-done.24), channel_id=1, source_target_pairs={{0,16},{16,0},{1,17},{17,1},{2,18},{18,2},{3,19},{19,3},{4,20},{20... | collective-permute-start | bytes 2359304 | tf_op jit(solution)/shard_map/ppermute | solution.py:240
  271.4 35.9 %collective-permute-start.30 = (bf16[2,192,768]{2,1,0:T(8,128)(2,1)}, bf16[2,192,768]{2,1,0:T(8,128)(2,1)}, u32[]{:S(2)}, u32[]{:S(2)}) collective-permute-start(bf16[2,192,768]{2,1,0:T(8,128)(2,1)} %pad_maximum_fusion.28), channel_id=1, source_target_pairs={{0,16},{16,0},{1,17},{17,1},{2,18},{18,2},{3,19},{19,3},{4,20},{20... | collective-permute-start | bytes 1769480 | tf_op jit(solution)/shard_map/ppermute | solution.py:240
  271.5 50.3 %collective-permute-start.31 = (bf16[3,768,768]{2,1,0:T(8,128)(2,1)}, bf16[3,768,768]{2,1,0:T(8,128)(2,1)S(1)}, u32[]{:S(2)}, u32[]{:S(2)}) collective-permute-start(bf16[3,768,768]{2,1,0:T(8,128)(2,1)} %all-gather.5.cloned.1.call-done), channel_id=1, source_target_pairs={{0,16},{16,0},{1,17},{17,1},{2,18},{18,2},{3,19},{19,3},{4,20},{20... | collective-permute-start | bytes 10616840 | tf_op jit(solution)/shard_map/ppermute | solution.py:240
  307.3 10.7 %collective-permute-start.28 = (bf16[192,512]{1,0:T(8,128)(2,1)S(1)}, bf16[192,512]{1,0:T(8,128)(2,1)S(1)}, u32[]{:S(2)}, u32[]{:S(2)}) collective-permute-start(bf16[192,512]{1,0:T(8,128)(2,1)S(1)} %get-tuple-element.137), channel_id=1, source_target_pairs={{0,17},{1,16},{2,19},{3,18},{16,1},{17,0},{18,3},{19,2},{4,21},{5,... | collective-permute-start | bytes 589832 | tf_op jit(solution)/shard_map/ppermute | solution.py:256
  319.6 19.8 %collective-permute-start.32 = (bf16[512,768]{1,0:T(8,128)(2,1)S(1)}, bf16[512,768]{1,0:T(8,128)(2,1)S(1)}, u32[]{:S(2)}, u32[]{:S(2)}) collective-permute-start(bf16[512,768]{1,0:T(8,128)(2,1)S(1)} %fusion.235), channel_id=1, source_target_pairs={{0,1},{1,0},{2,3},{3,2},{4,5},{5,4},{6,7},{7,6},{8,9},{9,8},{10,11... | collective-permute-start | bytes 2359304 | tf_op jit(solution)/shard_map/ppermute | solution.py:244
  344.4 19.0 %collective-permute-start.33 = (bf16[512,768]{1,0:T(8,128)(2,1)S(1)}, bf16[512,768]{1,0:T(8,128)(2,1)S(1)}, u32[]{:S(2)}, u32[]{:S(2)}) collective-permute-start(bf16[512,768]{1,0:T(8,128)(2,1)S(1)} %add_convert_fusion.7), channel_id=1, source_target_pairs={{0,1},{1,0},{2,3},{3,2},{4,5},{5,4},{6,7},{7,6},{8,9},{9,8},{10,11... | collective-permute-start | bytes 2359304 | tf_op jit(solution)/shard_map/ppermute | solution.py:244
  366.3 18.1 %collective-permute-start.37 = (bf16[512,768]{1,0:T(8,128)(2,1)S(1)}, bf16[512,768]{1,0:T(8,128)(2,1)S(1)}, u32[]{:S(2)}, u32[]{:S(2)}) collective-permute-start(bf16[512,768]{1,0:T(8,128)(2,1)S(1)} %fusion.391), channel_id=1, source_target_pairs={{0,1},{1,0},{2,3},{3,2},{4,5},{5,4},{6,7},{7,6},{8,9},{9,8},{10,11... | collective-permute-start | bytes 2359304 | tf_op jit(solution)/shard_map/ppermute | solution.py:244
  367.7 29.3 %collective-permute-start.34 = (bf16[512,768]{1,0:T(8,128)(2,1)S(1)}, bf16[512,768]{1,0:T(8,128)(2,1)S(1)}, u32[]{:S(2)}, u32[]{:S(2)}) collective-permute-start(bf16[512,768]{1,0:T(8,128)(2,1)S(1)} %get-tuple-element.101), channel_id=1, source_target_pairs={{0,0},{1,1},{2,16},{3,17},{16,2},{17,3},{18,18},{19,19},{4,4},{5,5... | collective-permute-start | bytes 2359304 | tf_op jit(solution)/shard_map/ppermute | solution.py:256
  368.4 28.6 %collective-permute-start.35 = (bf16[512,768]{1,0:T(8,128)(2,1)S(1)}, bf16[512,768]{1,0:T(8,128)(2,1)S(1)}, u32[]{:S(2)}, u32[]{:S(2)}) collective-permute-start(bf16[512,768]{1,0:T(8,128)(2,1)S(1)} %get-tuple-element.102), channel_id=1, source_target_pairs={{0,16},{1,17},{2,0},{3,1},{16,18},{17,19},{18,2},{19,3},{4,20},{5,... | collective-permute-start | bytes 2359304 | tf_op jit(solution)/shard_map/ppermute | solution.py:256
  392.1 134.0 %collective-permute-start.66 = (bf16[3,768,768]{2,1,0:T(8,128)(2,1)}, bf16[3,768,768]{2,1,0:T(8,128)(2,1)}, u32[]{:S(2)}, u32[]{:S(2)}) collective-permute-start(bf16[3,768,768]{2,1,0:T(8,128)(2,1)} %pad_maximum_fusion.1), channel_id=1, source_target_pairs={{0,16},{16,0},{1,17},{17,1},{2,18},{18,2},{3,19},{19,3},{4,20},{20... | collective-permute-start | bytes 10616840 | tf_op jit(solution)/shard_map/ppermute | solution.py:240
  396.6 20.0 %collective-permute-start.38 = (bf16[512,768]{1,0:T(8,128)(2,1)S(1)}, bf16[512,768]{1,0:T(8,128)(2,1)S(1)}, u32[]{:S(2)}, u32[]{:S(2)}) collective-permute-start(bf16[512,768]{1,0:T(8,128)(2,1)S(1)} %add_convert_fusion.5), channel_id=1, source_target_pairs={{0,1},{1,0},{2,3},{3,2},{4,5},{5,4},{6,7},{7,6},{8,9},{9,8},{10,11... | collective-permute-start | bytes 2359304 | tf_op jit(solution)/shard_map/ppermute | solution.py:244
  420.3 10.7 %collective-permute-start.41 = (bf16[192,512]{1,0:T(8,128)(2,1)S(1)}, bf16[192,512]{1,0:T(8,128)(2,1)S(1)}, u32[]{:S(2)}, u32[]{:S(2)}) collective-permute-start(bf16[192,512]{1,0:T(8,128)(2,1)S(1)} %get-tuple-element.133), channel_id=1, source_target_pairs={{0,17},{1,16},{2,19},{3,18},{16,1},{17,0},{18,3},{19,2},{4,21},{5,... | collective-permute-start | bytes 589832 | tf_op jit(solution)/shard_map/ppermute | solution.py:256
  423.6 58.9 %collective-permute-start.58 = (bf16[2,192,768]{2,1,0:T(8,128)(2,1)}, bf16[2,192,768]{2,1,0:T(8,128)(2,1)}, u32[]{:S(2)}, u32[]{:S(2)}) collective-permute-start(bf16[2,192,768]{2,1,0:T(8,128)(2,1)} %slice.488), channel_id=1, source_target_pairs={{0,16},{16,0},{1,17},{17,1},{2,18},{18,2},{3,19},{19,3},{4,20},{20... | collective-permute-start | bytes 1769480 | tf_op jit(solution)/shard_map/ppermute | solution.py:240
  483.8 9.9 %collective-permute-start.59 = (bf16[192,768]{1,0:T(8,128)(2,1)S(1)}, bf16[192,768]{1,0:T(8,128)(2,1)S(1)}, u32[]{:S(2)}, u32[]{:S(2)}) collective-permute-start(bf16[192,768]{1,0:T(8,128)(2,1)S(1)} %fusion.345), channel_id=1, source_target_pairs={{0,1},{1,0},{2,3},{3,2},{4,5},{5,4},{6,7},{7,6},{8,9},{9,8},{10,11... | collective-permute-start | bytes 884744 | tf_op jit(solution)/shard_map/ppermute | solution.py:244
  485.2 24.6 %collective-permute-start.43 = (bf16[512,768]{1,0:T(8,128)(2,1)S(1)}, bf16[512,768]{1,0:T(8,128)(2,1)S(1)}, u32[]{:S(2)}, u32[]{:S(2)}) collective-permute-start(bf16[512,768]{1,0:T(8,128)(2,1)S(1)} %fusion.93), channel_id=1, source_target_pairs={{0,1},{1,0},{2,3},{3,2},{4,5},{5,4},{6,7},{7,6},{8,9},{9,8},{10,11... | collective-permute-start | bytes 2359304 | tf_op jit(solution)/shard_map/ppermute | solution.py:244
  496.0 174.3 %collective-permute-start.60 = (bf16[192,768]{0,1:T(8,128)(2,1)}, bf16[192,768]{0,1:T(8,128)(2,1)}, u32[]{:S(2)}, u32[]{:S(2)}) collective-permute-start(bf16[192,768]{0,1:T(8,128)(2,1)} %get-tuple-element.116), channel_id=1, source_target_pairs={{0,4},{4,0},{8,12},{12,8},{1,5},{5,1},{9,13},{13,9},{2,6},{6,2},{1... | collective-permute-start | bytes 884744 | tf_op jit(solution)/shard_map/ppermute | solution.py:260
  496.0 174.4 %collective-permute-start.61 = (bf16[192,768]{0,1:T(8,128)(2,1)}, bf16[192,768]{0,1:T(8,128)(2,1)}, u32[]{:S(2)}, u32[]{:S(2)}) collective-permute-start(bf16[192,768]{0,1:T(8,128)(2,1)} %get-tuple-element.117), channel_id=1, source_target_pairs={{0,8},{4,12},{8,0},{12,4},{1,9},{5,13},{9,1},{13,5},{2,10},{6,14},... | collective-permute-start | bytes 884744 | tf_op jit(solution)/shard_map/ppermute | solution.py:260
  512.7 19.3 %collective-permute-start.44 = (bf16[512,768]{1,0:T(8,128)(2,1)}, bf16[512,768]{1,0:T(8,128)(2,1)}, u32[]{:S(2)}, u32[]{:S(2)}) collective-permute-start(bf16[512,768]{1,0:T(8,128)(2,1)} %fusion.392), channel_id=1, source_target_pairs={{0,1},{1,0},{2,3},{3,2},{4,5},{5,4},{6,7},{7,6},{8,9},{9,8},{10,11... | collective-permute-start | bytes 2359304 | tf_op jit(solution)/shard_map/ppermute | solution.py:244
  529.9 194.1 %reduce-scatter.3.cloned.1.call-start = ((), (), s32[]{:S(2)}) async-start(), calls=%async_computation.4 | async-start | bytes 4423680 | tf_op jit(solution)/shard_map/reduce_scatter | solution.py:552
  541.3 32.6 %collective-permute-start.65 = (bf16[3,768,768]{2,1,0:T(8,128)(2,1)S(1)}, bf16[3,768,768]{2,1,0:T(8,128)(2,1)S(1)}, u32[]{:S(2)}, u32[]{:S(2)}) collective-permute-start(bf16[3,768,768]{2,1,0:T(8,128)(2,1)S(1)} %pad_maximum_fusion), channel_id=1, source_target_pairs={{0,16},{16,0},{1,17},{17,1},{2,18},{18,2},{3,19},{19,3},{4,20},{20... | collective-permute-start | bytes 10616840 | tf_op jit(solution)/shard_map/ppermute | solution.py:240
  549.0 18.8 %collective-permute-start.45 = (bf16[512,768]{1,0:T(8,128)(2,1)S(1)}, bf16[512,768]{1,0:T(8,128)(2,1)S(1)}, u32[]{:S(2)}, u32[]{:S(2)}) collective-permute-start(bf16[512,768]{1,0:T(8,128)(2,1)S(1)} %add_convert_fusion.4), channel_id=1, source_target_pairs={{0,1},{1,0},{2,3},{3,2},{4,5},{5,4},{6,7},{7,6},{8,9},{9,8},{10,11... | collective-permute-start | bytes 2359304 | tf_op jit(solution)/shard_map/ppermute | solution.py:244
  573.6 8.2 %collective-permute-start.76 = (f32[2,2,768]{2,1,0:T(2,128)}, f32[2,2,768]{2,1,0:T(2,128)}, u32[]{:S(2)}, u32[]{:S(2)}) collective-permute-start(f32[2,2,768]{2,1,0:T(2,128)} %select_add_fusion), channel_id=1, source_target_pairs={{0,1},{1,0},{2,3},{3,2},{4,5},{5,4},{6,7},{7,6},{8,9},{9,8},{10,11... | collective-permute-start | bytes 36872 | tf_op jit(solution)/shard_map/ppermute | solution.py:244
  582.7 9.7 %collective-permute-start.79 = (f32[2,2,768]{2,1,0:T(2,128)S(1)}, f32[2,2,768]{2,1,0:T(2,128)S(1)}, u32[]{:S(2)}, u32[]{:S(2)}) collective-permute-start(f32[2,2,768]{2,1,0:T(2,128)S(1)} %add_add_fusion.7), channel_id=1, source_target_pairs={{0,4},{4,0},{8,12},{12,8},{1,5},{5,1},{9,13},{13,9},{2,6},{6,2},{1... | collective-permute-start | bytes 36872 | tf_op jit(solution)/shard_map/ppermute | solution.py:260
  599.0 76.3 %collective-permute-start.62 = (bf16[192,768]{0,1:T(8,128)(2,1)}, bf16[192,768]{0,1:T(8,128)(2,1)}, u32[]{:S(2)}, u32[]{:S(2)}) collective-permute-start(bf16[192,768]{0,1:T(8,128)(2,1)} %get-tuple-element.118), channel_id=1, source_target_pairs={{0,12},{4,8},{8,4},{12,0},{1,13},{5,9},{9,5},{13,1},{2,14},{6,10},... | collective-permute-start | bytes 884744 | tf_op jit(solution)/shard_map/ppermute | solution.py:260
  604.0 54.7 %collective-permute-start.53 = (bf16[2,192,768]{2,1,0:T(8,128)(2,1)S(1)}, bf16[2,192,768]{2,1,0:T(8,128)(2,1)}, u32[]{:S(2)}, u32[]{:S(2)}) collective-permute-start(bf16[2,192,768]{2,1,0:T(8,128)(2,1)S(1)} %slice.484), channel_id=1, source_target_pairs={{0,16},{16,0},{1,17},{17,1},{2,18},{18,2},{3,19},{19,3},{4,20},{20... | collective-permute-start | bytes 1769480 | tf_op jit(solution)/shard_map/ppermute | solution.py:240
  653.1 61.9 %collective-permute-start.49 = (bf16[2,512,768]{2,1,0:T(8,128)(2,1)}, bf16[2,512,768]{2,1,0:T(8,128)(2,1)}, u32[]{:S(2)}, u32[]{:S(2)}) collective-permute-start(bf16[2,512,768]{2,1,0:T(8,128)(2,1)} %pad_maximum_fusion.3), channel_id=1, source_target_pairs={{0,16},{16,0},{1,17},{17,1},{2,18},{18,2},{3,19},{19,3},{4,20},{20... | collective-permute-start | bytes 4718600 | tf_op jit(solution)/shard_map/ppermute | solution.py:240
  659.9 9.0 %collective-permute-start.54 = (bf16[192,768]{1,0:T(8,128)(2,1)S(1)}, bf16[192,768]{1,0:T(8,128)(2,1)S(1)}, u32[]{:S(2)}, u32[]{:S(2)}) collective-permute-start(bf16[192,768]{1,0:T(8,128)(2,1)S(1)} %fusion.344), channel_id=1, source_target_pairs={{0,1},{1,0},{2,3},{3,2},{4,5},{5,4},{6,7},{7,6},{8,9},{9,8},{10,11... | collective-permute-start | bytes 884744 | tf_op jit(solution)/shard_map/ppermute | solution.py:244
  670.2 15.2 %collective-permute-start.55 = (bf16[192,768]{0,1:T(8,128)(2,1)S(1)}, bf16[192,768]{0,1:T(8,128)(2,1)S(1)}, u32[]{:S(2)}, u32[]{:S(2)}) collective-permute-start(bf16[192,768]{0,1:T(8,128)(2,1)S(1)} %get-tuple-element.119), channel_id=1, source_target_pairs={{0,4},{4,0},{8,12},{12,8},{1,5},{5,1},{9,13},{13,9},{2,6},{6,2},{1... | collective-permute-start | bytes 884744 | tf_op jit(solution)/shard_map/ppermute | solution.py:260
  670.3 31.7 %collective-permute-start.56 = (bf16[192,768]{0,1:T(8,128)(2,1)S(1)}, bf16[192,768]{0,1:T(8,128)(2,1)S(1)}, u32[]{:S(2)}, u32[]{:S(2)}) collective-permute-start(bf16[192,768]{0,1:T(8,128)(2,1)S(1)} %get-tuple-element.120), channel_id=1, source_target_pairs={{0,8},{4,12},{8,0},{12,4},{1,9},{5,13},{9,1},{13,5},{2,10},{6,14},... | collective-permute-start | bytes 884744 | tf_op jit(solution)/shard_map/ppermute | solution.py:260
  670.4 31.7 %collective-permute-start.57 = (bf16[192,768]{0,1:T(8,128)(2,1)S(1)}, bf16[192,768]{0,1:T(8,128)(2,1)S(1)}, u32[]{:S(2)}, u32[]{:S(2)}) collective-permute-start(bf16[192,768]{0,1:T(8,128)(2,1)S(1)} %get-tuple-element.121), channel_id=1, source_target_pairs={{0,12},{4,8},{8,4},{12,0},{1,13},{5,9},{9,5},{13,1},{2,14},{6,10},... | collective-permute-start | bytes 884744 | tf_op jit(solution)/shard_map/ppermute | solution.py:260
  720.3 17.6 %collective-permute-start.50 = (bf16[512,768]{1,0:T(8,128)(2,1)}, bf16[512,768]{1,0:T(8,128)(2,1)}, u32[]{:S(2)}, u32[]{:S(2)}) collective-permute-start(bf16[512,768]{1,0:T(8,128)(2,1)} %fusion.87), channel_id=1, source_target_pairs={{0,1},{1,0},{2,3},{3,2},{4,5},{5,4},{6,7},{7,6},{8,9},{9,8},{10,11... | collective-permute-start | bytes 2359304 | tf_op jit(solution)/shard_map/ppermute | solution.py:244
  725.7 25.5 %collective-permute-start.67 = (bf16[3,192,768]{2,1,0:T(8,128)(2,1)S(1)}, bf16[3,192,768]{2,1,0:T(8,128)(2,1)S(1)}, u32[]{:S(2)}, u32[]{:S(2)}) collective-permute-start(bf16[3,192,768]{2,1,0:T(8,128)(2,1)S(1)} %get-tuple-element.105), channel_id=1, source_target_pairs={{0,0},{1,1},{2,16},{3,17},{16,2},{17,3},{18,18},{19,19},{4,4},{5,5... | collective-permute-start | bytes 2654216 | tf_op jit(solution)/shard_map/ppermute | solution.py:256
  726.6 27.0 %collective-permute-start.68 = (bf16[3,192,768]{2,1,0:T(8,128)(2,1)S(1)}, bf16[3,192,768]{2,1,0:T(8,128)(2,1)S(1)}, u32[]{:S(2)}, u32[]{:S(2)}) collective-permute-start(bf16[3,192,768]{2,1,0:T(8,128)(2,1)S(1)} %get-tuple-element.106), channel_id=1, source_target_pairs={{0,16},{1,17},{2,0},{3,1},{16,18},{17,19},{18,2},{19,3},{4,20},{5,... | collective-permute-start | bytes 2654216 | tf_op jit(solution)/shard_map/ppermute | solution.py:256
  740.5 27.6 %collective-permute-start.52 = (bf16[512,768]{1,0:T(8,128)(2,1)S(1)}, bf16[512,768]{1,0:T(8,128)(2,1)}, u32[]{:S(2)}, u32[]{:S(2)}) collective-permute-start(bf16[512,768]{1,0:T(8,128)(2,1)S(1)} %broadcast_select_fusion.4), channel_id=1, source_target_pairs={{0,16},{1,17},{2,0},{3,1},{16,18},{17,19},{18,2},{19,3},{4,20},{5,... | collective-permute-start | bytes 2359304 | tf_op jit(solution)/shard_map/ppermute | solution.py:256
  743.5 24.6 %collective-permute-start.51 = (bf16[512,768]{1,0:T(8,128)(2,1)}, bf16[512,768]{1,0:T(8,128)(2,1)}, u32[]{:S(2)}, u32[]{:S(2)}) collective-permute-start(bf16[512,768]{1,0:T(8,128)(2,1)} %get-tuple-element.67), channel_id=1, source_target_pairs={{0,0},{1,1},{2,16},{3,17},{16,2},{17,3},{18,18},{19,19},{4,4},{5,5... | collective-permute-start | bytes 2359304 | tf_op jit(solution)/shard_map/ppermute | solution.py:256
  773.3 12.8 %collective-permute-start.72 = (f32[8,128]{0,1:T(8,128)S(1)}, f32[8,128]{0,1:T(8,128)S(1)}, u32[]{:S(2)}, u32[]{:S(2)}) collective-permute-start(f32[8,128]{0,1:T(8,128)S(1)} %add_add_fusion.5), channel_id=1, source_target_pairs={{0,4},{4,0},{8,12},{12,8},{1,5},{5,1},{9,13},{13,9},{2,6},{6,2},{1... | collective-permute-start | bytes 12296 | tf_op jit(solution)/shard_map/ppermute | solution.py:260
  781.8 8.4 %collective-permute-start.73 = (f32[8,128]{0,1:T(8,128)S(1)}, f32[8,128]{0,1:T(8,128)S(1)}, u32[]{:S(2)}, u32[]{:S(2)}) collective-permute-start(f32[8,128]{0,1:T(8,128)S(1)} %add_add_fusion.5), channel_id=1, source_target_pairs={{0,8},{4,12},{8,0},{12,4},{1,9},{5,13},{9,1},{13,5},{2,10},{6,14},... | collective-permute-start | bytes 12296 | tf_op jit(solution)/shard_map/ppermute | solution.py:260
  (170 other events, 2828.0 us)
Sparse Core Ops, SparseCore 0:
  36.1 105.6 all-gather.2
  143.9 104.1 all-gather.4
  530.0 72.7 reduce-scatter.4
  604.9 66.6 reduce-scatter.2

commit v2 on v1

v2 whole, which is shorter than its diff:
```python
import functools

import jax
import jax.numpy as jnp
import numpy as np
from jax import lax
from jax.experimental import pallas as pl
from jax.experimental.pallas import tpu as pltpu
from jax.sharding import PartitionSpec as P

HEAD = 64
FQ, FK = 512, 512
BQ, BK = 256, 512
SAFE = 40.0
WINDOW = 1024


def doc_bounds(pos, ends, length):
    start = jnp.where(pos < ends[0], 0, jnp.where(pos < ends[1], ends[0], ends[1]))
    last = jnp.where(pos < ends[0], ends[0], jnp.where(pos < ends[1], ends[1], length)) - 1
    return jnp.maximum(start, pos - (WINDOW - 1)), jnp.minimum(last, pos + (WINDOW - 1))


def key_span(q_start, rows, ends, length, deep):
    low, _ = doc_bounds(q_start, ends, length)
    _, high = doc_bounds(q_start + rows - 1, ends, length)
    first = low // 128 * 128
    tiles = (high + 1 - first + deep - 1) // deep
    return jnp.minimum(first, length - tiles * deep), tiles


def attn_fwd_kernel(place, ends, near, far, matrix, cos, sin, out, lse, qkv, a_t, k_n, o_t, calm, *, heads):
    step = pl.program_id(0)
    width = heads * HEAD
    half = HEAD // 2
    length = qkv.shape[1]
    rows = length // 4

    @pl.when(step == 0)
    def _():
        a_t[...] = matrix[:, : 3 * width].T
        tops = [jnp.zeros((1, rows), jnp.float32) for _ in range(2 * heads)]
        for slab in range(4):
            src = near if slab < 2 else far
            start = pl.multiple_of(place[slab] * rows, rows)
            here = pl.ds(start, rows)
            proj = lax.dot_general(
                a_t[...], src[(slab % 2) * rows : (slab % 2 + 1) * rows, :], (((1,), (1,)), ((), ())),
                preferred_element_type=jnp.float32,
            )
            c, s = cos[:, here], sin[:, here]
            for i in range(2 * heads):
                first, second = proj[i * HEAD : i * HEAD + half], proj[i * HEAD + half : (i + 1) * HEAD]
                turned = jnp.concatenate([first * c - second * s, second * c + first * s], axis=0).astype(jnp.bfloat16)
                if i < heads:
                    turned = turned * jnp.bfloat16(HEAD**-0.5)
                else:
                    k_n[i - heads, here, :] = turned.T
                qkv[i * HEAD : (i + 1) * HEAD, here] = turned
                size = turned.astype(jnp.float32)
                tops[i] = jnp.maximum(tops[i], jnp.sum(size * size, axis=0, keepdims=True))
            qkv[2 * width :, here] = proj[2 * width :].astype(jnp.bfloat16)
        worst = jnp.float32(0.0)
        for h in range(heads):
            worst = jnp.maximum(worst, jnp.max(tops[h]) * jnp.max(tops[heads + h]))
        calm[0] = (worst <= SAFE * SAFE).astype(jnp.int32)

    q_start = pl.multiple_of(step * FQ, FQ)
    here = pl.ds(q_start, FQ)
    low, high = doc_bounds(q_start + lax.broadcasted_iota(jnp.int32, (1, FQ), 1), (ends[0], ends[1]), length)
    first, tiles = key_span(q_start, FQ, (ends[0], ends[1]), length, FK)

    def score(h, keys):
        return jnp.dot(k_n[h, keys, :], qkv[h * HEAD : (h + 1) * HEAD, here], preferred_element_type=jnp.float32)

    def weigh(h, keys, p):
        return jnp.dot(
            qkv[2 * width + h * HEAD : 2 * width + (h + 1) * HEAD, keys], p.astype(jnp.bfloat16),
            preferred_element_type=jnp.float32,
        )

    def mask(t):
        k_start = pl.multiple_of(first + t * FK, 128)
        pos = k_start + lax.broadcasted_iota(jnp.int32, (FK, FQ), 0)
        return pl.ds(k_start, FK), (pos >= low) & (pos <= high)

    def finish(h, total, acc, log_sum):
        o_t[h * HEAD : (h + 1) * HEAD, here] = (acc / total).astype(jnp.bfloat16)
        lse[h : h + 1, here] = log_sum

    @pl.when(calm[0] == 1)
    def _():
        def tile(t, carry):
            keys, allowed = mask(t)
            new = []
            nxt = score(0, keys)
            for h in range(heads):
                total, acc = carry[h]
                s = nxt
                if h + 1 < heads:
                    nxt = score(h + 1, keys)
                p = jnp.where(allowed, jnp.exp(s), 0.0)
                new.append((total + jnp.sum(p, axis=0, keepdims=True), acc + weigh(h, keys, p)))
            return tuple(new)

        init = tuple((jnp.zeros((1, FQ), jnp.float32), jnp.zeros((HEAD, FQ), jnp.float32)) for _ in range(heads))
        for h, (total, acc) in enumerate(lax.fori_loop(0, tiles, tile, init)):
            finish(h, total, acc, jnp.log(total))

    @pl.when(calm[0] == 0)
    def _():
        def tile(t, carry):
            keys, allowed = mask(t)
            new = []
            for h in range(heads):
                top, total, acc = carry[h]
                s = jnp.where(allowed, score(h, keys), -1e30)
                new_top = jnp.maximum(top, jnp.max(s, axis=0, keepdims=True))
                p = jnp.exp(s - new_top)
                alpha = jnp.exp(top - new_top)
                total = total * alpha + jnp.sum(p, axis=0, keepdims=True)
                new.append((new_top, total, acc * alpha + weigh(h, keys, p)))
            return tuple(new)

        init = tuple(
            (jnp.full((1, FQ), -1e30, jnp.float32), jnp.zeros((1, FQ), jnp.float32), jnp.zeros((HEAD, FQ), jnp.float32))
            for _ in range(heads)
        )
        for h, (top, total, acc) in enumerate(lax.fori_loop(0, tiles, tile, init)):
            finish(h, total, acc, top + jnp.log(total))

    @pl.when(step == pl.num_programs(0) - 1)
    def _():
        for slab in range(4):
            out[slab] = o_t[:, pl.ds(pl.multiple_of(place[slab] * rows, rows), rows)]


def whole_spec(a):
    return pl.BlockSpec(a.shape, lambda i: (0,) * len(a.shape))


def attn_fwd(place, ends, near, far, matrix, cos, sin):
    length = 2 * near.shape[0]
    rows = length // 4
    width = matrix.shape[1] // 4
    heads = width // HEAD
    smem = pl.BlockSpec(memory_space=pltpu.SMEM)
    ops = (near, far, matrix, cos, sin)
    outs = (
        jax.ShapeDtypeStruct((4, width, rows), jnp.bfloat16),
        jax.ShapeDtypeStruct((heads, length), jnp.float32),
        jax.ShapeDtypeStruct((3 * width, length), jnp.bfloat16),
    )
    return pl.pallas_call(
        functools.partial(attn_fwd_kernel, heads=heads),
        grid=(length // FQ,),
        in_specs=[smem, smem] + [whole_spec(a) for a in ops],
        out_specs=tuple(whole_spec(o) for o in outs),
        out_shape=outs,
        scratch_shapes=[
            pltpu.VMEM((3 * width, matrix.shape[0]), jnp.bfloat16),
            pltpu.VMEM((heads, length, HEAD), jnp.bfloat16),
            pltpu.VMEM((width, length), jnp.bfloat16),
            pltpu.SMEM((1,), jnp.int32),
        ],
        compiler_params=pltpu.CompilerParams(vmem_limit_bytes=48 << 20),
        cost_estimate=pl.CostEstimate(
            flops=6 * length * length * width, bytes_accessed=16 * length * width, transcendentals=heads * length * length
        ),
        name="attn_fwd",
    )(place, ends, *ops)


def attn_bwd_kernel(place, ends, qkv, dout, out_t, lse, cos, sin, dproj, q_n, k_n, v_n, do_t, do_n, delta, dq_t, dk, dv, *, heads):
    step = pl.program_id(0)
    width = heads * HEAD
    length = qkv.shape[1]
    rows = length // 4
    half = HEAD // 2

    @pl.when(step == 0)
    def _():
        for slab in range(4):
            start = pl.multiple_of(place[slab] * rows, rows)
            do_t[:, pl.ds(start, rows)] = dout[slab]
            prod = dout[slab].astype(jnp.float32) * out_t[slab].astype(jnp.float32)
            for h in range(heads):
                piece = slice(h * HEAD, (h + 1) * HEAD)
                delta[h : h + 1, pl.ds(start, rows)] = jnp.sum(prod[piece], axis=0, keepdims=True)
                do_n[h, pl.ds(start, rows), :] = dout[slab, piece, :].T
        for h in range(heads):
            q_n[h] = qkv[h * HEAD : (h + 1) * HEAD, :].T
            k_n[h] = qkv[width + h * HEAD : width + (h + 1) * HEAD, :].T
            v_n[h] = qkv[2 * width + h * HEAD : 2 * width + (h + 1) * HEAD, :].T
        dk[...] = jnp.zeros_like(dk)
        dv[...] = jnp.zeros_like(dv)

    q_start = pl.multiple_of(step * BQ, BQ)
    qs = pl.ds(q_start, BQ)
    low, high = doc_bounds(q_start + lax.broadcasted_iota(jnp.int32, (1, BQ), 1), (ends[0], ends[1]), length)
    first, tiles = key_span(q_start, BQ, (ends[0], ends[1]), length, BK)

    def tile(t, carry):
        k_start = pl.multiple_of(first + t * BK, 128)
        ks = pl.ds(k_start, BK)
        pos = k_start + lax.broadcasted_iota(jnp.int32, (BK, BQ), 0)
        allowed = (pos >= low) & (pos <= high)
        new = []

        def score(h):
            piece = slice(h * HEAD, (h + 1) * HEAD)
            return (
                jnp.dot(k_n[h, ks, :], qkv[piece, qs], preferred_element_type=jnp.float32),
                jnp.dot(v_n[h, ks, :], do_t[piece, qs], preferred_element_type=jnp.float32),
            )

        nxt = score(0)
        for h in range(heads):
            s, dp = nxt
            if h + 1 < heads:
                nxt = score(h + 1)
            p = jnp.where(allowed, jnp.exp(s - lse[h : h + 1, qs]), 0.0)
            ds = (p * (dp - delta[h : h + 1, qs])).astype(jnp.bfloat16)
            dv[h, ks, :] += jnp.dot(p.astype(jnp.bfloat16), do_n[h, qs, :], preferred_element_type=jnp.float32)
            dk[h, ks, :] += jnp.dot(ds, q_n[h, qs, :], preferred_element_type=jnp.float32)
            new.append(carry[h] + jnp.dot(qkv[width + h * HEAD : width + (h + 1) * HEAD, ks], ds, preferred_element_type=jnp.float32))
        return tuple(new)

    init = tuple(jnp.zeros((HEAD, BQ), jnp.float32) for _ in range(heads))
    done = lax.fori_loop(0, tiles, tile, init)
    for h in range(heads):
        dq_t[h * HEAD : (h + 1) * HEAD, qs] = done[h]

    @pl.when(step == pl.num_programs(0) - 1)
    def _():
        for slab in range(4):
            start = pl.multiple_of(place[slab] * rows, rows)
            c, s = cos[:, pl.ds(start, rows)], sin[:, pl.ds(start, rows)]
            for h in range(heads):
                gq = dq_t[h * HEAD : (h + 1) * HEAD, pl.ds(start, rows)] * HEAD**-0.5
                gk = dk[h, pl.ds(start, rows), :].T
                gv = dv[h, pl.ds(start, rows), :].T
                for kind, g in ((0, gq), (1, gk)):
                    g1, g2 = g[:half], g[half:]
                    at = kind * width + h * HEAD
                    dproj[slab, at : at + half, :] = (g1 * c + g2 * s).astype(jnp.bfloat16)
                    dproj[slab, at + half : at + HEAD, :] = (g2 * c - g1 * s).astype(jnp.bfloat16)
                at = 2 * width + h * HEAD
                dproj[slab, at : at + HEAD, :] = gv.astype(jnp.bfloat16)


def attn_bwd(place, ends, qkv, dout, out_t, lse, cos, sin):
    length = qkv.shape[1]
    rows = length // 4
    width = qkv.shape[0] // 3
    heads = width // HEAD
    smem = pl.BlockSpec(memory_space=pltpu.SMEM)
    ops = (qkv, dout, out_t, lse, cos, sin)
    natural = pltpu.VMEM((heads, length, HEAD), jnp.bfloat16)
    sums = pltpu.VMEM((heads, length, HEAD), jnp.float32)
    return pl.pallas_call(
        functools.partial(attn_bwd_kernel, heads=heads),
        grid=(length // BQ,),
        in_specs=[smem, smem] + [whole_spec(a) for a in ops],
        out_specs=pl.BlockSpec((4, 3 * width, rows), lambda i: (0, 0, 0)),
        out_shape=jax.ShapeDtypeStruct((4, 3 * width, rows), jnp.bfloat16),
        scratch_shapes=[natural, natural, natural, pltpu.VMEM((width, length), jnp.bfloat16), natural]
        + [pltpu.VMEM((heads, length), jnp.float32), pltpu.VMEM((width, length), jnp.float32), sums, sums],
        compiler_params=pltpu.CompilerParams(vmem_limit_bytes=56 << 20),
        cost_estimate=pl.CostEstimate(
            flops=10 * length * length * width, bytes_accessed=24 * length * width, transcendentals=heads * length * length
        ),
        name="attn_bwd",
    )(place, ends, *ops)


FT = 768


def ffn_specs(rows, deep, hidden, step_tiles):
    first = pl.BlockSpec((3, deep, FT), lambda b, j: (0, 0, jnp.where(b == 0, j, step_tiles - 1)))
    second = pl.BlockSpec((3, deep, FT), lambda b, j: (0, 0, jnp.where(b == 0, 0, j)))
    acts = pl.BlockSpec((1, rows, FT), lambda b, j: (b, 0, j))
    whole = pl.BlockSpec((rows, deep), lambda b, j: (0, 0))
    return first, second, acts, whole


NT = (((1,), (1,)), ((), ()))


def ffn_fwd_kernel(rows_ref, first, second, out, gate_out, up_out, total):
    b, j = pl.program_id(0), pl.program_id(1)

    def work(block, fresh):
        h = rows_ref[...]
        gate = jnp.dot(h, block[0], preferred_element_type=jnp.float32)
        up = jnp.dot(h, block[1], preferred_element_type=jnp.float32)
        gate_out[0] = gate.astype(jnp.bfloat16)
        up_out[0] = up.astype(jnp.bfloat16)
        inner = (gate / (1.0 + jnp.exp(-gate)) * up).astype(jnp.bfloat16)
        part = lax.dot_general(inner, block[2], NT, preferred_element_type=jnp.float32)
        total[...] = part if fresh else total[...] + part

    pl.when((b == 0) & (j == 0))(lambda: work(first, True))
    pl.when((b == 0) & (j > 0))(lambda: work(first, False))
    pl.when(b == 1)(lambda: work(second, False))

    @pl.when((b == 1) & (j == pl.num_programs(1) - 1))
    def _():
        out[...] = total[...].astype(out.dtype)


def ffn_fwd(rows, first, second, out_type):
    length, deep = rows.shape
    hidden = first.shape[2]
    tiles = hidden // FT
    w1, w2, acts, whole = ffn_specs(length, deep, hidden, tiles)
    act = jax.ShapeDtypeStruct((2, length, hidden), jnp.bfloat16)
    return pl.pallas_call(
        ffn_fwd_kernel,
        grid=(2, tiles),
        in_specs=[whole, w1, w2],
        out_specs=(whole, acts, acts),
        out_shape=(jax.ShapeDtypeStruct((length, deep), out_type), act, act),
        scratch_shapes=[pltpu.VMEM((length, deep), jnp.float32)],
        compiler_params=pltpu.CompilerParams(vmem_limit_bytes=40 << 20),
        cost_estimate=pl.CostEstimate(
            flops=12 * length * deep * hidden, bytes_accessed=12 * deep * hidden + 8 * length * hidden, transcendentals=2 * length * hidden
        ),
        name="ffn_fwd",
    )(rows, first, second)


def ffn_bwd_kernel(grad_ref, gate_ref, up_ref, first, second, out, grad_gate_out, grad_up_out, inner_out, total):
    b, j = pl.program_id(0), pl.program_id(1)

    def work(block, fresh):
        grad_inner = jnp.dot(grad_ref[...], block[2], preferred_element_type=jnp.float32)
        gate, up = gate_ref[0].astype(jnp.float32), up_ref[0].astype(jnp.float32)
        sig = 1.0 / (1.0 + jnp.exp(-gate))
        act = gate * sig
        grad_gate = (grad_inner * up * (sig + act * (1.0 - sig))).astype(jnp.bfloat16)
        grad_up = (grad_inner * act).astype(jnp.bfloat16)
        grad_gate_out[0] = grad_gate
        grad_up_out[0] = grad_up
        inner_out[0] = (act * up).astype(jnp.bfloat16)
        part = lax.dot_general(grad_gate, block[0], NT, preferred_element_type=jnp.float32)
        part += lax.dot_general(grad_up, block[1], NT, preferred_element_type=jnp.float32)
        total[...] = part if fresh else total[...] + part

    pl.when((b == 0) & (j == 0))(lambda: work(first, True))
    pl.when((b == 0) & (j > 0))(lambda: work(first, False))
    pl.when(b == 1)(lambda: work(second, False))

    @pl.when((b == 1) & (j == pl.num_programs(1) - 1))
    def _():
        out[...] = total[...].astype(out.dtype)


def ffn_bwd(grad, gate, up, first, second, out_type):
    length, deep = grad.shape
    hidden = first.shape[2]
    tiles = hidden // FT
    w1, w2, acts, whole = ffn_specs(length, deep, hidden, tiles)
    act = jax.ShapeDtypeStruct((2, length, hidden), jnp.bfloat16)
    return pl.pallas_call(
        ffn_bwd_kernel,
        grid=(2, tiles),
        in_specs=[whole, acts, acts, w1, w2],
        out_specs=(whole, acts, acts, acts),
        out_shape=(jax.ShapeDtypeStruct((length, deep), out_type), act, act, act),
        scratch_shapes=[pltpu.VMEM((length, deep), jnp.float32)],
        compiler_params=pltpu.CompilerParams(vmem_limit_bytes=40 << 20),
        cost_estimate=pl.CostEstimate(
            flops=12 * length * deep * hidden, bytes_accessed=12 * deep * hidden + 20 * length * hidden, transcendentals=2 * length * hidden
        ),
        name="ffn_bwd",
    )(grad, gate, up, first, second)


def ffn_grads_kernel(h0, h1, g0, g1, gate0, gate1, up0, up1, in0, in1, *rest, slot):
    *other, out, h_t, g_t = rest

    @pl.when(pl.program_id(0) == 0)
    def _():
        rows = h0.shape[0]
        h_t[:, :rows] = h0[...].T
        h_t[:, rows:] = h1[...].T
        g_t[:, :rows] = g0[...].T
        g_t[:, rows:] = g1[...].T

    for i, (left, a, b) in enumerate(((h_t, gate0, gate1), (h_t, up0, up1), (g_t, in0, in1))):
        both = jnp.concatenate([a[0], b[0]], axis=0)
        grad = jnp.dot(left[...], both, preferred_element_type=jnp.float32)
        if other:
            grad += other[0][i].astype(jnp.float32)
        out[i] = grad.astype(jnp.bfloat16)


def ffn_grads(slot, rows, grads, gates, ups, inners, *other):
    length, deep = rows[0].shape
    hidden = gates[0].shape[2]
    whole = pl.BlockSpec((length, deep), lambda j: (0, 0))
    acts = pl.BlockSpec((1, length, FT), lambda j: (slot, 0, j))
    weights = pl.BlockSpec((3, deep, FT), lambda j: (0, 0, j))
    both = pltpu.VMEM((deep, 2 * length), jnp.bfloat16)
    return pl.pallas_call(
        functools.partial(ffn_grads_kernel, slot=slot),
        grid=(hidden // FT,),
        in_specs=[whole] * 4 + [acts] * 6 + [weights] * len(other),
        out_specs=weights,
        out_shape=jax.ShapeDtypeStruct((3, deep, hidden), jnp.bfloat16),
        scratch_shapes=[both, both],
        compiler_params=pltpu.CompilerParams(vmem_limit_bytes=40 << 20),
        cost_estimate=pl.CostEstimate(
            flops=12 * length * deep * hidden, bytes_accessed=6 * deep * hidden + 12 * length * hidden, transcendentals=0
        ),
        name="ffn_grads",
    )(*rows, *grads, *gates, *ups, *inners, *other)


def proj_bwd_kernel(pair_grad, rest_grad, near, far, matrix, out_grad, pair, rest, grad, a_t, total):
    step = pl.program_id(0)
    width3 = total.shape[0]

    @pl.when(step == 0)
    def _():
        a_t[...] = matrix[:, :width3].T
        total[...] = jnp.zeros_like(total)

    def work(made, rows, out):
        total[...] += jnp.dot(made, rows, preferred_element_type=jnp.float32)
        out[0] = jnp.dot(made.T, a_t[...], preferred_element_type=jnp.float32).astype(jnp.bfloat16)

    pl.when(step == 0)(lambda: work(pair_grad[0], far[...], pair))
    pl.when(step == 1)(lambda: work(pair_grad[0], near[...], pair))
    pl.when(step == 2)(lambda: work(rest_grad[0], far[...], rest))
    pl.when(step == 3)(lambda: work(rest_grad[0], near[...], rest))

    @pl.when(step == 3)
    def _():
        grad[...] = jnp.concatenate([total[...], out_grad[...]], axis=0).astype(jnp.bfloat16).T


def proj_bwd(grad_proj, near, far, matrix, out_grad):
    slabs, width3, rows = grad_proj.shape
    features = matrix.shape[0]
    parts = jax.ShapeDtypeStruct((2, rows, features), jnp.bfloat16)
    return pl.pallas_call(
        proj_bwd_kernel,
        grid=(4,),
        in_specs=[
            pl.BlockSpec((1, width3, rows), lambda i: (jnp.where(i == 0, 3, 1), 0, 0)),
            pl.BlockSpec((1, width3, rows), lambda i: (jnp.where(i == 3, 0, 2), 0, 0)),
            pl.BlockSpec((rows, features), lambda i: (jnp.where(i == 3, 0, 1), 0)),
            pl.BlockSpec((rows, features), lambda i: (jnp.where(i == 0, 1, 0), 0)),
            pl.BlockSpec(matrix.shape, lambda i: (0, 0)),
            pl.BlockSpec(out_grad.shape, lambda i: (0, 0)),
        ],
        out_specs=(
            pl.BlockSpec((1, rows, features), lambda i: (jnp.minimum(i, 1), 0, 0)),
            pl.BlockSpec((1, rows, features), lambda i: (jnp.maximum(i - 2, 0), 0, 0)),
            pl.BlockSpec(matrix.shape, lambda i: (0, 0)),
        ),
        out_shape=(parts, parts, jax.ShapeDtypeStruct(matrix.shape, jnp.bfloat16)),
        scratch_shapes=[pltpu.VMEM((width3, features), jnp.bfloat16), pltpu.VMEM((width3, features), jnp.float32)],
        compiler_params=pltpu.CompilerParams(vmem_limit_bytes=40 << 20),
        cost_estimate=pl.CostEstimate(
            flops=16 * rows * features * width3, bytes_accessed=24 * rows * features, transcendentals=0
        ),
        name="proj_bwd",
    )(grad_proj, grad_proj, near, far, matrix, out_grad)


def mean_of(v):
    return jnp.mean(v, axis=-1, keepdims=True)


def mix_fwd_kernel(head0, head1, head2, head3, matrix, out1, out2, out3, rows, params, hidden, low, normed, inv, *, width):
    heads = jnp.concatenate([head0[...], head1[...], head2[...], head3[...]], axis=0).T
    weights = jnp.concatenate([matrix[:, 3 * width :], out1[...], out2[...], out3[...]], axis=1)
    mixed = rows[...].astype(jnp.float32) + lax.dot_general(heads, weights, NT, preferred_element_type=jnp.float32)
    centred = mixed - mean_of(mixed)
    inv_std = lax.rsqrt(mean_of(centred * centred) + NORM_EPS)
    unit = centred * inv_std
    out = unit * params[0:1, :] + params[1:2, :]
    hidden[...] = out
    low[...] = out.astype(jnp.bfloat16)
    normed[...] = unit
    inv[...] = inv_std


def mix_fwd(heads, matrix, outs, near, params):
    width, rows = heads[0].shape
    features = matrix.shape[0]
    whole = lambda a: pl.BlockSpec(a.shape, lambda i: (0,) * len(a.shape))
    block = pl.BlockSpec((rows, features), lambda i: (0, 0))
    shape = lambda t: jax.ShapeDtypeStruct((rows, features), t)
    return pl.pallas_call(
        functools.partial(mix_fwd_kernel, width=width),
        grid=(1,),
        in_specs=[whole(a) for a in (*heads, matrix, *outs)] + [block, whole(params)],
        out_specs=(block, block, block, pl.BlockSpec((rows, 1), lambda i: (0, 0))),
        out_shape=(shape(jnp.float32), shape(jnp.bfloat16), shape(jnp.float32), jax.ShapeDtypeStruct((rows, 1), jnp.float32)),
        compiler_params=pltpu.CompilerParams(vmem_limit_bytes=40 << 20),
        cost_estimate=pl.CostEstimate(
            flops=2 * rows * features * features, bytes_accessed=14 * rows * features + 2 * features * features, transcendentals=rows
        ),
        name="mix_fwd",
    )(*heads, matrix, *outs, near, params)


def mix_bwd_kernel(
    grad_mixed, own_part, far_part, normed, inv, params, head0, head1, head2, head3, matrix, out1, out2, out3,
    grad_out, norms, made0, made1, made2, made3, og0, og1, og2, og3, *, width,
):
    grad = grad_mixed[...] + own_part[...] + far_part[...].astype(jnp.float32)
    unit = normed[...]
    norms[0:1, :] = jnp.sum(grad * unit, axis=0, keepdims=True)
    norms[1:2, :] = jnp.sum(grad, axis=0, keepdims=True)
    grad_unit = grad * params[0:1, :]
    back = inv[...] * (grad_unit - mean_of(grad_unit) - unit * mean_of(grad_unit * unit))
    grad_out[...] = back
    low = back.astype(jnp.bfloat16)
    weights = (matrix[:, 3 * width :], out1[...], out2[...], out3[...])
    for weight, head, made, og in zip(weights, (head0, head1, head2, head3), (made0, made1, made2, made3), (og0, og1, og2, og3)):
        made[...] = lax.dot_general(weight.T, low, NT, preferred_element_type=jnp.float32).astype(jnp.bfloat16)
        og[...] = jnp.dot(head[...], low, preferred_element_type=jnp.float32).astype(jnp.bfloat16)


def mix_bwd(grad_mixed, own_part, far_part, normed, inv, params, heads, matrix, outs):
    width, rows = heads[0].shape
    features = matrix.shape[0]
    whole = lambda a: pl.BlockSpec(a.shape, lambda i: (0,) * len(a.shape))
    shapes = (
        [jax.ShapeDtypeStruct((rows, features), jnp.float32), jax.ShapeDtypeStruct((2, features), jnp.float32)]
        + [jax.ShapeDtypeStruct((width, rows), jnp.bfloat16)] * 4
        + [jax.ShapeDtypeStruct((width, features), jnp.bfloat16)] * 4
    )
    ops = (grad_mixed, own_part, far_part, normed, inv, params, *heads, matrix, *outs)
    got = pl.pallas_call(
        functools.partial(mix_bwd_kernel, width=width),
        grid=(1,),
        in_specs=[whole(a) for a in ops],
        out_specs=tuple(whole(a) for a in shapes),
        out_shape=tuple(shapes),
        compiler_params=pltpu.CompilerParams(vmem_limit_bytes=40 << 20),
        cost_estimate=pl.CostEstimate(
            flops=4 * rows * features * features, bytes_accessed=22 * rows * features + 4 * features * features, transcendentals=0
        ),
        name="mix_bwd",
    )(*ops)
    return got[0], got[1], got[2:6], got[6:10]


def lamb_step(weight, gradient, first_old, second):
    first_new = BETA_ONE * first_old + (1.0 - BETA_ONE) * gradient
    second_new = BETA_TWO * second + (1.0 - BETA_TWO) * gradient * gradient
    update = (
        first_new
        / (1.0 - BETA_ONE**STEP)
        / (jnp.sqrt(second_new / (1.0 - BETA_TWO**STEP)) + ADAM_EPS)
        + DECAY_RATE * weight
    )
    return first_new, second_new, update


def lamb_kernel(same, other, *refs, kinds):
    count = len(kinds)
    olds, news, late = refs[: 3 * count], refs[3 * count : 6 * count], refs[6 * count]
    late[...] = jnp.zeros_like(late)
    for i, (turned, parts) in enumerate(kinds):
        weight, first, second = olds[3 * i : 3 * i + 3]
        first_out, second_out, update_out = news[3 * i : 3 * i + 3]
        row = None
        for at, (index, columns) in enumerate(parts):
            gradient = same[index, :, columns].astype(jnp.float32) + other[index, :, columns].astype(jnp.float32)
            gradient = gradient.T if turned else gradient
            where = (at,) if len(weight.shape) == 3 else (slice(None),)
            first_new, second_new, update = lamb_step(weight[where], gradient, first[where], second[where])
            first_out[where] = first_new
            second_out[where] = second_new
            update_out[where] = update
            sums = jnp.sum(update * update, axis=0, keepdims=True)
            row = sums if row is None else row + sums
        late[i : i + 1, : row.shape[1]] = row


def lamb(same, other, kinds, olds, features):
    whole = lambda a: pl.BlockSpec(a.shape, lambda i: (0,) * len(a.shape))
    shapes = [jax.ShapeDtypeStruct(a.shape, jnp.float32) for a in olds]
    shapes.append(jax.ShapeDtypeStruct((len(kinds), features), jnp.float32))
    ops = (same, other, *olds)
    return pl.pallas_call(
        functools.partial(lamb_kernel, kinds=kinds),
        grid=(1,),
        in_specs=[whole(a) for a in ops],
        out_specs=tuple(whole(a) for a in shapes),
        out_shape=tuple(shapes),
        compiler_params=pltpu.CompilerParams(vmem_limit_bytes=48 << 20),
        cost_estimate=pl.CostEstimate(flops=20 * same.size, bytes_accessed=28 * same.size, transcendentals=same.size),
        name="lamb",
    )(*ops)


def finish_kernel(totals, now, first, second, *refs, count):
    weights, updates = refs[:count], refs[count : 2 * count]
    norm_out, first_out, second_out, trust = refs[2 * count : 2 * count + 4]
    news = refs[2 * count + 4 :]
    first_new, second_new, update = lamb_step(now[...], totals[0:4, :], first[...], second[...])
    norms = [jnp.sqrt(jnp.sum(v * v, axis=-1, keepdims=True)) for v in (now[...], update)]
    norm_out[...] = now[...] - LEARN_RATE * (norms[0] / norms[1]) * update
    first_out[...] = first_new
    second_out[...] = second_new
    sizes = jnp.sqrt(jnp.sum(totals[4:12, :], axis=-1, keepdims=True))
    trust[...] = jnp.concatenate([sizes[0:4], sizes[4:8]], axis=1)
    for i in range(count):
        ratio = LEARN_RATE * (sizes[i : i + 1] / sizes[4 + i : 5 + i])
        for at in range(weights[i].shape[0]) if len(weights[i].shape) == 3 else (slice(None),):
            news[i][at] = weights[i][at] - ratio * updates[i][at]


def finish(totals, now, first, second, weights, updates):
    whole = lambda a: pl.BlockSpec(a.shape, lambda i: (0,) * len(a.shape))
    shapes = [jax.ShapeDtypeStruct(now.shape, jnp.float32)] * 3 + [jax.ShapeDtypeStruct((4, 2), jnp.float32)]
    shapes += [jax.ShapeDtypeStruct(a.shape, jnp.float32) for a in weights]
    ops = (totals, now, first, second, *weights, *updates)
    size = sum(a.size for a in weights)
    return pl.pallas_call(
        functools.partial(finish_kernel, count=len(weights)),
        grid=(1,),
        in_specs=[whole(a) for a in ops],
        out_specs=tuple(whole(a) for a in shapes),
        out_shape=tuple(shapes),
        compiler_params=pltpu.CompilerParams(vmem_limit_bytes=48 << 20),
        cost_estimate=pl.CostEstimate(flops=3 * size, bytes_accessed=12 * size, transcendentals=0),
        name="finish",
    )(*ops)


STEP = 10

BETA_ONE = 0.9
BETA_TWO = 0.999
ADAM_EPS = 1e-06
DECAY_RATE = 0.01
LEARN_RATE = 0.2
NORM_EPS = 1e-05
ROPE_BASE = 1000.0

bf16 = jnp.bfloat16
f32 = jnp.float32

BOTH = ("section", "tensor")
CELLS = [(c, y, x) for c in range(2) for y in range(2) for x in range(2)]


def number(c, y, x):
    return c * 4 + y * 2 + x


def moves(target):
    return [(number(*cell), number(*target(*cell))) for cell in CELLS]


SWAP = moves(lambda c, y, x: (y, c, x))
SWAP_BACK = moves(lambda c, y, x: (1 - y, c, x))
SWAP_OUT = moves(lambda c, y, x: (y, 1 - c, x))
CORNER = moves(lambda c, y, x: (1 - c, y, 1 - x))


def over_section(v):
    return lax.ppermute(v, "section", [(0, 1), (1, 0)])


def over_x(v):
    return lax.ppermute(v, "tensor", [(0, 1), (1, 0), (2, 3), (3, 2)])


def over_y(v):
    return lax.ppermute(v, "tensor", [(0, 2), (1, 3), (2, 0), (3, 1)])


def over_diag(v):
    return lax.ppermute(v, "tensor", [(0, 3), (1, 2), (2, 1), (3, 0)])


def over_both(v, pairs):
    return lax.ppermute(v, BOTH, pairs)


def over_z(v, k):
    return lax.ppermute(v, "dp", [(i, i ^ k) for i in range(4)])


def quad():
    return lax.axis_size("dp") == 4


def gather_later(piece, axis):
    return lax.all_gather(piece, "dp", axis=axis, tiled=True)


def scatter_later(whole, axis):
    return lax.psum_scatter(whole, "dp", scatter_dimension=axis, tiled=True)


def chips_total(v):
    v = (v + over_x(v)) + (over_y(v) + over_diag(v))
    if not quad():
        return lax.psum(v, "dp")
    return (v + over_z(v, 1)) + (over_z(v, 2) + over_z(v, 3))


def rope_tables(length):
    half_size = HEAD // 2
    freq_vals = np.float32(ROPE_BASE) ** (-np.arange(half_size, dtype=np.float32) * np.float32(2.0 / HEAD))
    angles = freq_vals[:, None] * np.arange(length, dtype=np.float32)[None, :]
    return jnp.asarray(np.cos(angles)), jnp.asarray(np.sin(angles))


def norm_fwd(values, gain_row, bias_row):
    mean_val = jnp.mean(values, axis=-1, keepdims=True)
    centred = values - mean_val
    variance = jnp.mean(centred * centred, axis=-1, keepdims=True)
    inv_std = lax.rsqrt(variance + NORM_EPS)
    normed = centred * inv_std
    return (normed * gain_row + bias_row, normed, inv_std)


def norm_back(grad_out, normed, inv_std, gain_row):
    grad_gain = jnp.sum(grad_out * normed, axis=0)
    grad_bias = jnp.sum(grad_out, axis=0)
    grad_normed = grad_out * gain_row
    grad_vals = inv_std * (
        grad_normed
        - jnp.mean(grad_normed, axis=-1, keepdims=True)
        - normed * jnp.mean(grad_normed * normed, axis=-1, keepdims=True)
    )
    return (grad_vals, grad_gain, grad_bias)


def dot(spec, a, b):
    return jnp.einsum(spec, a, b, preferred_element_type=f32)


def after(value, *others):
    return lax.optimization_barrier((value,) + others)[0]


def layer_forward(near, far, matrix, ffn, params, env):
    place, ends, cos, sin = env
    mine, log_sums, qkv = attn_fwd(place, ends, near, far, matrix, cos, sin)
    out_own = matrix[:, 3 * (matrix.shape[1] // 4) :]
    out_across = over_x(out_own)
    outs = (over_section(out_own), out_across, over_section(after(out_across, log_sums)))
    all_heads = [mine[0], over_section(mine[1]), over_x(mine[2]), over_both(mine[3], CORNER)]
    hidden, hidden_low, normed_one, inv_one = mix_fwd(all_heads, matrix, outs, near, params[:, 0])
    ffn = (ffn, over_section(after(ffn, hidden_low)))
    hidden_rows = [hidden_low, over_x(hidden_low)]
    own_part, *own_acts = ffn_fwd(hidden_rows[0], *ffn, f32)
    far_part, *far_acts = ffn_fwd(hidden_rows[1], *ffn, bf16)
    ffn_out = own_part + over_x(far_part).astype(f32)
    output, normed_two, inv_two = norm_fwd(hidden + ffn_out, params[0, 1], params[1, 1])
    kept = (near, far, qkv, mine, log_sums, all_heads, normed_one, inv_one, hidden_rows, (own_acts, far_acts))
    return output.astype(bf16), outs, kept + (normed_two, inv_two, ffn)


def layer_backward(grad_out, kept, matrix, outs, params, env):
    place, ends, cos, sin = env
    (near, far, qkv, mine, log_sums, all_heads, normed_one, inv_one, hidden_rows, acts, normed_two, inv_two, ffn) = kept
    grad_mixed, gain_two, bias_two = norm_back(grad_out, normed_two, inv_two, params[0, 1])
    grad_low = grad_mixed.astype(bf16)
    grad_rows = [grad_low, over_x(grad_low)]
    own_part, *own_grads = ffn_bwd(grad_rows[0], *acts[0], *ffn, f32)
    far_part, *far_grads = ffn_bwd(grad_rows[1], *acts[1], *ffn, bf16)
    made = list(zip(own_grads, far_grads))
    ffn_other = ffn_grads(1, hidden_rows, grad_rows, *made)
    ffn_grad = ffn_grads(0, hidden_rows, grad_rows, *made, over_section(ffn_other))
    grad_mixed_one, norm_one, grad_heads, out_grad = mix_bwd(
        grad_mixed, own_part, over_x(far_part), normed_one, inv_one, params[:, 0], all_heads, matrix, outs
    )
    grad_mine = jnp.stack(
        [grad_heads[0], over_section(grad_heads[1]), over_x(grad_heads[2]), over_both(grad_heads[3], CORNER)]
    )
    out_own = [out_grad[0], over_section(out_grad[1]), over_x(out_grad[2]), over_both(out_grad[3], CORNER)]
    out_own = sum(g.astype(f32) for g in out_own)
    grad_proj = attn_bwd(place, ends, qkv, grad_mine, mine, log_sums, cos, sin)
    pair, rest, matrix_grad = proj_bwd(grad_proj, near, far, matrix, out_own)
    other = over_section(pair).astype(f32)
    far_sum = over_x((rest[0].astype(f32) + other[0]).astype(bf16))
    rows_sum = rest[1].astype(f32) + other[1] + far_sum.astype(f32)
    norm_grads = jnp.stack([jnp.stack([norm_one[0], gain_two]), jnp.stack([norm_one[1], bias_two])])
    return grad_mixed_one + rows_sum, matrix_grad, ffn_grad, norm_grads


def body(
    tokens,
    cotangent,
    segments,
    heads_in,
    heads_out,
    gate_up,
    project_down,
    norm_gain,
    norm_bias,
    heads_in_first,
    heads_in_second,
    heads_out_first,
    heads_out_second,
    gate_up_first,
    gate_up_second,
    project_down_first,
    project_down_second,
    norm_first,
    norm_second,
):
    section = lax.axis_index("section")
    spot = lax.axis_index("tensor")
    y, x = spot // 2, spot % 2
    rows = tokens.shape[1]
    length = segments.shape[-1]
    masters = (heads_in[0], heads_out[0], gate_up[0], project_down[0])
    deep, width = masters[0].shape[1:]

    attn_piece = jnp.concatenate(
        [masters[0].transpose(1, 0, 2).reshape(deep, 3 * width), masters[1].T], axis=1
    ).astype(bf16)
    ffn_piece = jnp.concatenate([masters[2], masters[3].T[None]], axis=0).astype(bf16)

    def to_block(piece, layer):
        got = []
        for to_y in range(2):
            pairs = [(number(layer, c, x), number(c, to_y, x)) for c in range(2) for x in range(2)]
            got.append(over_both(piece, pairs))
        return jnp.where(y == 0, got[0], got[1])

    own = over_both(lax.dynamic_index_in_dim(tokens, section, 0, keepdims=False), SWAP)
    first_matrix = gather_later(to_block(attn_piece, 0), 0)
    ffn_first = gather_later(to_block(after(ffn_piece, own), 0), 1)

    def four_slabs(rows):
        across = over_x(rows)
        return jnp.concatenate([rows, over_section(rows)]), jnp.concatenate([across, over_section(across)])

    both_params = jnp.stack([norm_gain[0], norm_bias[0]])
    other_params = over_section(both_params)
    params = [
        jnp.where(section == 0, both_params, other_params),
        jnp.where(section == 0, other_params, both_params),
    ]

    block = 2 * section + x
    place = jnp.stack([block, block ^ 2, block ^ 1, block ^ 3]).astype(jnp.int32)
    seq_seg = lax.dynamic_index_in_dim(segments, y, 0, keepdims=False)[0]
    ends = jnp.stack([jnp.sum((seq_seg <= d).astype(jnp.int32)) for d in range(2)])
    env = (place, ends) + rope_tables(length)

    near_zero, far_zero = four_slabs(own)
    low_zero, outs_zero, kept_zero = layer_forward(near_zero, far_zero, first_matrix, ffn_first, params[0], env)
    hidden_rows = kept_zero[8]
    second_piece = to_block(after(jnp.concatenate([attn_piece[None], ffn_piece]), ffn_first), 1)
    second_matrix = gather_later(after(second_piece[0], hidden_rows[0]), 0)
    ffn_second = gather_later(after(second_piece[1:], hidden_rows[1]), 1)
    near_one, far_one = four_slabs(low_zero)
    low_one, outs_one, kept_one = layer_forward(near_one, far_one, second_matrix, ffn_second, params[1], env)
    grad_top = over_both(after(lax.dynamic_index_in_dim(cotangent, section, 0, keepdims=False), low_zero), SWAP)
    grad_one, matrix_one, ffn_one, norm_one = layer_backward(
        grad_top.astype(f32), kept_one, second_matrix, outs_one, params[1], env
    )
    sent = grad_one.astype(bf16)
    grad_zero, matrix_zero, ffn_zero, norm_zero = layer_backward(
        sent.astype(f32), kept_zero, first_matrix, outs_zero, params[0], env
    )

    def home(zero, one):
        same = over_both(jnp.where(y == 0, zero, one), SWAP)
        other = over_both(jnp.where(y == 0, one, zero), SWAP_BACK)
        return same, other

    def by_micro(zero, one):
        same, other = home(zero, one)
        return jnp.stack([jnp.where(section == 0, same, other), jnp.where(section == 0, other, same)])

    layer_out = by_micro(low_zero, low_one)

    ffn_home = home(scatter_later(ffn_zero, 1), scatter_later(ffn_one, 1))
    attn_home = home(scatter_later(matrix_zero, 0)[None], scatter_later(matrix_one, 0)[None])
    norm_mine = jnp.where(section == 0, norm_zero, norm_one) + over_section(
        jnp.where(section == 0, norm_one, norm_zero)
    )
    features = norm_mine.shape[-1]
    firsts = (heads_in_first[0], heads_out_first[0], gate_up_first[0], project_down_first[0])
    seconds = (heads_in_second[0], heads_out_second[0], gate_up_second[0], project_down_second[0])
    olds = list(zip(masters, firsts, seconds))

    def squares(matrix):
        row = jnp.sum((matrix * matrix).reshape(-1, matrix.shape[-1]), axis=0)
        return jnp.pad(row, (0, features - row.shape[0]))

    columns = slice(0, masters[2].shape[-1])
    ffn_new = lamb(
        *ffn_home, ((False, ((0, columns), (1, columns))), (True, ((2, columns),))), olds[2] + olds[3], features
    )
    early = jnp.stack([squares(m) for m in masters])
    early = jnp.concatenate([norm_mine.reshape(4, -1), early], axis=0)
    attn_home = lax.optimization_barrier((*attn_home, early, ffn_new[-1]))[:2]
    pieces = tuple((0, slice(i * width, (i + 1) * width)) for i in range(4))
    attn_new = lamb(*attn_home, ((False, pieces[:3]), (True, pieces[3:])), olds[0] + olds[1], features)
    totals = chips_total(jnp.concatenate([early, attn_new[-1], ffn_new[-1]], axis=0))
    made = [attn_new[:3], attn_new[3:6], ffn_new[:3], ffn_new[3:6]]
    norm_shape = both_params.shape
    flat = [v.reshape(4, features) for v in (both_params, norm_first[0], norm_second[0])]
    *norms, trust_norms, in_new, out_new, gate_new, down_new = finish(
        totals, *flat, masters, [m[2] for m in made]
    )
    new_mats = (in_new, out_new, gate_new, down_new)
    input_grads = by_micro(after(grad_zero.astype(bf16), attn_new[-1]), sent).astype(f32)
    outs = [layer_out, input_grads]
    for i in range(4):
        outs += [new_mats[i], made[i][0], made[i][1]]
    outs += [v.reshape(norm_shape) for v in norms] + [trust_norms]
    return tuple(item[None] for item in outs)


def solution(mesh):
    rows = P(None, ("dp", "tensor"), None)
    out_rows = P("section", None, ("dp", "tensor"), None)
    columns = P("section", None, "dp", "tensor")
    turned = P("section", "tensor", "dp")
    vectors = P("section", None, None)
    pairs = P("section", None, None, None)
    return jax.shard_map(
        body,
        mesh=mesh,
        in_specs=(rows, rows, P(None, "dp", None), columns, turned, columns, turned, vectors, vectors)
        + (columns, columns, turned, turned, columns, columns, turned, turned, pairs, pairs),
        out_specs=(out_rows, out_rows)
        + (columns,) * 3
        + (turned,) * 3
        + (columns,) * 3
        + (turned,) * 3
        + (pairs,) * 3
        + (vectors,),
        check_vma=False,
    )
```

time: 818 us -> 723 us (0.88)
  matrix products: 123 us -> 0 us
  Pallas kernels: 140 us -> 222 us
  local copies, waits for them, and re-layouts: 63.3 us -> 118 us
  waiting for transfers between devices: 240 us -> 199 us
  other arithmetic: 82.4 us -> 48.5 us
  starting transfers between devices: 138 us -> 105 us
    dot_general x86 -> x0, matrix products: 123 us -> none  [dot(): return jnp.einsum(spec, a, b, preferred_element_type=f32)]
    pallas_call x2 -> x23, Pallas kernels: 55.2 us -> 160 us  [the longest x2 40.3 us: attn_fwd(): pl.pallas_call(functools.partial(attn_fwd_kernel, heads=heads), grid=(len...]
    unnamed x297 -> x420, local copies, waits for them, and re-layouts: 8.23 us -> 94.2 us
    ppermute x18 -> x3, waiting for transfers between devices: 70.6 us -> 0.01 us  [over_z(): return lax.ppermute(v, 'dp', [(i, i ^ k) for i in range(4)])]
    ppermute x18 -> x3, starting transfers between devices: 70.4 us -> 9.38 us  [over_z(): return lax.ppermute(v, 'dp', [(i, i ^ k) for i in range(4)])]
    dynamic_update_slice x8 -> x0, local copies, waits for them, and re-layouts: 36.7 us -> none  [gather_dp(): whole = lax.dynamic_update_slice_in_dim(whole, got, (z ^ k) * deep, axis)]
    pallas_call x2, Pallas kernels: 84.4 us -> 62.2 us  [attn_bwd(): pl.pallas_call(functools.partial(attn_bwd_kernel, heads=heads), grid=(len...]
    ppermute x18 -> x22, waiting for transfers between devices: 34.9 us -> 16.9 us  [over_both(): return lax.ppermute(v, BOTH, pairs)]
  transfers between devices with their start and end apart: 86 -> 78, of which waited for: 30 -> 21; matrix products, arithmetic and copies ran while one was open for 31% -> 11% of each run, Pallas kernels for 17% -> 29%
where the time goes in v2:
time: 723 us; the launch traced here: 709 us
  Pallas kernels  222 us (31%)
  waiting for transfers between devices  199 us (28%)
  local copies, waits for them, and re-layouts  118 us (16%)
  starting transfers between devices  105 us (15%)
  other arithmetic  48.5 us (7%)
  between operations  16.7 us (2%)
    ppermute x21, waiting for transfers between devices, over_x(): return lax.ppermute(v, 'tensor', [(0, 1), (1, 0), (2, 3), (3, 2)])  139 us
    unnamed x420, local copies, waits for them, and re-layouts  94.2 us
    pallas_call x2, Pallas kernels, attn_bwd(): pl.pallas_call(functools.partial(attn_bwd_kernel, heads=heads), grid=(len...  62.2 us
    ppermute x22, starting transfers between devices, over_both(): return lax.ppermute(v, BOTH, pairs)  50.3 us
    pallas_call x2, Pallas kernels, attn_fwd(): pl.pallas_call(functools.partial(attn_fwd_kernel, heads=heads), grid=(len...  40.3 us
    pallas_call x4, Pallas kernels, ffn_bwd(): pl.pallas_call(ffn_bwd_kernel, grid=(2, tiles), in_specs=[whole, acts, ac...  34.3 us
    pallas_call x4, Pallas kernels, ffn_grads(): pl.pallas_call(functools.partial(ffn_grads_kernel, slot=slot), grid=(hidd...  26.7 us
    ppermute x21, starting transfers between devices, over_x(): return lax.ppermute(v, 'tensor', [(0, 1), (1, 0), (2, 3), (3, 2)])  25.3 us
  transfers between devices with their start and end apart: 78, of which 21 were waited for; matrix products, arithmetic and copies ran while one was open for 11% of the time, Pallas kernels for 29%

profile of v2, /device:TPU:0, one launch (start us, length us, event | category | flops | bytes accessed | tf_op | source)
XLA Modules:
  0.0 709.0 jit_solution(5285058571860698378)
XLA Ops:
  11.4 5.5 collective-permute-start.5
  17.9 7.4 %collective-permute-start = (bf16[512,768]{1,0:T(8,128)(2,1)}, bf16[512,768]{1,0:T(8,128)(2,1)}, u32[]{:S(2)}, u32[]{:S(2)}) collective-permute-start(bf16[512,768]{1,0:T(8,128)(2,1)} %dynamic-slice_bitcast_fusion.1), channel_id=1, source_target_pairs={{0,0},{1,1},{2,16},{3,17},{16,2},{17,3},{18,18},{19,19},{4,4},{5,5... | collective-permute-start | bytes 2359304 | tf_op jit(solution)/shard_map/ppermute | solution.py:689
  29.3 6.1 collective-permute-start.14
  35.4 10.5 %collective-permute-done.14 = bf16[3,192,768]{2,1,0:T(8,128)(2,1)S(1)} collective-permute-done((bf16[3,192,768]{2,1,0:T(8,128)(2,1)S(1)}, bf16[3,192,768]{2,1,0:T(8,128)(2,1)S(1)}, u32[]{:S(2)}, u32[]{:S(2)}) %collective-permute-start.14) | collective-permute-done | bytes 884768 | tf_op jit(solution)/shard_map/ppermute | solution.py:689
  49.2 16.7 %collective-permute-done.2 = bf16[512,768]{1,0:T(8,128)(2,1)} collective-permute-done((bf16[512,768]{1,0:T(8,128)(2,1)}, bf16[512,768]{1,0:T(8,128)(2,1)}, u32[]{:S(2)}, u32[]{:S(2)}) %collective-permute-start.2) | collective-permute-done | bytes 786464 | tf_op jit(solution)/shard_map/ppermute | solution.py:677
  83.6 23.3 %attn_fwd.2 = (bf16[4,192,512]{2,1,0:T(8,128)(2,1)S(1)}, f32[3,2048]{1,0:T(4,128)S(1)}, bf16[576,2048]{1,0:T(8,128)(2,1)}) custom-call(s32[4]{0:T(128)S(1)} %pad_add_fusion.place, s32[2]{0:T(128)S(1)} %pad_add_fusion.1.ends, bf16[1024,768]{1,0:T(8,128)(2,1)S(1)} %copy-done.25, bf16[1024,768]{1,0:T(8,128)(2,1)S(1)} %copy-done.99, ...), custom_call_target="tpu_custom_call" | custom-call | flops 4831838208 | bytes 6291456 | tf_op jit(solution)/shard_map/attn_fwd/pallas_call | solution.py:154
  112.0 16.7 %all-gather.7.cloned.1.call-done.first = bf16[3,768,768]{2,1,0:T(8,128)(2,1)} async-done(((bf16[3,192,768]{2,1,0:T(8,128)(2,1)}), bf16[3,768,768]{2,1,0:T(8,128)(2,1)}) %all-gather.7.cloned.1.call-update) | async-done | bytes 3538960 | tf_op jit(solution)/shard_map/all_gather | solution.py:701
  135.8 2.5 mix_fwd.2
  138.4 2.3 collective-permute-start.15
  144.3 2.1 slice.131
  146.4 11.3 %collective-permute-done.16.rows_ref.h1 = bf16[512,768]{1,0:T(8,128)(2,1)S(1)} collective-permute-done((bf16[512,768]{1,0:T(8,128)(2,1)S(1)}, bf16[512,768]{1,0:T(8,128)(2,1)S(1)}, u32[]{:S(2)}, u32[]{:S(2)}) %collective-permute-start.16) | collective-permute-done | bytes 786464 | tf_op jit(solution)/shard_map/ppermute | solution.py:677
  158.0 7.5 %ffn_fwd.5 = (bf16[512,768]{1,0:T(8,128)(2,1)S(1)}, bf16[2,512,768]{2,1,0:T(8,128)(2,1)S(1)}, bf16[2,512,768]{2,1,0:T(8,128)(2,1)S(1)}) custom-call(bf16[512,768]{1,0:T(8,128)(2,1)S(1)} %collective-permute-done.16.rows_ref.h1, bf16[3,768,768]{2,1,0:T(8,128)(2,1)} %all-gather.7.cloned.1.call-done.first, bf16[3,768,768]{2,1,0:T(8,128)(2,1)} %collective-permute-done.15.second), custom_call_target="tpu_custom_call" | custom-call | flops 3623878656 | bytes 10223616 | tf_op jit(solution)/shard_map/ffn_fwd/pallas_call | solution.py:319
  169.4 7.6 %ffn_fwd.4 = (f32[512,768]{1,0:T(8,128)S(1)}, bf16[2,512,768]{2,1,0:T(8,128)(2,1)S(1)}, bf16[2,512,768]{2,1,0:T(8,128)(2,1)S(1)}) custom-call(bf16[512,768]{1,0:T(8,128)(2,1)S(1)} %get-tuple-element.124.rows_ref.h0, bf16[3,768,768]{2,1,0:T(8,128)(2,1)} %all-gather.7.cloned.1.call-done.first, bf16[3,768,768]{2,1,0:T(8,128)(2,1)} %collective-permute-done.15.second), custom_call_target="tpu_custom_call" | custom-call | flops 3623878656 | bytes 10223616 | tf_op jit(solution)/shard_map/ffn_fwd/pallas_call | solution.py:319
  177.0 6.4 collective-permute-done.17
  186.3 4.4 collective-permute-start.18
  190.7 10.9 %collective-permute-done.19 = bf16[512,768]{1,0:T(8,128)(2,1)} collective-permute-done((bf16[512,768]{1,0:T(8,128)(2,1)S(1)}, bf16[512,768]{1,0:T(8,128)(2,1)}, u32[]{:S(2)}, u32[]{:S(2)}) %collective-permute-start.19) | collective-permute-done | bytes 786464 | tf_op jit(solution)/shard_map/ppermute | solution.py:677
  201.6 3.9 collective-permute-start.20
  212.9 16.9 %attn_fwd.3 = (bf16[4,192,512]{2,1,0:T(8,128)(2,1)S(1)}, f32[3,2048]{1,0:T(4,128)S(1)}, bf16[576,2048]{1,0:T(8,128)(2,1)}) custom-call(s32[4]{0:T(128)S(1)} %pad_add_fusion.place, s32[2]{0:T(128)S(1)} %pad_add_fusion.1.ends, bf16[1024,768]{1,0:T(8,128)(2,1)S(1)} %pad_maximum_fusion.near.rows, bf16[1024,768]{1,0:T(8,128)(2,1)S(1)} %constant_dynamic-update-slice_fusion.4.far, ...), custom_call_target="tpu_custom_call" | custom-call | flops 4831838208 | bytes 6291456 | tf_op jit(solution)/shard_map/attn_fwd/pallas_call | solution.py:154
  232.1 6.2 collective-permute-done.24.head2
  238.3 2.6 collective-permute-done.25.head3
  252.6 17.7 %collective-permute-done.30.rows_ref.h1 = bf16[512,768]{1,0:T(8,128)(2,1)S(1)} collective-permute-done((bf16[512,768]{1,0:T(8,128)(2,1)S(1)}, bf16[512,768]{1,0:T(8,128)(2,1)S(1)}, u32[]{:S(2)}, u32[]{:S(2)}) %collective-permute-start.30) | collective-permute-done | bytes 786464 | tf_op jit(solution)/shard_map/ppermute | solution.py:677
  270.2 2.3 copy-done.123
  272.5 4.4 ffn_fwd.7
  280.0 4.8 ffn_fwd.6
  284.8 11.0 %collective-permute-done.31 = bf16[512,768]{1,0:T(8,128)(2,1)S(1)} collective-permute-done((bf16[512,768]{1,0:T(8,128)(2,1)S(1)}, bf16[512,768]{1,0:T(8,128)(2,1)S(1)}, u32[]{:S(2)}, u32[]{:S(2)}) %collective-permute-start.31) | collective-permute-done | bytes 786464 | tf_op jit(solution)/shard_map/ppermute | solution.py:677
  300.2 17.2 %collective-permute-done.35.grad_ref.g1 = bf16[512,768]{1,0:T(8,128)(2,1)S(1)} collective-permute-done((bf16[512,768]{1,0:T(8,128)(2,1)S(1)}, bf16[512,768]{1,0:T(8,128)(2,1)S(1)}, u32[]{:S(2)}, u32[]{:S(2)}) %collective-permute-start.35) | collective-permute-done | bytes 786464 | tf_op jit(solution)/shard_map/ppermute | solution.py:677
  317.4 8.7 %ffn_bwd.5 = (bf16[512,768]{1,0:T(8,128)(2,1)}, bf16[2,512,768]{2,1,0:T(8,128)(2,1)S(1)}, bf16[2,512,768]{2,1,0:T(8,128)(2,1)S(1)}, bf16[2,512,768]{2,1,0:T(8,128)(2,1)S(1)}) custom-call(bf16[512,768]{1,0:T(8,128)(2,1)S(1)} %collective-permute-done.35.grad_ref.g1, bf16[2,512,768]{2,1,0:T(8,128)(2,1)S(1)} %copy-done.140, ...), custom_call_target="tpu_custom_call" | custom-call | flops 3623878656 | bytes 14942208 | tf_op jit(solution)/shard_map/ffn_bwd/pallas_call | solution.py:366
  330.3 7.9 %ffn_bwd.4 = (f32[512,768]{1,0:T(8,128)S(1)}, bf16[2,512,768]{2,1,0:T(8,128)(2,1)S(1)}, bf16[2,512,768]{2,1,0:T(8,128)(2,1)S(1)}, bf16[2,512,768]{2,1,0:T(8,128)(2,1)S(1)}) custom-call(bf16[512,768]{1,0:T(8,128)(2,1)S(1)} %get-tuple-element.275.grad_ref.g0, bf16[2,512,768]{2,1,0:T(8,128)(2,1)S(1)} %copy-done.142, bf16[2,512,768]{2,1,0:T(8,128)(2,1)S(1)} %copy-done.144, ...), custom_call_target="tpu_custom_call" | custom-call | flops 3623878656 | bytes 14942208 | tf_op jit(solution)/shard_map/ffn_bwd/pallas_call | solution.py:366
  351.2 4.7 mix_bwd.2
  363.4 5.7 ffn_grads.6
  372.3 31.0 %attn_bwd.2.pair_grad.rest_grad = bf16[4,576,512]{2,1,0:T(8,128)(2,1)} custom-call(s32[4]{0:T(128)} %copy-done.122, s32[2]{0:T(128)} %copy-done.130, bf16[576,2048]{1,0:T(8,128)(2,1)} %get-tuple-element.150.qkv, bf16[4,192,512]{2,1,0:T(8,128)(2,1)} %pad_maximum_fusion.3.dout, bf16[4,192,512]{2,1,0:T(8,128)(2,1)} %copy-done.91, f32[3,2048]{1,0:T(4,128)} %copy-done.148, ...), custom_call_target="tpu_custom_call" | custom-call | flops 8053063680 | bytes 9437184 | tf_op jit(solution)/shard_map/attn_bwd/pallas_call | solution.py:261
  407.8 5.1 proj_bwd.2
  413.5 3.0 collective-permute-done.43
  421.2 7.7 %ffn_grads.7 = bf16[3,768,768]{2,1,0:T(8,128)(2,1)} custom-call(bf16[512,768]{1,0:T(8,128)(2,1)S(1)} %copy-done.33, bf16[512,768]{1,0:T(8,128)(2,1)S(1)} %copy-done.36, bf16[512,768]{1,0:T(8,128)(2,1)S(1)} %get-tuple-element.275.grad_ref.g0, bf16[512,768]{1,0:T(8,128)(2,1)S(1)} %copy-done.39, bf16[2,512,768]{2,1,0:T(8,128)(2,1)S(1)} %copy-done.16, ...), custom_call_target="tpu_custom_call" | custom-call | flops 3623878656 | bytes 8257536 | tf_op jit(solution)/shard_map/ffn_grads/pallas_call | solution.py:407
  429.4 9.5 %collective-permute-done.44 = bf16[512,768]{1,0:T(8,128)(2,1)} collective-permute-done((bf16[512,768]{1,0:T(8,128)(2,1)}, bf16[512,768]{1,0:T(8,128)(2,1)}, u32[]{:S(2)}, u32[]{:S(2)}) %collective-permute-start.44) | collective-permute-done | bytes 786464 | tf_op jit(solution)/shard_map/ppermute | solution.py:677
  438.9 4.4 fusion.13
  446.1 8.8 %ffn_bwd.6 = (f32[512,768]{1,0:T(8,128)S(1)}, bf16[2,512,768]{2,1,0:T(8,128)(2,1)S(1)}, bf16[2,512,768]{2,1,0:T(8,128)(2,1)S(1)}, bf16[2,512,768]{2,1,0:T(8,128)(2,1)S(1)}) custom-call(bf16[512,768]{1,0:T(8,128)(2,1)S(1)} %get-tuple-element.272.grad_ref.g0, bf16[2,512,768]{2,1,0:T(8,128)(2,1)S(1)} %copy-done.136, bf16[2,512,768]{2,1,0:T(8,128)(2,1)S(1)} %copy-done.138, ...), custom_call_target="tpu_custom_call" | custom-call | flops 3623878656 | bytes 14942208 | tf_op jit(solution)/shard_map/ffn_bwd/pallas_call | solution.py:366
  456.0 8.0 %collective-permute-done.45.grad_ref.g1 = bf16[512,768]{1,0:T(8,128)(2,1)S(1)} collective-permute-done((bf16[512,768]{1,0:T(8,128)(2,1)S(1)}, bf16[512,768]{1,0:T(8,128)(2,1)S(1)}, u32[]{:S(2)}, u32[]{:S(2)}) %collective-permute-start.45) | collective-permute-done | bytes 786464 | tf_op jit(solution)/shard_map/ppermute | solution.py:677
  465.5 9.0 %ffn_bwd.7 = (bf16[512,768]{1,0:T(8,128)(2,1)S(1)}, bf16[2,512,768]{2,1,0:T(8,128)(2,1)S(1)}, bf16[2,512,768]{2,1,0:T(8,128)(2,1)S(1)}, bf16[2,512,768]{2,1,0:T(8,128)(2,1)S(1)}) custom-call(bf16[512,768]{1,0:T(8,128)(2,1)S(1)} %collective-permute-done.45.grad_ref.g1, bf16[2,512,768]{2,1,0:T(8,128)(2,1)S(1)} %copy-done.132, ...), custom_call_target="tpu_custom_call" | custom-call | flops 3623878656 | bytes 14942208 | tf_op jit(solution)/shard_map/ffn_bwd/pallas_call | solution.py:366
  474.5 5.7 ffn_grads.4
  480.1 6.4 collective-permute-done.57.rest_0_
  488.4 7.7 %ffn_grads.5 = bf16[3,768,768]{2,1,0:T(8,128)(2,1)} custom-call(bf16[512,768]{1,0:T(8,128)(2,1)S(1)} %get-tuple-element.124.rows_ref.h0, bf16[512,768]{1,0:T(8,128)(2,1)S(1)} %copy-done.29, bf16[512,768]{1,0:T(8,128)(2,1)S(1)} %get-tuple-element.272.grad_ref.g0, bf16[512,768]{1,0:T(8,128)(2,1)S(1)} %collective-permute-done.45.grad_ref.g1, ...), custom_call_target="tpu_custom_call" | custom-call | flops 3623878656 | bytes 8257536 | tf_op jit(solution)/shard_map/ffn_grads/pallas_call | solution.py:407
  497.5 18.5 %collective-permute-done.46.far_part = bf16[512,768]{1,0:T(8,128)(2,1)S(1)} collective-permute-done((bf16[512,768]{1,0:T(8,128)(2,1)}, bf16[512,768]{1,0:T(8,128)(2,1)S(1)}, u32[]{:S(2)}, u32[]{:S(2)}) %collective-permute-start.46) | collective-permute-done | bytes 786464 | tf_op jit(solution)/shard_map/ppermute | solution.py:677
  523.2 3.7 mix_bwd.3
  531.7 3.7 collective-permute-done.49
  535.4 3.8 collective-permute-done.48
  540.2 31.2 %attn_bwd.3.pair_grad.rest_grad = bf16[4,576,512]{2,1,0:T(8,128)(2,1)} custom-call(s32[4]{0:T(128)} %copy-done.122, s32[2]{0:T(128)} %copy-done.130, bf16[576,2048]{1,0:T(8,128)(2,1)} %get-tuple-element.170.qkv, bf16[4,192,512]{2,1,0:T(8,128)(2,1)} %pad_maximum_fusion.4.dout, bf16[4,192,512]{2,1,0:T(8,128)(2,1)} %copy-done.90, f32[3,2048]{1,0:T(4,128)} %copy-done.147, ...), custom_call_target="tpu_custom_call" | custom-call | flops 8053063680 | bytes 9437184 | tf_op jit(solution)/shard_map/attn_bwd/pallas_call | solution.py:261
  574.4 6.0 proj_bwd.3
  589.1 3.3 convert_element_type.151
  592.5 2.9 broadcast_select_fusion.1
  597.2 2.6 fusion.25
  601.0 2.2 collective-permute-start.60
  605.2 7.4 %collective-permute-start.32 = (bf16[512,768]{1,0:T(8,128)(2,1)}, bf16[512,768]{1,0:T(8,128)(2,1)}, u32[]{:S(2)}, u32[]{:S(2)}) collective-permute-start(bf16[512,768]{1,0:T(8,128)(2,1)} %get-tuple-element.281), channel_id=1, source_target_pairs={{0,0},{1,1},{2,16},{3,17},{16,2},{17,3},{18,18},{19,19},{4,4},{5,5... | collective-permute-start | bytes 2359304 | tf_op jit(solution)/shard_map/ppermute | solution.py:689
  613.2 16.8 %reduce-scatter.5.cloned.1.call-done = bf16[192,768]{1,0:T(8,128)(2,1)} async-done(((bf16[768,768]{1,0:T(8,128)(2,1)}), bf16[192,768]{1,0:T(8,128)(2,1)}) %reduce-scatter.5.cloned.1.call-update) | async-done | bytes 294928 | tf_op jit(solution)/shard_map/reduce_scatter | solution.py:705
  632.2 2.8 collective-permute-start.56
  635.0 3.5 fusion.18
  639.7 6.1 lamb.2
  652.4 2.7 collective-permute-start.66
  656.9 7.4 %collective-permute-start.61 = (bf16[512,768]{1,0:T(8,128)(2,1)}, bf16[512,768]{1,0:T(8,128)(2,1)}, u32[]{:S(2)}, u32[]{:S(2)}) collective-permute-start(bf16[512,768]{1,0:T(8,128)(2,1)} %get-tuple-element.287), channel_id=1, source_target_pairs={{0,0},{1,1},{2,16},{3,17},{16,2},{17,3},{18,18},{19,19},{4,4},{5,5... | collective-permute-start | bytes 2359304 | tf_op jit(solution)/shard_map/ppermute | solution.py:689
  667.6 8.3 %collective-permute-start.69 = (f32[12,768]{1,0:T(8,128)}, f32[12,768]{1,0:T(8,128)}, u32[]{:S(2)}, u32[]{:S(2)}) collective-permute-start(f32[12,768]{1,0:T(8,128)} %add_add_fusion.3), channel_id=1, source_target_pairs={{0,12},{4,8},{8,4},{12,0},{1,13},{5,9},{9,5},{13,1},{2,14},{6,10},... | collective-permute-start | bytes 110600 | tf_op jit(solution)/shard_map/ppermute | solution.py:693
  677.2 2.3 copy.74
  679.5 2.2 copy.75
  686.0 2.8 finish.1
  691.5 2.2 copy.73
  (651 shorter events, 188.3 us)
Async XLA Ops:
  7.2 67.7 %all-gather.5.cloned.1.call-start = ((), (), s32[]{:S(2)}) async-start(), calls=%async_computation.4 | async-start | bytes 1474560 | tf_op jit(solution)/shard_map/all_gather | solution.py:701
  10.7 14.6 %collective-permute-start.4 = (bf16[192,768]{1,0:T(8,128)(2,1)S(1)}, bf16[192,768]{1,0:T(8,128)(2,1)S(1)}, u32[]{:S(2)}, u32[]{:S(2)}) collective-permute-start(bf16[192,768]{1,0:T(8,128)(2,1)S(1)} %pad_maximum_fusion.5), channel_id=1, source_target_pairs={{0,0},{1,1},{2,16},{3,17},{4,4},{5,5},{6,20},{7,21},{8,8},{9,9},{1... | collective-permute-start | bytes 884744 | tf_op jit(solution)/shard_map/ppermute | solution.py:689
  11.4 13.9 %collective-permute-start.5 = (bf16[192,768]{1,0:T(8,128)(2,1)S(1)}, bf16[192,768]{1,0:T(8,128)(2,1)S(1)}, u32[]{:S(2)}, u32[]{:S(2)}) collective-permute-start(bf16[192,768]{1,0:T(8,128)(2,1)S(1)} %pad_maximum_fusion.5), channel_id=1, source_target_pairs={{0,2},{1,3},{2,18},{3,19},{4,6},{5,7},{6,22},{7,23},{8,10},{9,11},... | collective-permute-start | bytes 884744 | tf_op jit(solution)/shard_map/ppermute | solution.py:689
  26.0 102.7 %all-gather.7.cloned.1.call-start = ((), (), s32[]{:S(2)}) async-start(), calls=%async_computation.5 | async-start | bytes 4423680 | tf_op jit(solution)/shard_map/all_gather | solution.py:701
  29.3 16.6 %collective-permute-start.14 = (bf16[3,192,768]{2,1,0:T(8,128)(2,1)S(1)}, bf16[3,192,768]{2,1,0:T(8,128)(2,1)S(1)}, u32[]{:S(2)}, u32[]{:S(2)}) collective-permute-start(bf16[3,192,768]{2,1,0:T(8,128)(2,1)S(1)} %pad_maximum_fusion.2), channel_id=1, source_target_pairs={{0,2},{1,3},{2,18},{3,19},{4,6},{5,7},{6,22},{7,23},{8,10},{9,11},... | collective-permute-start | bytes 2654216 | tf_op jit(solution)/shard_map/ppermute | solution.py:689
  46.9 158.5 %all-gather.9.cloned.1.call-start = ((), (), s32[]{:S(2)}) async-start(), calls=%async_computation.6 | async-start | bytes 1474560 | tf_op jit(solution)/shard_map/all_gather | solution.py:701
  47.0 18.9 %collective-permute-start.2 = (bf16[512,768]{1,0:T(8,128)(2,1)}, bf16[512,768]{1,0:T(8,128)(2,1)}, u32[]{:S(2)}, u32[]{:S(2)}) collective-permute-start(bf16[512,768]{1,0:T(8,128)(2,1)} %collective-permute-done), channel_id=1, source_target_pairs={{0,1},{1,0},{2,3},{3,2},{4,5},{5,4},{6,7},{7,6},{8,9},{9,8},{10,11... | collective-permute-start | bytes 2359304 | tf_op jit(solution)/shard_map/ppermute | solution.py:677
  49.1 24.6 %collective-permute-start.1 = (bf16[512,768]{1,0:T(8,128)(2,1)}, bf16[512,768]{1,0:T(8,128)(2,1)S(1)}, u32[]{:S(2)}, u32[]{:S(2)}) collective-permute-start(bf16[512,768]{1,0:T(8,128)(2,1)} %collective-permute-done), channel_id=1, source_target_pairs={{0,16},{16,0},{1,17},{17,1},{2,18},{18,2},{3,19},{19,3},{4,20},{20... | collective-permute-start | bytes 2359304 | tf_op jit(solution)/shard_map/ppermute | solution.py:673
  65.8 12.9 %collective-permute-start.3 = (bf16[512,768]{1,0:T(8,128)(2,1)}, bf16[512,768]{1,0:T(8,128)(2,1)}, u32[]{:S(2)}, u32[]{:S(2)}) collective-permute-start(bf16[512,768]{1,0:T(8,128)(2,1)} %collective-permute-done.2), channel_id=1, source_target_pairs={{0,16},{16,0},{1,17},{17,1},{2,18},{18,2},{3,19},{19,3},{4,20},{20... | collective-permute-start | bytes 2359304 | tf_op jit(solution)/shard_map/ppermute | solution.py:673
  66.5 42.6 %collective-permute-start.12 = (f32[2,2,768]{2,0,1:T(2,128)}, f32[2,2,768]{2,0,1:T(2,128)}, u32[]{:S(2)}, u32[]{:S(2)}) collective-permute-start(f32[2,2,768]{2,0,1:T(2,128)} %pad_maximum_fusion.6), channel_id=1, source_target_pairs={{0,16},{16,0},{1,17},{17,1},{2,18},{18,2},{3,19},{19,3},{4,20},{20... | collective-permute-start | bytes 36872 | tf_op jit(solution)/shard_map/ppermute | solution.py:673
  77.0 51.8 %collective-permute-start.9 = (bf16[768,192]{1,0:T(8,128)(2,1)}, bf16[768,192]{1,0:T(8,128)(2,1)S(1)}, u32[]{:S(2)}, u32[]{:S(2)}) collective-permute-start(bf16[768,192]{1,0:T(8,128)(2,1)} %slice.124), channel_id=1, source_target_pairs={{0,16},{16,0},{1,17},{17,1},{2,18},{18,2},{3,19},{19,3},{4,20},{20... | collective-permute-start | bytes 884744 | tf_op jit(solution)/shard_map/ppermute | solution.py:673
  77.0 31.1 %collective-permute-start.10 = (bf16[768,192]{1,0:T(8,128)(2,1)}, bf16[768,192]{1,0:T(8,128)(2,1)S(1)}, u32[]{:S(2)}, u32[]{:S(2)}) collective-permute-start(bf16[768,192]{1,0:T(8,128)(2,1)} %slice.124), channel_id=1, source_target_pairs={{0,1},{1,0},{2,3},{3,2},{4,5},{5,4},{6,7},{7,6},{8,9},{9,8},{10,11... | collective-permute-start | bytes 884744 | tf_op jit(solution)/shard_map/ppermute | solution.py:677
  107.8 23.0 %collective-permute-start.6 = (bf16[192,512]{1,0:T(8,128)(2,1)}, bf16[192,512]{1,0:T(8,128)(2,1)S(1)}, u32[]{:S(2)}, u32[]{:S(2)}) collective-permute-start(bf16[192,512]{1,0:T(8,128)(2,1)} %get-tuple-element.299), channel_id=1, source_target_pairs={{0,16},{16,0},{1,17},{17,1},{2,18},{18,2},{3,19},{19,3},{4,20},{20... | collective-permute-start | bytes 589832 | tf_op jit(solution)/shard_map/ppermute | solution.py:673
  108.0 24.2 %collective-permute-start.11 = (bf16[768,192]{1,0:T(8,128)(2,1)S(1)}, bf16[768,192]{1,0:T(8,128)(2,1)S(1)}, u32[]{:S(2)}, u32[]{:S(2)}) collective-permute-start(bf16[768,192]{1,0:T(8,128)(2,1)S(1)} %collective-permute-done.10.out2), channel_id=1, source_target_pairs={{0,16},{16,0},{1,17},{17,1},{2,18},{18,2},{3,19},{19,3},{4,20},{20... | collective-permute-start | bytes 884744 | tf_op jit(solution)/shard_map/ppermute | solution.py:673
  110.4 21.8 %collective-permute-start.7 = (bf16[192,512]{1,0:T(8,128)(2,1)}, bf16[192,512]{1,0:T(8,128)(2,1)}, u32[]{:S(2)}, u32[]{:S(2)}) collective-permute-start(bf16[192,512]{1,0:T(8,128)(2,1)} %get-tuple-element.298), channel_id=1, source_target_pairs={{0,1},{1,0},{2,3},{3,2},{4,5},{5,4},{6,7},{7,6},{8,9},{9,8},{10,11... | collective-permute-start | bytes 589832 | tf_op jit(solution)/shard_map/ppermute | solution.py:677
  110.7 21.5 %collective-permute-start.8 = (bf16[192,512]{1,0:T(8,128)(2,1)}, bf16[192,512]{1,0:T(8,128)(2,1)}, u32[]{:S(2)}, u32[]{:S(2)}) collective-permute-start(bf16[192,512]{1,0:T(8,128)(2,1)} %get-tuple-element.297), channel_id=1, source_target_pairs={{0,17},{1,16},{2,19},{3,18},{16,1},{17,0},{18,3},{19,2},{4,21},{5,... | collective-permute-start | bytes 589832 | tf_op jit(solution)/shard_map/ppermute | solution.py:689
  129.5 11.3 %collective-permute-start.21 = (bf16[4,192,768]{2,1,0:T(8,128)(2,1)}, bf16[4,192,768]{2,1,0:T(8,128)(2,1)S(1)}, u32[]{:S(2)}, u32[]{:S(2)}) collective-permute-start(bf16[4,192,768]{2,1,0:T(8,128)(2,1)} %pad_maximum_fusion.1), channel_id=1, source_target_pairs={{16,0},{17,1},{18,16},{19,17},{20,4},{21,5},{22,20},{23,21},{24,8}... | collective-permute-start | bytes 3538952 | tf_op jit(solution)/shard_map/ppermute | solution.py:689
  138.4 19.6 %collective-permute-start.15 = (bf16[3,768,768]{2,1,0:T(8,128)(2,1)}, bf16[3,768,768]{2,1,0:T(8,128)(2,1)}, u32[]{:S(2)}, u32[]{:S(2)}) collective-permute-start(bf16[3,768,768]{2,1,0:T(8,128)(2,1)} %all-gather.7.cloned.1.call-done.first), channel_id=1, source_target_pairs={{0,16},{16,0},{1,17},{17,1},{2,18},{18,2},{3,19},{19,3},{4,20},{20... | collective-permute-start | bytes 10616840 | tf_op jit(solution)/shard_map/ppermute | solution.py:673
  142.7 107.5 %all-gather.11.cloned.1.call-start = ((), (), s32[]{:S(2)}) async-start(), calls=%async_computation.7 | async-start | bytes 4423680 | tf_op jit(solution)/shard_map/all_gather | solution.py:701
  142.7 15.0 %collective-permute-start.16 = (bf16[512,768]{1,0:T(8,128)(2,1)S(1)}, bf16[512,768]{1,0:T(8,128)(2,1)S(1)}, u32[]{:S(2)}, u32[]{:S(2)}) collective-permute-start(bf16[512,768]{1,0:T(8,128)(2,1)S(1)} %get-tuple-element.124.rows_ref.h0), channel_id=1, source_target_pairs={{0,1},{1,0},{2,3},{3,2},{4,5},{5,4},{6,7},{7,6},{8,9},{9,8},{10,11... | collective-permute-start | bytes 2359304 | tf_op jit(solution)/shard_map/ppermute | solution.py:677
  157.7 434.7 %reduce-scatter.11.cloned.1.call-start = ((), (), s32[]{:S(2)}) async-start(), calls=%async_computation.11 | async-start | bytes 4423680 | tf_op jit(solution)/shard_map/reduce_scatter | solution.py:705
  167.8 15.6 %collective-permute-start.17 = (bf16[512,768]{1,0:T(8,128)(2,1)S(1)}, bf16[512,768]{1,0:T(8,128)(2,1)S(1)}, u32[]{:S(2)}, u32[]{:S(2)}) collective-permute-start(bf16[512,768]{1,0:T(8,128)(2,1)S(1)} %get-tuple-element.128), channel_id=1, source_target_pairs={{0,1},{1,0},{2,3},{3,2},{4,5},{5,4},{6,7},{7,6},{8,9},{9,8},{10,11... | collective-permute-start | bytes 2359304 | tf_op jit(solution)/shard_map/ppermute | solution.py:677
  184.8 16.7 %collective-permute-start.19 = (bf16[512,768]{1,0:T(8,128)(2,1)S(1)}, bf16[512,768]{1,0:T(8,128)(2,1)}, u32[]{:S(2)}, u32[]{:S(2)}) collective-permute-start(bf16[512,768]{1,0:T(8,128)(2,1)S(1)} %add_convert_fusion.1), channel_id=1, source_target_pairs={{0,1},{1,0},{2,3},{3,2},{4,5},{5,4},{6,7},{7,6},{8,9},{9,8},{10,11... | collective-permute-start | bytes 2359304 | tf_op jit(solution)/shard_map/ppermute | solution.py:677
  186.3 23.2 %collective-permute-start.18 = (bf16[512,768]{1,0:T(8,128)(2,1)S(1)}, bf16[512,768]{1,0:T(8,128)(2,1)}, u32[]{:S(2)}, u32[]{:S(2)}) collective-permute-start(bf16[512,768]{1,0:T(8,128)(2,1)S(1)} %add_convert_fusion.1), channel_id=1, source_target_pairs={{0,16},{16,0},{1,17},{17,1},{2,18},{18,2},{3,19},{19,3},{4,20},{20... | collective-permute-start | bytes 2359304 | tf_op jit(solution)/shard_map/ppermute | solution.py:673
  206.6 25.4 %collective-permute-start.26 = (bf16[768,192]{1,0:T(8,128)(2,1)S(1)}, bf16[768,192]{1,0:T(8,128)(2,1)S(1)}, u32[]{:S(2)}, u32[]{:S(2)}) collective-permute-start(bf16[768,192]{1,0:T(8,128)(2,1)S(1)} %slice.129), channel_id=1, source_target_pairs={{0,16},{16,0},{1,17},{17,1},{2,18},{18,2},{3,19},{19,3},{4,20},{20... | collective-permute-start | bytes 884744 | tf_op jit(solution)/shard_map/ppermute | solution.py:673
  206.7 23.1 %collective-permute-start.27 = (bf16[768,192]{1,0:T(8,128)(2,1)S(1)}, bf16[768,192]{1,0:T(8,128)(2,1)S(1)}, u32[]{:S(2)}, u32[]{:S(2)}) collective-permute-start(bf16[768,192]{1,0:T(8,128)(2,1)S(1)} %slice.129), channel_id=1, source_target_pairs={{0,1},{1,0},{2,3},{3,2},{4,5},{5,4},{6,7},{7,6},{8,9},{9,8},{10,11... | collective-permute-start | bytes 884744 | tf_op jit(solution)/shard_map/ppermute | solution.py:677
  229.9 11.1 %collective-permute-start.28 = (bf16[768,192]{1,0:T(8,128)(2,1)S(1)}, bf16[768,192]{1,0:T(8,128)(2,1)S(1)}, u32[]{:S(2)}, u32[]{:S(2)}) collective-permute-start(bf16[768,192]{1,0:T(8,128)(2,1)S(1)} %collective-permute-done.27.out2), channel_id=1, source_target_pairs={{0,16},{16,0},{1,17},{17,1},{2,18},{18,2},{3,19},{19,3},{4,20},{20... | collective-permute-start | bytes 884744 | tf_op jit(solution)/shard_map/ppermute | solution.py:673
  250.2 20.0 %collective-permute-start.29 = (bf16[3,768,768]{2,1,0:T(8,128)(2,1)}, bf16[3,768,768]{2,1,0:T(8,128)(2,1)S(1)}, u32[]{:S(2)}, u32[]{:S(2)}) collective-permute-start(bf16[3,768,768]{2,1,0:T(8,128)(2,1)} %all-gather.11.cloned.1.call-done.first), channel_id=1, source_target_pairs={{0,16},{16,0},{1,17},{17,1},{2,18},{18,2},{3,19},{19,3},{4,20},{20... | collective-permute-start | bytes 10616840 | tf_op jit(solution)/shard_map/ppermute | solution.py:673
  250.8 19.4 %collective-permute-start.30 = (bf16[512,768]{1,0:T(8,128)(2,1)S(1)}, bf16[512,768]{1,0:T(8,128)(2,1)S(1)}, u32[]{:S(2)}, u32[]{:S(2)}) collective-permute-start(bf16[512,768]{1,0:T(8,128)(2,1)S(1)} %get-tuple-element.135.rows_ref.h0), channel_id=1, source_target_pairs={{0,1},{1,0},{2,3},{3,2},{4,5},{5,4},{6,7},{7,6},{8,9},{9,8},{10,11... | collective-permute-start | bytes 2359304 | tf_op jit(solution)/shard_map/ppermute | solution.py:677
  277.0 18.9 %collective-permute-start.31 = (bf16[512,768]{1,0:T(8,128)(2,1)S(1)}, bf16[512,768]{1,0:T(8,128)(2,1)S(1)}, u32[]{:S(2)}, u32[]{:S(2)}) collective-permute-start(bf16[512,768]{1,0:T(8,128)(2,1)S(1)} %get-tuple-element.139), channel_id=1, source_target_pairs={{0,1},{1,0},{2,3},{3,2},{4,5},{5,4},{6,7},{7,6},{8,9},{9,8},{10,11... | collective-permute-start | bytes 2359304 | tf_op jit(solution)/shard_map/ppermute | solution.py:677
  279.1 17.4 %collective-permute-start.34 = (bf16[512,768]{1,0:T(8,128)(2,1)S(1)}, bf16[512,768]{1,0:T(8,128)(2,1)S(1)}, u32[]{:S(2)}, u32[]{:S(2)}) collective-permute-start(bf16[512,768]{1,0:T(8,128)(2,1)S(1)} %dynamic-slice_bitcast_fusion), channel_id=1, source_target_pairs={{0,0},{1,1},{2,16},{3,17},{16,2},{17,3},{18,18},{19,19},{4,4},{5,5... | collective-permute-start | bytes 2359304 | tf_op jit(solution)/shard_map/ppermute | solution.py:689
  298.4 19.0 %collective-permute-start.35 = (bf16[512,768]{1,0:T(8,128)(2,1)S(1)}, bf16[512,768]{1,0:T(8,128)(2,1)S(1)}, u32[]{:S(2)}, u32[]{:S(2)}) collective-permute-start(bf16[512,768]{1,0:T(8,128)(2,1)S(1)} %get-tuple-element.275.grad_ref.g0), channel_id=1, source_target_pairs={{0,1},{1,0},{2,3},{3,2},{4,5},{5,4},{6,7},{7,6},{8,9},{9,8},{10,11... | collective-permute-start | bytes 2359304 | tf_op jit(solution)/shard_map/ppermute | solution.py:677
  326.1 18.4 %collective-permute-start.36 = (bf16[512,768]{1,0:T(8,128)(2,1)}, bf16[512,768]{1,0:T(8,128)(2,1)}, u32[]{:S(2)}, u32[]{:S(2)}) collective-permute-start(bf16[512,768]{1,0:T(8,128)(2,1)} %get-tuple-element.146), channel_id=1, source_target_pairs={{0,1},{1,0},{2,3},{3,2},{4,5},{5,4},{6,7},{7,6},{8,9},{9,8},{10,11... | collective-permute-start | bytes 2359304 | tf_op jit(solution)/shard_map/ppermute | solution.py:677
  356.5 13.8 %collective-permute-start.39 = (bf16[192,512]{1,0:T(8,128)(2,1)S(1)}, bf16[192,512]{1,0:T(8,128)(2,1)S(1)}, u32[]{:S(2)}, u32[]{:S(2)}) collective-permute-start(bf16[192,512]{1,0:T(8,128)(2,1)S(1)} %get-tuple-element.154), channel_id=1, source_target_pairs={{0,17},{1,16},{2,19},{3,18},{16,1},{17,0},{18,3},{19,2},{4,21},{5,... | collective-permute-start | bytes 589832 | tf_op jit(solution)/shard_map/ppermute | solution.py:689
  356.5 14.8 %collective-permute-start.38 = (bf16[192,512]{1,0:T(8,128)(2,1)S(1)}, bf16[192,512]{1,0:T(8,128)(2,1)S(1)}, u32[]{:S(2)}, u32[]{:S(2)}) collective-permute-start(bf16[192,512]{1,0:T(8,128)(2,1)S(1)} %get-tuple-element.153), channel_id=1, source_target_pairs={{0,1},{1,0},{2,3},{3,2},{4,5},{5,4},{6,7},{7,6},{8,9},{9,8},{10,11... | collective-permute-start | bytes 589832 | tf_op jit(solution)/shard_map/ppermute | solution.py:677
  357.5 13.8 %collective-permute-start.37 = (bf16[192,512]{1,0:T(8,128)(2,1)S(1)}, bf16[192,512]{1,0:T(8,128)(2,1)S(1)}, u32[]{:S(2)}, u32[]{:S(2)}) collective-permute-start(bf16[192,512]{1,0:T(8,128)(2,1)S(1)} %get-tuple-element.152), channel_id=1, source_target_pairs={{0,16},{16,0},{1,17},{17,1},{2,18},{18,2},{3,19},{19,3},{4,20},{20... | collective-permute-start | bytes 589832 | tf_op jit(solution)/shard_map/ppermute | solution.py:673
  369.2 50.6 %collective-permute-start.58 = (bf16[3,768,768]{2,1,0:T(8,128)(2,1)}, bf16[3,768,768]{2,1,0:T(8,128)(2,1)}, u32[]{:S(2)}, u32[]{:S(2)}) collective-permute-start(bf16[3,768,768]{2,1,0:T(8,128)(2,1)} %ffn_grads.6), channel_id=1, source_target_pairs={{0,16},{16,0},{1,17},{17,1},{2,18},{18,2},{3,19},{19,3},{4,20},{20... | collective-permute-start | bytes 10616840 | tf_op jit(solution)/shard_map/ppermute | solution.py:673
  369.2 34.1 %collective-permute-start.42 = (bf16[192,768]{1,0:T(8,128)(2,1)}, bf16[192,768]{1,0:T(8,128)(2,1)S(1)}, u32[]{:S(2)}, u32[]{:S(2)}) collective-permute-start(bf16[192,768]{1,0:T(8,128)(2,1)} %get-tuple-element.158), channel_id=1, source_target_pairs={{0,17},{1,16},{2,19},{3,18},{16,1},{17,0},{18,3},{19,2},{4,21},{5,... | collective-permute-start | bytes 884744 | tf_op jit(solution)/shard_map/ppermute | solution.py:689
  370.3 33.1 %collective-permute-start.41 = (bf16[192,768]{1,0:T(8,128)(2,1)}, bf16[192,768]{1,0:T(8,128)(2,1)S(1)}, u32[]{:S(2)}, u32[]{:S(2)}) collective-permute-start(bf16[192,768]{1,0:T(8,128)(2,1)} %get-tuple-element.157), channel_id=1, source_target_pairs={{0,1},{1,0},{2,3},{3,2},{4,5},{5,4},{6,7},{7,6},{8,9},{9,8},{10,11... | collective-permute-start | bytes 884744 | tf_op jit(solution)/shard_map/ppermute | solution.py:677
  371.3 32.0 %collective-permute-start.40 = (bf16[192,768]{1,0:T(8,128)(2,1)}, bf16[192,768]{1,0:T(8,128)(2,1)S(1)}, u32[]{:S(2)}, u32[]{:S(2)}) collective-permute-start(bf16[192,768]{1,0:T(8,128)(2,1)} %get-tuple-element.156), channel_id=1, source_target_pairs={{0,16},{16,0},{1,17},{17,1},{2,18},{18,2},{3,19},{19,3},{4,20},{20... | collective-permute-start | bytes 884744 | tf_op jit(solution)/shard_map/ppermute | solution.py:673
  418.8 20.1 %collective-permute-start.44 = (bf16[512,768]{1,0:T(8,128)(2,1)}, bf16[512,768]{1,0:T(8,128)(2,1)}, u32[]{:S(2)}, u32[]{:S(2)}) collective-permute-start(bf16[512,768]{1,0:T(8,128)(2,1)} %fusion.24), channel_id=1, source_target_pairs={{0,1},{1,0},{2,3},{3,2},{4,5},{5,4},{6,7},{7,6},{8,9},{9,8},{10,11... | collective-permute-start | bytes 2359304 | tf_op jit(solution)/shard_map/ppermute | solution.py:677
  429.0 163.5 %reduce-scatter.9.cloned.1.call-start = ((), (), s32[]{:S(2)}) async-start(), calls=%async_computation.10 | async-start | bytes 4423680 | tf_op jit(solution)/shard_map/reduce_scatter | solution.py:705
  445.1 19.0 %collective-permute-start.45 = (bf16[512,768]{1,0:T(8,128)(2,1)S(1)}, bf16[512,768]{1,0:T(8,128)(2,1)S(1)}, u32[]{:S(2)}, u32[]{:S(2)}) collective-permute-start(bf16[512,768]{1,0:T(8,128)(2,1)S(1)} %get-tuple-element.272.grad_ref.g0), channel_id=1, source_target_pairs={{0,1},{1,0},{2,3},{3,2},{4,5},{5,4},{6,7},{7,6},{8,9},{9,8},{10,11... | collective-permute-start | bytes 2359304 | tf_op jit(solution)/shard_map/ppermute | solution.py:677
  496.1 117.1 %reduce-scatter.7.cloned.1.call-start = ((), (), s32[]{:S(2)}) async-start(), calls=%async_computation.9 | async-start | bytes 1474560 | tf_op jit(solution)/shard_map/reduce_scatter | solution.py:705
  496.2 19.9 %collective-permute-start.46 = (bf16[512,768]{1,0:T(8,128)(2,1)}, bf16[512,768]{1,0:T(8,128)(2,1)S(1)}, u32[]{:S(2)}, u32[]{:S(2)}) collective-permute-start(bf16[512,768]{1,0:T(8,128)(2,1)} %copy-done.125), channel_id=1, source_target_pairs={{0,1},{1,0},{2,3},{3,2},{4,5},{5,4},{6,7},{7,6},{8,9},{9,8},{10,11... | collective-permute-start | bytes 2359304 | tf_op jit(solution)/shard_map/ppermute | solution.py:677
  497.5 132.6 %reduce-scatter.5.cloned.1.call-start = ((), (), s32[]{:S(2)}) async-start(), calls=%async_computation.8 | async-start | bytes 1474560 | tf_op jit(solution)/shard_map/reduce_scatter | solution.py:705
  528.4 10.8 %collective-permute-start.48 = (bf16[192,512]{1,0:T(8,128)(2,1)S(1)}, bf16[192,512]{1,0:T(8,128)(2,1)S(1)}, u32[]{:S(2)}, u32[]{:S(2)}) collective-permute-start(bf16[192,512]{1,0:T(8,128)(2,1)S(1)} %get-tuple-element.173), channel_id=1, source_target_pairs={{0,1},{1,0},{2,3},{3,2},{4,5},{5,4},{6,7},{7,6},{8,9},{9,8},{10,11... | collective-permute-start | bytes 589832 | tf_op jit(solution)/shard_map/ppermute | solution.py:677
  530.1 41.3 %collective-permute-start.52 = (bf16[192,768]{1,0:T(8,128)(2,1)S(1)}, bf16[192,768]{1,0:T(8,128)(2,1)S(1)}, u32[]{:S(2)}, u32[]{:S(2)}) collective-permute-start(bf16[192,768]{1,0:T(8,128)(2,1)S(1)} %get-tuple-element.178), channel_id=1, source_target_pairs={{0,17},{1,16},{2,19},{3,18},{16,1},{17,0},{18,3},{19,2},{4,21},{5,... | collective-permute-start | bytes 884744 | tf_op jit(solution)/shard_map/ppermute | solution.py:689
  530.9 40.5 %collective-permute-start.51 = (bf16[192,768]{1,0:T(8,128)(2,1)S(1)}, bf16[192,768]{1,0:T(8,128)(2,1)S(1)}, u32[]{:S(2)}, u32[]{:S(2)}) collective-permute-start(bf16[192,768]{1,0:T(8,128)(2,1)S(1)} %get-tuple-element.177), channel_id=1, source_target_pairs={{0,1},{1,0},{2,3},{3,2},{4,5},{5,4},{6,7},{7,6},{8,9},{9,8},{10,11... | collective-permute-start | bytes 884744 | tf_op jit(solution)/shard_map/ppermute | solution.py:677
  535.4 36.0 %collective-permute-start.50 = (bf16[192,768]{1,0:T(8,128)(2,1)S(1)}, bf16[192,768]{1,0:T(8,128)(2,1)S(1)}, u32[]{:S(2)}, u32[]{:S(2)}) collective-permute-start(bf16[192,768]{1,0:T(8,128)(2,1)S(1)} %get-tuple-element.176), channel_id=1, source_target_pairs={{0,16},{16,0},{1,17},{17,1},{2,18},{18,2},{3,19},{19,3},{4,20},{20... | collective-permute-start | bytes 884744 | tf_op jit(solution)/shard_map/ppermute | solution.py:673
  588.9 23.7 %collective-permute-start.63 = (f32[2,2,768]{2,0,1:T(2,128)S(1)}, f32[2,2,768]{2,0,1:T(2,128)S(1)}, u32[]{:S(2)}, u32[]{:S(2)}) collective-permute-start(f32[2,2,768]{2,0,1:T(2,128)S(1)} %broadcast_select_fusion.9), channel_id=1, source_target_pairs={{0,16},{16,0},{1,17},{17,1},{2,18},{18,2},{3,19},{19,3},{4,20},{20... | collective-permute-start | bytes 36872 | tf_op jit(solution)/shard_map/ppermute | solution.py:673
  595.3 36.8 %collective-permute-start.59 = (bf16[3,192,768]{2,1,0:T(8,128)(2,1)}, bf16[3,192,768]{2,1,0:T(8,128)(2,1)S(1)}, u32[]{:S(2)}, u32[]{:S(2)}) collective-permute-start(bf16[3,192,768]{2,1,0:T(8,128)(2,1)} %get-tuple-element.284), channel_id=1, source_target_pairs={{0,0},{1,1},{2,16},{3,17},{16,2},{17,3},{18,18},{19,19},{4,4},{5,5... | collective-permute-start | bytes 2654216 | tf_op jit(solution)/shard_map/ppermute | solution.py:689
  599.8 31.4 %collective-permute-start.54 = (bf16[512,768]{1,0:T(8,128)(2,1)}, bf16[512,768]{1,0:T(8,128)(2,1)}, u32[]{:S(2)}, u32[]{:S(2)}) collective-permute-start(bf16[512,768]{1,0:T(8,128)(2,1)} %fusion.25), channel_id=1, source_target_pairs={{0,1},{1,0},{2,3},{3,2},{4,5},{5,4},{6,7},{7,6},{8,9},{9,8},{10,11... | collective-permute-start | bytes 2359304 | tf_op jit(solution)/shard_map/ppermute | solution.py:677
  601.0 37.5 %collective-permute-start.60 = (bf16[3,192,768]{2,1,0:T(8,128)(2,1)}, bf16[3,192,768]{2,1,0:T(8,128)(2,1)}, u32[]{:S(2)}, u32[]{:S(2)}) collective-permute-start(bf16[3,192,768]{2,1,0:T(8,128)(2,1)} %get-tuple-element.283), channel_id=1, source_target_pairs={{0,16},{1,17},{2,0},{3,1},{16,18},{17,19},{18,2},{19,3},{4,20},{5,... | collective-permute-start | bytes 2654216 | tf_op jit(solution)/shard_map/ppermute | solution.py:689
  605.2 51.8 %collective-permute-start.32 = (bf16[512,768]{1,0:T(8,128)(2,1)}, bf16[512,768]{1,0:T(8,128)(2,1)}, u32[]{:S(2)}, u32[]{:S(2)}) collective-permute-start(bf16[512,768]{1,0:T(8,128)(2,1)} %get-tuple-element.281), channel_id=1, source_target_pairs={{0,0},{1,1},{2,16},{3,17},{16,2},{17,3},{18,18},{19,19},{4,4},{5,5... | collective-permute-start | bytes 2359304 | tf_op jit(solution)/shard_map/ppermute | solution.py:689
  612.6 51.8 %collective-permute-start.33 = (bf16[512,768]{1,0:T(8,128)(2,1)}, bf16[512,768]{1,0:T(8,128)(2,1)}, u32[]{:S(2)}, u32[]{:S(2)}) collective-permute-start(bf16[512,768]{1,0:T(8,128)(2,1)} %get-tuple-element.282), channel_id=1, source_target_pairs={{0,16},{1,17},{2,0},{3,1},{16,18},{17,19},{18,2},{19,3},{4,20},{5,... | collective-permute-start | bytes 2359304 | tf_op jit(solution)/shard_map/ppermute | solution.py:689
  631.2 17.3 %collective-permute-start.55 = (bf16[1,192,768]{2,1,0:T(8,128)(2,1)S(1)}, bf16[1,192,768]{2,1,0:T(8,128)(2,1)S(1)}, u32[]{:S(2)}, u32[]{:S(2)}) collective-permute-start(bf16[1,192,768]{2,1,0:T(8,128)(2,1)S(1)} %get-tuple-element.304), channel_id=1, source_target_pairs={{0,0},{1,1},{2,16},{3,17},{16,2},{17,3},{18,18},{19,19},{4,4},{5,5... | collective-permute-start | bytes 884744 | tf_op jit(solution)/shard_map/ppermute | solution.py:689
  632.2 16.4 %collective-permute-start.56 = (bf16[1,192,768]{2,1,0:T(8,128)(2,1)S(1)}, bf16[1,192,768]{2,1,0:T(8,128)(2,1)S(1)}, u32[]{:S(2)}, u32[]{:S(2)}) collective-permute-start(bf16[1,192,768]{2,1,0:T(8,128)(2,1)S(1)} %get-tuple-element.303), channel_id=1, source_target_pairs={{0,16},{1,17},{2,0},{3,1},{16,18},{17,19},{18,2},{19,3},{4,20},{5,... | collective-permute-start | bytes 884744 | tf_op jit(solution)/shard_map/ppermute | solution.py:689
  652.1 13.7 %collective-permute-start.65 = (f32[12,768]{1,0:T(8,128)S(1)}, f32[12,768]{1,0:T(8,128)S(1)}, u32[]{:S(2)}, u32[]{:S(2)}) collective-permute-start(f32[12,768]{1,0:T(8,128)S(1)} %concatenate.60), channel_id=1, source_target_pairs={{0,2},{1,3},{2,0},{3,1},{4,6},{5,7},{6,4},{7,5},{8,10},{9,11},{10,... | collective-permute-start | bytes 110600 | tf_op jit(solution)/shard_map/ppermute | solution.py:681
  652.4 13.5 %collective-permute-start.66 = (f32[12,768]{1,0:T(8,128)S(1)}, f32[12,768]{1,0:T(8,128)S(1)}, u32[]{:S(2)}, u32[]{:S(2)}) collective-permute-start(f32[12,768]{1,0:T(8,128)S(1)} %concatenate.60), channel_id=1, source_target_pairs={{0,3},{1,2},{2,1},{3,0},{4,7},{5,6},{6,5},{7,4},{8,11},{9,10},{10,... | collective-permute-start | bytes 110600 | tf_op jit(solution)/shard_map/ppermute | solution.py:685
  656.9 41.3 %collective-permute-start.61 = (bf16[512,768]{1,0:T(8,128)(2,1)}, bf16[512,768]{1,0:T(8,128)(2,1)}, u32[]{:S(2)}, u32[]{:S(2)}) collective-permute-start(bf16[512,768]{1,0:T(8,128)(2,1)} %get-tuple-element.287), channel_id=1, source_target_pairs={{0,0},{1,1},{2,16},{3,17},{16,2},{17,3},{18,18},{19,19},{4,4},{5,5... | collective-permute-start | bytes 2359304 | tf_op jit(solution)/shard_map/ppermute | solution.py:689
  664.3 33.9 %collective-permute-start.62 = (bf16[512,768]{1,0:T(8,128)(2,1)}, bf16[512,768]{1,0:T(8,128)(2,1)}, u32[]{:S(2)}, u32[]{:S(2)}) collective-permute-start(bf16[512,768]{1,0:T(8,128)(2,1)} %get-tuple-element.288), channel_id=1, source_target_pairs={{0,16},{1,17},{2,0},{3,1},{16,18},{17,19},{18,2},{19,3},{4,20},{5,... | collective-permute-start | bytes 2359304 | tf_op jit(solution)/shard_map/ppermute | solution.py:689
  666.5 15.2 %collective-permute-start.68 = (f32[12,768]{1,0:T(8,128)}, f32[12,768]{1,0:T(8,128)}, u32[]{:S(2)}, u32[]{:S(2)}) collective-permute-start(f32[12,768]{1,0:T(8,128)} %add_add_fusion.3), channel_id=1, source_target_pairs={{0,8},{4,12},{8,0},{12,4},{1,9},{5,13},{9,1},{13,5},{2,10},{6,14},... | collective-permute-start | bytes 110600 | tf_op jit(solution)/shard_map/ppermute | solution.py:693
  667.6 14.1 %collective-permute-start.69 = (f32[12,768]{1,0:T(8,128)}, f32[12,768]{1,0:T(8,128)}, u32[]{:S(2)}, u32[]{:S(2)}) collective-permute-start(f32[12,768]{1,0:T(8,128)} %add_add_fusion.3), channel_id=1, source_target_pairs={{0,12},{4,8},{8,4},{12,0},{1,13},{5,9},{9,5},{13,1},{2,14},{6,10},... | collective-permute-start | bytes 110600 | tf_op jit(solution)/shard_map/ppermute | solution.py:693
  (218 other events, 1661.0 us)
Sparse Core Ops, SparseCore 0:
  26.1 31.2 all-gather.4
  59.6 69.0 all-gather.6
  142.8 36.2 all-gather.8
  181.1 69.0 all-gather.10
  429.1 68.9 reduce-scatter.10
  500.2 66.6 reduce-scatter.8
  569.8 29.4 reduce-scatter.6
  602.2 27.8 reduce-scatter.4

commit v3 on v2

--- a/solution.py
+++ b/solution.py
@@ -29,7 +29,7 @@
     return jnp.minimum(first, length - tiles * deep), tiles
 
 
-def attn_fwd_kernel(place, ends, near, far, matrix, cos, sin, out, lse, qkv, a_t, k_n, o_t, calm, *, heads):
+def attn_fwd_kernel(place, ends, slab0, slab1, slab2, slab3, matrix, cos, sin, out0, out1, out2, out3, lse, qkv, a_t, k_n, o_t, calm, *, heads):
     step = pl.program_id(0)
     width = heads * HEAD
     half = HEAD // 2
@@ -40,14 +40,10 @@
     def _():
         a_t[...] = matrix[:, : 3 * width].T
         tops = [jnp.zeros((1, rows), jnp.float32) for _ in range(2 * heads)]
-        for slab in range(4):
-            src = near if slab < 2 else far
+        for slab, src in enumerate((slab0, slab1, slab2, slab3)):
             start = pl.multiple_of(place[slab] * rows, rows)
             here = pl.ds(start, rows)
-            proj = lax.dot_general(
-                a_t[...], src[(slab % 2) * rows : (slab % 2 + 1) * rows, :], (((1,), (1,)), ((), ())),
-                preferred_element_type=jnp.float32,
-            )
+            proj = lax.dot_general(a_t[...], src[...], (((1,), (1,)), ((), ())), preferred_element_type=jnp.float32)
             c, s = cos[:, here], sin[:, here]
             for i in range(2 * heads):
                 first, second = proj[i * HEAD : i * HEAD + half], proj[i * HEAD + half : (i + 1) * HEAD]
@@ -131,23 +127,23 @@
 
     @pl.when(step == pl.num_programs(0) - 1)
     def _():
-        for slab in range(4):
-            out[slab] = o_t[:, pl.ds(pl.multiple_of(place[slab] * rows, rows), rows)]
+        for slab, out in enumerate((out0, out1, out2, out3)):
+            out[...] = o_t[:, pl.ds(pl.multiple_of(place[slab] * rows, rows), rows)]
 
 
 def whole_spec(a):
     return pl.BlockSpec(a.shape, lambda i: (0,) * len(a.shape))
 
 
-def attn_fwd(place, ends, near, far, matrix, cos, sin):
-    length = 2 * near.shape[0]
-    rows = length // 4
+def attn_fwd(place, ends, slabs, matrix, cos, sin):
+    rows = slabs[0].shape[0]
+    length = 4 * rows
     width = matrix.shape[1] // 4
     heads = width // HEAD
     smem = pl.BlockSpec(memory_space=pltpu.SMEM)
-    ops = (near, far, matrix, cos, sin)
+    ops = (*slabs, matrix, cos, sin)
     outs = (
-        jax.ShapeDtypeStruct((4, width, rows), jnp.bfloat16),
+        *[jax.ShapeDtypeStruct((width, rows), jnp.bfloat16)] * 4,
         jax.ShapeDtypeStruct((heads, length), jnp.float32),
         jax.ShapeDtypeStruct((3 * width, length), jnp.bfloat16),
     )
@@ -171,7 +167,7 @@
     )(place, ends, *ops)
 
 
-def attn_bwd_kernel(place, ends, qkv, dout, out_t, lse, cos, sin, dproj, q_n, k_n, v_n, do_t, do_n, delta, dq_t, dk, dv, *, heads):
+def attn_bwd_kernel(place, ends, qkv, do0, do1, do2, do3, out0, out1, out2, out3, lse, cos, sin, dproj, q_n, k_n, v_n, do_t, do_n, delta, dq_t, dk, dv, *, heads):
     step = pl.program_id(0)
     width = heads * HEAD
     length = qkv.shape[1]
@@ -180,14 +176,14 @@
 
     @pl.when(step == 0)
     def _():
-        for slab in range(4):
+        for slab, (dout, out) in enumerate(((do0, out0), (do1, out1), (do2, out2), (do3, out3))):
             start = pl.multiple_of(place[slab] * rows, rows)
-            do_t[:, pl.ds(start, rows)] = dout[slab]
-            prod = dout[slab].astype(jnp.float32) * out_t[slab].astype(jnp.float32)
+            do_t[:, pl.ds(start, rows)] = dout[...]
+            prod = dout[...].astype(jnp.float32) * out[...].astype(jnp.float32)
             for h in range(heads):
                 piece = slice(h * HEAD, (h + 1) * HEAD)
                 delta[h : h + 1, pl.ds(start, rows)] = jnp.sum(prod[piece], axis=0, keepdims=True)
-                do_n[h, pl.ds(start, rows), :] = dout[slab, piece, :].T
+                do_n[h, pl.ds(start, rows), :] = dout[piece, :].T
         for h in range(heads):
             q_n[h] = qkv[h * HEAD : (h + 1) * HEAD, :].T
             k_n[h] = qkv[width + h * HEAD : width + (h + 1) * HEAD, :].T
@@ -249,13 +245,13 @@
                 dproj[slab, at : at + HEAD, :] = gv.astype(jnp.bfloat16)
 
 
-def attn_bwd(place, ends, qkv, dout, out_t, lse, cos, sin):
+def attn_bwd(place, ends, qkv, douts, outs, lse, cos, sin):
     length = qkv.shape[1]
     rows = length // 4
     width = qkv.shape[0] // 3
     heads = width // HEAD
     smem = pl.BlockSpec(memory_space=pltpu.SMEM)
-    ops = (qkv, dout, out_t, lse, cos, sin)
+    ops = (qkv, *douts, *outs, lse, cos, sin)
     natural = pltpu.VMEM((heads, length, HEAD), jnp.bfloat16)
     sums = pltpu.VMEM((heads, length, HEAD), jnp.float32)
     return pl.pallas_call(
@@ -419,7 +415,7 @@
     )(*rows, *grads, *gates, *ups, *inners, *other)
 
 
-def proj_bwd_kernel(pair_grad, rest_grad, near, far, matrix, out_grad, pair, rest, grad, a_t, total):
+def proj_bwd_kernel(pair_grad, rest_grad, slab0, slab1, slab2, slab3, matrix, out_grad, made3, made1, made2, made0, grad, a_t, total):
     step = pl.program_id(0)
     width3 = total.shape[0]
 
@@ -430,46 +426,44 @@
 
     def work(made, rows, out):
         total[...] += jnp.dot(made, rows, preferred_element_type=jnp.float32)
-        out[0] = jnp.dot(made.T, a_t[...], preferred_element_type=jnp.float32).astype(jnp.bfloat16)
-
-    pl.when(step == 0)(lambda: work(pair_grad[0], far[...], pair))
-    pl.when(step == 1)(lambda: work(pair_grad[0], near[...], pair))
-    pl.when(step == 2)(lambda: work(rest_grad[0], far[...], rest))
-    pl.when(step == 3)(lambda: work(rest_grad[0], near[...], rest))
+        out[...] = jnp.dot(made.T, a_t[...], preferred_element_type=jnp.float32).astype(jnp.bfloat16)
+
+    pl.when(step == 0)(lambda: work(pair_grad[0], slab3[...], made3))
+    pl.when(step == 1)(lambda: work(pair_grad[0], slab1[...], made1))
+    pl.when(step == 2)(lambda: work(rest_grad[0], slab2[...], made2))
+    pl.when(step == 3)(lambda: work(rest_grad[0], slab0[...], made0))
 
     @pl.when(step == 3)
     def _():
         grad[...] = jnp.concatenate([total[...], out_grad[...]], axis=0).astype(jnp.bfloat16).T
 
 
-def proj_bwd(grad_proj, near, far, matrix, out_grad):
-    slabs, width3, rows = grad_proj.shape
+def proj_bwd(grad_proj, slabs, matrix, out_grad):
+    _, width3, rows = grad_proj.shape
     features = matrix.shape[0]
-    parts = jax.ShapeDtypeStruct((2, rows, features), jnp.bfloat16)
+    part = jax.ShapeDtypeStruct((rows, features), jnp.bfloat16)
     return pl.pallas_call(
         proj_bwd_kernel,
         grid=(4,),
         in_specs=[
             pl.BlockSpec((1, width3, rows), lambda i: (jnp.where(i == 0, 3, 1), 0, 0)),
             pl.BlockSpec((1, width3, rows), lambda i: (jnp.where(i == 3, 0, 2), 0, 0)),
-            pl.BlockSpec((rows, features), lambda i: (jnp.where(i == 3, 0, 1), 0)),
-            pl.BlockSpec((rows, features), lambda i: (jnp.where(i == 0, 1, 0), 0)),
+            *[pl.BlockSpec((rows, features), lambda i: (0, 0))] * 4,
             pl.BlockSpec(matrix.shape, lambda i: (0, 0)),
             pl.BlockSpec(out_grad.shape, lambda i: (0, 0)),
         ],
         out_specs=(
-            pl.BlockSpec((1, rows, features), lambda i: (jnp.minimum(i, 1), 0, 0)),
-            pl.BlockSpec((1, rows, features), lambda i: (jnp.maximum(i - 2, 0), 0, 0)),
+            *[pl.BlockSpec((rows, features), lambda i: (0, 0))] * 4,
             pl.BlockSpec(matrix.shape, lambda i: (0, 0)),
         ),
-        out_shape=(parts, parts, jax.ShapeDtypeStruct(matrix.shape, jnp.bfloat16)),
+        out_shape=(part, part, part, part, jax.ShapeDtypeStruct(matrix.shape, jnp.bfloat16)),
         scratch_shapes=[pltpu.VMEM((width3, features), jnp.bfloat16), pltpu.VMEM((width3, features), jnp.float32)],
-        compiler_params=pltpu.CompilerParams(vmem_limit_bytes=40 << 20),
+        compiler_params=pltpu.CompilerParams(vmem_limit_bytes=60 << 20),
         cost_estimate=pl.CostEstimate(
             flops=16 * rows * features * width3, bytes_accessed=24 * rows * features, transcendentals=0
         ),
         name="proj_bwd",
-    )(grad_proj, grad_proj, near, far, matrix, out_grad)
+    )(grad_proj, grad_proj, *slabs, matrix, out_grad)
 
 
 def mean_of(v):
@@ -490,7 +484,7 @@
     inv[...] = inv_std
 
 
-def mix_fwd(heads, matrix, outs, near, params):
+def mix_fwd(heads, matrix, outs, own, params):
     width, rows = heads[0].shape
     features = matrix.shape[0]
     whole = lambda a: pl.BlockSpec(a.shape, lambda i: (0,) * len(a.shape))
@@ -502,12 +496,12 @@
         in_specs=[whole(a) for a in (*heads, matrix, *outs)] + [block, whole(params)],
         out_specs=(block, block, block, pl.BlockSpec((rows, 1), lambda i: (0, 0))),
         out_shape=(shape(jnp.float32), shape(jnp.bfloat16), shape(jnp.float32), jax.ShapeDtypeStruct((rows, 1), jnp.float32)),
-        compiler_params=pltpu.CompilerParams(vmem_limit_bytes=40 << 20),
+        compiler_params=pltpu.CompilerParams(vmem_limit_bytes=60 << 20),
         cost_estimate=pl.CostEstimate(
             flops=2 * rows * features * features, bytes_accessed=14 * rows * features + 2 * features * features, transcendentals=rows
         ),
         name="mix_fwd",
-    )(*heads, matrix, *outs, near, params)
+    )(*heads, matrix, *outs, own, params)
 
 
 def mix_bwd_kernel(
@@ -544,13 +538,57 @@
         in_specs=[whole(a) for a in ops],
         out_specs=tuple(whole(a) for a in shapes),
         out_shape=tuple(shapes),
-        compiler_params=pltpu.CompilerParams(vmem_limit_bytes=40 << 20),
+        compiler_params=pltpu.CompilerParams(vmem_limit_bytes=60 << 20),
         cost_estimate=pl.CostEstimate(
             flops=4 * rows * features * features, bytes_accessed=22 * rows * features + 4 * features * features, transcendentals=0
         ),
         name="mix_bwd",
     )(*ops)
     return got[0], got[1], got[2:6], got[6:10]
+
+
+def top_bwd_kernel(first, second, third, fourth, normed, inv, gain, low_in, back, low, norms):
+    grad = first[...].astype(jnp.float32)
+    for part in (second, third, fourth):
+        if part is not None:
+            grad += part[...].astype(jnp.float32)
+    if low_in is not None:
+        low_in[...] = grad.astype(jnp.bfloat16)
+        grad = grad.astype(jnp.bfloat16).astype(jnp.float32)
+    unit = normed[...]
+    norms[0:1, :] = jnp.sum(grad * unit, axis=0, keepdims=True)
+    norms[1:2, :] = jnp.sum(grad, axis=0, keepdims=True)
+    grad_unit = grad * gain[...]
+    out = inv[...] * (grad_unit - mean_of(grad_unit) - unit * mean_of(grad_unit * unit))
+    back[...] = out
+    low[...] = out.astype(jnp.bfloat16)
+
+
+def top_bwd(parts, normed, inv, gain):
+    rows, features = normed.shape
+    several = len(parts) > 1
+    whole = lambda a: pl.BlockSpec(a.shape, lambda i: (0,) * len(a.shape))
+    shape = lambda t: jax.ShapeDtypeStruct((rows, features), t)
+    shapes = [shape(jnp.bfloat16)] * several + [shape(jnp.float32), shape(jnp.bfloat16)]
+    shapes.append(jax.ShapeDtypeStruct((2, features), jnp.float32))
+    ops = (*parts, normed, inv, gain)
+
+    def kernel(*refs):
+        ins, outs = refs[: len(ops)], refs[len(ops) :]
+        four = list(ins[: len(parts)]) + [None] * (4 - len(parts))
+        top_bwd_kernel(*four, *ins[len(parts) :], *((None,) * (not several)), *outs)
+
+    got = pl.pallas_call(
+        kernel,
+        grid=(1,),
+        in_specs=[whole(a) for a in ops],
+        out_specs=tuple(whole(a) for a in shapes),
+        out_shape=tuple(shapes),
+        compiler_params=pltpu.CompilerParams(vmem_limit_bytes=60 << 20),
+        cost_estimate=pl.CostEstimate(flops=12 * rows * features, bytes_accessed=18 * rows * features, transcendentals=0),
+        name="top_bwd",
+    )(*ops)
+    return tuple(got) if several else (None, *got)
 
 
 def lamb_step(weight, gradient, first_old, second):
@@ -565,8 +603,9 @@
     return first_new, second_new, update
 
 
-def lamb_kernel(same, other, *refs, kinds):
+def lamb_kernel(*refs, kinds, shards):
     count = len(kinds)
+    made, refs = refs[:shards], refs[shards:]
     olds, news, late = refs[: 3 * count], refs[3 * count : 6 * count], refs[6 * count]
     late[...] = jnp.zeros_like(late)
     for i, (turned, parts) in enumerate(kinds):
@@ -574,7 +613,7 @@
         first_out, second_out, update_out = news[3 * i : 3 * i + 3]
         row = None
         for at, (index, columns) in enumerate(parts):
-            gradient = same[index, :, columns].astype(jnp.float32) + other[index, :, columns].astype(jnp.float32)
+            gradient = sum(shard[index, :, columns].astype(jnp.float32) for shard in made)
             gradient = gradient.T if turned else gradient
             where = (at,) if len(weight.shape) == 3 else (slice(None),)
             first_new, second_new, update = lamb_step(weight[where], gradient, first[where], second[where])
@@ -586,19 +625,19 @@
         late[i : i + 1, : row.shape[1]] = row
 
 
-def lamb(same, other, kinds, olds, features):
+def lamb(made, kinds, olds, features):
     whole = lambda a: pl.BlockSpec(a.shape, lambda i: (0,) * len(a.shape))
     shapes = [jax.ShapeDtypeStruct(a.shape, jnp.float32) for a in olds]
     shapes.append(jax.ShapeDtypeStruct((len(kinds), features), jnp.float32))
-    ops = (same, other, *olds)
+    ops = (*made, *olds)
     return pl.pallas_call(
-        functools.partial(lamb_kernel, kinds=kinds),
+        functools.partial(lamb_kernel, kinds=kinds, shards=len(made)),
         grid=(1,),
         in_specs=[whole(a) for a in ops],
         out_specs=tuple(whole(a) for a in shapes),
         out_shape=tuple(shapes),
-        compiler_params=pltpu.CompilerParams(vmem_limit_bytes=48 << 20),
-        cost_estimate=pl.CostEstimate(flops=20 * same.size, bytes_accessed=28 * same.size, transcendentals=same.size),
+        compiler_params=pltpu.CompilerParams(vmem_limit_bytes=60 << 20),
+        cost_estimate=pl.CostEstimate(flops=20 * made[0].size, bytes_accessed=28 * made[0].size, transcendentals=made[0].size),
         name="lamb",
     )(*ops)
 
@@ -607,13 +646,14 @@
     weights, updates = refs[:count], refs[count : 2 * count]
     norm_out, first_out, second_out, trust = refs[2 * count : 2 * count + 4]
     news = refs[2 * count + 4 :]
-    first_new, second_new, update = lamb_step(now[...], totals[0:4, :], first[...], second[...])
-    norms = [jnp.sqrt(jnp.sum(v * v, axis=-1, keepdims=True)) for v in (now[...], update)]
-    norm_out[...] = now[...] - LEARN_RATE * (norms[0] / norms[1]) * update
-    first_out[...] = first_new
-    second_out[...] = second_new
+    for i in range(2):
+        first_new, second_new, update = lamb_step(now[i], totals[2 * i : 2 * i + 2, :], first[i], second[i])
+        norms = [jnp.sqrt(jnp.sum(v * v, axis=-1, keepdims=True)) for v in (now[i], update)]
+        norm_out[i] = now[i] - LEARN_RATE * (norms[0] / norms[1]) * update
+        first_out[i] = first_new
+        second_out[i] = second_new
     sizes = jnp.sqrt(jnp.sum(totals[4:12, :], axis=-1, keepdims=True))
-    trust[...] = jnp.concatenate([sizes[0:4], sizes[4:8]], axis=1)
+    trust[...] = jnp.concatenate([sizes[0:4], sizes[4:8]], axis=1).T
     for i in range(count):
         ratio = LEARN_RATE * (sizes[i : i + 1] / sizes[4 + i : 5 + i])
         for at in range(weights[i].shape[0]) if len(weights[i].shape) == 3 else (slice(None),):
@@ -622,7 +662,7 @@
 
 def finish(totals, now, first, second, weights, updates):
     whole = lambda a: pl.BlockSpec(a.shape, lambda i: (0,) * len(a.shape))
-    shapes = [jax.ShapeDtypeStruct(now.shape, jnp.float32)] * 3 + [jax.ShapeDtypeStruct((4, 2), jnp.float32)]
+    shapes = [jax.ShapeDtypeStruct(now.shape, jnp.float32)] * 3 + [jax.ShapeDtypeStruct((2, 4), jnp.float32)]
     shapes += [jax.ShapeDtypeStruct(a.shape, jnp.float32) for a in weights]
     ops = (totals, now, first, second, *weights, *updates)
     size = sum(a.size for a in weights)
@@ -632,7 +672,7 @@
         in_specs=[whole(a) for a in ops],
         out_specs=tuple(whole(a) for a in shapes),
         out_shape=tuple(shapes),
-        compiler_params=pltpu.CompilerParams(vmem_limit_bytes=48 << 20),
+        compiler_params=pltpu.CompilerParams(vmem_limit_bytes=60 << 20),
         cost_estimate=pl.CostEstimate(flops=3 * size, bytes_accessed=12 * size, transcendentals=0),
         name="finish",
     )(*ops)
@@ -705,6 +745,12 @@
     return lax.psum_scatter(whole, "dp", scatter_dimension=axis, tiled=True)
 
 
+def to_owner(shard, layer):
+    same = [pair for pair in SWAP if pair[1] // 4 == layer]
+    other = [pair for pair in SWAP_BACK if pair[1] // 4 == layer]
+    return over_both(shard, same), over_both(shard, other)
+
+
 def chips_total(v):
     v = (v + over_x(v)) + (over_y(v) + over_diag(v))
     if not quad():
@@ -728,18 +774,6 @@
     return (normed * gain_row + bias_row, normed, inv_std)
 
 
-def norm_back(grad_out, normed, inv_std, gain_row):
-    grad_gain = jnp.sum(grad_out * normed, axis=0)
-    grad_bias = jnp.sum(grad_out, axis=0)
-    grad_normed = grad_out * gain_row
-    grad_vals = inv_std * (
-        grad_normed
-        - jnp.mean(grad_normed, axis=-1, keepdims=True)
-        - normed * jnp.mean(grad_normed * normed, axis=-1, keepdims=True)
-    )
-    return (grad_vals, grad_gain, grad_bias)
-
-
 def dot(spec, a, b):
     return jnp.einsum(spec, a, b, preferred_element_type=f32)
 
@@ -748,50 +782,50 @@
     return lax.optimization_barrier((value,) + others)[0]
 
 
-def layer_forward(near, far, matrix, ffn, params, env):
+def layer_forward(slabs, matrix, ffn, params, env, late):
     place, ends, cos, sin = env
-    mine, log_sums, qkv = attn_fwd(place, ends, near, far, matrix, cos, sin)
+    *mine, log_sums, qkv = attn_fwd(place, ends, slabs, matrix, cos, sin)
     out_own = matrix[:, 3 * (matrix.shape[1] // 4) :]
     out_across = over_x(out_own)
     outs = (over_section(out_own), out_across, over_section(after(out_across, log_sums)))
     all_heads = [mine[0], over_section(mine[1]), over_x(mine[2]), over_both(mine[3], CORNER)]
-    hidden, hidden_low, normed_one, inv_one = mix_fwd(all_heads, matrix, outs, near, params[:, 0])
-    ffn = (ffn, over_section(after(ffn, hidden_low)))
+    hidden, hidden_low, normed_one, inv_one = mix_fwd(all_heads, matrix, outs, slabs[0], params[:, 0])
     hidden_rows = [hidden_low, over_x(hidden_low)]
+    ffn = (ffn, over_section(after(ffn, hidden_rows[late])))
     own_part, *own_acts = ffn_fwd(hidden_rows[0], *ffn, f32)
     far_part, *far_acts = ffn_fwd(hidden_rows[1], *ffn, bf16)
     ffn_out = own_part + over_x(far_part).astype(f32)
     output, normed_two, inv_two = norm_fwd(hidden + ffn_out, params[0, 1], params[1, 1])
-    kept = (near, far, qkv, mine, log_sums, all_heads, normed_one, inv_one, hidden_rows, (own_acts, far_acts))
+    kept = (slabs, qkv, mine, log_sums, all_heads, normed_one, inv_one, hidden_rows, (own_acts, far_acts))
     return output.astype(bf16), outs, kept + (normed_two, inv_two, ffn)
 
 
-def layer_backward(grad_out, kept, matrix, outs, params, env):
+def layer_backward(grad_parts, kept, matrix, outs, params, env, early=(), late=()):
     place, ends, cos, sin = env
-    (near, far, qkv, mine, log_sums, all_heads, normed_one, inv_one, hidden_rows, acts, normed_two, inv_two, ffn) = kept
-    grad_mixed, gain_two, bias_two = norm_back(grad_out, normed_two, inv_two, params[0, 1])
-    grad_low = grad_mixed.astype(bf16)
+    (slabs, qkv, mine, log_sums, all_heads, normed_one, inv_one, hidden_rows, acts, normed_two, inv_two, ffn) = kept
+    sent, grad_mixed, grad_low, norm_two = top_bwd(grad_parts, normed_two, inv_two, params[0, 1:2])
     grad_rows = [grad_low, over_x(grad_low)]
     own_part, *own_grads = ffn_bwd(grad_rows[0], *acts[0], *ffn, f32)
-    far_part, *far_grads = ffn_bwd(grad_rows[1], *acts[1], *ffn, bf16)
+    far_part, *far_grads = ffn_bwd(after(grad_rows[1], own_part, *early), *acts[1], *ffn, bf16)
     made = list(zip(own_grads, far_grads))
     ffn_other = ffn_grads(1, hidden_rows, grad_rows, *made)
     ffn_grad = ffn_grads(0, hidden_rows, grad_rows, *made, over_section(ffn_other))
+    far_part = over_x(far_part)
+    ffn_grad = after(ffn_grad, far_part)
     grad_mixed_one, norm_one, grad_heads, out_grad = mix_bwd(
-        grad_mixed, own_part, over_x(far_part), normed_one, inv_one, params[:, 0], all_heads, matrix, outs
-    )
-    grad_mine = jnp.stack(
-        [grad_heads[0], over_section(grad_heads[1]), over_x(grad_heads[2]), over_both(grad_heads[3], CORNER)]
-    )
-    out_own = [out_grad[0], over_section(out_grad[1]), over_x(out_grad[2]), over_both(out_grad[3], CORNER)]
-    out_own = sum(g.astype(f32) for g in out_own)
-    grad_proj = attn_bwd(place, ends, qkv, grad_mine, mine, log_sums, cos, sin)
-    pair, rest, matrix_grad = proj_bwd(grad_proj, near, far, matrix, out_own)
-    other = over_section(pair).astype(f32)
-    far_sum = over_x((rest[0].astype(f32) + other[0]).astype(bf16))
-    rows_sum = rest[1].astype(f32) + other[1] + far_sum.astype(f32)
-    norm_grads = jnp.stack([jnp.stack([norm_one[0], gain_two]), jnp.stack([norm_one[1], bias_two])])
-    return grad_mixed_one + rows_sum, matrix_grad, ffn_grad, norm_grads
+        grad_mixed, own_part, far_part, normed_one, inv_one, params[:, 0], all_heads, matrix, outs
+    )
+    grad_mine = (
+        grad_heads[0], over_section(grad_heads[1]), over_x(grad_heads[2]), over_both(grad_heads[3], CORNER)
+    )
+    *out_grad, _ = lax.optimization_barrier((*out_grad, grad_mine))
+    out_own = (out_grad[0], over_section(out_grad[1]), over_x(out_grad[2]), over_both(out_grad[3], CORNER))
+    grad_proj = attn_bwd(place, ends, qkv, after(grad_mine, *late), mine, log_sums, cos, sin)
+    out_own = sum(g.astype(f32) for g in after(out_own, grad_proj))
+    part3, part1, part2, part0, matrix_grad = proj_bwd(grad_proj, slabs, matrix, out_own)
+    far_sum = over_x((part2.astype(f32) + over_section(part3).astype(f32)).astype(bf16))
+    norm_grads = jnp.stack([jnp.stack([norm_one[0], norm_two[0]]), jnp.stack([norm_one[1], norm_two[1]])])
+    return sent, (grad_mixed_one, part0, over_section(part1), far_sum), matrix_grad, ffn_grad, norm_grads
 
 
 def body(
@@ -820,28 +854,32 @@
     y, x = spot // 2, spot % 2
     rows = tokens.shape[1]
     length = segments.shape[-1]
-    masters = (heads_in[0], heads_out[0], gate_up[0], project_down[0])
+    masters = (heads_in[0], heads_out[0], gate_up[0], project_down[0].T)
     deep, width = masters[0].shape[1:]
 
     attn_piece = jnp.concatenate(
         [masters[0].transpose(1, 0, 2).reshape(deep, 3 * width), masters[1].T], axis=1
     ).astype(bf16)
-    ffn_piece = jnp.concatenate([masters[2], masters[3].T[None]], axis=0).astype(bf16)
+    ffn_piece = jnp.concatenate([masters[2], masters[3][None]], axis=0).astype(bf16)
 
     def to_block(piece, layer):
         got = []
         for to_y in range(2):
             pairs = [(number(layer, c, x), number(c, to_y, x)) for c in range(2) for x in range(2)]
             got.append(over_both(piece, pairs))
+        return got
+
+    def for_y(got):
         return jnp.where(y == 0, got[0], got[1])
 
+    def four_slabs(rows, *along):
+        across, *along = lax.optimization_barrier((over_x(rows), *along))
+        return (rows, over_section(rows), across, over_section(across)), along
+
     own = over_both(lax.dynamic_index_in_dim(tokens, section, 0, keepdims=False), SWAP)
-    first_matrix = gather_later(to_block(attn_piece, 0), 0)
-    ffn_first = gather_later(to_block(after(ffn_piece, own), 0), 1)
-
-    def four_slabs(rows):
-        across = over_x(rows)
-        return jnp.concatenate([rows, over_section(rows)]), jnp.concatenate([across, over_section(across)])
+    first_matrix = gather_later(for_y(to_block(attn_piece, 0)), 0)
+    slabs_zero, ffn_pieces = four_slabs(own, *to_block(after(ffn_piece, own), 0))
+    ffn_first = gather_later(for_y(ffn_pieces), 1)
 
     both_params = jnp.stack([norm_gain[0], norm_bias[0]])
     other_params = over_section(both_params)
@@ -856,23 +894,14 @@
     ends = jnp.stack([jnp.sum((seq_seg <= d).astype(jnp.int32)) for d in range(2)])
     env = (place, ends) + rope_tables(length)
 
-    near_zero, far_zero = four_slabs(own)
-    low_zero, outs_zero, kept_zero = layer_forward(near_zero, far_zero, first_matrix, ffn_first, params[0], env)
-    hidden_rows = kept_zero[8]
-    second_piece = to_block(after(jnp.concatenate([attn_piece[None], ffn_piece]), ffn_first), 1)
+    low_zero, outs_zero, kept_zero = layer_forward(slabs_zero, first_matrix, ffn_first, params[0], env, 1)
+    hidden_rows = kept_zero[7]
+    second_piece = for_y(to_block(after(jnp.concatenate([attn_piece[None], ffn_piece]), slabs_zero[3]), 1))
     second_matrix = gather_later(after(second_piece[0], hidden_rows[0]), 0)
     ffn_second = gather_later(after(second_piece[1:], hidden_rows[1]), 1)
-    near_one, far_one = four_slabs(low_zero)
-    low_one, outs_one, kept_one = layer_forward(near_one, far_one, second_matrix, ffn_second, params[1], env)
+    slabs_one, _ = four_slabs(low_zero)
+    low_one, outs_one, kept_one = layer_forward(slabs_one, second_matrix, ffn_second, params[1], env, 0)
     grad_top = over_both(after(lax.dynamic_index_in_dim(cotangent, section, 0, keepdims=False), low_zero), SWAP)
-    grad_one, matrix_one, ffn_one, norm_one = layer_backward(
-        grad_top.astype(f32), kept_one, second_matrix, outs_one, params[1], env
-    )
-    sent = grad_one.astype(bf16)
-    grad_zero, matrix_zero, ffn_zero, norm_zero = layer_backward(
-        sent.astype(f32), kept_zero, first_matrix, outs_zero, params[0], env
-    )
-
     def home(zero, one):
         same = over_both(jnp.where(y == 0, zero, one), SWAP)
         other = over_both(jnp.where(y == 0, one, zero), SWAP_BACK)
@@ -883,15 +912,25 @@
         return jnp.stack([jnp.where(section == 0, same, other), jnp.where(section == 0, other, same)])
 
     layer_out = by_micro(low_zero, low_one)
-
-    ffn_home = home(scatter_later(ffn_zero, 1), scatter_later(ffn_one, 1))
-    attn_home = home(scatter_later(matrix_zero, 0)[None], scatter_later(matrix_one, 0)[None])
+    _, grads_one, matrix_one, ffn_one, norm_one = layer_backward(
+        (grad_top,), kept_one, second_matrix, outs_one, params[1], env, (layer_out,)
+    )
+    ffn_one = to_owner(scatter_later(ffn_one, 1), 1)
+    matrix_one = to_owner(scatter_later(matrix_one, 0)[None], 1)
+    sent, grads_zero, matrix_zero, ffn_zero, norm_zero = layer_backward(
+        grads_one, kept_zero, first_matrix, outs_zero, params[0], env, ffn_one, matrix_one
+    )
+    ffn_home = to_owner(scatter_later(ffn_zero, 1), 0) + ffn_one
+    attn_home = to_owner(scatter_later(matrix_zero, 0)[None], 0)
+    grad_zero = sum(g.astype(f32) for g in grads_zero)
+
+
     norm_mine = jnp.where(section == 0, norm_zero, norm_one) + over_section(
         jnp.where(section == 0, norm_one, norm_zero)
     )
     features = norm_mine.shape[-1]
-    firsts = (heads_in_first[0], heads_out_first[0], gate_up_first[0], project_down_first[0])
-    seconds = (heads_in_second[0], heads_out_second[0], gate_up_second[0], project_down_second[0])
+    firsts = (heads_in_first[0], heads_out_first[0], gate_up_first[0], project_down_first[0].T)
+    seconds = (heads_in_second[0], heads_out_second[0], gate_up_second[0], project_down_second[0].T)
     olds = list(zip(masters, firsts, seconds))
 
     def squares(matrix):
@@ -900,26 +939,25 @@
 
     columns = slice(0, masters[2].shape[-1])
     ffn_new = lamb(
-        *ffn_home, ((False, ((0, columns), (1, columns))), (True, ((2, columns),))), olds[2] + olds[3], features
+        ffn_home, ((False, ((0, columns), (1, columns))), (False, ((2, columns),))), olds[2] + olds[3], features
     )
     early = jnp.stack([squares(m) for m in masters])
     early = jnp.concatenate([norm_mine.reshape(4, -1), early], axis=0)
-    attn_home = lax.optimization_barrier((*attn_home, early, ffn_new[-1]))[:2]
+    attn_home = lax.optimization_barrier((*attn_home, early, ffn_new[-1]))[:2] + matrix_one
     pieces = tuple((0, slice(i * width, (i + 1) * width)) for i in range(4))
-    attn_new = lamb(*attn_home, ((False, pieces[:3]), (True, pieces[3:])), olds[0] + olds[1], features)
+    attn_new = lamb(attn_home, ((False, pieces[:3]), (True, pieces[3:])), olds[0] + olds[1], features)
     totals = chips_total(jnp.concatenate([early, attn_new[-1], ffn_new[-1]], axis=0))
     made = [attn_new[:3], attn_new[3:6], ffn_new[:3], ffn_new[3:6]]
-    norm_shape = both_params.shape
-    flat = [v.reshape(4, features) for v in (both_params, norm_first[0], norm_second[0])]
     *norms, trust_norms, in_new, out_new, gate_new, down_new = finish(
-        totals, *flat, masters, [m[2] for m in made]
-    )
-    new_mats = (in_new, out_new, gate_new, down_new)
-    input_grads = by_micro(after(grad_zero.astype(bf16), attn_new[-1]), sent).astype(f32)
+        totals, both_params, norm_first[0], norm_second[0], masters, [m[2] for m in made]
+    )
+    new_mats = (in_new, out_new, gate_new, down_new.T)
+    made[3] = [v.T for v in made[3]]
+    input_grads = by_micro(after(grad_zero.astype(bf16), attn_home[0]), sent).astype(f32)
     outs = [layer_out, input_grads]
     for i in range(4):
         outs += [new_mats[i], made[i][0], made[i][1]]
-    outs += [v.reshape(norm_shape) for v in norms] + [trust_norms]
+    outs += [*norms, trust_norms.T]
     return tuple(item[None] for item in outs)
 
 

time: 723 us -> 687 us (0.950)
  local copies, waits for them, and re-layouts: 118 us -> 56.2 us
  Pallas kernels: 222 us -> 249 us
  waiting for transfers between devices: 199 us -> 217 us
  other arithmetic: 48.5 us -> 34 us
    unnamed x420 -> x282, local copies, waits for them, and re-layouts: 94.2 us -> 46.7 us
    pallas_call x2 -> x4, Pallas kernels: 8 us -> 20.3 us  [the longest x2 10.9 us: lamb(): pl.pallas_call(functools.partial(lamb_kernel, kinds=kinds, shards=len(mad...]
    pallas_call x2, Pallas kernels: 11.1 us -> 20 us  [proj_bwd(): pl.pallas_call(proj_bwd_kernel, grid=(4,), in_specs=[pl.BlockSpec((1, wid...]
    ppermute x22 -> x24, starting transfers between devices: 15.8 us -> 8.08 us  [over_section(): return lax.ppermute(v, 'section', [(0, 1), (1, 0)])]
    pallas_call x2, Pallas kernels: 4.09 us -> 11.5 us  [mix_fwd(): pl.pallas_call(functools.partial(mix_fwd_kernel, width=width), grid=(1,),...]
    ppermute x22 -> x26, starting transfers between devices: 50.3 us -> 57.1 us  [over_both(): return lax.ppermute(v, BOTH, pairs)]
    ppermute x22 -> x24, waiting for transfers between devices: 9.52 us -> 16.3 us  [over_section(): return lax.ppermute(v, 'section', [(0, 1), (1, 0)])]
    ppermute x22 -> x26, waiting for transfers between devices: 16.9 us -> 21.5 us  [over_both(): return lax.ppermute(v, BOTH, pairs)]
  transfers between devices with their start and end apart: 78 -> 84, of which waited for: 21 -> 34; matrix products, arithmetic and copies ran while one was open for 11% -> 6% of each run, Pallas kernels for 29% -> 32%
where the time goes in v3:
time: 687 us; the launch traced here: 676 us
  Pallas kernels  249 us (36%)
  waiting for transfers between devices  217 us (32%)
  starting transfers between devices  103 us (15%)
  local copies, waits for them, and re-layouts  56.2 us (8%)
  other arithmetic  34 us (5%)
  between operations  16.2 us (2%)
    ppermute x21, waiting for transfers between devices, over_x(): return lax.ppermute(v, 'tensor', [(0, 1), (1, 0), (2, 3), (3, 2)])  140 us
    pallas_call x2, Pallas kernels, attn_bwd(): pl.pallas_call(functools.partial(attn_bwd_kernel, heads=heads), grid=(len...  62.5 us
    ppermute x26, starting transfers between devices, over_both(): return lax.ppermute(v, BOTH, pairs)  57.1 us
    unnamed x282, local copies, waits for them, and re-layouts  46.7 us
    pallas_call x2, Pallas kernels, attn_fwd(): pl.pallas_call(functools.partial(attn_fwd_kernel, heads=heads), grid=(len...  35 us
    pallas_call x4, Pallas kernels, ffn_bwd(): pl.pallas_call(ffn_bwd_kernel, grid=(2, tiles), in_specs=[whole, acts, ac...  31.6 us
    ppermute x21, starting transfers between devices, over_x(): return lax.ppermute(v, 'tensor', [(0, 1), (1, 0), (2, 3), (3, 2)])  27.8 us
    pallas_call x4, Pallas kernels, ffn_grads(): pl.pallas_call(functools.partial(ffn_grads_kernel, slot=slot), grid=(hidd...  26.8 us
  transfers between devices with their start and end apart: 84, of which 34 were waited for; matrix products, arithmetic and copies ran while one was open for 6% of the time, Pallas kernels for 32%

profile of v3, /device:TPU:0, one launch (start us, length us, event | category | flops | bytes accessed | tf_op | source)
XLA Modules:
  0.0 676.1 jit_solution(10233903962236946178)
XLA Ops:
  12.5 3.7 collective-permute-start.6
  16.3 3.8 collective-permute-start.7
  21.1 4.6 collective-permute-done.7
  29.3 8.8 %collective-permute-start.4 = (bf16[3,192,768]{2,1,0:T(8,128)(2,1)S(1)}, bf16[3,192,768]{2,1,0:T(8,128)(2,1)S(1)}, u32[]{:S(2)}, u32[]{:S(2)}) collective-permute-start(bf16[3,192,768]{2,1,0:T(8,128)(2,1)S(1)} %pad_maximum_fusion.2), channel_id=1, source_target_pairs={{0,2},{1,3},{2,18},{3,19},{4,6},{5,7},{6,22},{7,23},{8,10},{9,11},... | collective-permute-start | bytes 2654216 | tf_op jit(solution)/shard_map/ppermute | solution.py:729
  40.2 14.0 %collective-permute-done.2.slab2 = bf16[512,768]{1,0:T(8,128)(2,1)S(1)} collective-permute-done((bf16[512,768]{1,0:T(8,128)(2,1)S(1)}, bf16[512,768]{1,0:T(8,128)(2,1)S(1)}, u32[]{:S(2)}, u32[]{:S(2)}) %collective-permute-start.2) | collective-permute-done | bytes 786464 | tf_op jit(solution)/shard_map/ppermute | solution.py:717
  58.1 2.7 all-gather.5.cloned.1.call-done.matrix
  65.8 17.3 %attn_fwd.2 = (bf16[192,512]{1,0:T(8,128)(2,1)S(1)}, bf16[192,512]{1,0:T(8,128)(2,1)S(1)}, bf16[192,512]{1,0:T(8,128)(2,1)S(1)}, bf16[192,512]{1,0:T(8,128)(2,1)...) custom-call(s32[4]{0:T(128)S(1)} %pad_add_fusion.place, s32[2]{0:T(128)S(1)} %pad_add_fusion.1.ends, ...), custom_call_target="tpu_custom_call" | custom-call | flops 4831838208 | bytes 6291456 | tf_op jit(solution)/shard_map/attn_fwd/pallas_call | solution.py:150
  87.0 5.4 collective-permute-done.9.head2
  92.4 2.9 collective-permute-done.10.head3
  96.1 5.8 mix_fwd.2
  107.9 14.7 %collective-permute-done.15.rows_ref.h1 = bf16[512,768]{1,0:T(8,128)(2,1)S(1)} collective-permute-done((bf16[512,768]{1,0:T(8,128)(2,1)}, bf16[512,768]{1,0:T(8,128)(2,1)S(1)}, u32[]{:S(2)}, u32[]{:S(2)}) %collective-permute-start.15) | collective-permute-done | bytes 786464 | tf_op jit(solution)/shard_map/ppermute | solution.py:717
  122.6 9.5 %all-gather.7.cloned.1.call-done.first = bf16[3,768,768]{2,1,0:T(8,128)(2,1)} async-done(((bf16[3,192,768]{2,1,0:T(8,128)(2,1)}), bf16[3,768,768]{2,1,0:T(8,128)(2,1)}) %all-gather.7.cloned.1.call-update) | async-done | bytes 3538960 | tf_op jit(solution)/shard_map/all_gather | solution.py:741
  140.6 6.6 ffn_fwd.5
  150.4 6.5 ffn_fwd.4
  157.0 10.9 %collective-permute-done.17 = bf16[512,768]{1,0:T(8,128)(2,1)S(1)} collective-permute-done((bf16[512,768]{1,0:T(8,128)(2,1)S(1)}, bf16[512,768]{1,0:T(8,128)(2,1)S(1)}, u32[]{:S(2)}, u32[]{:S(2)}) %collective-permute-start.17) | collective-permute-done | bytes 786464 | tf_op jit(solution)/shard_map/ppermute | solution.py:717
  171.6 17.4 %collective-permute-done.19.slab2 = bf16[512,768]{1,0:T(8,128)(2,1)S(1)} collective-permute-done((bf16[512,768]{1,0:T(8,128)(2,1)S(1)}, bf16[512,768]{1,0:T(8,128)(2,1)S(1)}, u32[]{:S(2)}, u32[]{:S(2)}) %collective-permute-start.19) | collective-permute-done | bytes 786464 | tf_op jit(solution)/shard_map/ppermute | solution.py:717
  193.8 17.7 %attn_fwd.3 = (bf16[192,512]{1,0:T(8,128)(2,1)S(1)}, bf16[192,512]{1,0:T(8,128)(2,1)S(1)}, bf16[192,512]{1,0:T(8,128)(2,1)S(1)}, bf16[192,512]{1,0:T(8,128)(2,1)...) custom-call(s32[4]{0:T(128)S(1)} %pad_add_fusion.place, s32[2]{0:T(128)S(1)} %pad_add_fusion.1.ends, ...), custom_call_target="tpu_custom_call" | custom-call | flops 4831838208 | bytes 6291456 | tf_op jit(solution)/shard_map/attn_fwd/pallas_call | solution.py:150
  214.9 5.7 collective-permute-done.24.head2
  223.9 5.7 mix_fwd.3
  229.5 10.3 %all-gather.11.cloned.1.call-done.first = bf16[3,768,768]{2,1,0:T(8,128)(2,1)} async-done(((bf16[3,192,768]{2,1,0:T(8,128)(2,1)}), bf16[3,768,768]{2,1,0:T(8,128)(2,1)}) %all-gather.11.cloned.1.call-update) | async-done | bytes 3538960 | tf_op jit(solution)/shard_map/all_gather | solution.py:741
  241.3 18.7 %collective-permute-done.30.rows_ref.h1 = bf16[512,768]{1,0:T(8,128)(2,1)S(1)} collective-permute-done((bf16[512,768]{1,0:T(8,128)(2,1)}, bf16[512,768]{1,0:T(8,128)(2,1)S(1)}, u32[]{:S(2)}, u32[]{:S(2)}) %collective-permute-start.30) | collective-permute-done | bytes 786464 | tf_op jit(solution)/shard_map/ppermute | solution.py:717
  262.0 4.4 ffn_fwd.7
  270.3 4.6 ffn_fwd.6
  275.0 10.7 %collective-permute-done.31 = bf16[512,768]{1,0:T(8,128)(2,1)S(1)} collective-permute-done((bf16[512,768]{1,0:T(8,128)(2,1)S(1)}, bf16[512,768]{1,0:T(8,128)(2,1)S(1)}, u32[]{:S(2)}, u32[]{:S(2)}) %collective-permute-start.31) | collective-permute-done | bytes 786464 | tf_op jit(solution)/shard_map/ppermute | solution.py:717
  288.3 3.2 broadcast_select_fusion.5
  291.6 4.0 top_bwd.2
  301.6 7.7 %ffn_bwd.4 = (f32[512,768]{1,0:T(8,128)S(1)}, bf16[2,512,768]{2,1,0:T(8,128)(2,1)S(1)}, bf16[2,512,768]{2,1,0:T(8,128)(2,1)S(1)}, bf16[2,512,768]{2,1,0:T(8,128)(2,1)S(1)}) custom-call(bf16[512,768]{1,0:T(8,128)(2,1)S(1)} %copy-done.29, bf16[2,512,768]{2,1,0:T(8,128)(2,1)S(1)} %copy-done.72, bf16[2,512,768]{2,1,0:T(8,128)(2,1)S(1)} %copy-done.74, ...), custom_call_target="tpu_custom_call" | custom-call | flops 3623878656 | bytes 14942208 | tf_op jit(solution)/shard_map/ffn_bwd/pallas_call | solution.py:362
  309.4 4.7 collective-permute-done.35.grad_ref.g1
  316.1 7.8 %ffn_bwd.5 = (bf16[512,768]{1,0:T(8,128)(2,1)S(1)}, bf16[2,512,768]{2,1,0:T(8,128)(2,1)S(1)}, bf16[2,512,768]{2,1,0:T(8,128)(2,1)S(1)}, bf16[2,512,768]{2,1,0:T(8,128)(2,1)S(1)}) custom-call(bf16[512,768]{1,0:T(8,128)(2,1)S(1)} %collective-permute-done.35.grad_ref.g1, bf16[2,512,768]{2,1,0:T(8,128)(2,1)S(1)} %copy-done.68, ...), custom_call_target="tpu_custom_call" | custom-call | flops 3623878656 | bytes 14942208 | tf_op jit(solution)/shard_map/ffn_bwd/pallas_call | solution.py:362
  323.9 5.7 ffn_grads.4
  331.1 4.9 collective-permute-done.47.rest_0_
  337.8 7.7 %ffn_grads.5 = bf16[3,768,768]{2,1,0:T(8,128)(2,1)} custom-call(bf16[512,768]{1,0:T(8,128)(2,1)S(1)} %copy-done.23, bf16[512,768]{1,0:T(8,128)(2,1)S(1)} %collective-permute-done.30.rows_ref.h1, bf16[512,768]{1,0:T(8,128)(2,1)S(1)} %copy-done.30, bf16[512,768]{1,0:T(8,128)(2,1)S(1)} %collective-permute-done.35.grad_ref.g1, ...), custom_call_target="tpu_custom_call" | custom-call | flops 3623878656 | bytes 8257536 | tf_op jit(solution)/shard_map/ffn_grads/pallas_call | solution.py:403
  345.5 4.0 collective-permute-done.36.far_part
  350.9 7.7 %mix_bwd.2 = (f32[512,768]{1,0:T(8,128)}, f32[2,768]{1,0:T(2,128)}, bf16[192,512]{1,0:T(8,128)(2,1)}, bf16[192,512]{1,0:T(8,128)(2,1)}, bf16[192,512]{1,0:T(8,12...) custom-call(f32[512,768]{1,0:T(8,128)} %get-tuple-element.198.grad_m, ...), custom_call_target="tpu_custom_call" | custom-call | flops 1207959552 | bytes 11010048 | tf_op jit(solution)/shard_map/mix_bwd/pallas_call | solution.py:535
  360.5 6.1 collective-permute-done.38.do2
  366.6 3.3 collective-permute-done.39.do3
  372.0 31.1 %attn_bwd.2.pair_grad.rest_grad = bf16[4,576,512]{2,1,0:T(8,128)(2,1)} custom-call(s32[4]{0:T(128)} %copy-done.36, s32[2]{0:T(128)} %copy-done.58, bf16[576,2048]{1,0:T(8,128)(2,1)} %get-tuple-element.210.qkv, bf16[192,512]{1,0:T(8,128)(2,1)} %get-tuple-element.215.do0, bf16[192,512]{1,0:T(8,128)(2,1)} %copy-done.136, bf16[192,512]{1,0:T(8,128)(2,1)} %copy-done.137, ...), custom_call_target="tpu_custom_call" | custom-call | flops 8053063680 | bytes 9437184 | tf_op jit(solution)/shard_map/attn_bwd/pallas_call | solution.py:257
  404.1 10.0 %proj_bwd.2 = (bf16[512,768]{1,0:T(8,128)(2,1)}, bf16[512,768]{1,0:T(8,128)(2,1)}, bf16[512,768]{1,0:T(8,128)(2,1)}, bf16[512,768]{1,0:T(8,128)(2,1)}, bf16[768,768]{1,0:T(8,128)(2,1)}) custom-call(bf16[4,576,512]{2,1,0:T(8,128)(2,1)} %attn_bwd.2.pair_grad.rest_grad, bf16[4,576,512]{2,1,0:T(8,128)(2,1)} %attn_bwd.2.pair_grad.rest_grad, ...), custom_call_target="tpu_custom_call" | custom-call | flops 3623878656 | bytes 9437184 | tf_op jit(solution)/shard_map/proj_bwd/pallas_call | solution.py:445
  420.4 3.6 collective-permute-start.49
  424.9 13.2 %collective-permute-done.45.refs_3_ = bf16[512,768]{1,0:T(8,128)(2,1)S(1)} collective-permute-done((bf16[512,768]{1,0:T(8,128)(2,1)S(1)}, bf16[512,768]{1,0:T(8,128)(2,1)S(1)}, u32[]{:S(2)}, u32[]{:S(2)}) %collective-permute-start.45) | collective-permute-done | bytes 786464 | tf_op jit(solution)/shard_map/ppermute | solution.py:717
  439.0 5.4 top_bwd.3
  450.3 7.7 %ffn_bwd.6 = (f32[512,768]{1,0:T(8,128)S(1)}, bf16[2,512,768]{2,1,0:T(8,128)(2,1)S(1)}, bf16[2,512,768]{2,1,0:T(8,128)(2,1)S(1)}, bf16[2,512,768]{2,1,0:T(8,128)(2,1)S(1)}) custom-call(bf16[512,768]{1,0:T(8,128)(2,1)S(1)} %copy-done.24, bf16[2,512,768]{2,1,0:T(8,128)(2,1)S(1)} %copy-done.64, bf16[2,512,768]{2,1,0:T(8,128)(2,1)S(1)} %copy-done.66, ...), custom_call_target="tpu_custom_call" | custom-call | flops 3623878656 | bytes 14942208 | tf_op jit(solution)/shard_map/ffn_bwd/pallas_call | solution.py:362
  459.2 4.4 collective-permute-done.46.grad_ref.g1
  463.7 8.4 %ffn_bwd.7 = (bf16[512,768]{1,0:T(8,128)(2,1)S(1)}, bf16[2,512,768]{2,1,0:T(8,128)(2,1)S(1)}, bf16[2,512,768]{2,1,0:T(8,128)(2,1)S(1)}, bf16[2,512,768]{2,1,0:T(8,128)(2,1)S(1)}) custom-call(bf16[512,768]{1,0:T(8,128)(2,1)S(1)} %collective-permute-done.46.grad_ref.g1, bf16[2,512,768]{2,1,0:T(8,128)(2,1)S(1)} %copy-done.60, ...), custom_call_target="tpu_custom_call" | custom-call | flops 3623878656 | bytes 14942208 | tf_op jit(solution)/shard_map/ffn_bwd/pallas_call | solution.py:362
  472.2 5.7 ffn_grads.6
  479.4 5.1 collective-permute-done.64.rest_0_
  496.1 7.7 %ffn_grads.7 = bf16[3,768,768]{2,1,0:T(8,128)(2,1)} custom-call(bf16[512,768]{1,0:T(8,128)(2,1)S(1)} %copy-done.19, bf16[512,768]{1,0:T(8,128)(2,1)S(1)} %copy-done.22, bf16[512,768]{1,0:T(8,128)(2,1)S(1)} %copy-done.26, bf16[512,768]{1,0:T(8,128)(2,1)S(1)} %copy-done.28, bf16[2,512,768]{2,1,0:T(8,128)(2,1)S(1)} %get-tuple-element.281.gate0, ...), custom_call_target="tpu_custom_call" | custom-call | flops 3623878656 | bytes 8257536 | tf_op jit(solution)/shard_map/ffn_grads/pallas_call | solution.py:403
  504.7 6.3 reduce-scatter.7.cloned.1.call-done
  513.8 7.6 %mix_bwd.3 = (f32[512,768]{1,0:T(8,128)}, f32[2,768]{1,0:T(2,128)}, bf16[192,512]{1,0:T(8,128)(2,1)}, bf16[192,512]{1,0:T(8,128)(2,1)}, bf16[192,512]{1,0:T(8,12...) custom-call(f32[512,768]{1,0:T(8,128)} %get-tuple-element.235.grad_m, ...), custom_call_target="tpu_custom_call" | custom-call | flops 1207959552 | bytes 11010048 | tf_op jit(solution)/shard_map/mix_bwd/pallas_call | solution.py:535
  525.0 6.5 collective-permute-done.52.do2
  531.5 2.5 collective-permute-done.53.do3
  536.4 31.4 %attn_bwd.3.pair_grad.rest_grad = bf16[4,576,512]{2,1,0:T(8,128)(2,1)} custom-call(s32[4]{0:T(128)} %copy-done.36, s32[2]{0:T(128)} %copy-done.58, bf16[576,2048]{1,0:T(8,128)(2,1)} %get-tuple-element.254.qkv, bf16[192,512]{1,0:T(8,128)(2,1)} %get-tuple-element.260.do0, bf16[192,512]{1,0:T(8,128)(2,1)} %copy-done.133, bf16[192,512]{1,0:T(8,128)(2,1)} %copy-done.134, ...), custom_call_target="tpu_custom_call" | custom-call | flops 8053063680 | bytes 9437184 | tf_op jit(solution)/shard_map/attn_bwd/pallas_call | solution.py:257
  568.8 10.0 %proj_bwd.3 = (bf16[512,768]{1,0:T(8,128)(2,1)}, bf16[512,768]{1,0:T(8,128)(2,1)}, bf16[512,768]{1,0:T(8,128)(2,1)}, bf16[512,768]{1,0:T(8,128)(2,1)}, bf16[768,768]{1,0:T(8,128)(2,1)}) custom-call(bf16[4,576,512]{2,1,0:T(8,128)(2,1)} %attn_bwd.3.pair_grad.rest_grad, bf16[4,576,512]{2,1,0:T(8,128)(2,1)} %attn_bwd.3.pair_grad.rest_grad, ...), custom_call_target="tpu_custom_call" | custom-call | flops 3623878656 | bytes 9437184 | tf_op jit(solution)/shard_map/proj_bwd/pallas_call | solution.py:445
  586.3 8.3 %collective-permute-start.65 = (bf16[3,192,768]{2,1,0:T(8,128)(2,1)}, bf16[3,192,768]{2,1,0:T(8,128)(2,1)}, u32[]{:S(2)}, u32[]{:S(2)}) collective-permute-start(bf16[3,192,768]{2,1,0:T(8,128)(2,1)} %reduce-scatter.11.cloned.1.call-done), channel_id=1, source_target_pairs={{0,0},{1,1},{16,2},{17,3},{4,4},{5,5},{20,6},{21,7},{8,8},{9,9},{2... | collective-permute-start | bytes 2654216 | tf_op jit(solution)/shard_map/ppermute | solution.py:729
  599.0 2.9 collective-permute-start.33
  601.9 3.3 collective-permute-done.61
  605.2 6.6 reduce-scatter.9.cloned.1.call-done
  617.2 6.9 %lamb.2 = (f32[2,192,768]{2,1,0:T(8,128)}, f32[2,192,768]{2,1,0:T(8,128)}, f32[2,192,768]{2,1,0:T(8,128)}, f32[192,768]{1,0:T(8,128)}, f32[192,768]{1,0:T(8,128)}, /*index=5*/f32[192,768]{1,0:T(8,128)}, f32[2,768]{1,0:T(2,128)}) custom-call(bf16[3,192,768]{2,1,0:T(8,128)(2,1)} %collective-permute-done.65.refs_0_, ...), custom_call_target="tpu_custom_call" | custom-call | flops 8847360 | bytes 12386304 | tf_op jit(solution)/shard_map/lamb/pallas_call | solution.py:633
  624.1 5.7 collective-permute-done.63.refs_1_
  630.5 4.0 lamb.3
  640.1 7.4 %collective-permute-start.67 = (bf16[512,768]{1,0:T(8,128)(2,1)}, bf16[512,768]{1,0:T(8,128)(2,1)}, u32[]{:S(2)}, u32[]{:S(2)}) collective-permute-start(bf16[512,768]{1,0:T(8,128)(2,1)} %get-tuple-element.334), channel_id=1, source_target_pairs={{0,0},{1,1},{2,16},{3,17},{16,2},{17,3},{18,18},{19,19},{4,4},{5,5... | collective-permute-start | bytes 2359304 | tf_op jit(solution)/shard_map/ppermute | solution.py:729
  647.7 6.8 collective-permute-start.74
  656.5 3.8 collective-permute-done.75
  661.0 4.3 finish.1
  (492 shorter events, 154.1 us)
Async XLA Ops:
  7.2 53.6 %all-gather.5.cloned.1.call-start = ((), (), s32[]{:S(2)}) async-start(), calls=%async_computation.4 | async-start | bytes 1474560 | tf_op jit(solution)/shard_map/all_gather | solution.py:741
  16.3 9.4 %collective-permute-start.7 = (bf16[192,768]{1,0:T(8,128)(2,1)}, bf16[192,768]{1,0:T(8,128)(2,1)}, u32[]{:S(2)}, u32[]{:S(2)}) collective-permute-start(bf16[192,768]{1,0:T(8,128)(2,1)} %pad_maximum_fusion.3), channel_id=1, source_target_pairs={{0,2},{1,3},{2,18},{3,19},{4,6},{5,7},{6,22},{7,23},{8,10},{9,11},... | collective-permute-start | bytes 884744 | tf_op jit(solution)/shard_map/ppermute | solution.py:729
  27.4 104.6 %all-gather.7.cloned.1.call-start = ((), (), s32[]{:S(2)}) async-start(), calls=%async_computation.5 | async-start | bytes 4423680 | tf_op jit(solution)/shard_map/all_gather | solution.py:741
  28.4 25.8 %collective-permute-start.3 = (bf16[3,192,768]{2,1,0:T(8,128)(2,1)S(1)}, bf16[3,192,768]{2,1,0:T(8,128)(2,1)S(1)}, u32[]{:S(2)}, u32[]{:S(2)}) collective-permute-start(bf16[3,192,768]{2,1,0:T(8,128)(2,1)S(1)} %pad_maximum_fusion.2), channel_id=1, source_target_pairs={{0,0},{1,1},{2,16},{3,17},{4,4},{5,5},{6,20},{7,21},{8,8},{9,9},{1... | collective-permute-start | bytes 2654216 | tf_op jit(solution)/shard_map/ppermute | solution.py:729
  29.3 25.0 %collective-permute-start.4 = (bf16[3,192,768]{2,1,0:T(8,128)(2,1)S(1)}, bf16[3,192,768]{2,1,0:T(8,128)(2,1)S(1)}, u32[]{:S(2)}, u32[]{:S(2)}) collective-permute-start(bf16[3,192,768]{2,1,0:T(8,128)(2,1)S(1)} %pad_maximum_fusion.2), channel_id=1, source_target_pairs={{0,2},{1,3},{2,18},{3,19},{4,6},{5,7},{6,22},{7,23},{8,10},{9,11},... | collective-permute-start | bytes 2654216 | tf_op jit(solution)/shard_map/ppermute | solution.py:729
  38.1 16.2 %collective-permute-start.2 = (bf16[512,768]{1,0:T(8,128)(2,1)S(1)}, bf16[512,768]{1,0:T(8,128)(2,1)S(1)}, u32[]{:S(2)}, u32[]{:S(2)}) collective-permute-start(bf16[512,768]{1,0:T(8,128)(2,1)S(1)} %collective-permute-done.slab0.rows), channel_id=1, source_target_pairs={{0,1},{1,0},{2,3},{3,2},{4,5},{5,4},{6,7},{7,6},{8,9},{9,8},{10,11... | collective-permute-start | bytes 2359304 | tf_op jit(solution)/shard_map/ppermute | solution.py:717
  55.4 133.6 %all-gather.9.cloned.1.call-start = ((), (), s32[]{:S(2)}) async-start(), calls=%async_computation.6 | async-start | bytes 1474560 | tf_op jit(solution)/shard_map/all_gather | solution.py:741
  55.4 8.8 %collective-permute-start.1 = (bf16[512,768]{1,0:T(8,128)(2,1)S(1)}, bf16[512,768]{1,0:T(8,128)(2,1)S(1)}, u32[]{:S(2)}, u32[]{:S(2)}) collective-permute-start(bf16[512,768]{1,0:T(8,128)(2,1)S(1)} %collective-permute-done.slab0.rows), channel_id=1, source_target_pairs={{0,16},{16,0},{1,17},{17,1},{2,18},{18,2},{3,19},{19,3},{4,20},{20... | collective-permute-start | bytes 2359304 | tf_op jit(solution)/shard_map/ppermute | solution.py:713
  55.5 8.7 %collective-permute-start.5 = (bf16[512,768]{1,0:T(8,128)(2,1)S(1)}, bf16[512,768]{1,0:T(8,128)(2,1)}, u32[]{:S(2)}, u32[]{:S(2)}) collective-permute-start(bf16[512,768]{1,0:T(8,128)(2,1)S(1)} %collective-permute-done.2.slab2), channel_id=1, source_target_pairs={{0,16},{16,0},{1,17},{17,1},{2,18},{18,2},{3,19},{19,3},{4,20},{20... | collective-permute-start | bytes 2359304 | tf_op jit(solution)/shard_map/ppermute | solution.py:713
  62.7 24.2 %collective-permute-start.11 = (bf16[768,192]{1,0:T(8,128)(2,1)}, bf16[768,192]{1,0:T(8,128)(2,1)}, u32[]{:S(2)}, u32[]{:S(2)}) collective-permute-start(bf16[768,192]{1,0:T(8,128)(2,1)} %slice.76), channel_id=1, source_target_pairs={{0,16},{16,0},{1,17},{17,1},{2,18},{18,2},{3,19},{19,3},{4,20},{20... | collective-permute-start | bytes 884744 | tf_op jit(solution)/shard_map/ppermute | solution.py:713
  62.7 21.0 %collective-permute-start.12 = (bf16[768,192]{1,0:T(8,128)(2,1)}, bf16[768,192]{1,0:T(8,128)(2,1)}, u32[]{:S(2)}, u32[]{:S(2)}) collective-permute-start(bf16[768,192]{1,0:T(8,128)(2,1)} %slice.76), channel_id=1, source_target_pairs={{0,1},{1,0},{2,3},{3,2},{4,5},{5,4},{6,7},{7,6},{8,9},{9,8},{10,11... | collective-permute-start | bytes 884744 | tf_op jit(solution)/shard_map/ppermute | solution.py:717
  83.8 11.5 %collective-permute-start.13 = (bf16[768,192]{1,0:T(8,128)(2,1)}, bf16[768,192]{1,0:T(8,128)(2,1)S(1)}, u32[]{:S(2)}, u32[]{:S(2)}) collective-permute-start(bf16[768,192]{1,0:T(8,128)(2,1)} %collective-permute-done.12.out2), channel_id=1, source_target_pairs={{0,16},{16,0},{1,17},{17,1},{2,18},{18,2},{3,19},{19,3},{4,20},{20... | collective-permute-start | bytes 884744 | tf_op jit(solution)/shard_map/ppermute | solution.py:713
  85.6 9.7 %collective-permute-start.10 = (bf16[192,512]{1,0:T(8,128)(2,1)S(1)}, bf16[192,512]{1,0:T(8,128)(2,1)S(1)}, u32[]{:S(2)}, u32[]{:S(2)}) collective-permute-start(bf16[192,512]{1,0:T(8,128)(2,1)S(1)} %get-tuple-element.173.out3), channel_id=1, source_target_pairs={{0,17},{1,16},{2,19},{3,18},{16,1},{17,0},{18,3},{19,2},{4,21},{5,... | collective-permute-start | bytes 589832 | tf_op jit(solution)/shard_map/ppermute | solution.py:729
  101.9 20.6 %collective-permute-start.15 = (bf16[512,768]{1,0:T(8,128)(2,1)}, bf16[512,768]{1,0:T(8,128)(2,1)S(1)}, u32[]{:S(2)}, u32[]{:S(2)}) collective-permute-start(bf16[512,768]{1,0:T(8,128)(2,1)} %get-tuple-element.177.rows_ref.h0), channel_id=1, source_target_pairs={{0,1},{1,0},{2,3},{3,2},{4,5},{5,4},{6,7},{7,6},{8,9},{9,8},{10,11... | collective-permute-start | bytes 2359304 | tf_op jit(solution)/shard_map/ppermute | solution.py:717
  104.9 27.2 %collective-permute-start.21 = (bf16[4,192,768]{2,1,0:T(8,128)(2,1)}, bf16[4,192,768]{2,1,0:T(8,128)(2,1)S(1)}, u32[]{:S(2)}, u32[]{:S(2)}) collective-permute-start(bf16[4,192,768]{2,1,0:T(8,128)(2,1)} %pad_maximum_fusion.1), channel_id=1, source_target_pairs={{16,0},{17,1},{18,16},{19,17},{20,4},{21,5},{22,20},{23,21},{24,8}... | collective-permute-start | bytes 3538952 | tf_op jit(solution)/shard_map/ppermute | solution.py:729
  106.2 26.9 %collective-permute-start.22 = (bf16[4,192,768]{2,1,0:T(8,128)(2,1)}, bf16[4,192,768]{2,1,0:T(8,128)(2,1)}, u32[]{:S(2)}, u32[]{:S(2)}) collective-permute-start(bf16[4,192,768]{2,1,0:T(8,128)(2,1)} %pad_maximum_fusion.1), channel_id=1, source_target_pairs={{16,2},{17,3},{18,18},{19,19},{20,6},{21,7},{22,22},{23,23},{24,10... | collective-permute-start | bytes 3538952 | tf_op jit(solution)/shard_map/ppermute | solution.py:729
  135.2 104.6 %all-gather.11.cloned.1.call-start = ((), (), s32[]{:S(2)}) async-start(), calls=%async_computation.7 | async-start | bytes 4423680 | tf_op jit(solution)/shard_map/all_gather | solution.py:741
  136.3 283.4 %reduce-scatter.5.cloned.1.call-start = ((), (), s32[]{:S(2)}) async-start(), calls=%async_computation.8 | async-start | bytes 4423680 | tf_op jit(solution)/shard_map/reduce_scatter | solution.py:745
  148.4 19.6 %collective-permute-start.17 = (bf16[512,768]{1,0:T(8,128)(2,1)S(1)}, bf16[512,768]{1,0:T(8,128)(2,1)S(1)}, u32[]{:S(2)}, u32[]{:S(2)}) collective-permute-start(bf16[512,768]{1,0:T(8,128)(2,1)S(1)} %get-tuple-element.182), channel_id=1, source_target_pairs={{0,1},{1,0},{2,3},{3,2},{4,5},{5,4},{6,7},{7,6},{8,9},{9,8},{10,11... | collective-permute-start | bytes 2359304 | tf_op jit(solution)/shard_map/ppermute | solution.py:717
  170.1 18.9 %collective-permute-start.19 = (bf16[512,768]{1,0:T(8,128)(2,1)S(1)}, bf16[512,768]{1,0:T(8,128)(2,1)S(1)}, u32[]{:S(2)}, u32[]{:S(2)}) collective-permute-start(bf16[512,768]{1,0:T(8,128)(2,1)S(1)} %get-tuple-element.328.slab0.rows), channel_id=1, source_target_pairs={{0,1},{1,0},{2,3},{3,2},{4,5},{5,4},{6,7},{7,6},{8,9},{9,8},{10,11... | collective-permute-start | bytes 2359304 | tf_op jit(solution)/shard_map/ppermute | solution.py:717
  171.6 20.6 %collective-permute-start.18 = (bf16[512,768]{1,0:T(8,128)(2,1)S(1)}, bf16[512,768]{1,0:T(8,128)(2,1)S(1)}, u32[]{:S(2)}, u32[]{:S(2)}) collective-permute-start(bf16[512,768]{1,0:T(8,128)(2,1)S(1)} %get-tuple-element.328.slab0.rows), channel_id=1, source_target_pairs={{0,16},{16,0},{1,17},{17,1},{2,18},{18,2},{3,19},{19,3},{4,20},{20... | collective-permute-start | bytes 2359304 | tf_op jit(solution)/shard_map/ppermute | solution.py:713
  190.4 24.4 %collective-permute-start.26 = (bf16[768,192]{1,0:T(8,128)(2,1)S(1)}, bf16[768,192]{1,0:T(8,128)(2,1)S(1)}, u32[]{:S(2)}, u32[]{:S(2)}) collective-permute-start(bf16[768,192]{1,0:T(8,128)(2,1)S(1)} %slice.81), channel_id=1, source_target_pairs={{0,16},{16,0},{1,17},{17,1},{2,18},{18,2},{3,19},{19,3},{4,20},{20... | collective-permute-start | bytes 884744 | tf_op jit(solution)/shard_map/ppermute | solution.py:713
  190.7 21.5 %collective-permute-start.27 = (bf16[768,192]{1,0:T(8,128)(2,1)S(1)}, bf16[768,192]{1,0:T(8,128)(2,1)S(1)}, u32[]{:S(2)}, u32[]{:S(2)}) collective-permute-start(bf16[768,192]{1,0:T(8,128)(2,1)S(1)} %slice.81), channel_id=1, source_target_pairs={{0,1},{1,0},{2,3},{3,2},{4,5},{5,4},{6,7},{7,6},{8,9},{9,8},{10,11... | collective-permute-start | bytes 884744 | tf_op jit(solution)/shard_map/ppermute | solution.py:717
  212.2 10.8 %collective-permute-start.28 = (bf16[768,192]{1,0:T(8,128)(2,1)S(1)}, bf16[768,192]{1,0:T(8,128)(2,1)S(1)}, u32[]{:S(2)}, u32[]{:S(2)}) collective-permute-start(bf16[768,192]{1,0:T(8,128)(2,1)S(1)} %collective-permute-done.27.out2), channel_id=1, source_target_pairs={{0,16},{16,0},{1,17},{17,1},{2,18},{18,2},{3,19},{19,3},{4,20},{20... | collective-permute-start | bytes 884744 | tf_op jit(solution)/shard_map/ppermute | solution.py:713
  213.4 9.7 %collective-permute-start.25 = (bf16[192,512]{1,0:T(8,128)(2,1)S(1)}, bf16[192,512]{1,0:T(8,128)(2,1)S(1)}, u32[]{:S(2)}, u32[]{:S(2)}) collective-permute-start(bf16[192,512]{1,0:T(8,128)(2,1)S(1)} %get-tuple-element.188.out3), channel_id=1, source_target_pairs={{0,17},{1,16},{2,19},{3,18},{16,1},{17,0},{18,3},{19,2},{4,21},{5,... | collective-permute-start | bytes 589832 | tf_op jit(solution)/shard_map/ppermute | solution.py:729
  239.8 20.2 %collective-permute-start.29 = (bf16[3,768,768]{2,1,0:T(8,128)(2,1)}, bf16[3,768,768]{2,1,0:T(8,128)(2,1)S(1)}, u32[]{:S(2)}, u32[]{:S(2)}) collective-permute-start(bf16[3,768,768]{2,1,0:T(8,128)(2,1)} %all-gather.11.cloned.1.call-done.first), channel_id=1, source_target_pairs={{0,16},{16,0},{1,17},{17,1},{2,18},{18,2},{3,19},{19,3},{4,20},{20... | collective-permute-start | bytes 10616840 | tf_op jit(solution)/shard_map/ppermute | solution.py:713
  239.8 20.2 %collective-permute-start.30 = (bf16[512,768]{1,0:T(8,128)(2,1)}, bf16[512,768]{1,0:T(8,128)(2,1)S(1)}, u32[]{:S(2)}, u32[]{:S(2)}) collective-permute-start(bf16[512,768]{1,0:T(8,128)(2,1)} %get-tuple-element.192.rows_ref.h0), channel_id=1, source_target_pairs={{0,1},{1,0},{2,3},{3,2},{4,5},{5,4},{6,7},{7,6},{8,9},{9,8},{10,11... | collective-permute-start | bytes 2359304 | tf_op jit(solution)/shard_map/ppermute | solution.py:717
  266.4 19.2 %collective-permute-start.31 = (bf16[512,768]{1,0:T(8,128)(2,1)S(1)}, bf16[512,768]{1,0:T(8,128)(2,1)S(1)}, u32[]{:S(2)}, u32[]{:S(2)}) collective-permute-start(bf16[512,768]{1,0:T(8,128)(2,1)S(1)} %get-tuple-element.196), channel_id=1, source_target_pairs={{0,1},{1,0},{2,3},{3,2},{4,5},{5,4},{6,7},{7,6},{8,9},{9,8},{10,11... | collective-permute-start | bytes 2359304 | tf_op jit(solution)/shard_map/ppermute | solution.py:717
  268.6 22.9 %collective-permute-start.34 = (bf16[512,768]{1,0:T(8,128)(2,1)S(1)}, bf16[512,768]{1,0:T(8,128)(2,1)}, u32[]{:S(2)}, u32[]{:S(2)}) collective-permute-start(bf16[512,768]{1,0:T(8,128)(2,1)S(1)} %dynamic-slice_bitcast_fusion), channel_id=1, source_target_pairs={{0,0},{1,1},{2,16},{3,17},{16,2},{17,3},{18,18},{19,19},{4,4},{5,5... | collective-permute-start | bytes 2359304 | tf_op jit(solution)/shard_map/ppermute | solution.py:729
  295.6 18.5 %collective-permute-start.35 = (bf16[512,768]{1,0:T(8,128)(2,1)}, bf16[512,768]{1,0:T(8,128)(2,1)S(1)}, u32[]{:S(2)}, u32[]{:S(2)}) collective-permute-start(bf16[512,768]{1,0:T(8,128)(2,1)} %get-tuple-element.199.grad_ref.g0), channel_id=1, source_target_pairs={{0,1},{1,0},{2,3},{3,2},{4,5},{5,4},{6,7},{7,6},{8,9},{9,8},{10,11... | collective-permute-start | bytes 2359304 | tf_op jit(solution)/shard_map/ppermute | solution.py:717
  329.6 20.0 %collective-permute-start.36 = (bf16[512,768]{1,0:T(8,128)(2,1)S(1)}, bf16[512,768]{1,0:T(8,128)(2,1)S(1)}, u32[]{:S(2)}, u32[]{:S(2)}) collective-permute-start(bf16[512,768]{1,0:T(8,128)(2,1)S(1)} %get-tuple-element.206), channel_id=1, source_target_pairs={{0,1},{1,0},{2,3},{3,2},{4,5},{5,4},{6,7},{7,6},{8,9},{9,8},{10,11... | collective-permute-start | bytes 2359304 | tf_op jit(solution)/shard_map/ppermute | solution.py:717
  350.5 160.5 %reduce-scatter.7.cloned.1.call-start = ((), (), s32[]{:S(2)}) async-start(), calls=%async_computation.9 | async-start | bytes 1474560 | tf_op jit(solution)/shard_map/reduce_scatter | solution.py:745
  360.0 9.9 %collective-permute-start.39 = (bf16[192,512]{1,0:T(8,128)(2,1)}, bf16[192,512]{1,0:T(8,128)(2,1)S(1)}, u32[]{:S(2)}, u32[]{:S(2)}) collective-permute-start(bf16[192,512]{1,0:T(8,128)(2,1)} %get-tuple-element.214), channel_id=1, source_target_pairs={{0,17},{1,16},{2,19},{3,18},{16,1},{17,0},{18,3},{19,2},{4,21},{5,... | collective-permute-start | bytes 589832 | tf_op jit(solution)/shard_map/ppermute | solution.py:729
  369.9 33.2 %collective-permute-start.40 = (bf16[192,768]{1,0:T(8,128)(2,1)}, bf16[192,768]{1,0:T(8,128)(2,1)S(1)}, u32[]{:S(2)}, u32[]{:S(2)}) collective-permute-start(bf16[192,768]{1,0:T(8,128)(2,1)} %get-tuple-element.224), channel_id=1, source_target_pairs={{0,16},{16,0},{1,17},{17,1},{2,18},{18,2},{3,19},{19,3},{4,20},{20... | collective-permute-start | bytes 884744 | tf_op jit(solution)/shard_map/ppermute | solution.py:713
  370.6 32.5 %collective-permute-start.41 = (bf16[192,768]{1,0:T(8,128)(2,1)}, bf16[192,768]{1,0:T(8,128)(2,1)S(1)}, u32[]{:S(2)}, u32[]{:S(2)}) collective-permute-start(bf16[192,768]{1,0:T(8,128)(2,1)} %get-tuple-element.225), channel_id=1, source_target_pairs={{0,1},{1,0},{2,3},{3,2},{4,5},{5,4},{6,7},{7,6},{8,9},{9,8},{10,11... | collective-permute-start | bytes 884744 | tf_op jit(solution)/shard_map/ppermute | solution.py:717
  371.9 31.2 %collective-permute-start.42 = (bf16[192,768]{1,0:T(8,128)(2,1)}, bf16[192,768]{1,0:T(8,128)(2,1)S(1)}, u32[]{:S(2)}, u32[]{:S(2)}) collective-permute-start(bf16[192,768]{1,0:T(8,128)(2,1)} %get-tuple-element.226), channel_id=1, source_target_pairs={{0,17},{1,16},{2,19},{3,18},{16,1},{17,0},{18,3},{19,2},{4,21},{5,... | collective-permute-start | bytes 884744 | tf_op jit(solution)/shard_map/ppermute | solution.py:729
  414.8 10.1 %collective-permute-start.43 = (bf16[512,768]{1,0:T(8,128)(2,1)}, bf16[512,768]{1,0:T(8,128)(2,1)S(1)}, u32[]{:S(2)}, u32[]{:S(2)}) collective-permute-start(bf16[512,768]{1,0:T(8,128)(2,1)} %get-tuple-element.232), channel_id=1, source_target_pairs={{0,16},{16,0},{1,17},{17,1},{2,18},{18,2},{3,19},{19,3},{4,20},{20... | collective-permute-start | bytes 2359304 | tf_op jit(solution)/shard_map/ppermute | solution.py:713
  418.2 19.9 %collective-permute-start.45 = (bf16[512,768]{1,0:T(8,128)(2,1)S(1)}, bf16[512,768]{1,0:T(8,128)(2,1)S(1)}, u32[]{:S(2)}, u32[]{:S(2)}) collective-permute-start(bf16[512,768]{1,0:T(8,128)(2,1)S(1)} %add_convert_fusion.2), channel_id=1, source_target_pairs={{0,1},{1,0},{2,3},{3,2},{4,5},{5,4},{6,7},{7,6},{8,9},{9,8},{10,11... | collective-permute-start | bytes 2359304 | tf_op jit(solution)/shard_map/ppermute | solution.py:717
  419.6 44.0 %collective-permute-start.48 = (bf16[3,192,768]{2,1,0:T(8,128)(2,1)}, bf16[3,192,768]{2,1,0:T(8,128)(2,1)S(1)}, u32[]{:S(2)}, u32[]{:S(2)}) collective-permute-start(bf16[3,192,768]{2,1,0:T(8,128)(2,1)} %reduce-scatter.5.cloned.1.call-done), channel_id=1, source_target_pairs={{2,16},{3,17},{18,18},{19,19},{6,20},{7,21},{22,22},{23,23},{10,24... | collective-permute-start | bytes 2654216 | tf_op jit(solution)/shard_map/ppermute | solution.py:729
  420.4 43.2 %collective-permute-start.49 = (bf16[3,192,768]{2,1,0:T(8,128)(2,1)}, bf16[3,192,768]{2,1,0:T(8,128)(2,1)}, u32[]{:S(2)}, u32[]{:S(2)}) collective-permute-start(bf16[3,192,768]{2,1,0:T(8,128)(2,1)} %reduce-scatter.5.cloned.1.call-done), channel_id=1, source_target_pairs={{0,16},{1,17},{16,18},{17,19},{4,20},{5,21},{20,22},{21,23},{8,24}... | collective-permute-start | bytes 2654216 | tf_op jit(solution)/shard_map/ppermute | solution.py:729
  444.4 19.2 %collective-permute-start.46 = (bf16[512,768]{1,0:T(8,128)(2,1)}, bf16[512,768]{1,0:T(8,128)(2,1)S(1)}, u32[]{:S(2)}, u32[]{:S(2)}) collective-permute-start(bf16[512,768]{1,0:T(8,128)(2,1)} %get-tuple-element.236.grad_ref.g0), channel_id=1, source_target_pairs={{0,1},{1,0},{2,3},{3,2},{4,5},{5,4},{6,7},{7,6},{8,9},{9,8},{10,11... | collective-permute-start | bytes 2359304 | tf_op jit(solution)/shard_map/ppermute | solution.py:717
  477.9 108.4 %reduce-scatter.11.cloned.1.call-start = ((), (), s32[]{:S(2)}) async-start(), calls=%async_computation.11 | async-start | bytes 4423680 | tf_op jit(solution)/shard_map/reduce_scatter | solution.py:745
  478.0 25.8 %collective-permute-start.50 = (bf16[512,768]{1,0:T(8,128)(2,1)S(1)}, bf16[512,768]{1,0:T(8,128)(2,1)S(1)}, u32[]{:S(2)}, u32[]{:S(2)}) collective-permute-start(bf16[512,768]{1,0:T(8,128)(2,1)S(1)} %get-tuple-element.250), channel_id=1, source_target_pairs={{0,1},{1,0},{2,3},{3,2},{4,5},{5,4},{6,7},{7,6},{8,9},{9,8},{10,11... | collective-permute-start | bytes 2359304 | tf_op jit(solution)/shard_map/ppermute | solution.py:717
  504.7 107.1 %reduce-scatter.9.cloned.1.call-start = ((), (), s32[]{:S(2)}) async-start(), calls=%async_computation.10 | async-start | bytes 1474560 | tf_op jit(solution)/shard_map/reduce_scatter | solution.py:745
  510.9 14.0 %collective-permute-start.54 = (bf16[1,192,768]{2,1,0:T(8,128)(2,1)}, bf16[1,192,768]{2,1,0:T(8,128)(2,1)S(1)}, u32[]{:S(2)}, u32[]{:S(2)}) collective-permute-start(bf16[1,192,768]{2,1,0:T(8,128)(2,1)} %bitcast.149), channel_id=1, source_target_pairs={{2,16},{3,17},{18,18},{19,19},{6,20},{7,21},{22,22},{23,23},{10,24... | collective-permute-start | bytes 884744 | tf_op jit(solution)/shard_map/ppermute | solution.py:729
  511.6 13.3 %collective-permute-start.55 = (bf16[1,192,768]{2,1,0:T(8,128)(2,1)}, bf16[1,192,768]{2,1,0:T(8,128)(2,1)S(1)}, u32[]{:S(2)}, u32[]{:S(2)}) collective-permute-start(bf16[1,192,768]{2,1,0:T(8,128)(2,1)} %bitcast.150), channel_id=1, source_target_pairs={{0,16},{1,17},{16,18},{17,19},{4,20},{5,21},{20,22},{21,23},{8,24}... | collective-permute-start | bytes 884744 | tf_op jit(solution)/shard_map/ppermute | solution.py:729
  524.8 9.2 %collective-permute-start.53 = (bf16[192,512]{1,0:T(8,128)(2,1)}, bf16[192,512]{1,0:T(8,128)(2,1)S(1)}, u32[]{:S(2)}, u32[]{:S(2)}) collective-permute-start(bf16[192,512]{1,0:T(8,128)(2,1)} %get-tuple-element.258), channel_id=1, source_target_pairs={{0,17},{1,16},{2,19},{3,18},{16,1},{17,0},{18,3},{19,2},{4,21},{5,... | collective-permute-start | bytes 589832 | tf_op jit(solution)/shard_map/ppermute | solution.py:729
  533.9 33.8 %collective-permute-start.56 = (bf16[192,768]{1,0:T(8,128)(2,1)}, bf16[192,768]{1,0:T(8,128)(2,1)S(1)}, u32[]{:S(2)}, u32[]{:S(2)}) collective-permute-start(bf16[192,768]{1,0:T(8,128)(2,1)} %get-tuple-element.269), channel_id=1, source_target_pairs={{0,16},{16,0},{1,17},{17,1},{2,18},{18,2},{3,19},{19,3},{4,20},{20... | collective-permute-start | bytes 884744 | tf_op jit(solution)/shard_map/ppermute | solution.py:713
  535.0 32.8 %collective-permute-start.57 = (bf16[192,768]{1,0:T(8,128)(2,1)}, bf16[192,768]{1,0:T(8,128)(2,1)S(1)}, u32[]{:S(2)}, u32[]{:S(2)}) collective-permute-start(bf16[192,768]{1,0:T(8,128)(2,1)} %get-tuple-element.270), channel_id=1, source_target_pairs={{0,1},{1,0},{2,3},{3,2},{4,5},{5,4},{6,7},{7,6},{8,9},{9,8},{10,11... | collective-permute-start | bytes 884744 | tf_op jit(solution)/shard_map/ppermute | solution.py:717
  536.3 31.5 %collective-permute-start.58 = (bf16[192,768]{1,0:T(8,128)(2,1)}, bf16[192,768]{1,0:T(8,128)(2,1)S(1)}, u32[]{:S(2)}, u32[]{:S(2)}) collective-permute-start(bf16[192,768]{1,0:T(8,128)(2,1)} %get-tuple-element.271), channel_id=1, source_target_pairs={{0,17},{1,16},{2,19},{3,18},{16,1},{17,0},{18,3},{19,2},{4,21},{5,... | collective-permute-start | bytes 884744 | tf_op jit(solution)/shard_map/ppermute | solution.py:729
  581.0 18.0 %collective-permute-start.59 = (bf16[512,768]{1,0:T(8,128)(2,1)}, bf16[512,768]{1,0:T(8,128)(2,1)}, u32[]{:S(2)}, u32[]{:S(2)}) collective-permute-start(bf16[512,768]{1,0:T(8,128)(2,1)} %get-tuple-element.277), channel_id=1, source_target_pairs={{0,16},{16,0},{1,17},{17,1},{2,18},{18,2},{3,19},{19,3},{4,20},{20... | collective-permute-start | bytes 2359304 | tf_op jit(solution)/shard_map/ppermute | solution.py:713
  585.0 20.1 %collective-permute-start.61 = (bf16[512,768]{1,0:T(8,128)(2,1)}, bf16[512,768]{1,0:T(8,128)(2,1)}, u32[]{:S(2)}, u32[]{:S(2)}) collective-permute-start(bf16[512,768]{1,0:T(8,128)(2,1)} %add_convert_fusion.1), channel_id=1, source_target_pairs={{0,1},{1,0},{2,3},{3,2},{4,5},{5,4},{6,7},{7,6},{8,9},{9,8},{10,11... | collective-permute-start | bytes 2359304 | tf_op jit(solution)/shard_map/ppermute | solution.py:717
  586.3 27.1 %collective-permute-start.65 = (bf16[3,192,768]{2,1,0:T(8,128)(2,1)}, bf16[3,192,768]{2,1,0:T(8,128)(2,1)}, u32[]{:S(2)}, u32[]{:S(2)}) collective-permute-start(bf16[3,192,768]{2,1,0:T(8,128)(2,1)} %reduce-scatter.11.cloned.1.call-done), channel_id=1, source_target_pairs={{0,0},{1,1},{16,2},{17,3},{4,4},{5,5},{20,6},{21,7},{8,8},{9,9},{2... | collective-permute-start | bytes 2654216 | tf_op jit(solution)/shard_map/ppermute | solution.py:729
  594.6 22.6 %collective-permute-start.66 = (bf16[3,192,768]{2,1,0:T(8,128)(2,1)}, bf16[3,192,768]{2,1,0:T(8,128)(2,1)}, u32[]{:S(2)}, u32[]{:S(2)}) collective-permute-start(bf16[3,192,768]{2,1,0:T(8,128)(2,1)} %reduce-scatter.11.cloned.1.call-done), channel_id=1, source_target_pairs={{2,0},{3,1},{18,2},{19,3},{6,4},{7,5},{22,6},{23,7},{10,8},{11,9},... | collective-permute-start | bytes 2654216 | tf_op jit(solution)/shard_map/ppermute | solution.py:729
  597.2 42.9 %collective-permute-start.32 = (bf16[512,768]{1,0:T(8,128)(2,1)}, bf16[512,768]{1,0:T(8,128)(2,1)S(1)}, u32[]{:S(2)}, u32[]{:S(2)}) collective-permute-start(bf16[512,768]{1,0:T(8,128)(2,1)} %get-tuple-element.324), channel_id=1, source_target_pairs={{0,0},{1,1},{2,16},{3,17},{16,2},{17,3},{18,18},{19,19},{4,4},{5,5... | collective-permute-start | bytes 2359304 | tf_op jit(solution)/shard_map/ppermute | solution.py:729
  599.0 48.6 %collective-permute-start.33 = (bf16[512,768]{1,0:T(8,128)(2,1)}, bf16[512,768]{1,0:T(8,128)(2,1)S(1)}, u32[]{:S(2)}, u32[]{:S(2)}) collective-permute-start(bf16[512,768]{1,0:T(8,128)(2,1)} %broadcast_select_fusion.4), channel_id=1, source_target_pairs={{0,16},{1,17},{2,0},{3,1},{16,18},{17,19},{18,2},{19,3},{4,20},{5,... | collective-permute-start | bytes 2359304 | tf_op jit(solution)/shard_map/ppermute | solution.py:729
  611.8 12.3 %collective-permute-start.62 = (bf16[1,192,768]{2,1,0:T(8,128)(2,1)}, bf16[1,192,768]{2,1,0:T(8,128)(2,1)S(1)}, u32[]{:S(2)}, u32[]{:S(2)}) collective-permute-start(bf16[1,192,768]{2,1,0:T(8,128)(2,1)} %bitcast.147), channel_id=1, source_target_pairs={{0,0},{1,1},{16,2},{17,3},{4,4},{5,5},{20,6},{21,7},{8,8},{9,9},{2... | collective-permute-start | bytes 884744 | tf_op jit(solution)/shard_map/ppermute | solution.py:729
  613.4 16.4 %collective-permute-start.63 = (bf16[1,192,768]{2,1,0:T(8,128)(2,1)}, bf16[1,192,768]{2,1,0:T(8,128)(2,1)S(1)}, u32[]{:S(2)}, u32[]{:S(2)}) collective-permute-start(bf16[1,192,768]{2,1,0:T(8,128)(2,1)} %bitcast.148), channel_id=1, source_target_pairs={{2,0},{3,1},{18,2},{19,3},{6,4},{7,5},{22,6},{23,7},{10,8},{11,9},... | collective-permute-start | bytes 884744 | tf_op jit(solution)/shard_map/ppermute | solution.py:729
  635.3 12.4 %collective-permute-start.71 = (f32[12,768]{1,0:T(8,128)S(1)}, f32[12,768]{1,0:T(8,128)S(1)}, u32[]{:S(2)}, u32[]{:S(2)}) collective-permute-start(f32[12,768]{1,0:T(8,128)S(1)} %concatenate.44), channel_id=1, source_target_pairs={{0,2},{1,3},{2,0},{3,1},{4,6},{5,7},{6,4},{7,5},{8,10},{9,11},{10,... | collective-permute-start | bytes 110600 | tf_op jit(solution)/shard_map/ppermute | solution.py:721
  635.4 12.3 %collective-permute-start.72 = (f32[12,768]{1,0:T(8,128)S(1)}, f32[12,768]{1,0:T(8,128)S(1)}, u32[]{:S(2)}, u32[]{:S(2)}) collective-permute-start(f32[12,768]{1,0:T(8,128)S(1)} %concatenate.44), channel_id=1, source_target_pairs={{0,3},{1,2},{2,1},{3,0},{4,7},{5,6},{6,5},{7,4},{8,11},{9,10},{10,... | collective-permute-start | bytes 110600 | tf_op jit(solution)/shard_map/ppermute | solution.py:725
  637.5 10.1 %collective-permute-start.70 = (f32[12,768]{1,0:T(8,128)S(1)}, f32[12,768]{1,0:T(8,128)S(1)}, u32[]{:S(2)}, u32[]{:S(2)}) collective-permute-start(f32[12,768]{1,0:T(8,128)S(1)} %concatenate.44), channel_id=1, source_target_pairs={{0,1},{1,0},{2,3},{3,2},{4,5},{5,4},{6,7},{7,6},{8,9},{9,8},{10,11... | collective-permute-start | bytes 110600 | tf_op jit(solution)/shard_map/ppermute | solution.py:717
  640.1 25.2 %collective-permute-start.67 = (bf16[512,768]{1,0:T(8,128)(2,1)}, bf16[512,768]{1,0:T(8,128)(2,1)}, u32[]{:S(2)}, u32[]{:S(2)}) collective-permute-start(bf16[512,768]{1,0:T(8,128)(2,1)} %get-tuple-element.334), channel_id=1, source_target_pairs={{0,0},{1,1},{2,16},{3,17},{16,2},{17,3},{18,18},{19,19},{4,4},{5,5... | collective-permute-start | bytes 2359304 | tf_op jit(solution)/shard_map/ppermute | solution.py:729
  647.5 17.7 %collective-permute-start.68 = (bf16[512,768]{1,0:T(8,128)(2,1)}, bf16[512,768]{1,0:T(8,128)(2,1)}, u32[]{:S(2)}, u32[]{:S(2)}) collective-permute-start(bf16[512,768]{1,0:T(8,128)(2,1)} %get-tuple-element.335), channel_id=1, source_target_pairs={{0,16},{1,17},{2,0},{3,1},{16,18},{17,19},{18,2},{19,3},{4,20},{5,... | collective-permute-start | bytes 2359304 | tf_op jit(solution)/shard_map/ppermute | solution.py:729
  647.7 8.8 %collective-permute-start.74 = (f32[12,768]{1,0:T(8,128)S(1)}, f32[12,768]{1,0:T(8,128)S(1)}, u32[]{:S(2)}, u32[]{:S(2)}) collective-permute-start(f32[12,768]{1,0:T(8,128)S(1)} %add_add_fusion.3), channel_id=1, source_target_pairs={{0,8},{4,12},{8,0},{12,4},{1,9},{5,13},{9,1},{13,5},{2,10},{6,14},... | collective-permute-start | bytes 110600 | tf_op jit(solution)/shard_map/ppermute | solution.py:733
  (159 other events, 1870.5 us)
Sparse Core Ops, SparseCore 0:
  27.5 33.2 all-gather.4
  62.9 69.0 all-gather.6
  135.3 33.3 all-gather.8
  170.7 69.0 all-gather.10
  349.7 64.9 reduce-scatter.4
  478.0 32.8 reduce-scatter.6
  513.2 65.0 reduce-scatter.10
  581.2 30.5 reduce-scatter.8

commit v4 on v3

--- a/solution.py
+++ b/solution.py
@@ -319,7 +319,7 @@
         out_specs=(whole, acts, acts),
         out_shape=(jax.ShapeDtypeStruct((length, deep), out_type), act, act),
         scratch_shapes=[pltpu.VMEM((length, deep), jnp.float32)],
-        compiler_params=pltpu.CompilerParams(vmem_limit_bytes=40 << 20),
+        compiler_params=pltpu.CompilerParams(vmem_limit_bytes=32 << 20),
         cost_estimate=pl.CostEstimate(
             flops=12 * length * deep * hidden, bytes_accessed=12 * deep * hidden + 8 * length * hidden, transcendentals=2 * length * hidden
         ),
@@ -366,7 +366,7 @@
         out_specs=(whole, acts, acts, acts),
         out_shape=(jax.ShapeDtypeStruct((length, deep), out_type), act, act, act),
         scratch_shapes=[pltpu.VMEM((length, deep), jnp.float32)],
-        compiler_params=pltpu.CompilerParams(vmem_limit_bytes=40 << 20),
+        compiler_params=pltpu.CompilerParams(vmem_limit_bytes=32 << 20),
         cost_estimate=pl.CostEstimate(
             flops=12 * length * deep * hidden, bytes_accessed=12 * deep * hidden + 20 * length * hidden, transcendentals=2 * length * hidden
         ),
@@ -407,7 +407,7 @@
         out_specs=weights,
         out_shape=jax.ShapeDtypeStruct((3, deep, hidden), jnp.bfloat16),
         scratch_shapes=[both, both],
-        compiler_params=pltpu.CompilerParams(vmem_limit_bytes=40 << 20),
+        compiler_params=pltpu.CompilerParams(vmem_limit_bytes=32 << 20),
         cost_estimate=pl.CostEstimate(
             flops=12 * length * deep * hidden, bytes_accessed=6 * deep * hidden + 12 * length * hidden, transcendentals=0
         ),
@@ -466,14 +466,20 @@
     )(grad_proj, grad_proj, *slabs, matrix, out_grad)
 
 
+ROW_TILE = 256
+
+
 def mean_of(v):
     return jnp.mean(v, axis=-1, keepdims=True)
 
 
-def mix_fwd_kernel(head0, head1, head2, head3, matrix, out1, out2, out3, rows, params, hidden, low, normed, inv, *, width):
+def mix_fwd_kernel(head0, head1, head2, head3, matrix, out1, out2, out3, rows, params, hidden, low, normed, inv, weights, *, width):
+    @pl.when(pl.program_id(0) == 0)
+    def _():
+        weights[...] = jnp.concatenate([matrix[:, 3 * width :], out1[...], out2[...], out3[...]], axis=1)
+
     heads = jnp.concatenate([head0[...], head1[...], head2[...], head3[...]], axis=0).T
-    weights = jnp.concatenate([matrix[:, 3 * width :], out1[...], out2[...], out3[...]], axis=1)
-    mixed = rows[...].astype(jnp.float32) + lax.dot_general(heads, weights, NT, preferred_element_type=jnp.float32)
+    mixed = rows[...].astype(jnp.float32) + lax.dot_general(heads, weights[...], NT, preferred_element_type=jnp.float32)
     centred = mixed - mean_of(mixed)
     inv_std = lax.rsqrt(mean_of(centred * centred) + NORM_EPS)
     unit = centred * inv_std
@@ -488,13 +494,16 @@
     width, rows = heads[0].shape
     features = matrix.shape[0]
     whole = lambda a: pl.BlockSpec(a.shape, lambda i: (0,) * len(a.shape))
-    block = pl.BlockSpec((rows, features), lambda i: (0, 0))
+    block = pl.BlockSpec((ROW_TILE, features), lambda i: (i, 0))
     shape = lambda t: jax.ShapeDtypeStruct((rows, features), t)
     return pl.pallas_call(
         functools.partial(mix_fwd_kernel, width=width),
-        grid=(1,),
-        in_specs=[whole(a) for a in (*heads, matrix, *outs)] + [block, whole(params)],
-        out_specs=(block, block, block, pl.BlockSpec((rows, 1), lambda i: (0, 0))),
+        grid=(rows // ROW_TILE,),
+        in_specs=[pl.BlockSpec((width, ROW_TILE), lambda i: (0, i))] * 4
+        + [whole(a) for a in (matrix, *outs)]
+        + [block, whole(params)],
+        out_specs=(block, block, block, pl.BlockSpec((ROW_TILE, 1), lambda i: (i, 0))),
+        scratch_shapes=[pltpu.VMEM((features, 4 * width), jnp.bfloat16)],
         out_shape=(shape(jnp.float32), shape(jnp.bfloat16), shape(jnp.float32), jax.ShapeDtypeStruct((rows, 1), jnp.float32)),
         compiler_params=pltpu.CompilerParams(vmem_limit_bytes=60 << 20),
         cost_estimate=pl.CostEstimate(
@@ -506,20 +515,35 @@
 
 def mix_bwd_kernel(
     grad_mixed, own_part, far_part, normed, inv, params, head0, head1, head2, head3, matrix, out1, out2, out3,
-    grad_out, norms, made0, made1, made2, made3, og0, og1, og2, og3, *, width,
+    grad_out, norms, made0, made1, made2, made3, og0, og1, og2, og3, turned, total, *, width,
 ):
+    step = pl.program_id(0)
+
+    @pl.when(step == 0)
+    def _():
+        for i, weight in enumerate((matrix[:, 3 * width :], out1[...], out2[...], out3[...])):
+            turned[i * width : (i + 1) * width, :] = weight.T
+        total[...] = jnp.zeros_like(total)
+        norms[...] = jnp.zeros_like(norms)
+
     grad = grad_mixed[...] + own_part[...] + far_part[...].astype(jnp.float32)
     unit = normed[...]
-    norms[0:1, :] = jnp.sum(grad * unit, axis=0, keepdims=True)
-    norms[1:2, :] = jnp.sum(grad, axis=0, keepdims=True)
+    norms[0:1, :] += jnp.sum(grad * unit, axis=0, keepdims=True)
+    norms[1:2, :] += jnp.sum(grad, axis=0, keepdims=True)
     grad_unit = grad * params[0:1, :]
     back = inv[...] * (grad_unit - mean_of(grad_unit) - unit * mean_of(grad_unit * unit))
     grad_out[...] = back
     low = back.astype(jnp.bfloat16)
-    weights = (matrix[:, 3 * width :], out1[...], out2[...], out3[...])
-    for weight, head, made, og in zip(weights, (head0, head1, head2, head3), (made0, made1, made2, made3), (og0, og1, og2, og3)):
-        made[...] = lax.dot_general(weight.T, low, NT, preferred_element_type=jnp.float32).astype(jnp.bfloat16)
-        og[...] = jnp.dot(head[...], low, preferred_element_type=jnp.float32).astype(jnp.bfloat16)
+    made = lax.dot_general(turned[...], low, NT, preferred_element_type=jnp.float32).astype(jnp.bfloat16)
+    for i, out in enumerate((made0, made1, made2, made3)):
+        out[...] = made[i * width : (i + 1) * width]
+    heads = jnp.concatenate([head0[...], head1[...], head2[...], head3[...]], axis=0)
+    total[...] += jnp.dot(heads, low, preferred_element_type=jnp.float32)
+
+    @pl.when(step == pl.num_programs(0) - 1)
+    def _():
+        for i, og in enumerate((og0, og1, og2, og3)):
+            og[...] = total[i * width : (i + 1) * width, :].astype(jnp.bfloat16)
 
 
 def mix_bwd(grad_mixed, own_part, far_part, normed, inv, params, heads, matrix, outs):
@@ -532,12 +556,18 @@
         + [jax.ShapeDtypeStruct((width, features), jnp.bfloat16)] * 4
     )
     ops = (grad_mixed, own_part, far_part, normed, inv, params, *heads, matrix, *outs)
+    block = pl.BlockSpec((ROW_TILE, features), lambda i: (i, 0))
+    slab = pl.BlockSpec((width, ROW_TILE), lambda i: (0, i))
     got = pl.pallas_call(
         functools.partial(mix_bwd_kernel, width=width),
-        grid=(1,),
-        in_specs=[whole(a) for a in ops],
-        out_specs=tuple(whole(a) for a in shapes),
+        grid=(rows // ROW_TILE,),
+        in_specs=[block] * 4
+        + [pl.BlockSpec((ROW_TILE, 1), lambda i: (i, 0)), whole(params)]
+        + [slab] * 4
+        + [whole(a) for a in (matrix, *outs)],
+        out_specs=(block, whole(shapes[1]), *[slab] * 4, *[whole(a) for a in shapes[6:]]),
         out_shape=tuple(shapes),
+        scratch_shapes=[pltpu.VMEM((4 * width, features), jnp.bfloat16), pltpu.VMEM((4 * width, features), jnp.float32)],
         compiler_params=pltpu.CompilerParams(vmem_limit_bytes=60 << 20),
         cost_estimate=pl.CostEstimate(
             flops=4 * rows * features * features, bytes_accessed=22 * rows * features + 4 * features * features, transcendentals=0
@@ -556,8 +586,13 @@
         low_in[...] = grad.astype(jnp.bfloat16)
         grad = grad.astype(jnp.bfloat16).astype(jnp.float32)
     unit = normed[...]
-    norms[0:1, :] = jnp.sum(grad * unit, axis=0, keepdims=True)
-    norms[1:2, :] = jnp.sum(grad, axis=0, keepdims=True)
+
+    @pl.when(pl.program_id(0) == 0)
+    def _():
+        norms[...] = jnp.zeros_like(norms)
+
+    norms[0:1, :] += jnp.sum(grad * unit, axis=0, keepdims=True)
+    norms[1:2, :] += jnp.sum(grad, axis=0, keepdims=True)
     grad_unit = grad * gain[...]
     out = inv[...] * (grad_unit - mean_of(grad_unit) - unit * mean_of(grad_unit * unit))
     back[...] = out
@@ -572,6 +607,7 @@
     shapes = [shape(jnp.bfloat16)] * several + [shape(jnp.float32), shape(jnp.bfloat16)]
     shapes.append(jax.ShapeDtypeStruct((2, features), jnp.float32))
     ops = (*parts, normed, inv, gain)
+    block = pl.BlockSpec((ROW_TILE, features), lambda i: (i, 0))
 
     def kernel(*refs):
         ins, outs = refs[: len(ops)], refs[len(ops) :]
@@ -580,9 +616,9 @@
 
     got = pl.pallas_call(
         kernel,
-        grid=(1,),
-        in_specs=[whole(a) for a in ops],
-        out_specs=tuple(whole(a) for a in shapes),
+        grid=(rows // ROW_TILE,),
+        in_specs=[block] * (len(parts) + 1) + [pl.BlockSpec((ROW_TILE, 1), lambda i: (i, 0)), whole(gain)],
+        out_specs=(*[block] * (len(shapes) - 1), whole(shapes[-1])),
         out_shape=tuple(shapes),
         compiler_params=pltpu.CompilerParams(vmem_limit_bytes=60 << 20),
         cost_estimate=pl.CostEstimate(flops=12 * rows * features, bytes_accessed=18 * rows * features, transcendentals=0),
@@ -820,8 +856,8 @@
     )
     *out_grad, _ = lax.optimization_barrier((*out_grad, grad_mine))
     out_own = (out_grad[0], over_section(out_grad[1]), over_x(out_grad[2]), over_both(out_grad[3], CORNER))
-    grad_proj = attn_bwd(place, ends, qkv, after(grad_mine, *late), mine, log_sums, cos, sin)
-    out_own = sum(g.astype(f32) for g in after(out_own, grad_proj))
+    grad_proj = attn_bwd(place, ends, qkv, grad_mine, mine, log_sums, cos, sin)
+    out_own = sum(g.astype(f32) for g in after(out_own, grad_proj, *late))
     part3, part1, part2, part0, matrix_grad = proj_bwd(grad_proj, slabs, matrix, out_own)
     far_sum = over_x((part2.astype(f32) + over_section(part3).astype(f32)).astype(bf16))
     norm_grads = jnp.stack([jnp.stack([norm_one[0], norm_two[0]]), jnp.stack([norm_one[1], norm_two[1]])])
@@ -907,13 +943,13 @@
         other = over_both(jnp.where(y == 0, one, zero), SWAP_BACK)
         return same, other
 
-    def by_micro(zero, one):
-        same, other = home(zero, one)
+    def by_micro(same, other):
         return jnp.stack([jnp.where(section == 0, same, other), jnp.where(section == 0, other, same)])
 
-    layer_out = by_micro(low_zero, low_one)
+    layer_home = home(low_zero, low_one)
+    layer_out = by_micro(*layer_home)
     _, grads_one, matrix_one, ffn_one, norm_one = layer_backward(
-        (grad_top,), kept_one, second_matrix, outs_one, params[1], env, (layer_out,)
+        (grad_top,), kept_one, second_matrix, outs_one, params[1], env, layer_home
     )
     ffn_one = to_owner(scatter_later(ffn_one, 1), 1)
     matrix_one = to_owner(scatter_later(matrix_one, 0)[None], 1)
@@ -953,7 +989,7 @@
     )
     new_mats = (in_new, out_new, gate_new, down_new.T)
     made[3] = [v.T for v in made[3]]
-    input_grads = by_micro(after(grad_zero.astype(bf16), attn_home[0]), sent).astype(f32)
+    input_grads = by_micro(*home(after(grad_zero.astype(bf16), attn_home[0]), sent)).astype(f32)
     outs = [layer_out, input_grads]
     for i in range(4):
         outs += [new_mats[i], made[i][0], made[i][1]]

time: 687 us -> 677 us (0.985)
  waiting for transfers between devices: 217 us -> 190 us
  Pallas kernels: 249 us -> 271 us
    pallas_call x2, Pallas kernels: 35 us -> 53.9 us  [attn_fwd(): pl.pallas_call(functools.partial(attn_fwd_kernel, heads=heads), grid=(len...]
    all_gather x4, waiting for transfers between devices: 22.4 us -> 5.36 us  [gather_later(): return lax.all_gather(piece, 'dp', axis=axis, tiled=True)]
    pallas_call x2, Pallas kernels: 62.5 us -> 74 us  [attn_bwd(): pl.pallas_call(functools.partial(attn_bwd_kernel, heads=heads), grid=(len...]
    ppermute x21, waiting for transfers between devices: 140 us -> 131 us  [over_x(): return lax.ppermute(v, 'tensor', [(0, 1), (1, 0), (2, 3), (3, 2)])]
    unnamed x282 -> x278, local copies, waits for them, and re-layouts: 46.7 us -> 44.2 us
  transfers between devices with their start and end apart: 84 -> 84, of which waited for: 34 -> 33; matrix products, arithmetic and copies ran while one was open for 6% -> 5% of each run, Pallas kernels for 32% -> 36%
where the time goes in v4:
time: 677 us; the launch traced here: 666 us
  Pallas kernels  271 us (40%)
  waiting for transfers between devices  190 us (28%)
  starting transfers between devices  102 us (15%)
  local copies, waits for them, and re-layouts  54.6 us (8%)
  other arithmetic  31.6 us (5%)
  between operations  16.3 us (2%)
    ppermute x21, waiting for transfers between devices, over_x(): return lax.ppermute(v, 'tensor', [(0, 1), (1, 0), (2, 3), (3, 2)])  131 us
    pallas_call x2, Pallas kernels, attn_bwd(): pl.pallas_call(functools.partial(attn_bwd_kernel, heads=heads), grid=(len...  74 us
    ppermute x26, starting transfers between devices, over_both(): return lax.ppermute(v, BOTH, pairs)  62 us
    pallas_call x2, Pallas kernels, attn_fwd(): pl.pallas_call(functools.partial(attn_fwd_kernel, heads=heads), grid=(len...  53.9 us
    unnamed x278, local copies, waits for them, and re-layouts  44.2 us
    pallas_call x4, Pallas kernels, ffn_bwd(): pl.pallas_call(ffn_bwd_kernel, grid=(2, tiles), in_specs=[whole, acts, ac...  27.5 us
    ppermute x21, starting transfers between devices, over_x(): return lax.ppermute(v, 'tensor', [(0, 1), (1, 0), (2, 3), (3, 2)])  26.4 us
    pallas_call x4, Pallas kernels, ffn_grads(): pl.pallas_call(functools.partial(ffn_grads_kernel, slot=slot), grid=(hidd...  23 us
  transfers between devices with their start and end apart: 84, of which 33 were waited for; matrix products, arithmetic and copies ran while one was open for 5% of the time, Pallas kernels for 36%

profile of v4, /device:TPU:0, one launch (start us, length us, event | category | flops | bytes accessed | tf_op | source)
XLA Modules:
  0.0 665.7 jit_solution(15295724708819681385)
XLA Ops:
  12.5 3.7 collective-permute-start.6
  16.3 3.8 collective-permute-start.7
  21.1 4.6 collective-permute-done.7
  29.3 8.8 %collective-permute-start.4 = (bf16[3,192,768]{2,1,0:T(8,128)(2,1)S(1)}, bf16[3,192,768]{2,1,0:T(8,128)(2,1)S(1)}, u32[]{:S(2)}, u32[]{:S(2)}) collective-permute-start(bf16[3,192,768]{2,1,0:T(8,128)(2,1)S(1)} %pad_maximum_fusion.1), channel_id=1, source_target_pairs={{0,2},{1,3},{2,18},{3,19},{4,6},{5,7},{6,22},{7,23},{8,10},{9,11},... | collective-permute-start | bytes 2654216 | tf_op jit(solution)/shard_map/ppermute | solution.py:765
  38.1 2.1 collective-permute-start.2
  40.2 14.0 %collective-permute-done.2.slab2 = bf16[512,768]{1,0:T(8,128)(2,1)S(1)} collective-permute-done((bf16[512,768]{1,0:T(8,128)(2,1)S(1)}, bf16[512,768]{1,0:T(8,128)(2,1)S(1)}, u32[]{:S(2)}, u32[]{:S(2)}) %collective-permute-start.2) | collective-permute-done | bytes 786464 | tf_op jit(solution)/shard_map/ppermute | solution.py:753
  58.1 2.7 all-gather.5.cloned.1.call-done.matrix
  65.8 31.2 %attn_fwd.2 = (bf16[192,512]{1,0:T(8,128)(2,1)S(1)}, bf16[192,512]{1,0:T(8,128)(2,1)S(1)}, bf16[192,512]{1,0:T(8,128)(2,1)S(1)}, bf16[192,512]{1,0:T(8,128)(2,1)...) custom-call(s32[4]{0:T(128)S(1)} %pad_add_fusion.place, s32[2]{0:T(128)S(1)} %pad_add_fusion.1.ends, ...), custom_call_target="tpu_custom_call" | custom-call | flops 4831838208 | bytes 6291456 | tf_op jit(solution)/shard_map/attn_fwd/pallas_call | solution.py:150
  100.9 5.3 collective-permute-done.9.head2
  106.2 3.3 collective-permute-done.10.head3
  110.3 5.4 mix_fwd.2
  121.4 14.7 %collective-permute-done.15.rows_ref.h1 = bf16[512,768]{1,0:T(8,128)(2,1)S(1)} collective-permute-done((bf16[512,768]{1,0:T(8,128)(2,1)}, bf16[512,768]{1,0:T(8,128)(2,1)S(1)}, u32[]{:S(2)}, u32[]{:S(2)}) %collective-permute-start.15) | collective-permute-done | bytes 786464 | tf_op jit(solution)/shard_map/ppermute | solution.py:753
  144.7 6.7 %ffn_fwd.5 = (bf16[512,768]{1,0:T(8,128)(2,1)S(1)}, bf16[2,512,768]{2,1,0:T(8,128)(2,1)S(1)}, bf16[2,512,768]{2,1,0:T(8,128)(2,1)S(1)}) custom-call(bf16[512,768]{1,0:T(8,128)(2,1)S(1)} %collective-permute-done.15.rows_ref.h1, bf16[3,768,768]{2,1,0:T(8,128)(2,1)S(1)} %copy-done.36, bf16[3,768,768]{2,1,0:T(8,128)(2,1)} %collective-permute-done.16.second), custom_call_target="tpu_custom_call" | custom-call | flops 3623878656 | bytes 10223616 | tf_op jit(solution)/shard_map/ffn_fwd/pallas_call | solution.py:315
  153.8 6.5 ffn_fwd.4
  160.4 11.9 %collective-permute-done.17 = bf16[512,768]{1,0:T(8,128)(2,1)S(1)} collective-permute-done((bf16[512,768]{1,0:T(8,128)(2,1)S(1)}, bf16[512,768]{1,0:T(8,128)(2,1)S(1)}, u32[]{:S(2)}, u32[]{:S(2)}) %collective-permute-start.17) | collective-permute-done | bytes 786464 | tf_op jit(solution)/shard_map/ppermute | solution.py:753
  174.9 18.2 %collective-permute-done.19.slab2 = bf16[512,768]{1,0:T(8,128)(2,1)S(1)} collective-permute-done((bf16[512,768]{1,0:T(8,128)(2,1)S(1)}, bf16[512,768]{1,0:T(8,128)(2,1)S(1)}, u32[]{:S(2)}, u32[]{:S(2)}) %collective-permute-start.19) | collective-permute-done | bytes 786464 | tf_op jit(solution)/shard_map/ppermute | solution.py:753
  196.8 22.6 %attn_fwd.3 = (bf16[192,512]{1,0:T(8,128)(2,1)S(1)}, bf16[192,512]{1,0:T(8,128)(2,1)S(1)}, bf16[192,512]{1,0:T(8,128)(2,1)S(1)}, bf16[192,512]{1,0:T(8,128)(2,1)...) custom-call(s32[4]{0:T(128)S(1)} %pad_add_fusion.place, s32[2]{0:T(128)S(1)} %pad_add_fusion.1.ends, ...), custom_call_target="tpu_custom_call" | custom-call | flops 4831838208 | bytes 6291456 | tf_op jit(solution)/shard_map/attn_fwd/pallas_call | solution.py:150
  222.9 5.6 collective-permute-done.24.head2
  228.5 2.6 collective-permute-done.25.head3
  231.9 5.4 mix_fwd.3
  237.3 2.7 all-gather.11.cloned.1.call-done.first
  241.5 18.7 %collective-permute-done.30.rows_ref.h1 = bf16[512,768]{1,0:T(8,128)(2,1)S(1)} collective-permute-done((bf16[512,768]{1,0:T(8,128)(2,1)}, bf16[512,768]{1,0:T(8,128)(2,1)S(1)}, u32[]{:S(2)}, u32[]{:S(2)}) %collective-permute-start.30) | collective-permute-done | bytes 786464 | tf_op jit(solution)/shard_map/ppermute | solution.py:753
  262.2 4.4 ffn_fwd.7
  269.7 7.6 %collective-permute-start.34 = (bf16[512,768]{1,0:T(8,128)(2,1)}, bf16[512,768]{1,0:T(8,128)(2,1)}, u32[]{:S(2)}, u32[]{:S(2)}) collective-permute-start(bf16[512,768]{1,0:T(8,128)(2,1)} %dynamic-slice_bitcast_fusion), channel_id=1, source_target_pairs={{0,0},{1,1},{2,16},{3,17},{16,2},{17,3},{18,18},{19,19},{4,4},{5,5... | collective-permute-start | bytes 2359304 | tf_op jit(solution)/shard_map/ppermute | solution.py:765
  277.3 4.6 ffn_fwd.6
  281.9 3.9 collective-permute-done.31
  288.6 7.4 %collective-permute-start.32 = (bf16[512,768]{1,0:T(8,128)(2,1)}, bf16[512,768]{1,0:T(8,128)(2,1)}, u32[]{:S(2)}, u32[]{:S(2)}) collective-permute-start(bf16[512,768]{1,0:T(8,128)(2,1)} %get-tuple-element.308), channel_id=1, source_target_pairs={{0,0},{1,1},{2,16},{3,17},{16,2},{17,3},{18,18},{19,19},{4,4},{5,5... | collective-permute-start | bytes 2359304 | tf_op jit(solution)/shard_map/ppermute | solution.py:765
  298.1 3.4 top_bwd.2
  311.0 5.6 ffn_bwd.4
  316.6 4.6 collective-permute-done.35.grad_ref.g1
  321.2 5.8 ffn_bwd.5
  327.0 3.9 ffn_grads.4
  332.5 4.7 collective-permute-done.47.rest_0_
  337.2 5.7 ffn_grads.5
  342.9 8.1 %collective-permute-done.36.far_part = bf16[512,768]{1,0:T(8,128)(2,1)} collective-permute-done((bf16[512,768]{1,0:T(8,128)(2,1)S(1)}, bf16[512,768]{1,0:T(8,128)(2,1)}, u32[]{:S(2)}, u32[]{:S(2)}) %collective-permute-start.36) | collective-permute-done | bytes 786464 | tf_op jit(solution)/shard_map/ppermute | solution.py:753
  351.1 8.3 %mix_bwd.2 = (f32[512,768]{1,0:T(8,128)}, f32[2,768]{1,0:T(2,128)}, bf16[192,512]{1,0:T(8,128)(2,1)}, bf16[192,512]{1,0:T(8,128)(2,1)}, bf16[192,512]{1,0:T(8,12...) custom-call(f32[512,768]{1,0:T(8,128)} %get-tuple-element.190.grad_m, ...), custom_call_target="tpu_custom_call" | custom-call | flops 1207959552 | bytes 11010048 | tf_op jit(solution)/shard_map/mix_bwd/pallas_call | solution.py:561
  361.4 6.1 collective-permute-done.38.do2
  367.5 3.3 collective-permute-done.39.do3
  373.0 36.9 %attn_bwd.2.pair_grad.rest_grad = bf16[4,576,512]{2,1,0:T(8,128)(2,1)} custom-call(s32[4]{0:T(128)} %copy-done.35, s32[2]{0:T(128)} %copy-done.58, bf16[576,2048]{1,0:T(8,128)(2,1)} %get-tuple-element.202.qkv, bf16[192,512]{1,0:T(8,128)(2,1)} %get-tuple-element.203.do0, bf16[192,512]{1,0:T(8,128)(2,1)} %copy-done.134, bf16[192,512]{1,0:T(8,128)(2,1)} %copy-done.135, ...), custom_call_target="tpu_custom_call" | custom-call | flops 8053063680 | bytes 9437184 | tf_op jit(solution)/shard_map/attn_bwd/pallas_call | solution.py:257
  410.8 10.0 %proj_bwd.2 = (bf16[512,768]{1,0:T(8,128)(2,1)}, bf16[512,768]{1,0:T(8,128)(2,1)}, bf16[512,768]{1,0:T(8,128)(2,1)}, bf16[512,768]{1,0:T(8,128)(2,1)}, bf16[768,768]{1,0:T(8,128)(2,1)}) custom-call(bf16[4,576,512]{2,1,0:T(8,128)(2,1)} %attn_bwd.2.pair_grad.rest_grad, bf16[4,576,512]{2,1,0:T(8,128)(2,1)} %attn_bwd.2.pair_grad.rest_grad, ...), custom_call_target="tpu_custom_call" | custom-call | flops 3623878656 | bytes 9437184 | tf_op jit(solution)/shard_map/proj_bwd/pallas_call | solution.py:445
  427.1 3.5 collective-permute-start.49
  431.5 13.3 %collective-permute-done.45.refs_3_ = bf16[512,768]{1,0:T(8,128)(2,1)S(1)} collective-permute-done((bf16[512,768]{1,0:T(8,128)(2,1)S(1)}, bf16[512,768]{1,0:T(8,128)(2,1)S(1)}, u32[]{:S(2)}, u32[]{:S(2)}) %collective-permute-start.45) | collective-permute-done | bytes 786464 | tf_op jit(solution)/shard_map/ppermute | solution.py:753
  445.6 4.7 top_bwd.3
  456.4 7.7 %ffn_bwd.6 = (f32[512,768]{1,0:T(8,128)S(1)}, bf16[2,512,768]{2,1,0:T(8,128)(2,1)S(1)}, bf16[2,512,768]{2,1,0:T(8,128)(2,1)S(1)}, bf16[2,512,768]{2,1,0:T(8,128)(2,1)S(1)}) custom-call(bf16[512,768]{1,0:T(8,128)(2,1)S(1)} %copy-done.23, bf16[2,512,768]{2,1,0:T(8,128)(2,1)S(1)} %copy-done.64, bf16[2,512,768]{2,1,0:T(8,128)(2,1)S(1)} %copy-done.66, ...), custom_call_target="tpu_custom_call" | custom-call | flops 3623878656 | bytes 14942208 | tf_op jit(solution)/shard_map/ffn_bwd/pallas_call | solution.py:362
  465.3 4.3 collective-permute-done.46.grad_ref.g1
  469.7 8.4 %ffn_bwd.7 = (bf16[512,768]{1,0:T(8,128)(2,1)S(1)}, bf16[2,512,768]{2,1,0:T(8,128)(2,1)S(1)}, bf16[2,512,768]{2,1,0:T(8,128)(2,1)S(1)}, bf16[2,512,768]{2,1,0:T(8,128)(2,1)S(1)}) custom-call(bf16[512,768]{1,0:T(8,128)(2,1)S(1)} %collective-permute-done.46.grad_ref.g1, bf16[2,512,768]{2,1,0:T(8,128)(2,1)S(1)} %copy-done.60, ...), custom_call_target="tpu_custom_call" | custom-call | flops 3623878656 | bytes 14942208 | tf_op jit(solution)/shard_map/ffn_bwd/pallas_call | solution.py:362
  478.1 5.7 ffn_grads.6
  485.5 4.9 collective-permute-done.64.rest_0_
  502.1 7.7 %ffn_grads.7 = bf16[3,768,768]{2,1,0:T(8,128)(2,1)} custom-call(bf16[512,768]{1,0:T(8,128)(2,1)S(1)} %copy-done.18, bf16[512,768]{1,0:T(8,128)(2,1)S(1)} %copy-done.21, bf16[512,768]{1,0:T(8,128)(2,1)S(1)} %copy-done.25, bf16[512,768]{1,0:T(8,128)(2,1)S(1)} %copy-done.29, bf16[2,512,768]{2,1,0:T(8,128)(2,1)S(1)} %get-tuple-element.265.gate0, ...), custom_call_target="tpu_custom_call" | custom-call | flops 3623878656 | bytes 8257536 | tf_op jit(solution)/shard_map/ffn_grads/pallas_call | solution.py:403
  510.7 7.9 %mix_bwd.3 = (f32[512,768]{1,0:T(8,128)}, f32[2,768]{1,0:T(2,128)}, bf16[192,512]{1,0:T(8,128)(2,1)}, bf16[192,512]{1,0:T(8,128)(2,1)}, bf16[192,512]{1,0:T(8,12...) custom-call(f32[512,768]{1,0:T(8,128)} %get-tuple-element.223.grad_m, ...), custom_call_target="tpu_custom_call" | custom-call | flops 1207959552 | bytes 11010048 | tf_op jit(solution)/shard_map/mix_bwd/pallas_call | solution.py:561
  521.1 3.0 collective-permute-start.58
  524.1 2.5 collective-permute-done.52.do2
  526.7 3.1 collective-permute-done.53.do3
  532.1 37.2 %attn_bwd.3.pair_grad.rest_grad = bf16[4,576,512]{2,1,0:T(8,128)(2,1)} custom-call(s32[4]{0:T(128)} %copy-done.35, s32[2]{0:T(128)} %copy-done.58, bf16[576,2048]{1,0:T(8,128)(2,1)} %get-tuple-element.242.qkv, bf16[192,512]{1,0:T(8,128)(2,1)} %get-tuple-element.243.do0, bf16[192,512]{1,0:T(8,128)(2,1)} %copy-done.131, bf16[192,512]{1,0:T(8,128)(2,1)} %copy-done.132, ...), custom_call_target="tpu_custom_call" | custom-call | flops 8053063680 | bytes 9437184 | tf_op jit(solution)/shard_map/attn_bwd/pallas_call | solution.py:257
  570.3 10.0 %proj_bwd.3 = (bf16[512,768]{1,0:T(8,128)(2,1)}, bf16[512,768]{1,0:T(8,128)(2,1)}, bf16[512,768]{1,0:T(8,128)(2,1)}, bf16[512,768]{1,0:T(8,128)(2,1)}, bf16[768,768]{1,0:T(8,128)(2,1)}) custom-call(bf16[4,576,512]{2,1,0:T(8,128)(2,1)} %attn_bwd.3.pair_grad.rest_grad, bf16[4,576,512]{2,1,0:T(8,128)(2,1)} %attn_bwd.3.pair_grad.rest_grad, ...), custom_call_target="tpu_custom_call" | custom-call | flops 3623878656 | bytes 9437184 | tf_op jit(solution)/shard_map/proj_bwd/pallas_call | solution.py:445
  583.2 2.2 add_convert_fusion.1
  586.9 8.2 %collective-permute-start.65 = (bf16[3,192,768]{2,1,0:T(8,128)(2,1)}, bf16[3,192,768]{2,1,0:T(8,128)(2,1)}, u32[]{:S(2)}, u32[]{:S(2)}) collective-permute-start(bf16[3,192,768]{2,1,0:T(8,128)(2,1)} %reduce-scatter.11.cloned.1.call-done), channel_id=1, source_target_pairs={{0,0},{1,1},{16,2},{17,3},{4,4},{5,5},{20,6},{21,7},{8,8},{9,9},{2... | collective-permute-start | bytes 2654216 | tf_op jit(solution)/shard_map/ppermute | solution.py:765
  597.8 13.2 %reduce-scatter.9.cloned.1.call-done = bf16[192,768]{1,0:T(8,128)(2,1)} async-done(((bf16[768,768]{1,0:T(8,128)(2,1)}), bf16[192,768]{1,0:T(8,128)(2,1)}) %reduce-scatter.9.cloned.1.call-update) | async-done | bytes 294928 | tf_op jit(solution)/shard_map/reduce_scatter | solution.py:781
  615.9 6.9 %lamb.2 = (f32[2,192,768]{2,1,0:T(8,128)}, f32[2,192,768]{2,1,0:T(8,128)}, f32[2,192,768]{2,1,0:T(8,128)}, f32[192,768]{1,0:T(8,128)}, f32[192,768]{1,0:T(8,128)}, /*index=5*/f32[192,768]{1,0:T(8,128)}, f32[2,768]{1,0:T(2,128)}) custom-call(bf16[3,192,768]{2,1,0:T(8,128)(2,1)} %collective-permute-done.65.refs_0_, ...), custom_call_target="tpu_custom_call" | custom-call | flops 8847360 | bytes 12386304 | tf_op jit(solution)/shard_map/lamb/pallas_call | solution.py:669
  623.7 4.0 lamb.3
  628.4 2.7 collective-permute-start.71
  633.5 3.3 collective-permute-start.68
  646.1 4.3 finish.1
  650.4 4.7 collective-permute-done.68
  (488 shorter events, 141.2 us)
Async XLA Ops:
  7.2 53.6 %all-gather.5.cloned.1.call-start = ((), (), s32[]{:S(2)}) async-start(), calls=%async_computation.4 | async-start | bytes 1474560 | tf_op jit(solution)/shard_map/all_gather | solution.py:777
  12.5 8.5 %collective-permute-start.6 = (bf16[192,768]{1,0:T(8,128)(2,1)}, bf16[192,768]{1,0:T(8,128)(2,1)}, u32[]{:S(2)}, u32[]{:S(2)}) collective-permute-start(bf16[192,768]{1,0:T(8,128)(2,1)} %pad_maximum_fusion.2), channel_id=1, source_target_pairs={{0,0},{1,1},{2,16},{3,17},{4,4},{5,5},{6,20},{7,21},{8,8},{9,9},{1... | collective-permute-start | bytes 884744 | tf_op jit(solution)/shard_map/ppermute | solution.py:765
  16.3 9.4 %collective-permute-start.7 = (bf16[192,768]{1,0:T(8,128)(2,1)}, bf16[192,768]{1,0:T(8,128)(2,1)}, u32[]{:S(2)}, u32[]{:S(2)}) collective-permute-start(bf16[192,768]{1,0:T(8,128)(2,1)} %pad_maximum_fusion.2), channel_id=1, source_target_pairs={{0,2},{1,3},{2,18},{3,19},{4,6},{5,7},{6,22},{7,23},{8,10},{9,11},... | collective-permute-start | bytes 884744 | tf_op jit(solution)/shard_map/ppermute | solution.py:765
  20.2 8.2 %collective-permute-start = (bf16[512,768]{1,0:T(8,128)(2,1)S(1)}, bf16[512,768]{1,0:T(8,128)(2,1)S(1)}, u32[]{:S(2)}, u32[]{:S(2)}) collective-permute-start(bf16[512,768]{1,0:T(8,128)(2,1)S(1)} %dynamic-slice_bitcast_fusion.1), channel_id=1, source_target_pairs={{0,0},{1,1},{2,16},{3,17},{16,2},{17,3},{18,18},{19,19},{4,4},{5,5... | collective-permute-start | bytes 2359304 | tf_op jit(solution)/shard_map/ppermute | solution.py:765
  27.4 108.7 %all-gather.7.cloned.1.call-start = ((), (), s32[]{:S(2)}) async-start(), calls=%async_computation.5 | async-start | bytes 4423680 | tf_op jit(solution)/shard_map/all_gather | solution.py:777
  28.4 25.8 %collective-permute-start.3 = (bf16[3,192,768]{2,1,0:T(8,128)(2,1)S(1)}, bf16[3,192,768]{2,1,0:T(8,128)(2,1)S(1)}, u32[]{:S(2)}, u32[]{:S(2)}) collective-permute-start(bf16[3,192,768]{2,1,0:T(8,128)(2,1)S(1)} %pad_maximum_fusion.1), channel_id=1, source_target_pairs={{0,0},{1,1},{2,16},{3,17},{4,4},{5,5},{6,20},{7,21},{8,8},{9,9},{1... | collective-permute-start | bytes 2654216 | tf_op jit(solution)/shard_map/ppermute | solution.py:765
  29.3 25.0 %collective-permute-start.4 = (bf16[3,192,768]{2,1,0:T(8,128)(2,1)S(1)}, bf16[3,192,768]{2,1,0:T(8,128)(2,1)S(1)}, u32[]{:S(2)}, u32[]{:S(2)}) collective-permute-start(bf16[3,192,768]{2,1,0:T(8,128)(2,1)S(1)} %pad_maximum_fusion.1), channel_id=1, source_target_pairs={{0,2},{1,3},{2,18},{3,19},{4,6},{5,7},{6,22},{7,23},{8,10},{9,11},... | collective-permute-start | bytes 2654216 | tf_op jit(solution)/shard_map/ppermute | solution.py:765
  38.1 16.2 %collective-permute-start.2 = (bf16[512,768]{1,0:T(8,128)(2,1)S(1)}, bf16[512,768]{1,0:T(8,128)(2,1)S(1)}, u32[]{:S(2)}, u32[]{:S(2)}) collective-permute-start(bf16[512,768]{1,0:T(8,128)(2,1)S(1)} %collective-permute-done.slab0.rows), channel_id=1, source_target_pairs={{0,1},{1,0},{2,3},{3,2},{4,5},{5,4},{6,7},{7,6},{8,9},{9,8},{10,11... | collective-permute-start | bytes 2359304 | tf_op jit(solution)/shard_map/ppermute | solution.py:753
  55.4 137.8 %all-gather.9.cloned.1.call-start = ((), (), s32[]{:S(2)}) async-start(), calls=%async_computation.6 | async-start | bytes 1474560 | tf_op jit(solution)/shard_map/all_gather | solution.py:777
  55.4 8.8 %collective-permute-start.1 = (bf16[512,768]{1,0:T(8,128)(2,1)S(1)}, bf16[512,768]{1,0:T(8,128)(2,1)S(1)}, u32[]{:S(2)}, u32[]{:S(2)}) collective-permute-start(bf16[512,768]{1,0:T(8,128)(2,1)S(1)} %collective-permute-done.slab0.rows), channel_id=1, source_target_pairs={{0,16},{16,0},{1,17},{17,1},{2,18},{18,2},{3,19},{19,3},{4,20},{20... | collective-permute-start | bytes 2359304 | tf_op jit(solution)/shard_map/ppermute | solution.py:749
  55.5 8.7 %collective-permute-start.5 = (bf16[512,768]{1,0:T(8,128)(2,1)S(1)}, bf16[512,768]{1,0:T(8,128)(2,1)}, u32[]{:S(2)}, u32[]{:S(2)}) collective-permute-start(bf16[512,768]{1,0:T(8,128)(2,1)S(1)} %collective-permute-done.2.slab2), channel_id=1, source_target_pairs={{0,16},{16,0},{1,17},{17,1},{2,18},{18,2},{3,19},{19,3},{4,20},{20... | collective-permute-start | bytes 2359304 | tf_op jit(solution)/shard_map/ppermute | solution.py:749
  62.7 38.2 %collective-permute-start.11 = (bf16[768,192]{1,0:T(8,128)(2,1)}, bf16[768,192]{1,0:T(8,128)(2,1)}, u32[]{:S(2)}, u32[]{:S(2)}) collective-permute-start(bf16[768,192]{1,0:T(8,128)(2,1)} %slice.76), channel_id=1, source_target_pairs={{0,16},{16,0},{1,17},{17,1},{2,18},{18,2},{3,19},{19,3},{4,20},{20... | collective-permute-start | bytes 884744 | tf_op jit(solution)/shard_map/ppermute | solution.py:749
  62.7 35.0 %collective-permute-start.12 = (bf16[768,192]{1,0:T(8,128)(2,1)}, bf16[768,192]{1,0:T(8,128)(2,1)}, u32[]{:S(2)}, u32[]{:S(2)}) collective-permute-start(bf16[768,192]{1,0:T(8,128)(2,1)} %slice.76), channel_id=1, source_target_pairs={{0,1},{1,0},{2,3},{3,2},{4,5},{5,4},{6,7},{7,6},{8,9},{9,8},{10,11... | collective-permute-start | bytes 884744 | tf_op jit(solution)/shard_map/ppermute | solution.py:753
  97.7 11.7 %collective-permute-start.13 = (bf16[768,192]{1,0:T(8,128)(2,1)}, bf16[768,192]{1,0:T(8,128)(2,1)S(1)}, u32[]{:S(2)}, u32[]{:S(2)}) collective-permute-start(bf16[768,192]{1,0:T(8,128)(2,1)} %collective-permute-done.12.out2), channel_id=1, source_target_pairs={{0,16},{16,0},{1,17},{17,1},{2,18},{18,2},{3,19},{19,3},{4,20},{20... | collective-permute-start | bytes 884744 | tf_op jit(solution)/shard_map/ppermute | solution.py:749
  99.5 9.9 %collective-permute-start.10 = (bf16[192,512]{1,0:T(8,128)(2,1)S(1)}, bf16[192,512]{1,0:T(8,128)(2,1)S(1)}, u32[]{:S(2)}, u32[]{:S(2)}) collective-permute-start(bf16[192,512]{1,0:T(8,128)(2,1)S(1)} %get-tuple-element.165.out3), channel_id=1, source_target_pairs={{0,17},{1,16},{2,19},{3,18},{16,1},{17,0},{18,3},{19,2},{4,21},{5,... | collective-permute-start | bytes 589832 | tf_op jit(solution)/shard_map/ppermute | solution.py:765
  115.8 20.4 %collective-permute-start.15 = (bf16[512,768]{1,0:T(8,128)(2,1)}, bf16[512,768]{1,0:T(8,128)(2,1)S(1)}, u32[]{:S(2)}, u32[]{:S(2)}) collective-permute-start(bf16[512,768]{1,0:T(8,128)(2,1)} %get-tuple-element.169.rows_ref.h0), channel_id=1, source_target_pairs={{0,1},{1,0},{2,3},{3,2},{4,5},{5,4},{6,7},{7,6},{8,9},{9,8},{10,11... | collective-permute-start | bytes 2359304 | tf_op jit(solution)/shard_map/ppermute | solution.py:753
  118.4 17.7 %collective-permute-start.21 = (bf16[4,192,768]{2,1,0:T(8,128)(2,1)}, bf16[4,192,768]{2,1,0:T(8,128)(2,1)S(1)}, u32[]{:S(2)}, u32[]{:S(2)}) collective-permute-start(bf16[4,192,768]{2,1,0:T(8,128)(2,1)} %pad_maximum_fusion), channel_id=1, source_target_pairs={{16,0},{17,1},{18,16},{19,17},{20,4},{21,5},{22,20},{23,21},{24,8}... | collective-permute-start | bytes 3538952 | tf_op jit(solution)/shard_map/ppermute | solution.py:765
  119.7 17.5 %collective-permute-start.22 = (bf16[4,192,768]{2,1,0:T(8,128)(2,1)}, bf16[4,192,768]{2,1,0:T(8,128)(2,1)}, u32[]{:S(2)}, u32[]{:S(2)}) collective-permute-start(bf16[4,192,768]{2,1,0:T(8,128)(2,1)} %pad_maximum_fusion), channel_id=1, source_target_pairs={{16,2},{17,3},{18,18},{19,19},{20,6},{21,7},{22,22},{23,23},{24,10... | collective-permute-start | bytes 3538952 | tf_op jit(solution)/shard_map/ppermute | solution.py:765
  139.4 100.6 %all-gather.11.cloned.1.call-start = ((), (), s32[]{:S(2)}) async-start(), calls=%async_computation.7 | async-start | bytes 4423680 | tf_op jit(solution)/shard_map/all_gather | solution.py:777
  140.5 285.9 %reduce-scatter.5.cloned.1.call-start = ((), (), s32[]{:S(2)}) async-start(), calls=%async_computation.8 | async-start | bytes 4423680 | tf_op jit(solution)/shard_map/reduce_scatter | solution.py:781
  152.6 19.6 %collective-permute-start.17 = (bf16[512,768]{1,0:T(8,128)(2,1)S(1)}, bf16[512,768]{1,0:T(8,128)(2,1)S(1)}, u32[]{:S(2)}, u32[]{:S(2)}) collective-permute-start(bf16[512,768]{1,0:T(8,128)(2,1)S(1)} %get-tuple-element.174), channel_id=1, source_target_pairs={{0,1},{1,0},{2,3},{3,2},{4,5},{5,4},{6,7},{7,6},{8,9},{9,8},{10,11... | collective-permute-start | bytes 2359304 | tf_op jit(solution)/shard_map/ppermute | solution.py:753
  174.4 18.8 %collective-permute-start.19 = (bf16[512,768]{1,0:T(8,128)(2,1)S(1)}, bf16[512,768]{1,0:T(8,128)(2,1)S(1)}, u32[]{:S(2)}, u32[]{:S(2)}) collective-permute-start(bf16[512,768]{1,0:T(8,128)(2,1)S(1)} %get-tuple-element.312.slab0.rows), channel_id=1, source_target_pairs={{0,1},{1,0},{2,3},{3,2},{4,5},{5,4},{6,7},{7,6},{8,9},{9,8},{10,11... | collective-permute-start | bytes 2359304 | tf_op jit(solution)/shard_map/ppermute | solution.py:753
  174.9 20.5 %collective-permute-start.18 = (bf16[512,768]{1,0:T(8,128)(2,1)S(1)}, bf16[512,768]{1,0:T(8,128)(2,1)}, u32[]{:S(2)}, u32[]{:S(2)}) collective-permute-start(bf16[512,768]{1,0:T(8,128)(2,1)S(1)} %get-tuple-element.312.slab0.rows), channel_id=1, source_target_pairs={{0,16},{16,0},{1,17},{17,1},{2,18},{18,2},{3,19},{19,3},{4,20},{20... | collective-permute-start | bytes 2359304 | tf_op jit(solution)/shard_map/ppermute | solution.py:749
  194.6 28.2 %collective-permute-start.26 = (bf16[768,192]{1,0:T(8,128)(2,1)S(1)}, bf16[768,192]{1,0:T(8,128)(2,1)S(1)}, u32[]{:S(2)}, u32[]{:S(2)}) collective-permute-start(bf16[768,192]{1,0:T(8,128)(2,1)S(1)} %slice.81), channel_id=1, source_target_pairs={{0,16},{16,0},{1,17},{17,1},{2,18},{18,2},{3,19},{19,3},{4,20},{20... | collective-permute-start | bytes 884744 | tf_op jit(solution)/shard_map/ppermute | solution.py:749
  194.9 25.2 %collective-permute-start.27 = (bf16[768,192]{1,0:T(8,128)(2,1)S(1)}, bf16[768,192]{1,0:T(8,128)(2,1)S(1)}, u32[]{:S(2)}, u32[]{:S(2)}) collective-permute-start(bf16[768,192]{1,0:T(8,128)(2,1)S(1)} %slice.81), channel_id=1, source_target_pairs={{0,1},{1,0},{2,3},{3,2},{4,5},{5,4},{6,7},{7,6},{8,9},{9,8},{10,11... | collective-permute-start | bytes 884744 | tf_op jit(solution)/shard_map/ppermute | solution.py:753
  220.2 10.9 %collective-permute-start.28 = (bf16[768,192]{1,0:T(8,128)(2,1)S(1)}, bf16[768,192]{1,0:T(8,128)(2,1)S(1)}, u32[]{:S(2)}, u32[]{:S(2)}) collective-permute-start(bf16[768,192]{1,0:T(8,128)(2,1)S(1)} %collective-permute-done.27.out2), channel_id=1, source_target_pairs={{0,16},{16,0},{1,17},{17,1},{2,18},{18,2},{3,19},{19,3},{4,20},{20... | collective-permute-start | bytes 884744 | tf_op jit(solution)/shard_map/ppermute | solution.py:749
  222.1 9.0 %collective-permute-start.25 = (bf16[192,512]{1,0:T(8,128)(2,1)S(1)}, bf16[192,512]{1,0:T(8,128)(2,1)S(1)}, u32[]{:S(2)}, u32[]{:S(2)}) collective-permute-start(bf16[192,512]{1,0:T(8,128)(2,1)S(1)} %get-tuple-element.180.out3), channel_id=1, source_target_pairs={{0,17},{1,16},{2,19},{3,18},{16,1},{17,0},{18,3},{19,2},{4,21},{5,... | collective-permute-start | bytes 589832 | tf_op jit(solution)/shard_map/ppermute | solution.py:765
  240.0 20.2 %collective-permute-start.29 = (bf16[3,768,768]{2,1,0:T(8,128)(2,1)}, bf16[3,768,768]{2,1,0:T(8,128)(2,1)S(1)}, u32[]{:S(2)}, u32[]{:S(2)}) collective-permute-start(bf16[3,768,768]{2,1,0:T(8,128)(2,1)} %all-gather.11.cloned.1.call-done.first), channel_id=1, source_target_pairs={{0,16},{16,0},{1,17},{17,1},{2,18},{18,2},{3,19},{19,3},{4,20},{20... | collective-permute-start | bytes 10616840 | tf_op jit(solution)/shard_map/ppermute | solution.py:749
  240.0 20.2 %collective-permute-start.30 = (bf16[512,768]{1,0:T(8,128)(2,1)}, bf16[512,768]{1,0:T(8,128)(2,1)S(1)}, u32[]{:S(2)}, u32[]{:S(2)}) collective-permute-start(bf16[512,768]{1,0:T(8,128)(2,1)} %get-tuple-element.184.rows_ref.h0), channel_id=1, source_target_pairs={{0,1},{1,0},{2,3},{3,2},{4,5},{5,4},{6,7},{7,6},{8,9},{9,8},{10,11... | collective-permute-start | bytes 2359304 | tf_op jit(solution)/shard_map/ppermute | solution.py:753
  266.6 19.2 %collective-permute-start.31 = (bf16[512,768]{1,0:T(8,128)(2,1)S(1)}, bf16[512,768]{1,0:T(8,128)(2,1)S(1)}, u32[]{:S(2)}, u32[]{:S(2)}) collective-permute-start(bf16[512,768]{1,0:T(8,128)(2,1)S(1)} %get-tuple-element.188), channel_id=1, source_target_pairs={{0,1},{1,0},{2,3},{3,2},{4,5},{5,4},{6,7},{7,6},{8,9},{9,8},{10,11... | collective-permute-start | bytes 2359304 | tf_op jit(solution)/shard_map/ppermute | solution.py:753
  269.7 28.4 %collective-permute-start.34 = (bf16[512,768]{1,0:T(8,128)(2,1)}, bf16[512,768]{1,0:T(8,128)(2,1)}, u32[]{:S(2)}, u32[]{:S(2)}) collective-permute-start(bf16[512,768]{1,0:T(8,128)(2,1)} %dynamic-slice_bitcast_fusion), channel_id=1, source_target_pairs={{0,0},{1,1},{2,16},{3,17},{16,2},{17,3},{18,18},{19,19},{4,4},{5,5... | collective-permute-start | bytes 2359304 | tf_op jit(solution)/shard_map/ppermute | solution.py:765
  288.6 28.0 %collective-permute-start.32 = (bf16[512,768]{1,0:T(8,128)(2,1)}, bf16[512,768]{1,0:T(8,128)(2,1)}, u32[]{:S(2)}, u32[]{:S(2)}) collective-permute-start(bf16[512,768]{1,0:T(8,128)(2,1)} %get-tuple-element.308), channel_id=1, source_target_pairs={{0,0},{1,1},{2,16},{3,17},{16,2},{17,3},{18,18},{19,19},{4,4},{5,5... | collective-permute-start | bytes 2359304 | tf_op jit(solution)/shard_map/ppermute | solution.py:765
  297.2 19.4 %collective-permute-start.33 = (bf16[512,768]{1,0:T(8,128)(2,1)}, bf16[512,768]{1,0:T(8,128)(2,1)}, u32[]{:S(2)}, u32[]{:S(2)}) collective-permute-start(bf16[512,768]{1,0:T(8,128)(2,1)} %broadcast_select_fusion.4), channel_id=1, source_target_pairs={{0,16},{1,17},{2,0},{3,1},{16,18},{17,19},{18,2},{19,3},{4,20},{5,... | collective-permute-start | bytes 2359304 | tf_op jit(solution)/shard_map/ppermute | solution.py:765
  301.5 19.7 %collective-permute-start.35 = (bf16[512,768]{1,0:T(8,128)(2,1)}, bf16[512,768]{1,0:T(8,128)(2,1)S(1)}, u32[]{:S(2)}, u32[]{:S(2)}) collective-permute-start(bf16[512,768]{1,0:T(8,128)(2,1)} %get-tuple-element.191.grad_ref.g0), channel_id=1, source_target_pairs={{0,1},{1,0},{2,3},{3,2},{4,5},{5,4},{6,7},{7,6},{8,9},{9,8},{10,11... | collective-permute-start | bytes 2359304 | tf_op jit(solution)/shard_map/ppermute | solution.py:753
  331.0 20.1 %collective-permute-start.36 = (bf16[512,768]{1,0:T(8,128)(2,1)S(1)}, bf16[512,768]{1,0:T(8,128)(2,1)}, u32[]{:S(2)}, u32[]{:S(2)}) collective-permute-start(bf16[512,768]{1,0:T(8,128)(2,1)S(1)} %get-tuple-element.198), channel_id=1, source_target_pairs={{0,1},{1,0},{2,3},{3,2},{4,5},{5,4},{6,7},{7,6},{8,9},{9,8},{10,11... | collective-permute-start | bytes 2359304 | tf_op jit(solution)/shard_map/ppermute | solution.py:753
  351.1 169.4 %reduce-scatter.7.cloned.1.call-start = ((), (), s32[]{:S(2)}) async-start(), calls=%async_computation.9 | async-start | bytes 1474560 | tf_op jit(solution)/shard_map/reduce_scatter | solution.py:781
  359.5 8.0 %collective-permute-start.38 = (bf16[192,512]{1,0:T(8,128)(2,1)}, bf16[192,512]{1,0:T(8,128)(2,1)S(1)}, u32[]{:S(2)}, u32[]{:S(2)}) collective-permute-start(bf16[192,512]{1,0:T(8,128)(2,1)} %get-tuple-element.205), channel_id=1, source_target_pairs={{0,1},{1,0},{2,3},{3,2},{4,5},{5,4},{6,7},{7,6},{8,9},{9,8},{10,11... | collective-permute-start | bytes 589832 | tf_op jit(solution)/shard_map/ppermute | solution.py:753
  361.0 9.7 %collective-permute-start.39 = (bf16[192,512]{1,0:T(8,128)(2,1)}, bf16[192,512]{1,0:T(8,128)(2,1)S(1)}, u32[]{:S(2)}, u32[]{:S(2)}) collective-permute-start(bf16[192,512]{1,0:T(8,128)(2,1)} %get-tuple-element.206), channel_id=1, source_target_pairs={{0,17},{1,16},{2,19},{3,18},{16,1},{17,0},{18,3},{19,2},{4,21},{5,... | collective-permute-start | bytes 589832 | tf_op jit(solution)/shard_map/ppermute | solution.py:765
  370.8 39.1 %collective-permute-start.40 = (bf16[192,768]{1,0:T(8,128)(2,1)}, bf16[192,768]{1,0:T(8,128)(2,1)S(1)}, u32[]{:S(2)}, u32[]{:S(2)}) collective-permute-start(bf16[192,768]{1,0:T(8,128)(2,1)} %get-tuple-element.212), channel_id=1, source_target_pairs={{0,16},{16,0},{1,17},{17,1},{2,18},{18,2},{3,19},{19,3},{4,20},{20... | collective-permute-start | bytes 884744 | tf_op jit(solution)/shard_map/ppermute | solution.py:749
  371.5 38.4 %collective-permute-start.41 = (bf16[192,768]{1,0:T(8,128)(2,1)}, bf16[192,768]{1,0:T(8,128)(2,1)S(1)}, u32[]{:S(2)}, u32[]{:S(2)}) collective-permute-start(bf16[192,768]{1,0:T(8,128)(2,1)} %get-tuple-element.213), channel_id=1, source_target_pairs={{0,1},{1,0},{2,3},{3,2},{4,5},{5,4},{6,7},{7,6},{8,9},{9,8},{10,11... | collective-permute-start | bytes 884744 | tf_op jit(solution)/shard_map/ppermute | solution.py:753
  372.9 36.9 %collective-permute-start.42 = (bf16[192,768]{1,0:T(8,128)(2,1)}, bf16[192,768]{1,0:T(8,128)(2,1)S(1)}, u32[]{:S(2)}, u32[]{:S(2)}) collective-permute-start(bf16[192,768]{1,0:T(8,128)(2,1)} %get-tuple-element.214), channel_id=1, source_target_pairs={{0,17},{1,16},{2,19},{3,18},{16,1},{17,0},{18,3},{19,2},{4,21},{5,... | collective-permute-start | bytes 884744 | tf_op jit(solution)/shard_map/ppermute | solution.py:765
  421.4 10.1 %collective-permute-start.43 = (bf16[512,768]{1,0:T(8,128)(2,1)}, bf16[512,768]{1,0:T(8,128)(2,1)S(1)}, u32[]{:S(2)}, u32[]{:S(2)}) collective-permute-start(bf16[512,768]{1,0:T(8,128)(2,1)} %get-tuple-element.220), channel_id=1, source_target_pairs={{0,16},{16,0},{1,17},{17,1},{2,18},{18,2},{3,19},{19,3},{4,20},{20... | collective-permute-start | bytes 2359304 | tf_op jit(solution)/shard_map/ppermute | solution.py:749
  424.8 19.9 %collective-permute-start.45 = (bf16[512,768]{1,0:T(8,128)(2,1)S(1)}, bf16[512,768]{1,0:T(8,128)(2,1)S(1)}, u32[]{:S(2)}, u32[]{:S(2)}) collective-permute-start(bf16[512,768]{1,0:T(8,128)(2,1)S(1)} %add_convert_fusion.2), channel_id=1, source_target_pairs={{0,1},{1,0},{2,3},{3,2},{4,5},{5,4},{6,7},{7,6},{8,9},{9,8},{10,11... | collective-permute-start | bytes 2359304 | tf_op jit(solution)/shard_map/ppermute | solution.py:753
  426.4 43.2 %collective-permute-start.48 = (bf16[3,192,768]{2,1,0:T(8,128)(2,1)}, bf16[3,192,768]{2,1,0:T(8,128)(2,1)S(1)}, u32[]{:S(2)}, u32[]{:S(2)}) collective-permute-start(bf16[3,192,768]{2,1,0:T(8,128)(2,1)} %reduce-scatter.5.cloned.1.call-done), channel_id=1, source_target_pairs={{2,16},{3,17},{18,18},{19,19},{6,20},{7,21},{22,22},{23,23},{10,24... | collective-permute-start | bytes 2654216 | tf_op jit(solution)/shard_map/ppermute | solution.py:765
  427.1 42.5 %collective-permute-start.49 = (bf16[3,192,768]{2,1,0:T(8,128)(2,1)}, bf16[3,192,768]{2,1,0:T(8,128)(2,1)}, u32[]{:S(2)}, u32[]{:S(2)}) collective-permute-start(bf16[3,192,768]{2,1,0:T(8,128)(2,1)} %reduce-scatter.5.cloned.1.call-done), channel_id=1, source_target_pairs={{0,16},{1,17},{16,18},{17,19},{4,20},{5,21},{20,22},{21,23},{8,24}... | collective-permute-start | bytes 2654216 | tf_op jit(solution)/shard_map/ppermute | solution.py:765
  450.4 19.2 %collective-permute-start.46 = (bf16[512,768]{1,0:T(8,128)(2,1)}, bf16[512,768]{1,0:T(8,128)(2,1)S(1)}, u32[]{:S(2)}, u32[]{:S(2)}) collective-permute-start(bf16[512,768]{1,0:T(8,128)(2,1)} %get-tuple-element.224.grad_ref.g0), channel_id=1, source_target_pairs={{0,1},{1,0},{2,3},{3,2},{4,5},{5,4},{6,7},{7,6},{8,9},{9,8},{10,11... | collective-permute-start | bytes 2359304 | tf_op jit(solution)/shard_map/ppermute | solution.py:753
  483.9 103.0 %reduce-scatter.11.cloned.1.call-start = ((), (), s32[]{:S(2)}) async-start(), calls=%async_computation.11 | async-start | bytes 4423680 | tf_op jit(solution)/shard_map/reduce_scatter | solution.py:781
  484.0 25.8 %collective-permute-start.50 = (bf16[512,768]{1,0:T(8,128)(2,1)S(1)}, bf16[512,768]{1,0:T(8,128)(2,1)S(1)}, u32[]{:S(2)}, u32[]{:S(2)}) collective-permute-start(bf16[512,768]{1,0:T(8,128)(2,1)S(1)} %get-tuple-element.238), channel_id=1, source_target_pairs={{0,1},{1,0},{2,3},{3,2},{4,5},{5,4},{6,7},{7,6},{8,9},{9,8},{10,11... | collective-permute-start | bytes 2359304 | tf_op jit(solution)/shard_map/ppermute | solution.py:753
  510.7 100.3 %reduce-scatter.9.cloned.1.call-start = ((), (), s32[]{:S(2)}) async-start(), calls=%async_computation.10 | async-start | bytes 1474560 | tf_op jit(solution)/shard_map/reduce_scatter | solution.py:781
  520.2 9.6 %collective-permute-start.53 = (bf16[192,512]{1,0:T(8,128)(2,1)}, bf16[192,512]{1,0:T(8,128)(2,1)S(1)}, u32[]{:S(2)}, u32[]{:S(2)}) collective-permute-start(bf16[192,512]{1,0:T(8,128)(2,1)} %get-tuple-element.246), channel_id=1, source_target_pairs={{0,17},{1,16},{2,19},{3,18},{16,1},{17,0},{18,3},{19,2},{4,21},{5,... | collective-permute-start | bytes 589832 | tf_op jit(solution)/shard_map/ppermute | solution.py:765
  520.4 48.8 %collective-permute-start.57 = (bf16[1,192,768]{2,1,0:T(8,128)(2,1)}, bf16[1,192,768]{2,1,0:T(8,128)(2,1)S(1)}, u32[]{:S(2)}, u32[]{:S(2)}) collective-permute-start(bf16[1,192,768]{2,1,0:T(8,128)(2,1)} %bitcast.149), channel_id=1, source_target_pairs={{2,16},{3,17},{18,18},{19,19},{6,20},{7,21},{22,22},{23,23},{10,24... | collective-permute-start | bytes 884744 | tf_op jit(solution)/shard_map/ppermute | solution.py:765
  521.1 48.1 %collective-permute-start.58 = (bf16[1,192,768]{2,1,0:T(8,128)(2,1)}, bf16[1,192,768]{2,1,0:T(8,128)(2,1)S(1)}, u32[]{:S(2)}, u32[]{:S(2)}) collective-permute-start(bf16[1,192,768]{2,1,0:T(8,128)(2,1)} %bitcast.150), channel_id=1, source_target_pairs={{0,16},{1,17},{16,18},{17,19},{4,20},{5,21},{20,22},{21,23},{8,24}... | collective-permute-start | bytes 884744 | tf_op jit(solution)/shard_map/ppermute | solution.py:765
  529.8 39.5 %collective-permute-start.54 = (bf16[192,768]{1,0:T(8,128)(2,1)}, bf16[192,768]{1,0:T(8,128)(2,1)S(1)}, u32[]{:S(2)}, u32[]{:S(2)}) collective-permute-start(bf16[192,768]{1,0:T(8,128)(2,1)} %get-tuple-element.252), channel_id=1, source_target_pairs={{0,16},{16,0},{1,17},{17,1},{2,18},{18,2},{3,19},{19,3},{4,20},{20... | collective-permute-start | bytes 884744 | tf_op jit(solution)/shard_map/ppermute | solution.py:749
  530.5 38.7 %collective-permute-start.55 = (bf16[192,768]{1,0:T(8,128)(2,1)}, bf16[192,768]{1,0:T(8,128)(2,1)S(1)}, u32[]{:S(2)}, u32[]{:S(2)}) collective-permute-start(bf16[192,768]{1,0:T(8,128)(2,1)} %get-tuple-element.253), channel_id=1, source_target_pairs={{0,1},{1,0},{2,3},{3,2},{4,5},{5,4},{6,7},{7,6},{8,9},{9,8},{10,11... | collective-permute-start | bytes 884744 | tf_op jit(solution)/shard_map/ppermute | solution.py:753
  532.0 37.3 %collective-permute-start.56 = (bf16[192,768]{1,0:T(8,128)(2,1)}, bf16[192,768]{1,0:T(8,128)(2,1)S(1)}, u32[]{:S(2)}, u32[]{:S(2)}) collective-permute-start(bf16[192,768]{1,0:T(8,128)(2,1)} %get-tuple-element.254), channel_id=1, source_target_pairs={{0,17},{1,16},{2,19},{3,18},{16,1},{17,0},{18,3},{19,2},{4,21},{5,... | collective-permute-start | bytes 884744 | tf_op jit(solution)/shard_map/ppermute | solution.py:765
  581.5 31.1 %collective-permute-start.59 = (bf16[512,768]{1,0:T(8,128)(2,1)}, bf16[512,768]{1,0:T(8,128)(2,1)}, u32[]{:S(2)}, u32[]{:S(2)}) collective-permute-start(bf16[512,768]{1,0:T(8,128)(2,1)} %get-tuple-element.261), channel_id=1, source_target_pairs={{0,16},{16,0},{1,17},{17,1},{2,18},{18,2},{3,19},{19,3},{4,20},{20... | collective-permute-start | bytes 2359304 | tf_op jit(solution)/shard_map/ppermute | solution.py:749
  585.4 28.8 %collective-permute-start.61 = (bf16[512,768]{1,0:T(8,128)(2,1)}, bf16[512,768]{1,0:T(8,128)(2,1)}, u32[]{:S(2)}, u32[]{:S(2)}) collective-permute-start(bf16[512,768]{1,0:T(8,128)(2,1)} %add_convert_fusion.1), channel_id=1, source_target_pairs={{0,1},{1,0},{2,3},{3,2},{4,5},{5,4},{6,7},{7,6},{8,9},{9,8},{10,11... | collective-permute-start | bytes 2359304 | tf_op jit(solution)/shard_map/ppermute | solution.py:753
  586.9 29.0 %collective-permute-start.65 = (bf16[3,192,768]{2,1,0:T(8,128)(2,1)}, bf16[3,192,768]{2,1,0:T(8,128)(2,1)}, u32[]{:S(2)}, u32[]{:S(2)}) collective-permute-start(bf16[3,192,768]{2,1,0:T(8,128)(2,1)} %reduce-scatter.11.cloned.1.call-done), channel_id=1, source_target_pairs={{0,0},{1,1},{16,2},{17,3},{4,4},{5,5},{20,6},{21,7},{8,8},{9,9},{2... | collective-permute-start | bytes 2654216 | tf_op jit(solution)/shard_map/ppermute | solution.py:765
  595.2 20.8 %collective-permute-start.66 = (bf16[3,192,768]{2,1,0:T(8,128)(2,1)}, bf16[3,192,768]{2,1,0:T(8,128)(2,1)}, u32[]{:S(2)}, u32[]{:S(2)}) collective-permute-start(bf16[3,192,768]{2,1,0:T(8,128)(2,1)} %reduce-scatter.11.cloned.1.call-done), channel_id=1, source_target_pairs={{2,0},{3,1},{18,2},{19,3},{6,4},{7,5},{22,6},{23,7},{10,8},{11,9},... | collective-permute-start | bytes 2654216 | tf_op jit(solution)/shard_map/ppermute | solution.py:765
  611.0 11.9 %collective-permute-start.62 = (bf16[1,192,768]{2,1,0:T(8,128)(2,1)}, bf16[1,192,768]{2,1,0:T(8,128)(2,1)S(1)}, u32[]{:S(2)}, u32[]{:S(2)}) collective-permute-start(bf16[1,192,768]{2,1,0:T(8,128)(2,1)} %bitcast.147), channel_id=1, source_target_pairs={{0,0},{1,1},{16,2},{17,3},{4,4},{5,5},{20,6},{21,7},{8,8},{9,9},{2... | collective-permute-start | bytes 884744 | tf_op jit(solution)/shard_map/ppermute | solution.py:765
  612.6 10.3 %collective-permute-start.63 = (bf16[1,192,768]{2,1,0:T(8,128)(2,1)}, bf16[1,192,768]{2,1,0:T(8,128)(2,1)S(1)}, u32[]{:S(2)}, u32[]{:S(2)}) collective-permute-start(bf16[1,192,768]{2,1,0:T(8,128)(2,1)} %bitcast.148), channel_id=1, source_target_pairs={{2,0},{3,1},{18,2},{19,3},{6,4},{7,5},{22,6},{23,7},{10,8},{11,9},... | collective-permute-start | bytes 884744 | tf_op jit(solution)/shard_map/ppermute | solution.py:765
  628.4 9.8 %collective-permute-start.71 = (f32[12,768]{1,0:T(8,128)S(1)}, f32[12,768]{1,0:T(8,128)S(1)}, u32[]{:S(2)}, u32[]{:S(2)}) collective-permute-start(f32[12,768]{1,0:T(8,128)S(1)} %concatenate.44), channel_id=1, source_target_pairs={{0,2},{1,3},{2,0},{3,1},{4,6},{5,7},{6,4},{7,5},{8,10},{9,11},{10,... | collective-permute-start | bytes 110600 | tf_op jit(solution)/shard_map/ppermute | solution.py:757
  632.8 17.6 %collective-permute-start.67 = (bf16[512,768]{1,0:T(8,128)(2,1)S(1)}, bf16[512,768]{1,0:T(8,128)(2,1)S(1)}, u32[]{:S(2)}, u32[]{:S(2)}) collective-permute-start(bf16[512,768]{1,0:T(8,128)(2,1)S(1)} %get-tuple-element.318), channel_id=1, source_target_pairs={{0,0},{1,1},{2,16},{3,17},{16,2},{17,3},{18,18},{19,19},{4,4},{5,5... | collective-permute-start | bytes 2359304 | tf_op jit(solution)/shard_map/ppermute | solution.py:765
  633.5 21.6 %collective-permute-start.68 = (bf16[512,768]{1,0:T(8,128)(2,1)S(1)}, bf16[512,768]{1,0:T(8,128)(2,1)}, u32[]{:S(2)}, u32[]{:S(2)}) collective-permute-start(bf16[512,768]{1,0:T(8,128)(2,1)S(1)} %get-tuple-element.319), channel_id=1, source_target_pairs={{0,16},{1,17},{2,0},{3,1},{16,18},{17,19},{18,2},{19,3},{4,20},{5,... | collective-permute-start | bytes 2359304 | tf_op jit(solution)/shard_map/ppermute | solution.py:765
  (157 other events, 1859.1 us)
Sparse Core Ops, SparseCore 0:
  27.5 33.2 all-gather.4
  62.9 69.0 all-gather.6
  139.5 29.3 all-gather.8
  170.9 69.0 all-gather.10
  351.2 64.0 reduce-scatter.4
  484.0 27.0 reduce-scatter.6
  513.5 65.0 reduce-scatter.10
  581.5 29.4 reduce-scatter.8

commit v5 on v4

--- a/solution.py
+++ b/solution.py
@@ -374,42 +374,40 @@
     )(grad, gate, up, first, second)
 
 
-def ffn_grads_kernel(h0, h1, g0, g1, gate0, gate1, up0, up1, in0, in1, *rest, slot):
-    *other, out, h_t, g_t = rest
-
-    @pl.when(pl.program_id(0) == 0)
-    def _():
-        rows = h0.shape[0]
-        h_t[:, :rows] = h0[...].T
-        h_t[:, rows:] = h1[...].T
-        g_t[:, :rows] = g0[...].T
-        g_t[:, rows:] = g1[...].T
-
-    for i, (left, a, b) in enumerate(((h_t, gate0, gate1), (h_t, up0, up1), (g_t, in0, in1))):
-        both = jnp.concatenate([a[0], b[0]], axis=0)
-        grad = jnp.dot(left[...], both, preferred_element_type=jnp.float32)
+def ffn_grads_kernel(*refs, sets, other):
+    rows, grads, gates, ups, inners = (refs[i * sets : (i + 1) * sets] for i in range(5))
+    more, (out, h_t, g_t) = refs[5 * sets : 5 * sets + other], refs[5 * sets + other :]
+    at = 0
+    for h, g in zip(rows, grads):
+        size = h.shape[0]
+        h_t[:, at : at + size] = h[...].T
+        g_t[:, at : at + size] = g[...].T
+        at += size
+    for i, (left, acts) in enumerate(((h_t, gates), (h_t, ups), (g_t, inners))):
+        whole = jnp.concatenate([a[0] for a in acts], axis=0)
+        grad = jnp.dot(left[...], whole, preferred_element_type=jnp.float32)
         if other:
-            grad += other[0][i].astype(jnp.float32)
+            grad += more[0][i].astype(jnp.float32)
         out[i] = grad.astype(jnp.bfloat16)
 
 
 def ffn_grads(slot, rows, grads, gates, ups, inners, *other):
-    length, deep = rows[0].shape
-    hidden = gates[0].shape[2]
-    whole = pl.BlockSpec((length, deep), lambda j: (0, 0))
-    acts = pl.BlockSpec((1, length, FT), lambda j: (slot, 0, j))
-    weights = pl.BlockSpec((3, deep, FT), lambda j: (0, 0, j))
-    both = pltpu.VMEM((deep, 2 * length), jnp.bfloat16)
+    deep, hidden = rows[0].shape[1], gates[0].shape[2]
+    length = sum(r.shape[0] for r in rows)
+    whole = [pl.BlockSpec(r.shape, lambda i: (0, 0)) for r in rows]
+    acts = [pl.BlockSpec((1, r.shape[0], hidden), lambda i: (slot, 0, 0)) for r in rows]
+    weights = pl.BlockSpec((3, deep, hidden), lambda i: (0, 0, 0))
+    both = pltpu.VMEM((deep, length), jnp.bfloat16)
     return pl.pallas_call(
-        functools.partial(ffn_grads_kernel, slot=slot),
-        grid=(hidden // FT,),
-        in_specs=[whole] * 4 + [acts] * 6 + [weights] * len(other),
+        functools.partial(ffn_grads_kernel, sets=len(rows), other=len(other)),
+        grid=(1,),
+        in_specs=whole * 2 + acts * 3 + [weights] * len(other),
         out_specs=weights,
         out_shape=jax.ShapeDtypeStruct((3, deep, hidden), jnp.bfloat16),
         scratch_shapes=[both, both],
         compiler_params=pltpu.CompilerParams(vmem_limit_bytes=32 << 20),
         cost_estimate=pl.CostEstimate(
-            flops=12 * length * deep * hidden, bytes_accessed=6 * deep * hidden + 12 * length * hidden, transcendentals=0
+            flops=6 * length * deep * hidden, bytes_accessed=6 * deep * hidden + 6 * length * hidden, transcendentals=0
         ),
         name="ffn_grads",
     )(*rows, *grads, *gates, *ups, *inners, *other)
@@ -818,6 +816,10 @@
     return lax.optimization_barrier((value,) + others)[0]
 
 
+def halves(v):
+    return jnp.split(v, 2, axis=0)
+
+
 def layer_forward(slabs, matrix, ffn, params, env, late):
     place, ends, cos, sin = env
     *mine, log_sums, qkv = attn_fwd(place, ends, slabs, matrix, cos, sin)
@@ -826,13 +828,14 @@
     outs = (over_section(out_own), out_across, over_section(after(out_across, log_sums)))
     all_heads = [mine[0], over_section(mine[1]), over_x(mine[2]), over_both(mine[3], CORNER)]
     hidden, hidden_low, normed_one, inv_one = mix_fwd(all_heads, matrix, outs, slabs[0], params[:, 0])
-    hidden_rows = [hidden_low, over_x(hidden_low)]
+    hidden_rows = [hidden_low] + [over_x(part) for part in halves(hidden_low)]
     ffn = (ffn, over_section(after(ffn, hidden_rows[late])))
     own_part, *own_acts = ffn_fwd(hidden_rows[0], *ffn, f32)
-    far_part, *far_acts = ffn_fwd(hidden_rows[1], *ffn, bf16)
-    ffn_out = own_part + over_x(far_part).astype(f32)
+    first_part, *first_acts = ffn_fwd(hidden_rows[1], *ffn, bf16)
+    second_part, *second_acts = ffn_fwd(after(hidden_rows[2], first_part), *ffn, bf16)
+    ffn_out = own_part + jnp.concatenate([over_x(first_part), over_x(second_part)]).astype(f32)
     output, normed_two, inv_two = norm_fwd(hidden + ffn_out, params[0, 1], params[1, 1])
-    kept = (slabs, qkv, mine, log_sums, all_heads, normed_one, inv_one, hidden_rows, (own_acts, far_acts))
+    kept = (slabs, qkv, mine, log_sums, all_heads, normed_one, inv_one, hidden_rows, (own_acts, first_acts, second_acts))
     return output.astype(bf16), outs, kept + (normed_two, inv_two, ffn)
 
 
@@ -840,13 +843,14 @@
     place, ends, cos, sin = env
     (slabs, qkv, mine, log_sums, all_heads, normed_one, inv_one, hidden_rows, acts, normed_two, inv_two, ffn) = kept
     sent, grad_mixed, grad_low, norm_two = top_bwd(grad_parts, normed_two, inv_two, params[0, 1:2])
-    grad_rows = [grad_low, over_x(grad_low)]
+    grad_rows = [grad_low] + [over_x(part) for part in halves(grad_low)]
     own_part, *own_grads = ffn_bwd(grad_rows[0], *acts[0], *ffn, f32)
-    far_part, *far_grads = ffn_bwd(after(grad_rows[1], own_part, *early), *acts[1], *ffn, bf16)
-    made = list(zip(own_grads, far_grads))
+    first_part, *first_grads = ffn_bwd(after(grad_rows[1], own_part, *early), *acts[1], *ffn, bf16)
+    second_part, *second_grads = ffn_bwd(after(grad_rows[2], first_part), *acts[2], *ffn, bf16)
+    made = list(zip(own_grads, first_grads, second_grads))
     ffn_other = ffn_grads(1, hidden_rows, grad_rows, *made)
     ffn_grad = ffn_grads(0, hidden_rows, grad_rows, *made, over_section(ffn_other))
-    far_part = over_x(far_part)
+    far_part = jnp.concatenate([over_x(first_part), over_x(second_part)])
     ffn_grad = after(ffn_grad, far_part)
     grad_mixed_one, norm_one, grad_heads, out_grad = mix_bwd(
         grad_mixed, own_part, far_part, normed_one, inv_one, params[:, 0], all_heads, matrix, outs

time: 677 us -> 688 us (1.016)
  waiting for transfers between devices: 190 us -> 157 us
  local copies, waits for them, and re-layouts: 54.6 us -> 79.6 us
  starting transfers between devices: 102 us -> 114 us
    unnamed x278 -> x318, local copies, waits for them, and re-layouts: 44.2 us -> 60.8 us
    ppermute x24, waiting for transfers between devices: 16.1 us -> 6.05 us  [over_section(): return lax.ppermute(v, 'section', [(0, 1), (1, 0)])]
    ppermute x21 -> x29, waiting for transfers between devices: 131 us -> 123 us  [over_x(): return lax.ppermute(v, 'tensor', [(0, 1), (1, 0), (2, 3), (3, 2)])]
    ppermute x26, starting transfers between devices: 62 us -> 69.7 us  [over_both(): return lax.ppermute(v, BOTH, pairs)]
    pallas_call x4 -> x6, Pallas kernels: 27.5 us -> 32.7 us  [ffn_bwd(): pl.pallas_call(ffn_bwd_kernel, grid=(2, tiles), in_specs=[whole, acts, ac...]
    pallas_call x4 -> x6, Pallas kernels: 22.2 us -> 25.5 us  [ffn_fwd(): pl.pallas_call(ffn_fwd_kernel, grid=(2, tiles), in_specs=[whole, w1, w2],...]
    ppermute x21 -> x29, starting transfers between devices: 26.4 us -> 27.7 us  [over_x(): return lax.ppermute(v, 'tensor', [(0, 1), (1, 0), (2, 3), (3, 2)])]
  transfers between devices with their start and end apart: 84 -> 92, of which waited for: 33 -> 28; matrix products, arithmetic and copies ran while one was open for 5% -> 7% of each run, Pallas kernels for 36% -> 37%
where the time goes in v5:
time: 688 us; the launch traced here: 676 us
  Pallas kernels  276 us (40%)
  waiting for transfers between devices  157 us (23%)
  starting transfers between devices  114 us (17%)
  local copies, waits for them, and re-layouts  79.6 us (12%)
  other arithmetic  32.8 us (5%)
  between operations  16.5 us (2%)
    ppermute x29, waiting for transfers between devices, over_x(): return lax.ppermute(v, 'tensor', [(0, 1), (1, 0), (2, 3), (3, 2)])  123 us
    pallas_call x2, Pallas kernels, attn_bwd(): pl.pallas_call(functools.partial(attn_bwd_kernel, heads=heads), grid=(len...  74 us
    ppermute x26, starting transfers between devices, over_both(): return lax.ppermute(v, BOTH, pairs)  69.7 us
    unnamed x318, local copies, waits for them, and re-layouts  60.8 us
    pallas_call x2, Pallas kernels, attn_fwd(): pl.pallas_call(functools.partial(attn_fwd_kernel, heads=heads), grid=(len...  53 us
    pallas_call x6, Pallas kernels, ffn_bwd(): pl.pallas_call(ffn_bwd_kernel, grid=(2, tiles), in_specs=[whole, acts, ac...  32.7 us
    ppermute x29, starting transfers between devices, over_x(): return lax.ppermute(v, 'tensor', [(0, 1), (1, 0), (2, 3), (3, 2)])  27.7 us
    pallas_call x6, Pallas kernels, ffn_fwd(): pl.pallas_call(ffn_fwd_kernel, grid=(2, tiles), in_specs=[whole, w1, w2],...  25.5 us
  transfers between devices with their start and end apart: 92, of which 28 were waited for; matrix products, arithmetic and copies ran while one was open for 7% of the time, Pallas kernels for 37%

profile of v5, /device:TPU:0, one launch (start us, length us, event | category | flops | bytes accessed | tf_op | source)
XLA Modules:
  0.0 675.8 jit_solution(14793152116752734415)
XLA Ops:
  12.9 3.7 collective-permute-start.6
  16.6 3.8 collective-permute-start.7
  27.9 10.5 %collective-permute-start.4 = (bf16[3,192,768]{2,1,0:T(8,128)(2,1)S(1)}, bf16[3,192,768]{2,1,0:T(8,128)(2,1)S(1)}, u32[]{:S(2)}, u32[]{:S(2)}) collective-permute-start(bf16[3,192,768]{2,1,0:T(8,128)(2,1)S(1)} %pad_maximum_fusion.1), channel_id=1, source_target_pairs={{0,2},{1,3},{2,18},{3,19},{4,6},{5,7},{6,22},{7,23},{8,10},{9,11},... | collective-permute-start | bytes 2654216 | tf_op jit(solution)/shard_map/ppermute | solution.py:763
  38.4 2.1 collective-permute-start.2
  40.5 14.1 %collective-permute-done.2.slab2 = bf16[512,768]{1,0:T(8,128)(2,1)S(1)} collective-permute-done((bf16[512,768]{1,0:T(8,128)(2,1)S(1)}, bf16[512,768]{1,0:T(8,128)(2,1)S(1)}, u32[]{:S(2)}, u32[]{:S(2)}) %collective-permute-start.2) | collective-permute-done | bytes 786464 | tf_op jit(solution)/shard_map/ppermute | solution.py:751
  70.8 30.6 %attn_fwd.2 = (bf16[192,512]{1,0:T(8,128)(2,1)S(1)}, bf16[192,512]{1,0:T(8,128)(2,1)S(1)}, bf16[192,512]{1,0:T(8,128)(2,1)S(1)}, bf16[192,512]{1,0:T(8,128)(2,1)...) custom-call(s32[4]{0:T(128)S(1)} %pad_add_fusion.place, s32[2]{0:T(128)S(1)} %pad_add_fusion.1.ends, ...), custom_call_target="tpu_custom_call" | custom-call | flops 4831838208 | bytes 6291456 | tf_op jit(solution)/shard_map/attn_fwd/pallas_call | solution.py:150
  114.1 4.0 collective-permute-done.9.head2
  118.9 5.4 mix_fwd.2
  127.2 9.4 %collective-permute-done.15.rows_ref.refs_1_ = bf16[256,768]{1,0:T(8,128)(2,1)S(1)} collective-permute-done((bf16[256,768]{1,0:T(8,128)(2,1)S(1)}, bf16[256,768]{1,0:T(8,128)(2,1)S(1)}, u32[]{:S(2)}, u32[]{:S(2)}) %collective-permute-start.15) | collective-permute-done | bytes 393248 | tf_op jit(solution)/shard_map/ppermute | solution.py:751
  145.2 4.7 ffn_fwd.7
  152.6 4.7 ffn_fwd.8
  160.8 6.6 ffn_fwd.6
  167.4 3.8 collective-permute-done.19
  174.3 17.7 %collective-permute-done.21.slab2 = bf16[512,768]{1,0:T(8,128)(2,1)S(1)} collective-permute-done((bf16[512,768]{1,0:T(8,128)(2,1)S(1)}, bf16[512,768]{1,0:T(8,128)(2,1)S(1)}, u32[]{:S(2)}, u32[]{:S(2)}) %collective-permute-start.21) | collective-permute-done | bytes 786464 | tf_op jit(solution)/shard_map/ppermute | solution.py:751
  201.9 22.3 %attn_fwd.3 = (bf16[192,512]{1,0:T(8,128)(2,1)S(1)}, bf16[192,512]{1,0:T(8,128)(2,1)S(1)}, bf16[192,512]{1,0:T(8,128)(2,1)S(1)}, bf16[192,512]{1,0:T(8,128)(2,1)...) custom-call(s32[4]{0:T(128)S(1)} %pad_add_fusion.place, s32[2]{0:T(128)S(1)} %pad_add_fusion.1.ends, ...), custom_call_target="tpu_custom_call" | custom-call | flops 4831838208 | bytes 6291456 | tf_op jit(solution)/shard_map/attn_fwd/pallas_call | solution.py:150
  228.1 5.5 collective-permute-done.26.head2
  233.6 2.8 collective-permute-done.27.head3
  237.2 5.4 mix_fwd.3
  247.9 9.0 %collective-permute-done.32.rows_ref.refs_1_ = bf16[256,768]{1,0:T(8,128)(2,1)S(1)} collective-permute-done((bf16[256,768]{1,0:T(8,128)(2,1)S(1)}, bf16[256,768]{1,0:T(8,128)(2,1)S(1)}, u32[]{:S(2)}, u32[]{:S(2)}) %collective-permute-start.32) | collective-permute-done | bytes 393248 | tf_op jit(solution)/shard_map/ppermute | solution.py:751
  256.9 2.1 copy-done.4
  259.0 2.5 ffn_fwd.10
  264.5 2.5 ffn_fwd.11
  270.3 7.5 %collective-permute-start.38 = (bf16[512,768]{1,0:T(8,128)(2,1)}, bf16[512,768]{1,0:T(8,128)(2,1)}, u32[]{:S(2)}, u32[]{:S(2)}) collective-permute-start(bf16[512,768]{1,0:T(8,128)(2,1)} %dynamic-slice_bitcast_fusion), channel_id=1, source_target_pairs={{0,0},{1,1},{2,16},{3,17},{16,2},{17,3},{18,18},{19,19},{4,4},{5,5... | collective-permute-start | bytes 2359304 | tf_op jit(solution)/shard_map/ppermute | solution.py:763
  277.9 4.6 ffn_fwd.9
  287.9 7.4 %collective-permute-start.36 = (bf16[512,768]{1,0:T(8,128)(2,1)}, bf16[512,768]{1,0:T(8,128)(2,1)}, u32[]{:S(2)}, u32[]{:S(2)}) collective-permute-start(bf16[512,768]{1,0:T(8,128)(2,1)} %get-tuple-element.344), channel_id=1, source_target_pairs={{0,0},{1,1},{2,16},{3,17},{16,2},{17,3},{18,18},{19,19},{4,4},{5,5... | collective-permute-start | bytes 2359304 | tf_op jit(solution)/shard_map/ppermute | solution.py:763
  296.2 3.6 top_bwd.2
  308.5 5.6 ffn_bwd.6
  315.3 3.0 ffn_bwd.7
  318.4 3.2 ffn_bwd.8
  321.7 3.9 ffn_grads.4
  327.7 9.9 %collective-permute-done.40 = bf16[256,768]{1,0:T(8,128)(2,1)S(1)} collective-permute-done((bf16[256,768]{1,0:T(8,128)(2,1)S(1)}, bf16[256,768]{1,0:T(8,128)(2,1)S(1)}, u32[]{:S(2)}, u32[]{:S(2)}) %collective-permute-start.40) | collective-permute-done | bytes 393248 | tf_op jit(solution)/shard_map/ppermute | solution.py:751
  337.6 7.9 %collective-permute-done.42 = bf16[256,768]{1,0:T(8,128)(2,1)S(1)} collective-permute-done((bf16[256,768]{1,0:T(8,128)(2,1)S(1)}, bf16[256,768]{1,0:T(8,128)(2,1)S(1)}, u32[]{:S(2)}, u32[]{:S(2)}) %collective-permute-start.42) | collective-permute-done | bytes 393248 | tf_op jit(solution)/shard_map/ppermute | solution.py:751
  345.6 3.9 ffn_grads.5
  351.4 8.9 %mix_bwd.2 = (f32[512,768]{1,0:T(8,128)}, f32[2,768]{1,0:T(2,128)}, bf16[192,512]{1,0:T(8,128)(2,1)}, bf16[192,512]{1,0:T(8,128)(2,1)}, bf16[192,512]{1,0:T(8,12...) custom-call(f32[512,768]{1,0:T(8,128)} %get-tuple-element.212.grad_m, ...), custom_call_target="tpu_custom_call" | custom-call | flops 1207959552 | bytes 11010048 | tf_op jit(solution)/shard_map/mix_bwd/pallas_call | solution.py:559
  362.3 6.1 collective-permute-done.44.do2
  368.4 3.3 collective-permute-done.45.do3
  373.8 36.9 %attn_bwd.2.pair_grad.rest_grad = bf16[4,576,512]{2,1,0:T(8,128)(2,1)} custom-call(s32[4]{0:T(128)} %copy-done.69, s32[2]{0:T(128)} %copy-done.90, bf16[576,2048]{1,0:T(8,128)(2,1)} %get-tuple-element.228.qkv, bf16[192,512]{1,0:T(8,128)(2,1)} %get-tuple-element.229.do0, bf16[192,512]{1,0:T(8,128)(2,1)} %copy-done.153, bf16[192,512]{1,0:T(8,128)(2,1)} %copy-done.154, ...), custom_call_target="tpu_custom_call" | custom-call | flops 8053063680 | bytes 9437184 | tf_op jit(solution)/shard_map/attn_bwd/pallas_call | solution.py:257
  411.6 10.0 %proj_bwd.2 = (bf16[512,768]{1,0:T(8,128)(2,1)}, bf16[512,768]{1,0:T(8,128)(2,1)}, bf16[512,768]{1,0:T(8,128)(2,1)}, bf16[512,768]{1,0:T(8,128)(2,1)}, bf16[768,768]{1,0:T(8,128)(2,1)}) custom-call(bf16[4,576,512]{2,1,0:T(8,128)(2,1)} %attn_bwd.2.pair_grad.rest_grad, bf16[4,576,512]{2,1,0:T(8,128)(2,1)} %attn_bwd.2.pair_grad.rest_grad, ...), custom_call_target="tpu_custom_call" | custom-call | flops 3623878656 | bytes 9437184 | tf_op jit(solution)/shard_map/proj_bwd/pallas_call | solution.py:443
  428.1 2.6 collective-permute-start.55
  431.5 14.3 %collective-permute-done.51.refs_3_ = bf16[512,768]{1,0:T(8,128)(2,1)S(1)} collective-permute-done((bf16[512,768]{1,0:T(8,128)(2,1)S(1)}, bf16[512,768]{1,0:T(8,128)(2,1)S(1)}, u32[]{:S(2)}, u32[]{:S(2)}) %collective-permute-start.51) | collective-permute-done | bytes 786464 | tf_op jit(solution)/shard_map/ppermute | solution.py:751
  446.7 4.8 top_bwd.3
  458.2 7.7 %ffn_bwd.9 = (f32[512,768]{1,0:T(8,128)S(1)}, bf16[2,512,768]{2,1,0:T(8,128)(2,1)S(1)}, bf16[2,512,768]{2,1,0:T(8,128)(2,1)S(1)}, bf16[2,512,768]{2,1,0:T(8,128)(2,1)S(1)}) custom-call(bf16[512,768]{1,0:T(8,128)(2,1)S(1)} %copy-done.15, bf16[2,512,768]{2,1,0:T(8,128)(2,1)S(1)} %copy-done.92, bf16[2,512,768]{2,1,0:T(8,128)(2,1)S(1)} %copy-done.94, ...), custom_call_target="tpu_custom_call" | custom-call | flops 3623878656 | bytes 14942208 | tf_op jit(solution)/shard_map/ffn_bwd/pallas_call | solution.py:362
  467.2 6.8 %ffn_bwd.10 = (bf16[256,768]{1,0:T(8,128)(2,1)S(1)}, bf16[2,256,768]{2,1,0:T(8,128)(2,1)S(1)}, bf16[2,256,768]{2,1,0:T(8,128)(2,1)S(1)}, bf16[2,256,768]{2,1,0:T(8,128)(2,1)S(1)}) custom-call(bf16[256,768]{1,0:T(8,128)(2,1)S(1)} %collective-permute-done.52.grad_ref.refs_4_, bf16[2,256,768]{2,1,0:T(8,128)(2,1)S(1)} %copy-done.55, ...), custom_call_target="tpu_custom_call" | custom-call | flops 1811939328 | bytes 11010048 | tf_op jit(solution)/shard_map/ffn_bwd/pallas_call | solution.py:362
  474.1 6.3 ffn_bwd.11
  480.5 5.7 ffn_grads.6
  488.6 10.1 %collective-permute-done.56 = bf16[256,768]{1,0:T(8,128)(2,1)S(1)} collective-permute-done((bf16[256,768]{1,0:T(8,128)(2,1)}, bf16[256,768]{1,0:T(8,128)(2,1)S(1)}, u32[]{:S(2)}, u32[]{:S(2)}) %collective-permute-start.56) | collective-permute-done | bytes 393248 | tf_op jit(solution)/shard_map/ppermute | solution.py:751
  498.7 8.0 %collective-permute-done.58 = bf16[256,768]{1,0:T(8,128)(2,1)S(1)} collective-permute-done((bf16[256,768]{1,0:T(8,128)(2,1)}, bf16[256,768]{1,0:T(8,128)(2,1)S(1)}, u32[]{:S(2)}, u32[]{:S(2)}) %collective-permute-start.58) | collective-permute-done | bytes 393248 | tf_op jit(solution)/shard_map/ppermute | solution.py:751
  517.3 5.9 ffn_grads.7
  525.0 8.5 %mix_bwd.3 = (f32[512,768]{1,0:T(8,128)}, f32[2,768]{1,0:T(2,128)}, bf16[192,512]{1,0:T(8,128)(2,1)}, bf16[192,512]{1,0:T(8,128)(2,1)}, bf16[192,512]{1,0:T(8,12...) custom-call(f32[512,768]{1,0:T(8,128)} %get-tuple-element.249.grad_m, ...), custom_call_target="tpu_custom_call" | custom-call | flops 1207959552 | bytes 11010048 | tf_op jit(solution)/shard_map/mix_bwd/pallas_call | solution.py:559
  536.1 2.9 collective-permute-start.66
  539.1 2.5 collective-permute-done.60.do2
  541.6 3.3 collective-permute-done.61.do3
  546.9 37.2 %attn_bwd.3.pair_grad.rest_grad = bf16[4,576,512]{2,1,0:T(8,128)(2,1)} custom-call(s32[4]{0:T(128)} %copy-done.69, s32[2]{0:T(128)} %copy-done.90, bf16[576,2048]{1,0:T(8,128)(2,1)} %get-tuple-element.275.qkv, bf16[192,512]{1,0:T(8,128)(2,1)} %get-tuple-element.276.do0, bf16[192,512]{1,0:T(8,128)(2,1)} %copy-done.150, bf16[192,512]{1,0:T(8,128)(2,1)} %copy-done.151, ...), custom_call_target="tpu_custom_call" | custom-call | flops 8053063680 | bytes 9437184 | tf_op jit(solution)/shard_map/attn_bwd/pallas_call | solution.py:257
  585.1 10.0 %proj_bwd.3 = (bf16[512,768]{1,0:T(8,128)(2,1)}, bf16[512,768]{1,0:T(8,128)(2,1)}, bf16[512,768]{1,0:T(8,128)(2,1)}, bf16[512,768]{1,0:T(8,128)(2,1)}, bf16[768,768]{1,0:T(8,128)(2,1)}) custom-call(bf16[4,576,512]{2,1,0:T(8,128)(2,1)} %attn_bwd.3.pair_grad.rest_grad, bf16[4,576,512]{2,1,0:T(8,128)(2,1)} %attn_bwd.3.pair_grad.rest_grad, ...), custom_call_target="tpu_custom_call" | custom-call | flops 3623878656 | bytes 9437184 | tf_op jit(solution)/shard_map/proj_bwd/pallas_call | solution.py:443
  598.2 2.2 add_convert_fusion.1
  600.7 8.2 %collective-permute-start.73 = (bf16[3,192,768]{2,1,0:T(8,128)(2,1)}, bf16[3,192,768]{2,1,0:T(8,128)(2,1)}, u32[]{:S(2)}, u32[]{:S(2)}) collective-permute-start(bf16[3,192,768]{2,1,0:T(8,128)(2,1)} %reduce-scatter.11.cloned.1.call-done), channel_id=1, source_target_pairs={{0,0},{1,1},{16,2},{17,3},{4,4},{5,5},{20,6},{21,7},{8,8},{9,9},{2... | collective-permute-start | bytes 2654216 | tf_op jit(solution)/shard_map/ppermute | solution.py:763
  611.5 9.6 %reduce-scatter.9.cloned.1.call-done = bf16[192,768]{1,0:T(8,128)(2,1)} async-done(((bf16[768,768]{1,0:T(8,128)(2,1)}), bf16[192,768]{1,0:T(8,128)(2,1)}) %reduce-scatter.9.cloned.1.call-update) | async-done | bytes 294928 | tf_op jit(solution)/shard_map/reduce_scatter | solution.py:779
  626.1 6.9 %lamb.2 = (f32[2,192,768]{2,1,0:T(8,128)}, f32[2,192,768]{2,1,0:T(8,128)}, f32[2,192,768]{2,1,0:T(8,128)}, f32[192,768]{1,0:T(8,128)}, f32[192,768]{1,0:T(8,128)}, /*index=5*/f32[192,768]{1,0:T(8,128)}, f32[2,768]{1,0:T(2,128)}) custom-call(bf16[3,192,768]{2,1,0:T(8,128)(2,1)} %collective-permute-done.73.refs_0_, ...), custom_call_target="tpu_custom_call" | custom-call | flops 8847360 | bytes 12386304 | tf_op jit(solution)/shard_map/lamb/pallas_call | solution.py:667
  633.8 4.0 lamb.3
  640.0 2.6 collective-permute-start.79
  643.5 3.3 collective-permute-start.76
  650.1 2.7 collective-permute-start.83
  656.8 4.3 finish.1
  661.0 4.2 collective-permute-done.76
  (554 shorter events, 175.8 us)
Async XLA Ops:
  7.2 52.8 %all-gather.5.cloned.1.call-start = ((), (), s32[]{:S(2)}) async-start(), calls=%async_computation.4 | async-start | bytes 1474560 | tf_op jit(solution)/shard_map/all_gather | solution.py:775
  12.9 10.4 %collective-permute-start.6 = (bf16[192,768]{1,0:T(8,128)(2,1)}, bf16[192,768]{1,0:T(8,128)(2,1)}, u32[]{:S(2)}, u32[]{:S(2)}) collective-permute-start(bf16[192,768]{1,0:T(8,128)(2,1)} %pad_maximum_fusion.2), channel_id=1, source_target_pairs={{0,0},{1,1},{2,16},{3,17},{4,4},{5,5},{6,20},{7,21},{8,8},{9,9},{1... | collective-permute-start | bytes 884744 | tf_op jit(solution)/shard_map/ppermute | solution.py:763
  26.6 110.0 %all-gather.7.cloned.1.call-start = ((), (), s32[]{:S(2)}) async-start(), calls=%async_computation.5 | async-start | bytes 4423680 | tf_op jit(solution)/shard_map/all_gather | solution.py:775
  27.0 27.6 %collective-permute-start.3 = (bf16[3,192,768]{2,1,0:T(8,128)(2,1)S(1)}, bf16[3,192,768]{2,1,0:T(8,128)(2,1)S(1)}, u32[]{:S(2)}, u32[]{:S(2)}) collective-permute-start(bf16[3,192,768]{2,1,0:T(8,128)(2,1)S(1)} %pad_maximum_fusion.1), channel_id=1, source_target_pairs={{0,0},{1,1},{2,16},{3,17},{4,4},{5,5},{6,20},{7,21},{8,8},{9,9},{1... | collective-permute-start | bytes 2654216 | tf_op jit(solution)/shard_map/ppermute | solution.py:763
  27.9 26.8 %collective-permute-start.4 = (bf16[3,192,768]{2,1,0:T(8,128)(2,1)S(1)}, bf16[3,192,768]{2,1,0:T(8,128)(2,1)S(1)}, u32[]{:S(2)}, u32[]{:S(2)}) collective-permute-start(bf16[3,192,768]{2,1,0:T(8,128)(2,1)S(1)} %pad_maximum_fusion.1), channel_id=1, source_target_pairs={{0,2},{1,3},{2,18},{3,19},{4,6},{5,7},{6,22},{7,23},{8,10},{9,11},... | collective-permute-start | bytes 2654216 | tf_op jit(solution)/shard_map/ppermute | solution.py:763
  38.4 16.3 %collective-permute-start.2 = (bf16[512,768]{1,0:T(8,128)(2,1)S(1)}, bf16[512,768]{1,0:T(8,128)(2,1)S(1)}, u32[]{:S(2)}, u32[]{:S(2)}) collective-permute-start(bf16[512,768]{1,0:T(8,128)(2,1)S(1)} %collective-permute-done.slab0.rows), channel_id=1, source_target_pairs={{0,1},{1,0},{2,3},{3,2},{4,5},{5,4},{6,7},{7,6},{8,9},{9,8},{10,11... | collective-permute-start | bytes 2359304 | tf_op jit(solution)/shard_map/ppermute | solution.py:751
  55.8 137.2 %all-gather.9.cloned.1.call-start = ((), (), s32[]{:S(2)}) async-start(), calls=%async_computation.6 | async-start | bytes 1474560 | tf_op jit(solution)/shard_map/all_gather | solution.py:775
  62.0 42.6 %collective-permute-start.12 = (bf16[768,192]{1,0:T(8,128)(2,1)}, bf16[768,192]{1,0:T(8,128)(2,1)}, u32[]{:S(2)}, u32[]{:S(2)}) collective-permute-start(bf16[768,192]{1,0:T(8,128)(2,1)} %slice.76), channel_id=1, source_target_pairs={{0,1},{1,0},{2,3},{3,2},{4,5},{5,4},{6,7},{7,6},{8,9},{9,8},{10,11... | collective-permute-start | bytes 884744 | tf_op jit(solution)/shard_map/ppermute | solution.py:751
  63.4 46.0 %collective-permute-start.11 = (bf16[768,192]{1,0:T(8,128)(2,1)}, bf16[768,192]{1,0:T(8,128)(2,1)}, u32[]{:S(2)}, u32[]{:S(2)}) collective-permute-start(bf16[768,192]{1,0:T(8,128)(2,1)} %slice.76), channel_id=1, source_target_pairs={{0,16},{16,0},{1,17},{17,1},{2,18},{18,2},{3,19},{19,3},{4,20},{20... | collective-permute-start | bytes 884744 | tf_op jit(solution)/shard_map/ppermute | solution.py:747
  104.5 13.6 %collective-permute-start.13 = (bf16[768,192]{1,0:T(8,128)(2,1)}, bf16[768,192]{1,0:T(8,128)(2,1)S(1)}, u32[]{:S(2)}, u32[]{:S(2)}) collective-permute-start(bf16[768,192]{1,0:T(8,128)(2,1)} %collective-permute-done.12.out2), channel_id=1, source_target_pairs={{0,16},{16,0},{1,17},{17,1},{2,18},{18,2},{3,19},{19,3},{4,20},{20... | collective-permute-start | bytes 884744 | tf_op jit(solution)/shard_map/ppermute | solution.py:747
  106.4 30.2 %collective-permute-start.23 = (bf16[4,192,768]{2,1,0:T(8,128)(2,1)S(1)}, bf16[4,192,768]{2,1,0:T(8,128)(2,1)}, u32[]{:S(2)}, u32[]{:S(2)}) collective-permute-start(bf16[4,192,768]{2,1,0:T(8,128)(2,1)S(1)} %pad_maximum_fusion), channel_id=1, source_target_pairs={{16,0},{17,1},{18,16},{19,17},{20,4},{21,5},{22,20},{23,21},{24,8}... | collective-permute-start | bytes 3538952 | tf_op jit(solution)/shard_map/ppermute | solution.py:763
  107.7 28.9 %collective-permute-start.24 = (bf16[4,192,768]{2,1,0:T(8,128)(2,1)S(1)}, bf16[4,192,768]{2,1,0:T(8,128)(2,1)}, u32[]{:S(2)}, u32[]{:S(2)}) collective-permute-start(bf16[4,192,768]{2,1,0:T(8,128)(2,1)S(1)} %pad_maximum_fusion), channel_id=1, source_target_pairs={{16,2},{17,3},{18,18},{19,19},{20,6},{21,7},{22,22},{23,23},{24,10... | collective-permute-start | bytes 3538952 | tf_op jit(solution)/shard_map/ppermute | solution.py:763
  126.2 10.4 %collective-permute-start.15 = (bf16[256,768]{1,0:T(8,128)(2,1)S(1)}, bf16[256,768]{1,0:T(8,128)(2,1)S(1)}, u32[]{:S(2)}, u32[]{:S(2)}) collective-permute-start(bf16[256,768]{1,0:T(8,128)(2,1)S(1)} %get-tuple-element.367), channel_id=1, source_target_pairs={{0,1},{1,0},{2,3},{3,2},{4,5},{5,4},{6,7},{7,6},{8,9},{9,8},{10,11... | collective-permute-start | bytes 1179656 | tf_op jit(solution)/shard_map/ppermute | solution.py:751
  138.8 103.9 %all-gather.11.cloned.1.call-start = ((), (), s32[]{:S(2)}) async-start(), calls=%async_computation.7 | async-start | bytes 4423680 | tf_op jit(solution)/shard_map/all_gather | solution.py:775
  139.8 286.6 %reduce-scatter.5.cloned.1.call-start = ((), (), s32[]{:S(2)}) async-start(), calls=%async_computation.8 | async-start | bytes 4423680 | tf_op jit(solution)/shard_map/reduce_scatter | solution.py:779
  140.1 12.5 %collective-permute-start.18 = (bf16[256,768]{1,0:T(8,128)(2,1)}, bf16[256,768]{1,0:T(8,128)(2,1)S(1)}, u32[]{:S(2)}, u32[]{:S(2)}) collective-permute-start(bf16[256,768]{1,0:T(8,128)(2,1)} %get-tuple-element.366), channel_id=1, source_target_pairs={{0,1},{1,0},{2,3},{3,2},{4,5},{5,4},{6,7},{7,6},{8,9},{9,8},{10,11... | collective-permute-start | bytes 1179656 | tf_op jit(solution)/shard_map/ppermute | solution.py:751
  151.7 19.5 %collective-permute-start.17 = (bf16[256,768]{1,0:T(8,128)(2,1)S(1)}, bf16[256,768]{1,0:T(8,128)(2,1)S(1)}, u32[]{:S(2)}, u32[]{:S(2)}) collective-permute-start(bf16[256,768]{1,0:T(8,128)(2,1)S(1)} %get-tuple-element.192), channel_id=1, source_target_pairs={{0,1},{1,0},{2,3},{3,2},{4,5},{5,4},{6,7},{7,6},{8,9},{9,8},{10,11... | collective-permute-start | bytes 1179656 | tf_op jit(solution)/shard_map/ppermute | solution.py:751
  159.1 12.1 %collective-permute-start.19 = (bf16[256,768]{1,0:T(8,128)(2,1)S(1)}, bf16[256,768]{1,0:T(8,128)(2,1)S(1)}, u32[]{:S(2)}, u32[]{:S(2)}) collective-permute-start(bf16[256,768]{1,0:T(8,128)(2,1)S(1)} %get-tuple-element.194), channel_id=1, source_target_pairs={{0,1},{1,0},{2,3},{3,2},{4,5},{5,4},{6,7},{7,6},{8,9},{9,8},{10,11... | collective-permute-start | bytes 1179656 | tf_op jit(solution)/shard_map/ppermute | solution.py:751
  173.3 18.7 %collective-permute-start.21 = (bf16[512,768]{1,0:T(8,128)(2,1)S(1)}, bf16[512,768]{1,0:T(8,128)(2,1)S(1)}, u32[]{:S(2)}, u32[]{:S(2)}) collective-permute-start(bf16[512,768]{1,0:T(8,128)(2,1)S(1)} %get-tuple-element.348.slab0.rows), channel_id=1, source_target_pairs={{0,1},{1,0},{2,3},{3,2},{4,5},{5,4},{6,7},{7,6},{8,9},{9,8},{10,11... | collective-permute-start | bytes 2359304 | tf_op jit(solution)/shard_map/ppermute | solution.py:751
  174.3 21.2 %collective-permute-start.20 = (bf16[512,768]{1,0:T(8,128)(2,1)S(1)}, bf16[512,768]{1,0:T(8,128)(2,1)S(1)}, u32[]{:S(2)}, u32[]{:S(2)}) collective-permute-start(bf16[512,768]{1,0:T(8,128)(2,1)S(1)} %get-tuple-element.348.slab0.rows), channel_id=1, source_target_pairs={{0,16},{16,0},{1,17},{17,1},{2,18},{18,2},{3,19},{19,3},{4,20},{20... | collective-permute-start | bytes 2359304 | tf_op jit(solution)/shard_map/ppermute | solution.py:747
  194.1 30.8 %collective-permute-start.29 = (bf16[768,192]{1,0:T(8,128)(2,1)S(1)}, bf16[768,192]{1,0:T(8,128)(2,1)S(1)}, u32[]{:S(2)}, u32[]{:S(2)}) collective-permute-start(bf16[768,192]{1,0:T(8,128)(2,1)S(1)} %slice.81), channel_id=1, source_target_pairs={{0,1},{1,0},{2,3},{3,2},{4,5},{5,4},{6,7},{7,6},{8,9},{9,8},{10,11... | collective-permute-start | bytes 884744 | tf_op jit(solution)/shard_map/ppermute | solution.py:751
  195.3 32.8 %collective-permute-start.28 = (bf16[768,192]{1,0:T(8,128)(2,1)S(1)}, bf16[768,192]{1,0:T(8,128)(2,1)S(1)}, u32[]{:S(2)}, u32[]{:S(2)}) collective-permute-start(bf16[768,192]{1,0:T(8,128)(2,1)S(1)} %slice.81), channel_id=1, source_target_pairs={{0,16},{16,0},{1,17},{17,1},{2,18},{18,2},{3,19},{19,3},{4,20},{20... | collective-permute-start | bytes 884744 | tf_op jit(solution)/shard_map/ppermute | solution.py:747
  224.9 11.5 %collective-permute-start.30 = (bf16[768,192]{1,0:T(8,128)(2,1)S(1)}, bf16[768,192]{1,0:T(8,128)(2,1)S(1)}, u32[]{:S(2)}, u32[]{:S(2)}) collective-permute-start(bf16[768,192]{1,0:T(8,128)(2,1)S(1)} %collective-permute-done.29.out2), channel_id=1, source_target_pairs={{0,16},{16,0},{1,17},{17,1},{2,18},{18,2},{3,19},{19,3},{4,20},{20... | collective-permute-start | bytes 884744 | tf_op jit(solution)/shard_map/ppermute | solution.py:747
  242.7 14.2 %collective-permute-start.31 = (bf16[3,768,768]{2,1,0:T(8,128)(2,1)}, bf16[3,768,768]{2,1,0:T(8,128)(2,1)S(1)}, u32[]{:S(2)}, u32[]{:S(2)}) collective-permute-start(bf16[3,768,768]{2,1,0:T(8,128)(2,1)} %all-gather.11.cloned.1.call-done.first), channel_id=1, source_target_pairs={{0,16},{16,0},{1,17},{17,1},{2,18},{18,2},{3,19},{19,3},{4,20},{20... | collective-permute-start | bytes 10616840 | tf_op jit(solution)/shard_map/ppermute | solution.py:747
  244.8 12.0 %collective-permute-start.32 = (bf16[256,768]{1,0:T(8,128)(2,1)S(1)}, bf16[256,768]{1,0:T(8,128)(2,1)S(1)}, u32[]{:S(2)}, u32[]{:S(2)}) collective-permute-start(bf16[256,768]{1,0:T(8,128)(2,1)S(1)} %get-tuple-element.364), channel_id=1, source_target_pairs={{0,1},{1,0},{2,3},{3,2},{4,5},{5,4},{6,7},{7,6},{8,9},{9,8},{10,11... | collective-permute-start | bytes 1179656 | tf_op jit(solution)/shard_map/ppermute | solution.py:751
  245.8 18.7 %collective-permute-start.34 = (bf16[256,768]{1,0:T(8,128)(2,1)S(1)}, bf16[256,768]{1,0:T(8,128)(2,1)S(1)}, u32[]{:S(2)}, u32[]{:S(2)}) collective-permute-start(bf16[256,768]{1,0:T(8,128)(2,1)S(1)} %get-tuple-element.365), channel_id=1, source_target_pairs={{0,1},{1,0},{2,3},{3,2},{4,5},{5,4},{6,7},{7,6},{8,9},{9,8},{10,11... | collective-permute-start | bytes 1179656 | tf_op jit(solution)/shard_map/ppermute | solution.py:751
  263.4 19.1 %collective-permute-start.33 = (bf16[256,768]{1,0:T(8,128)(2,1)S(1)}, bf16[256,768]{1,0:T(8,128)(2,1)S(1)}, u32[]{:S(2)}, u32[]{:S(2)}) collective-permute-start(bf16[256,768]{1,0:T(8,128)(2,1)S(1)} %get-tuple-element.208), channel_id=1, source_target_pairs={{0,1},{1,0},{2,3},{3,2},{4,5},{5,4},{6,7},{7,6},{8,9},{9,8},{10,11... | collective-permute-start | bytes 1179656 | tf_op jit(solution)/shard_map/ppermute | solution.py:751
  268.8 13.7 %collective-permute-start.35 = (bf16[256,768]{1,0:T(8,128)(2,1)S(1)}, bf16[256,768]{1,0:T(8,128)(2,1)S(1)}, u32[]{:S(2)}, u32[]{:S(2)}) collective-permute-start(bf16[256,768]{1,0:T(8,128)(2,1)S(1)} %get-tuple-element.210), channel_id=1, source_target_pairs={{0,1},{1,0},{2,3},{3,2},{4,5},{5,4},{6,7},{7,6},{8,9},{9,8},{10,11... | collective-permute-start | bytes 1179656 | tf_op jit(solution)/shard_map/ppermute | solution.py:751
  270.3 25.8 %collective-permute-start.38 = (bf16[512,768]{1,0:T(8,128)(2,1)}, bf16[512,768]{1,0:T(8,128)(2,1)}, u32[]{:S(2)}, u32[]{:S(2)}) collective-permute-start(bf16[512,768]{1,0:T(8,128)(2,1)} %dynamic-slice_bitcast_fusion), channel_id=1, source_target_pairs={{0,0},{1,1},{2,16},{3,17},{16,2},{17,3},{18,18},{19,19},{4,4},{5,5... | collective-permute-start | bytes 2359304 | tf_op jit(solution)/shard_map/ppermute | solution.py:763
  287.9 27.3 %collective-permute-start.37 = (bf16[512,768]{1,0:T(8,128)(2,1)}, bf16[512,768]{1,0:T(8,128)(2,1)}, u32[]{:S(2)}, u32[]{:S(2)}) collective-permute-start(bf16[512,768]{1,0:T(8,128)(2,1)} %broadcast_select_fusion.4), channel_id=1, source_target_pairs={{0,16},{1,17},{2,0},{3,1},{16,18},{17,19},{18,2},{19,3},{4,20},{5,... | collective-permute-start | bytes 2359304 | tf_op jit(solution)/shard_map/ppermute | solution.py:763
  287.9 27.3 %collective-permute-start.36 = (bf16[512,768]{1,0:T(8,128)(2,1)}, bf16[512,768]{1,0:T(8,128)(2,1)}, u32[]{:S(2)}, u32[]{:S(2)}) collective-permute-start(bf16[512,768]{1,0:T(8,128)(2,1)} %get-tuple-element.344), channel_id=1, source_target_pairs={{0,0},{1,1},{2,16},{3,17},{16,2},{17,3},{18,18},{19,19},{4,4},{5,5... | collective-permute-start | bytes 2359304 | tf_op jit(solution)/shard_map/ppermute | solution.py:763
  301.0 14.3 %collective-permute-start.39 = (bf16[256,768]{1,0:T(8,128)(2,1)S(1)}, bf16[256,768]{1,0:T(8,128)(2,1)S(1)}, u32[]{:S(2)}, u32[]{:S(2)}) collective-permute-start(bf16[256,768]{1,0:T(8,128)(2,1)S(1)} %get-tuple-element.363), channel_id=1, source_target_pairs={{0,1},{1,0},{2,3},{3,2},{4,5},{5,4},{6,7},{7,6},{8,9},{9,8},{10,11... | collective-permute-start | bytes 1179656 | tf_op jit(solution)/shard_map/ppermute | solution.py:751
  302.1 16.2 %collective-permute-start.41 = (bf16[256,768]{1,0:T(8,128)(2,1)S(1)}, bf16[256,768]{1,0:T(8,128)(2,1)S(1)}, u32[]{:S(2)}, u32[]{:S(2)}) collective-permute-start(bf16[256,768]{1,0:T(8,128)(2,1)S(1)} %get-tuple-element.362), channel_id=1, source_target_pairs={{0,1},{1,0},{2,3},{3,2},{4,5},{5,4},{6,7},{7,6},{8,9},{9,8},{10,11... | collective-permute-start | bytes 1179656 | tf_op jit(solution)/shard_map/ppermute | solution.py:751
  325.5 20.1 %collective-permute-start.53 = (bf16[3,768,768]{2,1,0:T(8,128)(2,1)S(1)}, bf16[3,768,768]{2,1,0:T(8,128)(2,1)S(1)}, u32[]{:S(2)}, u32[]{:S(2)}) collective-permute-start(bf16[3,768,768]{2,1,0:T(8,128)(2,1)S(1)} %ffn_grads.4), channel_id=1, source_target_pairs={{0,16},{16,0},{1,17},{17,1},{2,18},{18,2},{3,19},{19,3},{4,20},{20... | collective-permute-start | bytes 10616840 | tf_op jit(solution)/shard_map/ppermute | solution.py:747
  325.6 12.0 %collective-permute-start.40 = (bf16[256,768]{1,0:T(8,128)(2,1)S(1)}, bf16[256,768]{1,0:T(8,128)(2,1)S(1)}, u32[]{:S(2)}, u32[]{:S(2)}) collective-permute-start(bf16[256,768]{1,0:T(8,128)(2,1)S(1)} %get-tuple-element.220), channel_id=1, source_target_pairs={{0,1},{1,0},{2,3},{3,2},{4,5},{5,4},{6,7},{7,6},{8,9},{9,8},{10,11... | collective-permute-start | bytes 1179656 | tf_op jit(solution)/shard_map/ppermute | solution.py:751
  326.8 18.8 %collective-permute-start.42 = (bf16[256,768]{1,0:T(8,128)(2,1)S(1)}, bf16[256,768]{1,0:T(8,128)(2,1)S(1)}, u32[]{:S(2)}, u32[]{:S(2)}) collective-permute-start(bf16[256,768]{1,0:T(8,128)(2,1)S(1)} %get-tuple-element.224), channel_id=1, source_target_pairs={{0,1},{1,0},{2,3},{3,2},{4,5},{5,4},{6,7},{7,6},{8,9},{9,8},{10,11... | collective-permute-start | bytes 1179656 | tf_op jit(solution)/shard_map/ppermute | solution.py:751
  351.4 184.1 %reduce-scatter.7.cloned.1.call-start = ((), (), s32[]{:S(2)}) async-start(), calls=%async_computation.9 | async-start | bytes 1474560 | tf_op jit(solution)/shard_map/reduce_scatter | solution.py:779
  361.0 10.7 %collective-permute-start.45 = (bf16[192,512]{1,0:T(8,128)(2,1)}, bf16[192,512]{1,0:T(8,128)(2,1)S(1)}, u32[]{:S(2)}, u32[]{:S(2)}) collective-permute-start(bf16[192,512]{1,0:T(8,128)(2,1)} %get-tuple-element.232), channel_id=1, source_target_pairs={{0,17},{1,16},{2,19},{3,18},{16,1},{17,0},{18,3},{19,2},{4,21},{5,... | collective-permute-start | bytes 589832 | tf_op jit(solution)/shard_map/ppermute | solution.py:763
  371.7 38.9 %collective-permute-start.46 = (bf16[192,768]{1,0:T(8,128)(2,1)}, bf16[192,768]{1,0:T(8,128)(2,1)S(1)}, u32[]{:S(2)}, u32[]{:S(2)}) collective-permute-start(bf16[192,768]{1,0:T(8,128)(2,1)} %get-tuple-element.238), channel_id=1, source_target_pairs={{0,16},{16,0},{1,17},{17,1},{2,18},{18,2},{3,19},{19,3},{4,20},{20... | collective-permute-start | bytes 884744 | tf_op jit(solution)/shard_map/ppermute | solution.py:747
  372.4 38.3 %collective-permute-start.47 = (bf16[192,768]{1,0:T(8,128)(2,1)}, bf16[192,768]{1,0:T(8,128)(2,1)S(1)}, u32[]{:S(2)}, u32[]{:S(2)}) collective-permute-start(bf16[192,768]{1,0:T(8,128)(2,1)} %get-tuple-element.239), channel_id=1, source_target_pairs={{0,1},{1,0},{2,3},{3,2},{4,5},{5,4},{6,7},{7,6},{8,9},{9,8},{10,11... | collective-permute-start | bytes 884744 | tf_op jit(solution)/shard_map/ppermute | solution.py:751
  372.9 37.8 %collective-permute-start.48 = (bf16[192,768]{1,0:T(8,128)(2,1)}, bf16[192,768]{1,0:T(8,128)(2,1)S(1)}, u32[]{:S(2)}, u32[]{:S(2)}) collective-permute-start(bf16[192,768]{1,0:T(8,128)(2,1)} %get-tuple-element.240), channel_id=1, source_target_pairs={{0,17},{1,16},{2,19},{3,18},{16,1},{17,0},{18,3},{19,2},{4,21},{5,... | collective-permute-start | bytes 884744 | tf_op jit(solution)/shard_map/ppermute | solution.py:763
  425.9 19.9 %collective-permute-start.51 = (bf16[512,768]{1,0:T(8,128)(2,1)S(1)}, bf16[512,768]{1,0:T(8,128)(2,1)S(1)}, u32[]{:S(2)}, u32[]{:S(2)}) collective-permute-start(bf16[512,768]{1,0:T(8,128)(2,1)S(1)} %add_convert_fusion.2), channel_id=1, source_target_pairs={{0,1},{1,0},{2,3},{3,2},{4,5},{5,4},{6,7},{7,6},{8,9},{9,8},{10,11... | collective-permute-start | bytes 2359304 | tf_op jit(solution)/shard_map/ppermute | solution.py:751
  426.4 40.7 %collective-permute-start.54 = (bf16[3,192,768]{2,1,0:T(8,128)(2,1)}, bf16[3,192,768]{2,1,0:T(8,128)(2,1)}, u32[]{:S(2)}, u32[]{:S(2)}) collective-permute-start(bf16[3,192,768]{2,1,0:T(8,128)(2,1)} %reduce-scatter.5.cloned.1.call-done), channel_id=1, source_target_pairs={{2,16},{3,17},{18,18},{19,19},{6,20},{7,21},{22,22},{23,23},{10,24... | collective-permute-start | bytes 2654216 | tf_op jit(solution)/shard_map/ppermute | solution.py:763
  428.1 39.0 %collective-permute-start.55 = (bf16[3,192,768]{2,1,0:T(8,128)(2,1)}, bf16[3,192,768]{2,1,0:T(8,128)(2,1)}, u32[]{:S(2)}, u32[]{:S(2)}) collective-permute-start(bf16[3,192,768]{2,1,0:T(8,128)(2,1)} %reduce-scatter.5.cloned.1.call-done), channel_id=1, source_target_pairs={{0,16},{1,17},{16,18},{17,19},{4,20},{5,21},{20,22},{21,23},{8,24}... | collective-permute-start | bytes 2654216 | tf_op jit(solution)/shard_map/ppermute | solution.py:763
  452.7 14.4 %collective-permute-start.52 = (bf16[256,768]{1,0:T(8,128)(2,1)S(1)}, bf16[256,768]{1,0:T(8,128)(2,1)S(1)}, u32[]{:S(2)}, u32[]{:S(2)}) collective-permute-start(bf16[256,768]{1,0:T(8,128)(2,1)S(1)} %get-tuple-element.361), channel_id=1, source_target_pairs={{0,1},{1,0},{2,3},{3,2},{4,5},{5,4},{6,7},{7,6},{8,9},{9,8},{10,11... | collective-permute-start | bytes 1179656 | tf_op jit(solution)/shard_map/ppermute | solution.py:751
  453.2 20.8 %collective-permute-start.57 = (bf16[256,768]{1,0:T(8,128)(2,1)S(1)}, bf16[256,768]{1,0:T(8,128)(2,1)S(1)}, u32[]{:S(2)}, u32[]{:S(2)}) collective-permute-start(bf16[256,768]{1,0:T(8,128)(2,1)S(1)} %get-tuple-element.360), channel_id=1, source_target_pairs={{0,1},{1,0},{2,3},{3,2},{4,5},{5,4},{6,7},{7,6},{8,9},{9,8},{10,11... | collective-permute-start | bytes 1179656 | tf_op jit(solution)/shard_map/ppermute | solution.py:751
  486.3 21.3 %collective-permute-start.72 = (bf16[3,768,768]{2,1,0:T(8,128)(2,1)}, bf16[3,768,768]{2,1,0:T(8,128)(2,1)}, u32[]{:S(2)}, u32[]{:S(2)}) collective-permute-start(bf16[3,768,768]{2,1,0:T(8,128)(2,1)} %ffn_grads.6), channel_id=1, source_target_pairs={{0,16},{16,0},{1,17},{17,1},{2,18},{18,2},{3,19},{19,3},{4,20},{20... | collective-permute-start | bytes 10616840 | tf_op jit(solution)/shard_map/ppermute | solution.py:747
  486.4 114.3 %reduce-scatter.11.cloned.1.call-start = ((), (), s32[]{:S(2)}) async-start(), calls=%async_computation.11 | async-start | bytes 4423680 | tf_op jit(solution)/shard_map/reduce_scatter | solution.py:779
  486.5 12.2 %collective-permute-start.56 = (bf16[256,768]{1,0:T(8,128)(2,1)}, bf16[256,768]{1,0:T(8,128)(2,1)S(1)}, u32[]{:S(2)}, u32[]{:S(2)}) collective-permute-start(bf16[256,768]{1,0:T(8,128)(2,1)} %copy-done.79), channel_id=1, source_target_pairs={{0,1},{1,0},{2,3},{3,2},{4,5},{5,4},{6,7},{7,6},{8,9},{9,8},{10,11... | collective-permute-start | bytes 1179656 | tf_op jit(solution)/shard_map/ppermute | solution.py:751
  487.0 19.7 %collective-permute-start.58 = (bf16[256,768]{1,0:T(8,128)(2,1)}, bf16[256,768]{1,0:T(8,128)(2,1)S(1)}, u32[]{:S(2)}, u32[]{:S(2)}) collective-permute-start(bf16[256,768]{1,0:T(8,128)(2,1)} %copy-done.80), channel_id=1, source_target_pairs={{0,1},{1,0},{2,3},{3,2},{4,5},{5,4},{6,7},{7,6},{8,9},{9,8},{10,11... | collective-permute-start | bytes 1179656 | tf_op jit(solution)/shard_map/ppermute | solution.py:751
  525.0 96.2 %reduce-scatter.9.cloned.1.call-start = ((), (), s32[]{:S(2)}) async-start(), calls=%async_computation.10 | async-start | bytes 1474560 | tf_op jit(solution)/shard_map/reduce_scatter | solution.py:779
  533.7 11.2 %collective-permute-start.61 = (bf16[192,512]{1,0:T(8,128)(2,1)}, bf16[192,512]{1,0:T(8,128)(2,1)S(1)}, u32[]{:S(2)}, u32[]{:S(2)}) collective-permute-start(bf16[192,512]{1,0:T(8,128)(2,1)} %get-tuple-element.279), channel_id=1, source_target_pairs={{0,17},{1,16},{2,19},{3,18},{16,1},{17,0},{18,3},{19,2},{4,21},{5,... | collective-permute-start | bytes 589832 | tf_op jit(solution)/shard_map/ppermute | solution.py:763
  535.5 48.6 %collective-permute-start.65 = (bf16[1,192,768]{2,1,0:T(8,128)(2,1)}, bf16[1,192,768]{2,1,0:T(8,128)(2,1)S(1)}, u32[]{:S(2)}, u32[]{:S(2)}) collective-permute-start(bf16[1,192,768]{2,1,0:T(8,128)(2,1)} %bitcast.149), channel_id=1, source_target_pairs={{2,16},{3,17},{18,18},{19,19},{6,20},{7,21},{22,22},{23,23},{10,24... | collective-permute-start | bytes 884744 | tf_op jit(solution)/shard_map/ppermute | solution.py:763
  536.1 48.0 %collective-permute-start.66 = (bf16[1,192,768]{2,1,0:T(8,128)(2,1)}, bf16[1,192,768]{2,1,0:T(8,128)(2,1)S(1)}, u32[]{:S(2)}, u32[]{:S(2)}) collective-permute-start(bf16[1,192,768]{2,1,0:T(8,128)(2,1)} %bitcast.150), channel_id=1, source_target_pairs={{0,16},{1,17},{16,18},{17,19},{4,20},{5,21},{20,22},{21,23},{8,24}... | collective-permute-start | bytes 884744 | tf_op jit(solution)/shard_map/ppermute | solution.py:763
  544.9 39.2 %collective-permute-start.62 = (bf16[192,768]{1,0:T(8,128)(2,1)}, bf16[192,768]{1,0:T(8,128)(2,1)S(1)}, u32[]{:S(2)}, u32[]{:S(2)}) collective-permute-start(bf16[192,768]{1,0:T(8,128)(2,1)} %get-tuple-element.285), channel_id=1, source_target_pairs={{0,16},{16,0},{1,17},{17,1},{2,18},{18,2},{3,19},{19,3},{4,20},{20... | collective-permute-start | bytes 884744 | tf_op jit(solution)/shard_map/ppermute | solution.py:747
  545.6 38.6 %collective-permute-start.63 = (bf16[192,768]{1,0:T(8,128)(2,1)}, bf16[192,768]{1,0:T(8,128)(2,1)S(1)}, u32[]{:S(2)}, u32[]{:S(2)}) collective-permute-start(bf16[192,768]{1,0:T(8,128)(2,1)} %get-tuple-element.286), channel_id=1, source_target_pairs={{0,1},{1,0},{2,3},{3,2},{4,5},{5,4},{6,7},{7,6},{8,9},{9,8},{10,11... | collective-permute-start | bytes 884744 | tf_op jit(solution)/shard_map/ppermute | solution.py:751
  545.8 38.3 %collective-permute-start.64 = (bf16[192,768]{1,0:T(8,128)(2,1)}, bf16[192,768]{1,0:T(8,128)(2,1)S(1)}, u32[]{:S(2)}, u32[]{:S(2)}) collective-permute-start(bf16[192,768]{1,0:T(8,128)(2,1)} %get-tuple-element.287), channel_id=1, source_target_pairs={{0,17},{1,16},{2,19},{3,18},{16,1},{17,0},{18,3},{19,2},{4,21},{5,... | collective-permute-start | bytes 884744 | tf_op jit(solution)/shard_map/ppermute | solution.py:763
  596.4 26.4 %collective-permute-start.67 = (bf16[512,768]{1,0:T(8,128)(2,1)}, bf16[512,768]{1,0:T(8,128)(2,1)}, u32[]{:S(2)}, u32[]{:S(2)}) collective-permute-start(bf16[512,768]{1,0:T(8,128)(2,1)} %get-tuple-element.294), channel_id=1, source_target_pairs={{0,16},{16,0},{1,17},{17,1},{2,18},{18,2},{3,19},{19,3},{4,20},{20... | collective-permute-start | bytes 2359304 | tf_op jit(solution)/shard_map/ppermute | solution.py:747
  600.4 23.9 %collective-permute-start.69 = (bf16[512,768]{1,0:T(8,128)(2,1)}, bf16[512,768]{1,0:T(8,128)(2,1)}, u32[]{:S(2)}, u32[]{:S(2)}) collective-permute-start(bf16[512,768]{1,0:T(8,128)(2,1)} %add_convert_fusion.1), channel_id=1, source_target_pairs={{0,1},{1,0},{2,3},{3,2},{4,5},{5,4},{6,7},{7,6},{8,9},{9,8},{10,11... | collective-permute-start | bytes 2359304 | tf_op jit(solution)/shard_map/ppermute | solution.py:751
  600.7 25.3 %collective-permute-start.73 = (bf16[3,192,768]{2,1,0:T(8,128)(2,1)}, bf16[3,192,768]{2,1,0:T(8,128)(2,1)}, u32[]{:S(2)}, u32[]{:S(2)}) collective-permute-start(bf16[3,192,768]{2,1,0:T(8,128)(2,1)} %reduce-scatter.11.cloned.1.call-done), channel_id=1, source_target_pairs={{0,0},{1,1},{16,2},{17,3},{4,4},{5,5},{20,6},{21,7},{8,8},{9,9},{2... | collective-permute-start | bytes 2654216 | tf_op jit(solution)/shard_map/ppermute | solution.py:763
  608.9 17.1 %collective-permute-start.74 = (bf16[3,192,768]{2,1,0:T(8,128)(2,1)}, bf16[3,192,768]{2,1,0:T(8,128)(2,1)}, u32[]{:S(2)}, u32[]{:S(2)}) collective-permute-start(bf16[3,192,768]{2,1,0:T(8,128)(2,1)} %reduce-scatter.11.cloned.1.call-done), channel_id=1, source_target_pairs={{2,0},{3,1},{18,2},{19,3},{6,4},{7,5},{22,6},{23,7},{10,8},{11,9},... | collective-permute-start | bytes 2654216 | tf_op jit(solution)/shard_map/ppermute | solution.py:763
  621.1 11.8 %collective-permute-start.70 = (bf16[1,192,768]{2,1,0:T(8,128)(2,1)}, bf16[1,192,768]{2,1,0:T(8,128)(2,1)S(1)}, u32[]{:S(2)}, u32[]{:S(2)}) collective-permute-start(bf16[1,192,768]{2,1,0:T(8,128)(2,1)} %bitcast.147), channel_id=1, source_target_pairs={{0,0},{1,1},{16,2},{17,3},{4,4},{5,5},{20,6},{21,7},{8,8},{9,9},{2... | collective-permute-start | bytes 884744 | tf_op jit(solution)/shard_map/ppermute | solution.py:763
  642.8 18.2 %collective-permute-start.75 = (bf16[512,768]{1,0:T(8,128)(2,1)S(1)}, bf16[512,768]{1,0:T(8,128)(2,1)S(1)}, u32[]{:S(2)}, u32[]{:S(2)}) collective-permute-start(bf16[512,768]{1,0:T(8,128)(2,1)S(1)} %get-tuple-element.354), channel_id=1, source_target_pairs={{0,0},{1,1},{2,16},{3,17},{16,2},{17,3},{18,18},{19,19},{4,4},{5,5... | collective-permute-start | bytes 2359304 | tf_op jit(solution)/shard_map/ppermute | solution.py:763
  643.5 21.7 %collective-permute-start.76 = (bf16[512,768]{1,0:T(8,128)(2,1)S(1)}, bf16[512,768]{1,0:T(8,128)(2,1)}, u32[]{:S(2)}, u32[]{:S(2)}) collective-permute-start(bf16[512,768]{1,0:T(8,128)(2,1)S(1)} %get-tuple-element.355), channel_id=1, source_target_pairs={{0,16},{1,17},{2,0},{3,1},{16,18},{17,19},{18,2},{19,3},{4,20},{5,... | collective-permute-start | bytes 2359304 | tf_op jit(solution)/shard_map/ppermute | solution.py:763
  (184 other events, 1657.2 us)
Sparse Core Ops, SparseCore 0:
  26.8 33.2 all-gather.4
  62.2 69.0 all-gather.6
  138.9 30.0 all-gather.8
  171.1 69.0 all-gather.10
  351.5 63.2 reduce-scatter.4
  486.5 25.4 reduce-scatter.6
  525.1 62.5 reduce-scatter.10
  595.3 25.7 reduce-scatter.8
